TPU v7x, 32 devices: a whole 2x2x4 slice. The times are simulated.
32 devices in a mesh: group: 2 (over x), ep: 16 (over z, y, core).
Axes of the slice: x: 2, y: 2, z: 4, core: 2. Of those that a mesh axis runs over, the one named last changes fastest.
Arguments:
- hidden_rows: bfloat16 [256, 7168], P(('group', 'ep')), parts along dimension 0, may hold values from -6 to 6
- group_ids: int32 [256, 2], P(('group', 'ep')), parts along dimension 0, may hold values from 0 to 1, all different within a row; in each aligned block of 8 rows (0 to 7, 8 to 15, ...) at most 8 rows name the same one
- route_gates: float32 [256, 2], P(('group', 'ep')), parts along dimension 0, may hold values from 0.1 to 1
- w_gate: bfloat16 [16, 7168, 128], P('ep'), may hold values from -0.0625 to 0.0625
- w_up: bfloat16 [16, 7168, 128], P('ep'), may hold values from -0.0625 to 0.0625
- w_down: bfloat16 [16, 128, 7168], P('ep'), may hold values from -0.1875 to 0.1875
- queries: bfloat16 [128, 128, 576], P(('group', 'ep')), parts along dimension 0, may hold values from -24 to 24
- new_latent: bfloat16 [128, 576], P(('group', 'ep')), parts along dimension 0, may hold values from -4 to 4
- latent_cache: bfloat16 [128, 1024, 576], P(('group', 'ep')), parts along dimension 0, may hold values from -4 to 4
- cache_lengths: int32 [128], P('group'), parts along dimension 0, may hold values from 2 to 1024, as said below
- moved_slot: int32 [32], P('group'), parts along dimension 0, may hold values from 0 to 3, as said below
Outputs:
- moe_out: bfloat16 [256, 7168], P(('group', 'ep')), parts along dimension 0
- attn_out: bfloat16 [128, 128, 512], P(('group', 'ep')), parts along dimension 0
There are 2 independent parts, one for each index of `group`. A program takes and returns all parts, laid end to end along the dimension named above; an argument that names none is the same for every part. Nothing has to cross between parts.
Inputs may be any that keep to these rules, and one draw needn't show every extreme that they name: `group_ids`: each row names 2 different groups; no group is named by more than 8 rows of one device. The request in slot moved_slot[d] of device d moves to device d + 1 (the last to the first) and takes slot moved_slot[d + 1] there. `cache_lengths`: some request holds 1024 positions in every draw.
All inputs are finite; a program needn't handle non-finite values.
Results may differ from a plain program's by a relative error of at most 0.0065.
Values may be sent and summed in bfloat16 or wider, within the bound.
No kernel may reach another device: no remote copies, remote signals or barrier semaphores. Data moves between devices by JAX's collectives and lax.ppermute only.
A program may use at most 128 MiB of HBM per device.

v0:
```python
import math

import jax
import jax.numpy as jnp
from jax import lax
from jax.sharding import PartitionSpec as P

NOPE = 512
SPLIT = 8


score_scale = 1.0 / math.sqrt(192.0)


def shifted(value, axis, steps):
    count = lax.axis_size(axis)
    pairs = [(source, (source + steps) % count) for source in range(count)]
    return lax.ppermute(value, axis, pairs)


def attend(query, own_key, keys, valid):
    scores = (
        jnp.einsum("rhl,rcl->rhc", query, keys, preferred_element_type=jnp.float32) * score_scale
    )
    own_score = (
        jnp.einsum("rhl,rl->rh", query, own_key, preferred_element_type=jnp.float32) * score_scale
    )
    live_mask = jnp.arange(keys.shape[1], dtype=jnp.int32)[None, None, :] < valid[:, None, None]
    scores = jnp.where(live_mask, scores, -jnp.inf)
    top_score = jnp.maximum(jnp.max(scores, axis=2), own_score)
    raised = jnp.exp(scores - top_score[:, :, None])
    raised_own = jnp.exp(own_score - top_score)
    totals = jnp.sum(raised, axis=2) + raised_own
    weights = (raised / totals[:, :, None]).astype(jnp.bfloat16)
    weight_own = (raised_own / totals).astype(jnp.bfloat16)
    mixed = jnp.einsum(
        "rhc,rcn->rhn", weights, keys[:, :, :NOPE], preferred_element_type=jnp.float32
    )
    mixed = mixed + jnp.einsum(
        "rh,rn->rhn", weight_own, own_key[:, :NOPE], preferred_element_type=jnp.float32
    )
    return mixed.astype(jnp.bfloat16)


def expert_rows(row_block, w_gate, w_up, w_down):
    flat_rows = row_block.reshape(-1, row_block.shape[-1])
    gate_part = jnp.dot(flat_rows, w_gate[0], preferred_element_type=jnp.float32)
    up_part = jnp.dot(flat_rows, w_up[0], preferred_element_type=jnp.float32)
    activated = (jax.nn.silu(gate_part) * up_part).astype(jnp.bfloat16)
    projected = jnp.dot(activated, w_down[0], preferred_element_type=jnp.float32)
    return projected.reshape(row_block.shape[:-1] + (projected.shape[-1],))


def per_device(
    hidden_rows,
    group_ids,
    route_gates,
    w_gate,
    w_up,
    w_down,
    queries,
    new_latent,
    latent_cache,
    cache_lengths,
    moved_slot,
):
    tokens_here = hidden_rows.shape[0]
    model_width = hidden_rows.shape[1]
    groups = lax.axis_size("ep") // SPLIT
    group_iota = jnp.arange(groups, dtype=jnp.int32)
    chosen = group_ids[:, :, None] == group_iota[None, None, :]
    member_of = jnp.sum(chosen.astype(jnp.int32), axis=1)
    weight_of = jnp.sum(jnp.where(chosen, route_gates[:, :, None], 0.0), axis=1)
    before = jnp.cumsum(member_of, axis=0) - member_of
    slot_iota = jnp.arange(tokens_here, dtype=jnp.int32)
    placed = (member_of[:, :, None] == 1) & (before[:, :, None] == slot_iota[None, None, :])
    outgoing = jnp.einsum(
        "tgc,td->gcd", placed.astype(jnp.bfloat16), hidden_rows, preferred_element_type=jnp.float32
    ).astype(jnp.bfloat16)
    combine_map = jnp.where(placed, weight_of[:, :, None], 0.0).reshape(
        tokens_here, groups * tokens_here
    )
    copies = jnp.repeat(outgoing, SPLIT, axis=0)
    returned = lax.all_to_all(
        expert_rows(
            lax.all_to_all(copies, "ep", split_axis=0, concat_axis=0, tiled=True),
            w_gate,
            w_up,
            w_down,
        ),
        "ep",
        split_axis=0,
        concat_axis=0,
        tiled=True,
    )
    results = jnp.sum(returned.reshape(groups, SPLIT, tokens_here, model_width), axis=1)
    flat_results = results.reshape(groups * tokens_here, model_width)
    mixed_rows = jnp.dot(
        combine_map,
        flat_results,
        precision=lax.Precision.HIGHEST,
        preferred_element_type=jnp.float32,
    )
    moe_out = mixed_rows.astype(jnp.bfloat16)
    requests = latent_cache.shape[0]
    rank_count = lax.axis_size("ep")
    position = lax.axis_index("ep")
    previous = (position + rank_count - 1) % rank_count
    leaving = lax.dynamic_index_in_dim(moved_slot, position, 0, keepdims=False)
    arriving = lax.dynamic_index_in_dim(moved_slot, previous, 0, keepdims=False)
    own_lengths = lax.dynamic_slice_in_dim(cache_lengths, position * requests, requests)
    outgoing_cache = lax.dynamic_index_in_dim(latent_cache, leaving, 0, keepdims=True)
    incoming_cache = shifted(outgoing_cache, "ep", 1)
    incoming_length = lax.dynamic_index_in_dim(
        cache_lengths, previous * requests + arriving, 0, keepdims=True
    )
    cache_now = lax.dynamic_update_slice_in_dim(latent_cache, incoming_cache, leaving, 0)
    lengths_now = lax.dynamic_update_slice_in_dim(own_lengths, incoming_length, leaving, 0)
    attn_out = attend(queries, new_latent, cache_now, lengths_now)
    return (moe_out, attn_out)


def solution(mesh):
    placed = (
        P(("group", "ep"), None),
        P(("group", "ep"), None),
        P(("group", "ep"), None),
        P("ep", None, None),
        P("ep", None, None),
        P("ep", None, None),
        P(("group", "ep"), None, None),
        P(("group", "ep"), None),
        P(("group", "ep"), None, None),
        P("group"),
        P("group"),
    )
    return jax.shard_map(
        per_device,
        mesh=mesh,
        in_specs=placed,
        out_specs=(P(("group", "ep"), None), P(("group", "ep"), None, None)),
        check_vma=False,
    )
```

profile of v0, /device:TPU:16, one launch (start us, length us, event | category | flops | bytes accessed | tf_op | source)
XLA Modules:
  0.0 172.9 jit_solution(9880552579500527174)
XLA Ops:
  0.6 0.8 convert_reduce_fusion
  1.5 0.2 reduce_window_sum.11
  1.7 1.2 convolution_convert_fusion
  2.9 0.2 broadcast_in_dim.54
  3.1 48.1 %all_to_all.10 = bf16[16,8,7168]{2,1,0:T(8,128)(2,1)S(1)} all-to-all(bf16[16,8,7168]{2,1,0:T(8,128)(2,1)S(1)} %bitcast.64), channel_id=1, replica_groups=mesh['group'=2,'ep'=16] {'ep'}, dimensions={0} | all-to-all | bytes 3670016 | tf_op jit(solution)/shard_map/all_to_all | solution.py:86
  51.2 1.3 copy-done.1
  52.4 0.6 fusion.8
  53.1 5.1 %fusion.4 = f32[16,8,7168]{2,1,0:T(8,128)} fusion(bf16[1,128,7168]{2,1,0:T(8,128)(2,1)S(1)} %copy-done, bf16[1,7168,128]{2,1,0:T(8,128)(2,1)} %param.15, bf16[16,8,7168]{2,1,0:T(8,128)(2,1)} %copy-done.1, f32[128,128]{1,0:T(8,128)S(1)} %fusion.8), kind=kOutput, calls=%fused_computation.11 | convolution fusion | flops 469860352 | bytes 9240576 | tf_op jit(solution)/shard_map/dot_general | solution.py:50
  58.2 5.3 %all-to-all-start.1 = ((f32[16,8,7168]{2,1,0:T(8,128)}), f32[16,8,7168]{2,1,0:T(8,128)}, u32[]{:S(2)}, u32[]{:S(2)}) async-start(f32[16,8,7168]{2,1,0:T(8,128)} %fusion.4), calls=%async_computation.1 | async-start | bytes 7340032 | tf_op jit(solution)/shard_map/all_to_all | solution.py:84
  63.5 0.6 fusion.68
  66.1 1.4 constant_dynamic-slice_fusion
  67.5 0.2 collective-permute-start
  67.7 7.7 %copy.28 = bf16[4,1024,576]{2,1,0:T(8,128)(2,1)} copy(bf16[4,1024,576]{1,2,0:T(8,128)(2,1)} %param.19) | data formatting | bytes 9437184 | tf_op args[8]
  76.0 0.1 dynamic_slice.18
  76.1 0.2 dynamic-slice_dynamic-update-slice_fusion
  76.4 1.3 fusion.50
  77.6 80.0 %collective-permute-done = bf16[1,1024,576]{1,2,0:T(8,128)(2,1)} collective-permute-done((bf16[1,1024,576]{1,2,0:T(8,128)(2,1)S(1)}, bf16[1,1024,576]{1,2,0:T(8,128)(2,1)}, u32[]{:S(2)}, u32[]{:S(2)}) %collective-permute-start) | collective-permute-done | bytes 1179680 | tf_op jit(solution)/shard_map/ppermute | solution.py:18
  157.6 1.7 copy.29
  159.3 1.2 constant_dynamic-update-slice_fusion
  160.5 4.8 %bitcast_reduce_fusion.1 = (f32[4,128]{1,0:T(4,128)S(1)}, f32[4,1024,128]{2,1,0:T(8,128)S(1)}) fusion(pred[4,1024]{1,0:T(4,128)(4,1)S(1)} %iota_compare_fusion, bf16[4,1024,576]{2,1,0:T(8,128)(2,1)} %constant_dynamic-update-slice_fusion, bf16[4,128,576]{1,2,0:T(8,128)(2,1)S(1)} %copy-done.4), kind=kOutput, calls=%fused_computation.7 | convolution fusion | flops 605552128 | bytes 7411712 | tf_op jit(solution)/shard_map/rhl,rcl->rhc/dot_general | solution.py:23
  165.4 0.8 fusion.12
  166.2 3.3 %fusion.16 = bf16[4,128,512]{2,1,0:T(8,128)(2,1)} fusion(bf16[4,1024,576]{2,1,0:T(8,128)(2,1)S(1)} %copy-done.2, f32[4,1024,128]{2,1,0:T(8,128)S(1)} %get-tuple-element.7, f32[4,128]{1,0:T(4,128)S(1)} %get-tuple-element.3, f32[4,128]{1,0:T(4,128)S(1)} %multiply_maximum_fusion, pred[4,1024]{1,0:T(4,128)(4,1)S(1)} %iota_compare_fusion, ...), kind=kOutput, calls=%fused_computation.21 | convolution fusion | flops 540278784 | bytes 6834176 | tf_op jit(solution)/shard_map/rhc,rcn->rhn/dot_general | solution.py:36
  169.5 2.3 %bitcast_reduce_fusion = f32[2,8,7168]{2,1,0:T(8,128)S(1)} fusion(f32[16,8,7168]{2,1,0:T(8,128)} %all-to-all-done.1), kind=kLoop, calls=%fused_computation.5 | loop fusion | flops 802816 | bytes 4128768 | tf_op jit(solution)/shard_map/reduce_sum | solution.py:96
  171.8 1.1 fusion
  (27 shorter events, 0.2 us)
Async XLA Ops:
  0.6 52.4 %copy-start = (bf16[1,128,7168]{2,1,0:T(8,128)(2,1)S(1)}, bf16[1,128,7168]{2,1,0:T(8,128)(2,1)}, u32[]{:S(2)}) copy-start(bf16[1,128,7168]{2,1,0:T(8,128)(2,1)} %param.16) | copy-start | bytes 5505028
  3.1 49.4 %copy-start.3 = (bf16[1,7168,128]{2,1,0:T(8,128)(2,1)S(1)}, bf16[1,7168,128]{2,1,0:T(8,128)(2,1)}, u32[]{:S(2)}) copy-start(bf16[1,7168,128]{2,1,0:T(8,128)(2,1)} %param.14) | copy-start | bytes 5505028
  51.2 1.3 copy-start.1
  58.2 5.3 %copy-start.7 = (s32[16]{0:T(128)S(1)}, s32[16]{0:T(128)}, u32[]{:S(2)}) copy-start(s32[16]{0:T(128)} %param.21) | copy-start | bytes 196
  58.2 111.3 %all-to-all-start.1 = ((f32[16,8,7168]{2,1,0:T(8,128)}), f32[16,8,7168]{2,1,0:T(8,128)}, u32[]{:S(2)}, u32[]{:S(2)}) async-start(f32[16,8,7168]{2,1,0:T(8,128)} %fusion.4), calls=%async_computation.1 | async-start | bytes 7340032 | tf_op jit(solution)/shard_map/all_to_all | solution.py:84
  67.4 8.6 %copy-start.9 = (s32[64]{0:T(128)S(1)}, s32[64]{0:T(128)}, u32[]{:S(2)}) copy-start(s32[64]{0:T(128)} %param.20) | copy-start | bytes 772
  67.4 8.8 %copy-start.6 = (s32[8,2]{0,1:T(2,128)S(1)}, s32[8,2]{0,1:T(2,128)}, u32[]{:S(2)}) copy-start(s32[8,2]{0,1:T(2,128)} %param.12) | copy-start | bytes 196
  67.4 8.8 %copy-start.8 = (f32[8,2]{0,1:T(2,128)S(1)}, f32[8,2]{0,1:T(2,128)}, u32[]{:S(2)}) copy-start(f32[8,2]{0,1:T(2,128)} %param.13) | copy-start | bytes 196
  67.5 8.9 %copy-start.5 = (bf16[4,576]{1,0:T(4,128)(2,1)S(1)}, bf16[4,576]{1,0:T(4,128)(2,1)}, u32[]{:S(2)}) copy-start(bf16[4,576]{1,0:T(4,128)(2,1)} %param.18) | copy-start | bytes 13828
  67.5 90.1 %collective-permute-start = (bf16[1,1024,576]{1,2,0:T(8,128)(2,1)S(1)}, bf16[1,1024,576]{1,2,0:T(8,128)(2,1)}, u32[]{:S(2)}, u32[]{:S(2)}) collective-permute-start(bf16[1,1024,576]{1,2,0:T(8,128)(2,1)S(1)} %constant_dynamic-slice_fusion), channel_id=1, source_target_pairs={{0,1},{1,2},{2,3},{3,4},{4,5},{5,6},{6,7},{7,8},{8,9},{9,10},{10,1... | collective-permute-start | bytes 3538952 | tf_op jit(solution)/shard_map/ppermute | solution.py:18
  159.3 1.2 copy-start.4
  160.5 5.7 %copy-start.2 = (bf16[4,1024,576]{2,1,0:T(8,128)(2,1)S(1)}, bf16[4,1024,576]{2,1,0:T(8,128)(2,1)}, u32[]{:S(2)}) copy-start(bf16[4,1024,576]{2,1,0:T(8,128)(2,1)} %constant_dynamic-update-slice_fusion) | copy-start | bytes 14155780
where the time goes:
time: 174 us; the launch traced here: 173 us
  waiting for transfers between devices  80 us (46%)
  blocking collectives  48.1 us (28%)
  matrix products  17.5 us (10%)
  local copies, waits for them, and re-layouts  14.2 us (8%)
  starting transfers between devices  5.51 us (3%)
  other arithmetic  4.26 us (2%)
  between operations  3.39 us (2%)
    ppermute x1, waiting for transfers between devices, shifted(): return lax.ppermute(value, axis, pairs)  80 us
    all_to_all x1, blocking collectives, per_device(): lax.all_to_all(copies, 'ep', split_axis=0, concat_axis=0, tiled=True)  48.1 us
    unnamed x21, local copies, waits for them, and re-layouts  9 us
    all_to_all x1, starting transfers between devices, per_device(): lax.all_to_all(expert_rows(lax.all_to_all(copies, 'ep', split_axis=0, con...  5.3 us
    dot_general x1, matrix products, expert_rows(): jnp.dot(activated, w_down[0], preferred_element_type=jnp.float32)  5.13 us
    dot_general x1, matrix products, attend(): jnp.einsum('rhl,rcl->rhc', query, keys, preferred_element_type=jnp.float32)  4.83 us
  transfers between devices with their start and end apart: 2, of which 1 were waited for; matrix products, arithmetic and copies ran while one was open for 13% of the time, Pallas kernels for 0%

commit v1 on v0

v1 whole, which is shorter than its diff:
```python
import functools
import math

import jax
import jax.numpy as jnp
from jax import lax
from jax.experimental import pallas as pl
from jax.experimental.pallas import tpu as pltpu
from jax.sharding import PartitionSpec as P

NOPE = 512
SPLIT = 8
LANES = 128

score_scale = 1.0 / math.sqrt(192.0)


def shifted(value, axis, steps):
    count = lax.axis_size(axis)
    pairs = [(source, (source + steps) % count) for source in range(count)]
    return lax.ppermute(value, axis, pairs)


def attend_body(slots, valid, query_ref, own_ref, cache_ref, out_ref):
    step = pl.program_id(0)
    query = query_ref[0].T
    keys = cache_ref[0]
    own = own_ref[0]
    scores = jnp.dot(query, keys, preferred_element_type=jnp.float32) * score_scale
    own_score = (
        jnp.sum(query.astype(jnp.float32) * own.astype(jnp.float32), axis=1, keepdims=True)
        * score_scale
    )
    places = lax.broadcasted_iota(jnp.int32, scores.shape, 1)
    scores = jnp.where(places < valid[step], scores, -jnp.inf)
    top_score = jnp.maximum(jnp.max(scores, axis=1, keepdims=True), own_score)
    raised = jnp.exp(scores - top_score)
    raised_own = jnp.exp(own_score - top_score)
    totals = jnp.sum(raised, axis=1, keepdims=True) + raised_own
    weights = (raised / totals).astype(jnp.bfloat16)
    weight_own = (raised_own / totals).astype(jnp.bfloat16).astype(jnp.float32)
    mixed = lax.dot_general(
        weights, keys[:NOPE], (((1,), (1,)), ((), ())), preferred_element_type=jnp.float32
    )
    mixed = mixed + weight_own * own[:, :NOPE].astype(jnp.float32)
    out_ref[0] = mixed.astype(jnp.bfloat16)


def attend(slots, valid, query_t, own_keys, cache_t, query_slots, out_count):
    steps = slots.shape[0]
    width, heads = query_t.shape[1:]
    positions = cache_t.shape[2]
    if query_slots:
        place = lambda i, s, v: (s[i], 0, 0)
    else:
        place = lambda i, s, v: (i, 0, 0)
    return pl.pallas_call(
        attend_body,
        out_shape=jax.ShapeDtypeStruct((out_count, heads, NOPE), jnp.bfloat16),
        grid_spec=pltpu.PrefetchScalarGridSpec(
            num_scalar_prefetch=2,
            grid=(steps,),
            in_specs=[
                pl.BlockSpec((1, width, heads), place),
                pl.BlockSpec((1, 1, width), place),
                pl.BlockSpec((1, width, positions), lambda i, s, v: (s[i], 0, 0)),
            ],
            out_specs=pl.BlockSpec((1, heads, NOPE), place),
        ),
        compiler_params=pltpu.CompilerParams(vmem_limit_bytes=24 * 1024 * 1024),
        cost_estimate=pl.CostEstimate(
            flops=2 * steps * heads * positions * (width + NOPE),
            bytes_accessed=2 * steps * width * positions,
            transcendentals=steps * heads * positions,
        ),
    )(slots, valid, query_t, own_keys[:, None, :], cache_t)


def per_device(
    hidden_rows,
    group_ids,
    route_gates,
    w_gate,
    w_up,
    w_down,
    queries,
    new_latent,
    latent_cache,
    cache_lengths,
    moved_slot,
):
    model_width = hidden_rows.shape[1]
    rank_count = lax.axis_size("ep")
    position = lax.axis_index("ep")
    groups = rank_count // SPLIT
    requests = latent_cache.shape[0]

    leaving = lax.dynamic_index_in_dim(moved_slot, position, 0, keepdims=False)
    query_t = jnp.swapaxes(queries, 1, 2)
    cache_t = jnp.swapaxes(latent_cache, 1, 2)
    sent_query = lax.dynamic_index_in_dim(query_t, leaving, 0, keepdims=True)
    sent_own = lax.dynamic_index_in_dim(new_latent, leaving, 0, keepdims=True)
    visiting_query = shifted(sent_query, "ep", -1)
    visiting_own = shifted(sent_own, "ep", -1)

    chosen = group_ids[:, :, None] == jnp.arange(groups, dtype=jnp.int32)[None, None, :]
    coefficient = jnp.sum(jnp.where(chosen, route_gates[:, :, None], 0.0), axis=1)
    high = lax.reduce_precision(coefficient, 8, 7)
    middle = lax.reduce_precision(coefficient - high, 8, 7)
    low = coefficient - high - middle
    tail = jnp.concatenate([high, middle, low], axis=1).astype(jnp.bfloat16)
    spare = -tail.shape[1] % LANES
    rows = jnp.concatenate([hidden_rows, jnp.pad(tail, ((0, 0), (0, spare)))], axis=1)
    all_rows = lax.all_gather(rows, "ep", axis=0, tiled=True)

    own_lengths = lax.dynamic_slice_in_dim(cache_lengths, position * requests, requests)
    staying = jnp.arange(requests - 1, dtype=jnp.int32)
    staying = staying + (staying >= leaving).astype(jnp.int32)
    home_out = attend(
        staying, own_lengths[staying], query_t, new_latent, cache_t, True, requests
    )
    moved = leaving[None]
    away_out = attend(
        moved, own_lengths[moved], visiting_query, visiting_own, cache_t, False, 1
    )
    returned = shifted(away_out, "ep", 1)

    tokens = all_rows[:, :model_width]
    gate_part = jnp.dot(tokens, w_gate[0], preferred_element_type=jnp.float32)
    up_part = jnp.dot(tokens, w_up[0], preferred_element_type=jnp.float32)
    activated = (jax.nn.silu(gate_part) * up_part).astype(jnp.bfloat16)
    projected = jnp.dot(activated, w_down[0], preferred_element_type=jnp.float32)
    parts = all_rows[:, model_width:].astype(jnp.float32)
    lane = jnp.arange(parts.shape[1], dtype=jnp.int32)
    mine = (lane % groups == position // SPLIT) & (lane < 3 * groups)
    scale = jnp.sum(jnp.where(mine[None, :], parts, 0.0), axis=1, keepdims=True)
    partial = (projected * scale).astype(jnp.bfloat16)
    moe_out = lax.psum_scatter(partial, "ep", scatter_dimension=0, tiled=True)
    attn_out = lax.dynamic_update_slice_in_dim(home_out, returned, leaving, 0)
    return (moe_out, attn_out)


def solution(mesh):
    placed = (
        P(("group", "ep"), None),
        P(("group", "ep"), None),
        P(("group", "ep"), None),
        P("ep", None, None),
        P("ep", None, None),
        P("ep", None, None),
        P(("group", "ep"), None, None),
        P(("group", "ep"), None),
        P(("group", "ep"), None, None),
        P("group"),
        P("group"),
    )
    return jax.shard_map(
        per_device,
        mesh=mesh,
        in_specs=placed,
        out_specs=(P(("group", "ep"), None), P(("group", "ep"), None, None)),
        check_vma=False,
    )
```

time: 174 us -> 129 us (0.74)
  the two profiles are of different devices: /device:TPU:16 before, /device:TPU:0 now
where the time goes in v1:
time: 129 us
  waiting for transfers between devices  81.3 us (63%)
  between operations  18.1 us (14%)
  local copies, waits for them, and re-layouts  8.3 us (6%)
  matrix products  7.21 us (6%)
  Pallas kernels  6.52 us (5%)
  other arithmetic  4.58 us (4%)
  starting transfers between devices  2.58 us (2%)
    all_gather x1, waiting for transfers between devices, per_device(): all_rows = lax.all_gather(rows, 'ep', axis=0, tiled=True)  44.4 us
    reduce_scatter x1, waiting for transfers between devices, per_device(): moe_out = lax.psum_scatter(partial, 'ep', scatter_dimension=0, tiled=True)  36.9 us
    pallas_call x2, Pallas kernels, attend(): pl.pallas_call(attend_body, out_shape=jax.ShapeDtypeStruct((out_count, he...  6.52 us
    unnamed x15, local copies, waits for them, and re-layouts  5.65 us
    dot_general x1, matrix products, per_device(): jnp.dot(activated, w_down[0], preferred_element_type=jnp.float32)  4.52 us
    dot_general x1, matrix products, per_device(): gate_part = jnp.dot(tokens, w_gate[0], preferred_element_type=jnp.float32)  2.69 us
  transfers between devices with their start and end apart: 5, of which 2 were waited for; matrix products, arithmetic and copies ran while one was open for 3% of the time, Pallas kernels for 5%

profile of v1, /device:TPU:0, one launch (start us, length us, event | category | flops | bytes accessed | tf_op | source)
XLA Modules:
  0.0 128.6 jit_solution(176092471591583575)
XLA Ops:
  7.2 0.8 fusion.30
  8.1 0.1 copy.20
  8.2 1.6 %fusion.23 = bf16[8,7296]{1,0:T(8,128)(2,1)} fusion(bf16[8,6]{1,0:T(8,128)(2,1)S(1)} %copy.20, bf16[8,7168]{1,0:T(8,128)(2,1)} %param.11), kind=kLoop, calls=%fused_computation.15 | loop fusion | flops 350208 | bytes 231520 | tf_op jit(solution)/shard_map/concatenate | solution.py:113
  9.8 0.0 reduce-scatter.2.cloned.1.call-start
  9.8 44.4 %all-gather.2.cloned.1.call-done = bf16[128,7296]{1,0:T(8,128)(2,1)} async-done(((bf16[8,7296]{1,0:T(8,128)(2,1)}), bf16[128,7296]{1,0:T(8,128)(2,1)}) %all-gather.2.cloned.1.call-update) | async-done | bytes 1867792 | tf_op jit(solution)/shard_map/all_gather | solution.py:114
  54.2 0.9 select_reduce_fusion
  55.1 2.7 %fusion.4 = f32[128,128]{1,0:T(8,128)S(1)} fusion(bf16[1,7168,128]{2,1,0:T(8,128)(2,1)} %param.14, bf16[128,7296]{1,0:T(8,128)(2,1)} %all-gather.2.cloned.1.call-done), kind=kOutput, calls=%fused_computation.6 | convolution fusion | flops 234881024 | bytes 3735552 | tf_op jit(solution)/shard_map/dot_general | solution.py:129
  57.8 4.5 %fusion = bf16[128,7168]{1,0:T(8,128)(2,1)} fusion(bf16[1,128,7168]{2,1,0:T(8,128)(2,1)S(1)} %copy-done, f32[128]{0:T(128)S(1)} %select_reduce_fusion, bf16[1,7168,128]{2,1,0:T(8,128)(2,1)} %param.15, bf16[128,7296]{1,0:T(8,128)(2,1)} %all-gather.2.cloned.1.call-done, f32[128,128]{1,0:T(8,128)S(1)} %fusion.4), kind=kOutput, calls=%fused_computation.2 | convolution fusion | flops 471695360 | bytes 7406080 | tf_op jit(solution)/shard_map/dot_general | solution.py:132
  62.4 0.6 copy-done.5
  63.0 0.6 dynamic_slice.15.slots
  65.5 1.9 %collective-permute-start = (bf16[1,576,128]{2,1,0:T(8,128)(2,1)S(1)}, bf16[1,576,128]{2,1,0:T(8,128)(2,1)S(1)}, u32[]{:S(2)}, u32[]{:S(2)}) collective-permute-start(bf16[1,576,128]{2,1,0:T(8,128)(2,1)S(1)} %dynamic-slice_bitcast_fusion), channel_id=1, source_target_pairs={{0,15},{1,0},{2,1},{3,2},{4,3},{5,4},{6,5},{7,6},{8,7},{9,8},{10,9... | collective-permute-start | bytes 442376 | tf_op jit(solution)/shard_map/ppermute | solution.py:21
  67.4 0.3 collective-permute-start.1
  67.7 0.7 fusion.34
  70.4 0.7 dynamic-slice.6.valid
  71.0 2.5 %copy-done.1 = bf16[4,1024,576]{1,2,0:T(8,128)(2,1)S(1)} copy-done((bf16[4,1024,576]{1,2,0:T(8,128)(2,1)S(1)}, bf16[4,1024,576]{1,2,0:T(8,128)(2,1)}, u32[]{:S(2)}) %copy-start.1) | copy-done | bytes 4718616
  73.5 2.3 %shard_map.123 = bf16[1,128,512]{2,1,0:T(8,128)(2,1)S(1)} custom-call(s32[1]{0:T(128)} %dynamic_slice.15.slots, s32[1]{0:T(128)} %dynamic-slice.6.valid, bf16[1,576,128]{2,1,0:T(8,128)(2,1)S(1)} %collective-permute-done.query_ref, bf16[1,1,576]{2,1,0:T(2,128)(2,1)S(1)} %bitcast.28, bf16[4,576,1024]{2,1,0:T(8,128)(2,1)S(1)} %bitcast.25), custom_call_target="tpu_custom_call" | custom-call | flops 285212672 | bytes 1179648 | tf_op jit(solution)/shard_map/pallas_call | solution.py:57
  75.8 0.3 collective-permute-start.2
  76.1 0.6 fusion.32.slots
  76.8 0.1 dynamic_slice.16
  76.9 0.6 gather_fusion
  77.5 2.4 %copy-done.2 = bf16[4,1024,576]{1,2,0:T(8,128)(2,1)S(1)} copy-done((bf16[4,1024,576]{1,2,0:T(8,128)(2,1)S(1)}, bf16[4,1024,576]{1,2,0:T(8,128)(2,1)}, u32[]{:S(2)}) %copy-start.2) | copy-done | bytes 4718616
  80.0 4.2 %shard_map.122 = bf16[4,128,512]{2,1,0:T(8,128)(2,1)} custom-call(s32[3]{0:T(128)S(1)} %fusion.32.slots, s32[3]{0:T(128)S(1)} %gather_fusion, bf16[4,576,128]{2,1,0:T(8,128)(2,1)S(1)} %bitcast.27, bf16[4,1,576]{2,1,0:T(2,128)(2,1)S(1)} %copy.19.own_ref, bf16[4,576,1024]{2,1,0:T(8,128)(2,1)S(1)} %bitcast.26), custom_call_target="tpu_custom_call" | custom-call | flops 855638016 | bytes 3538944 | tf_op jit(solution)/shard_map/pallas_call | solution.py:57
  84.2 0.7 constant_dynamic-update-slice_fusion
  84.9 36.9 %reduce-scatter.2.cloned.1.call-done = bf16[8,7168]{1,0:T(8,128)(2,1)} async-done(((bf16[128,7168]{1,0:T(8,128)(2,1)}), bf16[8,7168]{1,0:T(8,128)(2,1)}) %reduce-scatter.2.cloned.1.call-update) | async-done | bytes 114704 | tf_op jit(solution)/shard_map/reduce_scatter | solution.py:138
  (24 shorter events, 0.2 us)
Async XLA Ops:
  7.2 50.6 %copy-start = (bf16[1,128,7168]{2,1,0:T(8,128)(2,1)S(1)}, bf16[1,128,7168]{2,1,0:T(8,128)(2,1)}, u32[]{:S(2)}) copy-start(bf16[1,128,7168]{2,1,0:T(8,128)(2,1)} %param.16) | copy-start | bytes 5505028
  7.2 47.0 %all-gather.2.cloned.1.call-start = ((), (), s32[]{:S(2)}) async-start(), calls=%async_computation.1 | async-start | bytes 1984512 | tf_op jit(solution)/shard_map/all_gather | solution.py:114
  9.8 112.0 %reduce-scatter.2.cloned.1.call-start = ((), (), s32[]{:S(2)}) async-start(), calls=%async_computation.2 | async-start | bytes 1949696 | tf_op jit(solution)/shard_map/reduce_scatter | solution.py:138
  62.3 0.7 copy-start.5
  62.3 3.2 %copy-start.3 = (bf16[4,128,576]{1,2,0:T(8,128)(2,1)S(1)}, bf16[4,128,576]{1,2,0:T(8,128)(2,1)}, u32[]{:S(2)}) copy-start(bf16[4,128,576]{1,2,0:T(8,128)(2,1)} %param.17) | copy-start | bytes 1769476
  62.3 5.1 %copy-start.4 = (bf16[4,576]{1,0:T(4,128)(2,1)S(1)}, bf16[4,576]{1,0:T(4,128)(2,1)}, u32[]{:S(2)}) copy-start(bf16[4,576]{1,0:T(4,128)(2,1)} %param.18) | copy-start | bytes 13828
  62.3 8.0 %copy-start.6 = (s32[64]{0:T(128)S(1)}, s32[64]{0:T(128)}, u32[]{:S(2)}) copy-start(s32[64]{0:T(128)} %param.20) | copy-start | bytes 772
  65.5 5.5 %collective-permute-start = (bf16[1,576,128]{2,1,0:T(8,128)(2,1)S(1)}, bf16[1,576,128]{2,1,0:T(8,128)(2,1)S(1)}, u32[]{:S(2)}, u32[]{:S(2)}) collective-permute-start(bf16[1,576,128]{2,1,0:T(8,128)(2,1)S(1)} %dynamic-slice_bitcast_fusion), channel_id=1, source_target_pairs={{0,15},{1,0},{2,1},{3,2},{4,3},{5,4},{6,5},{7,6},{8,7},{9,8},{10,9... | collective-permute-start | bytes 442376 | tf_op jit(solution)/shard_map/ppermute | solution.py:21
  67.4 3.6 %collective-permute-start.1 = (bf16[1,576]{1,0:T(2,128)(2,1)S(1)}, bf16[1,576]{1,0:T(2,128)(2,1)S(1)}, u32[]{:S(2)}, u32[]{:S(2)}) collective-permute-start(bf16[1,576]{1,0:T(2,128)(2,1)S(1)} %constant_dynamic-slice_fusion), channel_id=1, source_target_pairs={{0,15},{1,0},{2,1},{3,2},{4,3},{5,4},{6,5},{7,6},{8,7},{9,8},{10,9... | collective-permute-start | bytes 3464 | tf_op jit(solution)/shard_map/ppermute | solution.py:21
  71.0 2.5 %copy-start.1 = (bf16[4,1024,576]{1,2,0:T(8,128)(2,1)S(1)}, bf16[4,1024,576]{1,2,0:T(8,128)(2,1)}, u32[]{:S(2)}) copy-start(bf16[4,1024,576]{1,2,0:T(8,128)(2,1)} %param.19) | copy-start | bytes 14155780
  75.8 8.4 %collective-permute-start.2 = (bf16[1,128,512]{2,1,0:T(8,128)(2,1)S(1)}, bf16[1,128,512]{2,1,0:T(8,128)(2,1)S(1)}, u32[]{:S(2)}, u32[]{:S(2)}) collective-permute-start(bf16[1,128,512]{2,1,0:T(8,128)(2,1)S(1)} %shard_map.123), channel_id=1, source_target_pairs={{0,1},{1,2},{2,3},{3,4},{4,5},{5,6},{6,7},{7,8},{8,9},{9,10},{10,1... | collective-permute-start | bytes 393224 | tf_op jit(solution)/shard_map/ppermute | solution.py:21
  77.5 2.4 %copy-start.2 = (bf16[4,1024,576]{1,2,0:T(8,128)(2,1)S(1)}, bf16[4,1024,576]{1,2,0:T(8,128)(2,1)}, u32[]{:S(2)}) copy-start(bf16[4,1024,576]{1,2,0:T(8,128)(2,1)} %param.19) | copy-start | bytes 14155780
Sparse Core Ops, SparseCore 0:
  10.7 43.4 all-gather.1
  62.5 59.2 reduce-scatter.1

commit v2 on v1

--- a/solution.py
+++ b/solution.py
@@ -19,6 +19,39 @@
     count = lax.axis_size(axis)
     pairs = [(source, (source + steps) % count) for source in range(count)]
     return lax.ppermute(value, axis, pairs)
+
+
+def rotated(value, axis, steps):
+    return shifted(value, axis, 4 * steps)
+
+
+def swapped(value, axis, bit):
+    pairs = [(source, source ^ bit) for source in range(lax.axis_size(axis))]
+    return lax.ppermute(value, axis, pairs)
+
+
+def gathered(rows, axis):
+    turns = lax.axis_size(axis) // 4
+    columns = [rows] + [rotated(rows, axis, r) for r in range(1, turns)]
+    pairs = [jnp.concatenate([own, swapped(own, axis, 2)], axis=0) for own in columns]
+    others = [swapped(pair, axis, 1) for pair in pairs]
+    return jnp.concatenate(pairs + others, axis=0)
+
+
+def added(*terms):
+    return sum(term.astype(jnp.float32) for term in terms).astype(jnp.bfloat16)
+
+
+def summed(partial, axis):
+    turns = lax.axis_size(axis) // 4
+    count = partial.shape[0] // (4 * turns)
+    blocks = partial.reshape(2, turns, 2 * count, partial.shape[1])
+    terms = []
+    for r in list(range(1, turns)) + [0]:
+        chip = added(blocks[0, r], swapped(blocks[1, r], axis, 1))
+        both = added(chip[:count], swapped(chip[count:], axis, 2))
+        terms.append(both if r == 0 else rotated(both, axis, -r))
+    return added(*terms)
 
 
 def attend_body(slots, valid, query_ref, own_ref, cache_ref, out_ref):
@@ -111,7 +144,7 @@
     tail = jnp.concatenate([high, middle, low], axis=1).astype(jnp.bfloat16)
     spare = -tail.shape[1] % LANES
     rows = jnp.concatenate([hidden_rows, jnp.pad(tail, ((0, 0), (0, spare)))], axis=1)
-    all_rows = lax.all_gather(rows, "ep", axis=0, tiled=True)
+    all_rows = gathered(rows, "ep")
 
     own_lengths = lax.dynamic_slice_in_dim(cache_lengths, position * requests, requests)
     staying = jnp.arange(requests - 1, dtype=jnp.int32)
@@ -135,7 +168,7 @@
     mine = (lane % groups == position // SPLIT) & (lane < 3 * groups)
     scale = jnp.sum(jnp.where(mine[None, :], parts, 0.0), axis=1, keepdims=True)
     partial = (projected * scale).astype(jnp.bfloat16)
-    moe_out = lax.psum_scatter(partial, "ep", scatter_dimension=0, tiled=True)
+    moe_out = summed(partial, "ep")
     attn_out = lax.dynamic_update_slice_in_dim(home_out, returned, leaving, 0)
     return (moe_out, attn_out)
 

time: 129 us -> 83.1 us (0.64)
  waiting for transfers between devices: 81.3 us -> 13.7 us
  starting transfers between devices: 2.58 us -> 23.9 us
  between operations: 18.1 us -> 4.96 us
  local copies, waits for them, and re-layouts: 8.3 us -> 19.3 us
  other arithmetic: 4.58 us -> 7.56 us
    all_gather x1 -> x0, waiting for transfers between devices: 44.4 us -> none  [per_device(): all_rows = lax.all_gather(rows, 'ep', axis=0, tiled=True)]
    reduce_scatter x1 -> x0, waiting for transfers between devices: 36.9 us -> none  [per_device(): moe_out = lax.psum_scatter(partial, 'ep', scatter_dimension=0, tiled=True)]
    ppermute x0 -> x16, starting transfers between devices: none -> 11.7 us  [swapped(): return lax.ppermute(value, axis, pairs)]
    ppermute x3 -> x9, starting transfers between devices: 2.5 us -> 12.3 us  [shifted(): return lax.ppermute(value, axis, pairs)]
    ppermute x0 -> x16, waiting for transfers between devices: none -> 8.19 us  [swapped(): return lax.ppermute(value, axis, pairs)]
    unnamed x15 -> x27, local copies, waits for them, and re-layouts: 5.65 us -> 11.5 us
    ppermute x3 -> x9, waiting for transfers between devices: 0.01 us -> 5.55 us  [shifted(): return lax.ppermute(value, axis, pairs)]
    convert_element_type x0 -> x5, other arithmetic: none -> 1.93 us  [added(): sum((term.astype(jnp.float32) for term in terms)).astype(jnp.bfloat16)]
  transfers between devices with their start and end apart: 5 -> 25, of which waited for: 2 -> 8; matrix products, arithmetic and copies ran while one was open for 3% -> 31% of each run, Pallas kernels for 5% -> 8%
where the time goes in v2:
time: 83.1 us; the launch traced here: 82.5 us
  starting transfers between devices  23.9 us (29%)
  local copies, waits for them, and re-layouts  19.3 us (23%)
  waiting for transfers between devices  13.7 us (16%)
  other arithmetic  7.56 us (9%)
  matrix products  6.67 us (8%)
  Pallas kernels  6.43 us (8%)
  between operations  4.96 us (6%)
    ppermute x9, starting transfers between devices, shifted(): return lax.ppermute(value, axis, pairs)  12.3 us
    ppermute x16, starting transfers between devices, swapped(): return lax.ppermute(value, axis, pairs)  11.7 us
    unnamed x27, local copies, waits for them, and re-layouts  11.5 us
    ppermute x16, waiting for transfers between devices, swapped(): return lax.ppermute(value, axis, pairs)  8.19 us
    pallas_call x2, Pallas kernels, attend(): pl.pallas_call(attend_body, out_shape=jax.ShapeDtypeStruct((out_count, he...  6.43 us
    ppermute x9, waiting for transfers between devices, shifted(): return lax.ppermute(value, axis, pairs)  5.55 us
    dot_general x1, matrix products, per_device(): jnp.dot(activated, w_down[0], preferred_element_type=jnp.float32)  4.5 us
    dot_general x1, matrix products, per_device(): up_part = jnp.dot(tokens, w_up[0], preferred_element_type=jnp.float32)  2.17 us
  transfers between devices with their start and end apart: 25, of which 8 were waited for; matrix products, arithmetic and copies ran while one was open for 31% of the time, Pallas kernels for 8%

profile of v2, /device:TPU:0, one launch (start us, length us, event | category | flops | bytes accessed | tf_op | source)
XLA Modules:
  0.0 82.5 jit_solution(2910004420479251641)
XLA Ops:
  1.6 1.6 %pad_maximum_fusion.4 = (bf16[8,7296]{1,0:T(8,128)(2,1)S(1)}, bf16[128,7296]{1,0:T(8,128)(2,1)}) fusion(bf16[8,128]{1,0:T(8,128)(2,1)S(1)} %pad.4.clone, bf16[8,7168]{1,0:T(8,128)(2,1)} %param.11), kind=kLoop, calls=%fused_computation.36 | loop fusion | flops 233471 | bytes 350208 | tf_op jit(solution)/shard_map/concatenate | solution.py:146
  3.2 3.0 %collective-permute-start = (bf16[8,7296]{1,0:T(8,128)(2,1)S(1)}, bf16[8,7296]{1,0:T(8,128)(2,1)S(1)}, u32[]{:S(2)}, u32[]{:S(2)}) collective-permute-start(bf16[8,7296]{1,0:T(8,128)(2,1)S(1)} %get-tuple-element.21), channel_id=1, source_target_pairs={{0,2},{1,3},{2,0},{3,1},{4,6},{5,7},{6,4},{7,5},{8,10},{9,11},{10,... | collective-permute-start | bytes 350216 | tf_op jit(solution)/shard_map/ppermute | solution.py:30
  6.1 1.6 %collective-permute-start.1 = (bf16[8,7296]{1,0:T(8,128)(2,1)S(1)}, bf16[8,7296]{1,0:T(8,128)(2,1)S(1)}, u32[]{:S(2)}, u32[]{:S(2)}) collective-permute-start(bf16[8,7296]{1,0:T(8,128)(2,1)S(1)} %get-tuple-element.21), channel_id=1, source_target_pairs={{0,4},{1,5},{2,6},{3,7},{4,8},{5,9},{6,10},{7,11},{8,12},{9,13},{1... | collective-permute-start | bytes 350216 | tf_op jit(solution)/shard_map/ppermute | solution.py:21
  7.7 2.6 %collective-permute-start.3 = (bf16[8,7296]{1,0:T(8,128)(2,1)S(1)}, bf16[8,7296]{1,0:T(8,128)(2,1)S(1)}, u32[]{:S(2)}, u32[]{:S(2)}) collective-permute-start(bf16[8,7296]{1,0:T(8,128)(2,1)S(1)} %get-tuple-element.21), channel_id=1, source_target_pairs={{0,8},{1,9},{2,10},{3,11},{4,12},{5,13},{6,14},{7,15},{8,0},{9,1},... | collective-permute-start | bytes 350216 | tf_op jit(solution)/shard_map/ppermute | solution.py:21
  10.3 1.3 %collective-permute-start.5 = (bf16[8,7296]{1,0:T(8,128)(2,1)S(1)}, bf16[8,7296]{1,0:T(8,128)(2,1)S(1)}, u32[]{:S(2)}, u32[]{:S(2)}) collective-permute-start(bf16[8,7296]{1,0:T(8,128)(2,1)S(1)} %get-tuple-element.21), channel_id=1, source_target_pairs={{0,12},{1,13},{2,14},{3,15},{4,0},{5,1},{6,2},{7,3},{8,4},{9,5},{1... | collective-permute-start | bytes 350216 | tf_op jit(solution)/shard_map/ppermute | solution.py:21
  11.7 1.3 %dynamic_slice.15.slots = s32[1]{0:T(128)} dynamic-slice(s32[16]{0:T(128)} %param.21, s32[]{:T(128)S(6)} %select_n.54), dynamic_slice_sizes={1} | dynamic-slice | bytes 12 | tf_op jit(solution)/shard_map/jit(dynamic_index_in_dim)/dynamic_slice | solution.py:131
  15.0 1.6 %dynamic-slice_bitcast_fusion = bf16[1,576,128]{2,1,0:T(8,128)(2,1)} fusion(bf16[4,128,576]{1,2,0:T(8,128)(2,1)} %param.17, s32[]{:T(128)S(6)} %select_n.58), kind=kLoop, calls=%fused_computation.35 | loop fusion | bytes 294916 | tf_op jit(solution)/shard_map/jit(dynamic_index_in_dim)/dynamic_slice | solution.py:134
  19.9 1.5 %collective-permute-start.4 = (bf16[8,7296]{1,0:T(8,128)(2,1)S(1)}, bf16[8,7296]{1,0:T(8,128)(2,1)S(1)}, u32[]{:S(2)}, u32[]{:S(2)}) collective-permute-start(bf16[8,7296]{1,0:T(8,128)(2,1)S(1)} %collective-permute-done.3), channel_id=1, source_target_pairs={{0,2},{1,3},{2,0},{3,1},{4,6},{5,7},{6,4},{7,5},{8,10},{9,11},{10,... | collective-permute-start | bytes 350216 | tf_op jit(solution)/shard_map/ppermute | solution.py:30
  21.9 2.9 %collective-permute-done.2 = bf16[8,7296]{1,0:T(8,128)(2,1)S(1)} collective-permute-done((bf16[8,7296]{1,0:T(8,128)(2,1)S(1)}, bf16[8,7296]{1,0:T(8,128)(2,1)S(1)}, u32[]{:S(2)}, u32[]{:S(2)}) %collective-permute-start.2) | collective-permute-done | bytes 116768 | tf_op jit(solution)/shard_map/ppermute | solution.py:30
  24.9 2.4 %collective-permute-done.4 = bf16[8,7296]{1,0:T(8,128)(2,1)S(1)} collective-permute-done((bf16[8,7296]{1,0:T(8,128)(2,1)S(1)}, bf16[8,7296]{1,0:T(8,128)(2,1)S(1)}, u32[]{:S(2)}, u32[]{:S(2)}) %collective-permute-start.4) | collective-permute-done | bytes 116768 | tf_op jit(solution)/shard_map/ppermute | solution.py:30
  27.4 1.4 %collective-permute-done.6 = bf16[8,7296]{1,0:T(8,128)(2,1)S(1)} collective-permute-done((bf16[8,7296]{1,0:T(8,128)(2,1)S(1)}, bf16[8,7296]{1,0:T(8,128)(2,1)S(1)}, u32[]{:S(2)}, u32[]{:S(2)}) %collective-permute-start.6) | collective-permute-done | bytes 116768 | tf_op jit(solution)/shard_map/ppermute | solution.py:30
  35.1 2.2 %fusion.2 = f32[128,128]{1,0:T(8,128)S(1)} fusion(bf16[1,7168,128]{2,1,0:T(8,128)(2,1)S(1)} %copy-done.6, bf16[128,7296]{1,0:T(8,128)(2,1)} %constant_dynamic-update-slice_fusion), kind=kOutput, calls=%fused_computation.4 | convolution fusion | flops 234881024 | bytes 3735552 | tf_op jit(solution)/shard_map/dot_general | solution.py:163
  38.2 4.5 %fusion = bf16[128,7168]{1,0:T(8,128)(2,1)} fusion(bf16[1,128,7168]{2,1,0:T(8,128)(2,1)S(1)} %copy-done, f32[128]{0:T(128)S(1)} %select_reduce_fusion, f32[128,128]{1,0:T(8,128)S(1)} %fusion.2, bf16[1,7168,128]{2,1,0:T(8,128)(2,1)} %param.14, bf16[128,7296]{1,0:T(8,128)(2,1)} %constant_dynamic-update-slice_fusion), kind=kOutput, calls=%fused_computation.2 | convolution fusion | flops 471695360 | bytes 7406080 | tf_op jit(solution)/shard_map/dot_general | solution.py:165
  42.7 1.5 %slice_bitcast_fusion = (bf16[16,7168]{1,0:T(8,128)(2,1)S(1)}, bf16[16,7168]{1,0:T(8,128)(2,1)S(1)}, bf16[16,7168]{1,0:T(8,128)(2,1)S(1)}, bf16[16,7168]{1,0:T(8,128)(2,1)S(1)}) fusion(bf16[2,4,16,7168]{3,2,1,0:T(8,128)(2,1)} %bitcast.56), kind=kLoop, calls=%fused_computation.22 | loop fusion | bytes 1835008 | tf_op jit(solution)/shard_map/squeeze | solution.py:51
  46.0 2.1 %collective-permute-start.23 = (bf16[1,576]{1,0:T(2,128)(2,1)S(1)}, bf16[1,576]{1,0:T(2,128)(2,1)S(1)}, u32[]{:S(2)}, u32[]{:S(2)}) collective-permute-start(bf16[1,576]{1,0:T(2,128)(2,1)S(1)} %constant_dynamic-slice_fusion), channel_id=1, source_target_pairs={{0,15},{1,0},{2,1},{3,2},{4,3},{5,4},{6,5},{7,6},{8,7},{9,8},{10,9... | collective-permute-start | bytes 3464 | tf_op jit(solution)/shard_map/ppermute | solution.py:21
  50.5 2.3 %copy-done.1 = bf16[4,1024,576]{1,2,0:T(8,128)(2,1)S(1)} copy-done((bf16[4,1024,576]{1,2,0:T(8,128)(2,1)S(1)}, bf16[4,1024,576]{1,2,0:T(8,128)(2,1)}, u32[]{:S(2)}) %copy-start.1) | copy-done | bytes 4718616
  52.8 4.2 %shard_map.122 = bf16[4,128,512]{2,1,0:T(8,128)(2,1)} custom-call(s32[3]{0:T(128)S(1)} %fusion.23.slots, s32[3]{0:T(128)S(1)} %gather_fusion, bf16[4,576,128]{2,1,0:T(8,128)(2,1)S(1)} %bitcast.54, bf16[4,1,576]{2,1,0:T(2,128)(2,1)S(1)} %copy.19.own_ref, bf16[4,576,1024]{2,1,0:T(8,128)(2,1)S(1)} %bitcast.52), custom_call_target="tpu_custom_call" | custom-call | flops 855638016 | bytes 3538944 | tf_op jit(solution)/shard_map/pallas_call | solution.py:90
  59.7 2.3 %copy-done.2 = bf16[4,1024,576]{1,2,0:T(8,128)(2,1)S(1)} copy-done((bf16[4,1024,576]{1,2,0:T(8,128)(2,1)S(1)}, bf16[4,1024,576]{1,2,0:T(8,128)(2,1)}, u32[]{:S(2)}) %copy-start.2) | copy-done | bytes 4718616
  62.0 2.2 %shard_map.123 = bf16[1,128,512]{2,1,0:T(8,128)(2,1)S(1)} custom-call(s32[1]{0:T(128)} %dynamic_slice.15.slots, s32[1]{0:T(128)} %dynamic-slice.6.valid, bf16[1,576,128]{2,1,0:T(8,128)(2,1)S(1)} %collective-permute-done.22.query_ref, bf16[1,1,576]{2,1,0:T(2,128)(2,1)S(1)} %bitcast.55, bf16[4,576,1024]{2,1,0:T(8,128)(2,1)S(1)} %bitcast.53), custom_call_target="tpu_custom_call" | custom-call | flops 285212672 | bytes 1179648 | tf_op jit(solution)/shard_map/pallas_call | solution.py:90
  64.3 2.0 %collective-permute-start.15 = (bf16[8,7168]{1,0:T(8,128)(2,1)S(1)}, bf16[8,7168]{1,0:T(8,128)(2,1)S(1)}, u32[]{:S(2)}, u32[]{:S(2)}) collective-permute-start(bf16[8,7168]{1,0:T(8,128)(2,1)S(1)} %slice.88), channel_id=1, source_target_pairs={{0,2},{1,3},{2,0},{3,1},{4,6},{5,7},{6,4},{7,5},{8,10},{9,11},{10,... | collective-permute-start | bytes 344072 | tf_op jit(solution)/shard_map/ppermute | solution.py:30
  66.5 2.0 %collective-permute-start.21 = (bf16[8,7168]{1,0:T(8,128)(2,1)S(1)}, bf16[8,7168]{1,0:T(8,128)(2,1)S(1)}, u32[]{:S(2)}, u32[]{:S(2)}) collective-permute-start(bf16[8,7168]{1,0:T(8,128)(2,1)S(1)} %slice.96), channel_id=1, source_target_pairs={{0,2},{1,3},{2,0},{3,1},{4,6},{5,7},{6,4},{7,5},{8,10},{9,11},{10,... | collective-permute-start | bytes 344072 | tf_op jit(solution)/shard_map/ppermute | solution.py:30
  69.9 3.0 %collective-permute-start.16 = (bf16[8,7168]{1,0:T(8,128)(2,1)S(1)}, bf16[8,7168]{1,0:T(8,128)(2,1)S(1)}, u32[]{:S(2)}, u32[]{:S(2)}) collective-permute-start(bf16[8,7168]{1,0:T(8,128)(2,1)S(1)} %add_convert_fusion.3), channel_id=1, source_target_pairs={{0,8},{1,9},{2,10},{3,11},{4,12},{5,13},{6,14},{7,15},{8,0},{9,1},... | collective-permute-start | bytes 344072 | tf_op jit(solution)/shard_map/ppermute | solution.py:21
  73.9 1.5 %collective-permute-start.19 = (bf16[8,7168]{1,0:T(8,128)(2,1)S(1)}, bf16[8,7168]{1,0:T(8,128)(2,1)S(1)}, u32[]{:S(2)}, u32[]{:S(2)}) collective-permute-start(bf16[8,7168]{1,0:T(8,128)(2,1)S(1)} %add_convert_fusion.2), channel_id=1, source_target_pairs={{0,4},{1,5},{2,6},{3,7},{4,8},{5,9},{6,10},{7,11},{8,12},{9,13},{1... | collective-permute-start | bytes 344072 | tf_op jit(solution)/shard_map/ppermute | solution.py:21
  76.4 5.4 %collective-permute-done.19 = bf16[8,7168]{1,0:T(8,128)(2,1)S(1)} collective-permute-done((bf16[8,7168]{1,0:T(8,128)(2,1)S(1)}, bf16[8,7168]{1,0:T(8,128)(2,1)S(1)}, u32[]{:S(2)}, u32[]{:S(2)}) %collective-permute-start.19) | collective-permute-done | bytes 114720 | tf_op jit(solution)/shard_map/ppermute | solution.py:21
  (90 shorter events, 21.2 us)
Async XLA Ops:
  3.2 13.4 %collective-permute-start = (bf16[8,7296]{1,0:T(8,128)(2,1)S(1)}, bf16[8,7296]{1,0:T(8,128)(2,1)S(1)}, u32[]{:S(2)}, u32[]{:S(2)}) collective-permute-start(bf16[8,7296]{1,0:T(8,128)(2,1)S(1)} %get-tuple-element.21), channel_id=1, source_target_pairs={{0,2},{1,3},{2,0},{3,1},{4,6},{5,7},{6,4},{7,5},{8,10},{9,11},{10,... | collective-permute-start | bytes 350216 | tf_op jit(solution)/shard_map/ppermute | solution.py:30
  6.1 12.6 %collective-permute-start.1 = (bf16[8,7296]{1,0:T(8,128)(2,1)S(1)}, bf16[8,7296]{1,0:T(8,128)(2,1)S(1)}, u32[]{:S(2)}, u32[]{:S(2)}) collective-permute-start(bf16[8,7296]{1,0:T(8,128)(2,1)S(1)} %get-tuple-element.21), channel_id=1, source_target_pairs={{0,4},{1,5},{2,6},{3,7},{4,8},{5,9},{6,10},{7,11},{8,12},{9,13},{1... | collective-permute-start | bytes 350216 | tf_op jit(solution)/shard_map/ppermute | solution.py:21
  7.7 12.2 %collective-permute-start.3 = (bf16[8,7296]{1,0:T(8,128)(2,1)S(1)}, bf16[8,7296]{1,0:T(8,128)(2,1)S(1)}, u32[]{:S(2)}, u32[]{:S(2)}) collective-permute-start(bf16[8,7296]{1,0:T(8,128)(2,1)S(1)} %get-tuple-element.21), channel_id=1, source_target_pairs={{0,8},{1,9},{2,10},{3,11},{4,12},{5,13},{6,14},{7,15},{8,0},{9,1},... | collective-permute-start | bytes 350216 | tf_op jit(solution)/shard_map/ppermute | solution.py:21
  10.3 11.1 %collective-permute-start.5 = (bf16[8,7296]{1,0:T(8,128)(2,1)S(1)}, bf16[8,7296]{1,0:T(8,128)(2,1)S(1)}, u32[]{:S(2)}, u32[]{:S(2)}) collective-permute-start(bf16[8,7296]{1,0:T(8,128)(2,1)S(1)} %get-tuple-element.21), channel_id=1, source_target_pairs={{0,12},{1,13},{2,14},{3,15},{4,0},{5,1},{6,2},{7,3},{8,4},{9,5},{1... | collective-permute-start | bytes 350216 | tf_op jit(solution)/shard_map/ppermute | solution.py:21
  16.6 43.1 %collective-permute-start.22 = (bf16[1,576,128]{2,1,0:T(8,128)(2,1)}, bf16[1,576,128]{2,1,0:T(8,128)(2,1)S(1)}, u32[]{:S(2)}, u32[]{:S(2)}) collective-permute-start(bf16[1,576,128]{2,1,0:T(8,128)(2,1)} %dynamic-slice_bitcast_fusion), channel_id=1, source_target_pairs={{0,15},{1,0},{2,1},{3,2},{4,3},{5,4},{6,5},{7,6},{8,7},{9,8},{10,9... | collective-permute-start | bytes 442376 | tf_op jit(solution)/shard_map/ppermute | solution.py:21
  17.5 14.7 %collective-permute-start.7 = (bf16[16,7296]{1,0:T(8,128)(2,1)S(1)}, bf16[16,7296]{1,0:T(8,128)(2,1)S(1)}, u32[]{:S(2)}, u32[]{:S(2)}) collective-permute-start(bf16[16,7296]{1,0:T(8,128)(2,1)S(1)} %pad_maximum_fusion), channel_id=1, source_target_pairs={{0,1},{1,0},{2,3},{3,2},{4,5},{5,4},{6,7},{7,6},{8,9},{9,8},{10,11... | collective-permute-start | bytes 700424 | tf_op jit(solution)/shard_map/ppermute | solution.py:30
  18.7 6.1 %collective-permute-start.2 = (bf16[8,7296]{1,0:T(8,128)(2,1)S(1)}, bf16[8,7296]{1,0:T(8,128)(2,1)S(1)}, u32[]{:S(2)}, u32[]{:S(2)}) collective-permute-start(bf16[8,7296]{1,0:T(8,128)(2,1)S(1)} %collective-permute-done.1), channel_id=1, source_target_pairs={{0,2},{1,3},{2,0},{3,1},{4,6},{5,7},{6,4},{7,5},{8,10},{9,11},{10,... | collective-permute-start | bytes 350216 | tf_op jit(solution)/shard_map/ppermute | solution.py:30
  19.9 7.4 %collective-permute-start.4 = (bf16[8,7296]{1,0:T(8,128)(2,1)S(1)}, bf16[8,7296]{1,0:T(8,128)(2,1)S(1)}, u32[]{:S(2)}, u32[]{:S(2)}) collective-permute-start(bf16[8,7296]{1,0:T(8,128)(2,1)S(1)} %collective-permute-done.3), channel_id=1, source_target_pairs={{0,2},{1,3},{2,0},{3,1},{4,6},{5,7},{6,4},{7,5},{8,10},{9,11},{10,... | collective-permute-start | bytes 350216 | tf_op jit(solution)/shard_map/ppermute | solution.py:30
  21.4 7.4 %collective-permute-start.6 = (bf16[8,7296]{1,0:T(8,128)(2,1)S(1)}, bf16[8,7296]{1,0:T(8,128)(2,1)S(1)}, u32[]{:S(2)}, u32[]{:S(2)}) collective-permute-start(bf16[8,7296]{1,0:T(8,128)(2,1)S(1)} %collective-permute-done.5), channel_id=1, source_target_pairs={{0,2},{1,3},{2,0},{3,1},{4,6},{5,7},{6,4},{7,5},{8,10},{9,11},{10,... | collective-permute-start | bytes 350216 | tf_op jit(solution)/shard_map/ppermute | solution.py:30
  24.8 8.1 %collective-permute-start.8 = (bf16[16,7296]{1,0:T(8,128)(2,1)S(1)}, bf16[16,7296]{1,0:T(8,128)(2,1)S(1)}, u32[]{:S(2)}, u32[]{:S(2)}) collective-permute-start(bf16[16,7296]{1,0:T(8,128)(2,1)S(1)} %pad_maximum_fusion.1), channel_id=1, source_target_pairs={{0,1},{1,0},{2,3},{3,2},{4,5},{5,4},{6,7},{7,6},{8,9},{9,8},{10,11... | collective-permute-start | bytes 700424 | tf_op jit(solution)/shard_map/ppermute | solution.py:30
  27.3 6.3 %collective-permute-start.9 = (bf16[16,7296]{1,0:T(8,128)(2,1)S(1)}, bf16[16,7296]{1,0:T(8,128)(2,1)S(1)}, u32[]{:S(2)}, u32[]{:S(2)}) collective-permute-start(bf16[16,7296]{1,0:T(8,128)(2,1)S(1)} %pad_maximum_fusion.2), channel_id=1, source_target_pairs={{0,1},{1,0},{2,3},{3,2},{4,5},{5,4},{6,7},{7,6},{8,9},{9,8},{10,11... | collective-permute-start | bytes 700424 | tf_op jit(solution)/shard_map/ppermute | solution.py:30
  28.9 5.5 %collective-permute-start.10 = (bf16[16,7296]{1,0:T(8,128)(2,1)S(1)}, bf16[16,7296]{1,0:T(8,128)(2,1)S(1)}, u32[]{:S(2)}, u32[]{:S(2)}) collective-permute-start(bf16[16,7296]{1,0:T(8,128)(2,1)S(1)} %pad_maximum_fusion.3), channel_id=1, source_target_pairs={{0,1},{1,0},{2,3},{3,2},{4,5},{5,4},{6,7},{7,6},{8,9},{9,8},{10,11... | collective-permute-start | bytes 700424 | tf_op jit(solution)/shard_map/ppermute | solution.py:30
  44.7 3.4 %collective-permute-start.14 = (bf16[16,7168]{1,0:T(8,128)(2,1)S(1)}, bf16[16,7168]{1,0:T(8,128)(2,1)S(1)}, u32[]{:S(2)}, u32[]{:S(2)}) collective-permute-start(bf16[16,7168]{1,0:T(8,128)(2,1)S(1)} %get-tuple-element.19), channel_id=1, source_target_pairs={{0,1},{1,0},{2,3},{3,2},{4,5},{5,4},{6,7},{7,6},{8,9},{9,8},{10,11... | collective-permute-start | bytes 688136 | tf_op jit(solution)/shard_map/ppermute | solution.py:30
  44.8 3.3 %collective-permute-start.17 = (bf16[16,7168]{1,0:T(8,128)(2,1)S(1)}, bf16[16,7168]{1,0:T(8,128)(2,1)S(1)}, u32[]{:S(2)}, u32[]{:S(2)}) collective-permute-start(bf16[16,7168]{1,0:T(8,128)(2,1)S(1)} %get-tuple-element.18), channel_id=1, source_target_pairs={{0,1},{1,0},{2,3},{3,2},{4,5},{5,4},{6,7},{7,6},{8,9},{9,8},{10,11... | collective-permute-start | bytes 688136 | tf_op jit(solution)/shard_map/ppermute | solution.py:30
  45.2 2.9 %collective-permute-start.20 = (bf16[16,7168]{1,0:T(8,128)(2,1)S(1)}, bf16[16,7168]{1,0:T(8,128)(2,1)S(1)}, u32[]{:S(2)}, u32[]{:S(2)}) collective-permute-start(bf16[16,7168]{1,0:T(8,128)(2,1)S(1)} %get-tuple-element.17), channel_id=1, source_target_pairs={{0,1},{1,0},{2,3},{3,2},{4,5},{5,4},{6,7},{7,6},{8,9},{9,8},{10,11... | collective-permute-start | bytes 688136 | tf_op jit(solution)/shard_map/ppermute | solution.py:30
  46.0 13.6 %collective-permute-start.23 = (bf16[1,576]{1,0:T(2,128)(2,1)S(1)}, bf16[1,576]{1,0:T(2,128)(2,1)S(1)}, u32[]{:S(2)}, u32[]{:S(2)}) collective-permute-start(bf16[1,576]{1,0:T(2,128)(2,1)S(1)} %constant_dynamic-slice_fusion), channel_id=1, source_target_pairs={{0,15},{1,0},{2,1},{3,2},{4,3},{5,4},{6,5},{7,6},{8,7},{9,8},{10,9... | collective-permute-start | bytes 3464 | tf_op jit(solution)/shard_map/ppermute | solution.py:21
  49.0 19.5 %collective-permute-start.12 = (bf16[8,7168]{1,0:T(8,128)(2,1)}, bf16[8,7168]{1,0:T(8,128)(2,1)}, u32[]{:S(2)}, u32[]{:S(2)}) collective-permute-start(bf16[8,7168]{1,0:T(8,128)(2,1)} %slice.84), channel_id=1, source_target_pairs={{0,2},{1,3},{2,0},{3,1},{4,6},{5,7},{6,4},{7,5},{8,10},{9,11},{10,... | collective-permute-start | bytes 344072 | tf_op jit(solution)/shard_map/ppermute | solution.py:30
  64.2 11.1 %collective-permute-start.24 = (bf16[1,128,512]{2,1,0:T(8,128)(2,1)S(1)}, bf16[1,128,512]{2,1,0:T(8,128)(2,1)S(1)}, u32[]{:S(2)}, u32[]{:S(2)}) collective-permute-start(bf16[1,128,512]{2,1,0:T(8,128)(2,1)S(1)} %shard_map.123), channel_id=1, source_target_pairs={{0,1},{1,2},{2,3},{3,4},{4,5},{5,6},{6,7},{7,8},{8,9},{9,10},{10,1... | collective-permute-start | bytes 393224 | tf_op jit(solution)/shard_map/ppermute | solution.py:21
  64.3 5.5 %collective-permute-start.15 = (bf16[8,7168]{1,0:T(8,128)(2,1)S(1)}, bf16[8,7168]{1,0:T(8,128)(2,1)S(1)}, u32[]{:S(2)}, u32[]{:S(2)}) collective-permute-start(bf16[8,7168]{1,0:T(8,128)(2,1)S(1)} %slice.88), channel_id=1, source_target_pairs={{0,2},{1,3},{2,0},{3,1},{4,6},{5,7},{6,4},{7,5},{8,10},{9,11},{10,... | collective-permute-start | bytes 344072 | tf_op jit(solution)/shard_map/ppermute | solution.py:30
  66.4 7.5 %collective-permute-start.18 = (bf16[8,7168]{1,0:T(8,128)(2,1)S(1)}, bf16[8,7168]{1,0:T(8,128)(2,1)S(1)}, u32[]{:S(2)}, u32[]{:S(2)}) collective-permute-start(bf16[8,7168]{1,0:T(8,128)(2,1)S(1)} %slice.92), channel_id=1, source_target_pairs={{0,2},{1,3},{2,0},{3,1},{4,6},{5,7},{6,4},{7,5},{8,10},{9,11},{10,... | collective-permute-start | bytes 344072 | tf_op jit(solution)/shard_map/ppermute | solution.py:30
  66.5 9.8 %collective-permute-start.21 = (bf16[8,7168]{1,0:T(8,128)(2,1)S(1)}, bf16[8,7168]{1,0:T(8,128)(2,1)S(1)}, u32[]{:S(2)}, u32[]{:S(2)}) collective-permute-start(bf16[8,7168]{1,0:T(8,128)(2,1)S(1)} %slice.96), channel_id=1, source_target_pairs={{0,2},{1,3},{2,0},{3,1},{4,6},{5,7},{6,4},{7,5},{8,10},{9,11},{10,... | collective-permute-start | bytes 344072 | tf_op jit(solution)/shard_map/ppermute | solution.py:30
  69.5 6.8 %collective-permute-start.13 = (bf16[8,7168]{1,0:T(8,128)(2,1)S(1)}, bf16[8,7168]{1,0:T(8,128)(2,1)S(1)}, u32[]{:S(2)}, u32[]{:S(2)}) collective-permute-start(bf16[8,7168]{1,0:T(8,128)(2,1)S(1)} %add_convert_fusion.4), channel_id=1, source_target_pairs={{0,12},{1,13},{2,14},{3,15},{4,0},{5,1},{6,2},{7,3},{8,4},{9,5},{1... | collective-permute-start | bytes 344072 | tf_op jit(solution)/shard_map/ppermute | solution.py:21
  69.9 6.6 %collective-permute-start.16 = (bf16[8,7168]{1,0:T(8,128)(2,1)S(1)}, bf16[8,7168]{1,0:T(8,128)(2,1)S(1)}, u32[]{:S(2)}, u32[]{:S(2)}) collective-permute-start(bf16[8,7168]{1,0:T(8,128)(2,1)S(1)} %add_convert_fusion.3), channel_id=1, source_target_pairs={{0,8},{1,9},{2,10},{3,11},{4,12},{5,13},{6,14},{7,15},{8,0},{9,1},... | collective-permute-start | bytes 344072 | tf_op jit(solution)/shard_map/ppermute | solution.py:21
  73.9 8.0 %collective-permute-start.19 = (bf16[8,7168]{1,0:T(8,128)(2,1)S(1)}, bf16[8,7168]{1,0:T(8,128)(2,1)S(1)}, u32[]{:S(2)}, u32[]{:S(2)}) collective-permute-start(bf16[8,7168]{1,0:T(8,128)(2,1)S(1)} %add_convert_fusion.2), channel_id=1, source_target_pairs={{0,4},{1,5},{2,6},{3,7},{4,8},{5,9},{6,10},{7,11},{8,12},{9,13},{1... | collective-permute-start | bytes 344072 | tf_op jit(solution)/shard_map/ppermute | solution.py:21
  (9 other events, 77.1 us)

commit v3 on v1

v3 whole, which is shorter than its diff:
```python
import functools
import math

import jax
import jax.numpy as jnp
from jax import lax
from jax.experimental import pallas as pl
from jax.experimental.pallas import tpu as pltpu
from jax.sharding import PartitionSpec as P

NOPE = 512
SPLIT = 8
LANES = 128
CHUNK = 1024
MIB = 1024 * 1024

score_scale = 1.0 / math.sqrt(192.0)

WHOLE = pl.BlockSpec(memory_space=pltpu.VMEM)
SCALARS = pl.BlockSpec(memory_space=pltpu.SMEM)
APART = pl.BlockSpec(memory_space=pl.ANY)
MAIN = pl.BlockSpec(memory_space=pltpu.HBM)


def shifted(value, axis, steps):
    count = lax.axis_size(axis)
    pairs = [(source, (source + steps) % count) for source in range(count)]
    return lax.ppermute(value, axis, pairs)


def rotated(value, axis, steps):
    return shifted(value, axis, 4 * steps)


def swapped(value, axis, bit):
    pairs = [(source, source ^ bit) for source in range(lax.axis_size(axis))]
    return lax.ppermute(value, axis, pairs)


def prepare_body(groups, place, moved, hidden, ids, gates, query, own, rows, payload, sem):
    leaving = moved[place[0]]
    width = query.shape[1]
    copy = pltpu.make_async_copy(query.at[leaving], payload.at[pl.ds(0, width)], sem)
    copy.start()
    tokens, model_width = hidden.shape
    rows[:, :model_width] = hidden[...]
    lane = lax.broadcasted_iota(jnp.int32, (tokens, rows.shape[1] - model_width), 1)
    part = (lane >= groups).astype(jnp.int32) + (lane >= 2 * groups).astype(jnp.int32)
    group = lane - groups * part
    coefficient = jnp.zeros(lane.shape, jnp.float32)
    for k in range(ids.shape[1]):
        coefficient += jnp.where(ids[:, k : k + 1] == group, gates[:, k : k + 1], 0.0)
    high = coefficient.astype(jnp.bfloat16).astype(jnp.float32)
    middle = (coefficient - high).astype(jnp.bfloat16).astype(jnp.float32)
    low = coefficient - high - middle
    pieces = jnp.where(part == 0, high, jnp.where(part == 1, middle, low))
    rows[:, model_width:] = jnp.where(lane < 3 * groups, pieces, 0.0).astype(jnp.bfloat16)
    slots = lax.broadcasted_iota(jnp.int32, own.shape, 0)
    latent = jnp.sum(
        jnp.where(slots == leaving, own[...].astype(jnp.float32), 0.0), axis=0, keepdims=True
    )
    extra = payload.shape[0] - width
    row = lax.broadcasted_iota(jnp.int32, (extra, LANES), 0)
    block = jnp.zeros((extra, LANES), jnp.float32)
    latent = jnp.concatenate([latent, jnp.zeros((1, -width % LANES), jnp.float32)], axis=1)
    for r in range(latent.shape[1] // LANES):
        block = jnp.where(row == r, latent[:, r * LANES : (r + 1) * LANES], block)
    payload[width:, :] = block.astype(jnp.bfloat16)
    copy.wait()


def prepare(place, moved, hidden, ids, gates, query_t, own, groups):
    tokens, model_width = hidden.shape
    requests, width, heads = query_t.shape
    tail = -(-3 * groups // LANES) * LANES
    extra = -(-width // (16 * LANES)) * 16
    return pl.pallas_call(
        functools.partial(prepare_body, groups),
        out_shape=[
            jax.ShapeDtypeStruct((tokens, model_width + tail), jnp.bfloat16),
            jax.ShapeDtypeStruct((width + extra, heads), jnp.bfloat16),
        ],
        in_specs=[SCALARS, SCALARS, WHOLE, WHOLE, WHOLE, MAIN, WHOLE],
        out_specs=[WHOLE, WHOLE],
        scratch_shapes=[pltpu.SemaphoreType.DMA],
        compiler_params=pltpu.CompilerParams(vmem_limit_bytes=8 * MIB),
    )(place, moved, hidden, ids, gates, query_t, own)


def attend_body(place, moved, lengths, query, own, payload, cache, after, home, away, keys, sems):
    requests, width, positions = cache.shape
    copies = [
        pltpu.make_async_copy(cache.at[j], keys.at[j], sems.at[j]) for j in range(requests)
    ]
    for copy in copies:
        copy.start()
    leaving = moved[place[0]]
    tail = payload[width:, :].astype(jnp.float32)
    visiting = jnp.concatenate([tail[r : r + 1] for r in range(-(-width // LANES))], axis=1)
    visiting = visiting[:, :width]
    for j in range(requests):
        here = leaving == j
        asked = jnp.where(here, payload[:width, :], query[j]).T
        latent = jnp.where(here, visiting, own[j : j + 1, :].astype(jnp.float32))
        copies[j].wait()
        scores = jnp.dot(asked, keys[j], preferred_element_type=jnp.float32) * score_scale
        own_score = (
            jnp.sum(asked.astype(jnp.float32) * latent, axis=1, keepdims=True) * score_scale
        )
        live = lax.broadcasted_iota(jnp.int32, scores.shape, 1)
        scores = jnp.where(live < lengths[place[0] * requests + j], scores, -jnp.inf)
        top_score = jnp.maximum(jnp.max(scores, axis=1, keepdims=True), own_score)
        raised = jnp.exp(scores - top_score)
        raised_own = jnp.exp(own_score - top_score)
        share = 1.0 / (jnp.sum(raised, axis=1, keepdims=True) + raised_own)
        weights = (raised * share).astype(jnp.bfloat16)
        weight_own = (raised_own * share).astype(jnp.bfloat16).astype(jnp.float32)
        mixed = lax.dot_general(
            weights,
            keys[j, :NOPE],
            (((1,), (1,)), ((), ())),
            preferred_element_type=jnp.float32,
        )
        result = (mixed + weight_own * latent[:, :NOPE]).astype(jnp.bfloat16)
        home[j] = result

        @pl.when(here)
        def _():
            away[...] = result


def attend(place, moved, lengths, query_t, own, payload, cache_t, after):
    requests, width, heads = query_t.shape
    positions = cache_t.shape[2]
    return pl.pallas_call(
        attend_body,
        out_shape=[
            jax.ShapeDtypeStruct((requests, heads, NOPE), jnp.bfloat16),
            jax.ShapeDtypeStruct((heads, NOPE), jnp.bfloat16),
        ],
        in_specs=[SCALARS, SCALARS, SCALARS, WHOLE, WHOLE, WHOLE, MAIN, APART],
        out_specs=[WHOLE, WHOLE],
        scratch_shapes=[
            pltpu.VMEM((requests, width, positions), jnp.bfloat16),
            pltpu.SemaphoreType.DMA((requests,)),
        ],
        compiler_params=pltpu.CompilerParams(vmem_limit_bytes=24 * MIB),
        cost_estimate=pl.CostEstimate(
            flops=2 * requests * heads * positions * (width + NOPE),
            bytes_accessed=2 * requests * width * positions,
            transcendentals=requests * heads * positions,
        ),
    )(place, moved, lengths, query_t, own, payload, cache_t, after)


def expert_body(count, groups, place, w_gate, w_up, w_down, after, *refs):
    blocks, outs = refs[:count], refs[count:-4]
    first, second, sems, last_sem = refs[-4:]
    keeps, sends = outs[: count // 2], outs[count // 2 :]
    model_width = w_gate.shape[1]
    hidden = w_gate.shape[2]
    steps = model_width // CHUNK
    copies = []
    for s in range(steps):
        at = pl.ds(s * CHUNK, CHUNK)
        copies.append(
            [
                pltpu.make_async_copy(w_gate.at[0, at], first.at[at, :hidden], sems.at[2 * s]),
                pltpu.make_async_copy(w_up.at[0, at], first.at[at, hidden:], sems.at[2 * s + 1]),
            ]
        )
    for pair in copies:
        for copy in pair:
            copy.start()
    last = pltpu.make_async_copy(w_down.at[0], second, last_sem)
    last.start()

    def joined(at):
        return jnp.concatenate([block[:, at].astype(jnp.float32) for block in blocks], axis=0)

    total = None
    for s in range(steps):
        at = slice(s * CHUNK, (s + 1) * CHUNK)
        rows = joined(at).astype(jnp.bfloat16)
        for copy in copies[s]:
            copy.wait()
        term = jnp.dot(rows, first[at, :], preferred_element_type=jnp.float32)
        total = term if total is None else total + term
    gate, up = total[:, :hidden], total[:, hidden:]
    activated = (gate / (1.0 + jnp.exp(-gate)) * up).astype(jnp.bfloat16)
    parts = joined(slice(model_width, blocks[0].shape[1]))
    lane = lax.broadcasted_iota(jnp.int32, parts.shape, 1)
    mine = place[0] // SPLIT
    picked = (lane == mine) | (lane == mine + groups) | (lane == mine + 2 * groups)
    scale = jnp.sum(jnp.where(picked, parts, 0.0), axis=1, keepdims=True)
    tokens = blocks[0].shape[0]
    half = count // 2 * tokens
    last.wait()
    for s in range(steps):
        at = slice(s * CHUNK, (s + 1) * CHUNK)
        part = jnp.dot(activated, second[:, at], preferred_element_type=jnp.float32) * scale
        for i, send in enumerate(sends):
            low = half + 2 * tokens * i
            send[:, at] = part[low : low + 2 * tokens].astype(jnp.bfloat16)
        for i, keep in enumerate(keeps):
            keep[:, at] = part[tokens * i : tokens * (i + 1)].astype(jnp.bfloat16)


def expert(place, w_gate, w_up, w_down, after, blocks, groups):
    count = len(blocks)
    tokens = blocks[0].shape[0]
    _, model_width, hidden = w_gate.shape
    keep = jax.ShapeDtypeStruct((tokens, model_width), jnp.bfloat16)
    send = jax.ShapeDtypeStruct((2 * tokens, model_width), jnp.bfloat16)
    outs = pl.pallas_call(
        functools.partial(expert_body, count, groups),
        out_shape=[keep] * (count // 2) + [send] * (count // 4),
        in_specs=[SCALARS, MAIN, MAIN, MAIN, APART] + [WHOLE] * count,
        out_specs=[WHOLE] * (count // 2 + count // 4),
        scratch_shapes=[
            pltpu.VMEM((model_width, 2 * hidden), jnp.bfloat16),
            pltpu.VMEM((hidden, model_width), jnp.bfloat16),
            pltpu.SemaphoreType.DMA((2 * (model_width // CHUNK),)),
            pltpu.SemaphoreType.DMA,
        ],
        compiler_params=pltpu.CompilerParams(vmem_limit_bytes=40 * MIB),
        cost_estimate=pl.CostEstimate(
            flops=6 * count * tokens * model_width * hidden,
            bytes_accessed=6 * model_width * hidden,
            transcendentals=count * tokens * hidden,
        ),
    )(place, w_gate, w_up, w_down, after, *blocks)
    return outs[: count // 2], outs[count // 2 :]


def added(*terms):
    return sum(term.astype(jnp.float32) for term in terms).astype(jnp.bfloat16)


def per_device(
    hidden_rows,
    group_ids,
    route_gates,
    w_gate,
    w_up,
    w_down,
    queries,
    new_latent,
    latent_cache,
    cache_lengths,
    moved_slot,
):
    axis = "ep"
    ranks = lax.axis_size(axis)
    turns = ranks // 4
    groups = ranks // SPLIT
    tokens = hidden_rows.shape[0]
    position = lax.axis_index(axis)
    place = position[None]
    query_t = jnp.swapaxes(queries, 1, 2)
    cache_t = jnp.swapaxes(latent_cache, 1, 2)

    rows, payload = prepare(
        place, moved_slot, hidden_rows, group_ids, route_gates, query_t, new_latent, groups
    )

    columns = [rows] + [rotated(rows, axis, r) for r in range(1, turns)]
    across = [swapped(own, axis, 2) for own in columns]
    near = [block for pair in zip(columns, across) for block in pair]
    blocks = near + [swapped(block, axis, 1) for block in near]

    visiting = shifted(payload, axis, -1)
    home, away = attend(
        place, moved_slot, cache_lengths, query_t, new_latent, visiting, cache_t, columns[-1]
    )
    returned = shifted(away, axis, 1)

    keeps, sends = expert(place, w_gate, w_up, w_down, away, blocks, groups)
    terms = []
    for r in list(range(1, turns)) + [0]:
        chip = swapped(sends[r], axis, 1)
        crossed = swapped(added(keeps[2 * r + 1], chip[tokens:]), axis, 2)
        both = [keeps[2 * r], chip[:tokens], crossed]
        terms += both if r == 0 else [rotated(added(*both), axis, -r)]
    moe_out = added(*terms)
    leaving = lax.dynamic_index_in_dim(moved_slot, position, 0, keepdims=False)
    attn_out = lax.dynamic_update_slice_in_dim(home, returned[None], leaving, 0)
    return (moe_out, attn_out)


def solution(mesh):
    placed = (
        P(("group", "ep"), None),
        P(("group", "ep"), None),
        P(("group", "ep"), None),
        P("ep", None, None),
        P("ep", None, None),
        P("ep", None, None),
        P(("group", "ep"), None, None),
        P(("group", "ep"), None),
        P(("group", "ep"), None, None),
        P("group"),
        P("group"),
    )
    return jax.shard_map(
        per_device,
        mesh=mesh,
        in_specs=placed,
        out_specs=(P(("group", "ep"), None), P(("group", "ep"), None, None)),
        check_vma=False,
    )
```

time: 129 us -> 72.4 us (0.56)
  waiting for transfers between devices: 81.3 us -> 25 us
  starting transfers between devices: 2.58 us -> 20.7 us
  between operations: 18.1 us -> 2.75 us
  matrix products: 7.21 us -> 0 us
  Pallas kernels: 6.52 us -> 11 us
  other arithmetic: 4.58 us -> 1 us
  local copies, waits for them, and re-layouts: 8.3 us -> 11.5 us
    all_gather x1 -> x0, waiting for transfers between devices: 44.4 us -> none  [per_device(): all_rows = lax.all_gather(rows, 'ep', axis=0, tiled=True)]
    reduce_scatter x1 -> x0, waiting for transfers between devices: 36.9 us -> none  [per_device(): moe_out = lax.psum_scatter(partial, 'ep', scatter_dimension=0, tiled=True)]
    ppermute x3 -> x8, waiting for transfers between devices: 0.01 us -> 13.8 us  [shifted(): return lax.ppermute(value, axis, pairs)]
    ppermute x0 -> x20, starting transfers between devices: none -> 11.3 us  [swapped(): return lax.ppermute(value, axis, pairs)]
    ppermute x0 -> x20, waiting for transfers between devices: none -> 11.3 us  [swapped(): return lax.ppermute(value, axis, pairs)]
    dot_general x2 -> x0, matrix products: 7.21 us -> none  [the longest x1 4.52 us: per_device(): jnp.dot(activated, w_down[0], preferred_element_type=jnp.float32)]
    ppermute x3 -> x8, starting transfers between devices: 2.5 us -> 9.42 us  [shifted(): return lax.ppermute(value, axis, pairs)]
    unnamed x15 -> x28, local copies, waits for them, and re-layouts: 5.65 us -> 10.2 us
  transfers between devices with their start and end apart: 5 -> 28, of which waited for: 2 -> 10; matrix products, arithmetic and copies ran while one was open for 3% -> 2% of each run, Pallas kernels for 5% -> 9%
where the time goes in v3:
time: 72.4 us; the launch traced here: 72 us
  waiting for transfers between devices  25 us (35%)
  starting transfers between devices  20.7 us (29%)
  local copies, waits for them, and re-layouts  11.5 us (16%)
  Pallas kernels  11 us (15%)
  between operations  2.75 us (4%)
  other arithmetic  1 us (1%)
    ppermute x8, waiting for transfers between devices, shifted(): return lax.ppermute(value, axis, pairs)  13.8 us
    ppermute x20, starting transfers between devices, swapped(): return lax.ppermute(value, axis, pairs)  11.3 us
    ppermute x20, waiting for transfers between devices, swapped(): return lax.ppermute(value, axis, pairs)  11.3 us
    unnamed x28, local copies, waits for them, and re-layouts  10.2 us
    ppermute x8, starting transfers between devices, shifted(): return lax.ppermute(value, axis, pairs)  9.42 us
    pallas_call x1, Pallas kernels, attend(): pl.pallas_call(attend_body, out_shape=[jax.ShapeDtypeStruct((requests, he...  6.71 us
    pallas_call x1, Pallas kernels, expert(): pl.pallas_call(functools.partial(expert_body, count, groups), out_shape=[...  3.46 us
  transfers between devices with their start and end apart: 28, of which 10 were waited for; matrix products, arithmetic and copies ran while one was open for 2% of the time, Pallas kernels for 9%

profile of v3, /device:TPU:0, one launch (start us, length us, event | category | flops | bytes accessed | tf_op | source)
XLA Modules:
  0.0 72.0 jit_solution(6430964193161403213)
XLA Ops:
  2.1 1.1 %copy-done.1 = bf16[4,128,576]{1,2,0:T(8,128)(2,1)S(1)} copy-done((bf16[4,128,576]{1,2,0:T(8,128)(2,1)S(1)}, bf16[4,128,576]{1,2,0:T(8,128)(2,1)}, u32[]{:S(2)}) %copy-start.1) | copy-done | bytes 589848
  3.2 0.9 %copy-done.6 = bf16[8,7168]{1,0:T(8,128)(2,1)S(1)} copy-done((bf16[8,7168]{1,0:T(8,128)(2,1)S(1)}, bf16[8,7168]{1,0:T(8,128)(2,1)}, u32[]{:S(2)}) %copy-start.6) | copy-done | bytes 114712
  5.5 0.8 %shard_map.122 = (bf16[8,7296]{1,0:T(8,128)(2,1)S(1)}, bf16[592,128]{1,0:T(8,128)(2,1)S(1)}) custom-call(s32[1]{0:T(128)} %bitcast.place, s32[16]{0:T(128)S(1)} %copy-done.9, bf16[8,7168]{1,0:T(8,128)(2,1)S(1)} %copy-done.6, s32[8,2]{1,0:T(8,128)S(1)} %copy.13.ids, f32[8,2]{1,0:T(8,128)S(1)} %copy.14.gates, bf16[4,576,128]{2,1,0:T(8,128)(2,1)S(1)} %bitcast.7, ...), custom_call_target="tpu_custom_call" | custom-call | tf_op jit(solution)/shard_map/pallas_call | solution.py:77
  6.3 5.1 %collective-permute-start.1 = (bf16[8,7296]{1,0:T(8,128)(2,1)S(1)}, bf16[8,7296]{1,0:T(8,128)(2,1)S(1)}, u32[]{:S(2)}, u32[]{:S(2)}) collective-permute-start(bf16[8,7296]{1,0:T(8,128)(2,1)S(1)} %get-tuple-element.19.refs_0_), channel_id=1, source_target_pairs={{0,12},{1,13},{2,14},{3,15},{4,0},{5,1},{6,2},{7,3},{8,4},{9,5},{1... | collective-permute-start | bytes 350216 | tf_op jit(solution)/shard_map/ppermute | solution.py:28
  12.0 1.6 %collective-permute-start.3 = (bf16[8,7296]{1,0:T(8,128)(2,1)S(1)}, bf16[8,7296]{1,0:T(8,128)(2,1)S(1)}, u32[]{:S(2)}, u32[]{:S(2)}) collective-permute-start(bf16[8,7296]{1,0:T(8,128)(2,1)S(1)} %get-tuple-element.19.refs_0_), channel_id=1, source_target_pairs={{0,4},{1,5},{2,6},{3,7},{4,8},{5,9},{6,10},{7,11},{8,12},{9,13},{1... | collective-permute-start | bytes 350216 | tf_op jit(solution)/shard_map/ppermute | solution.py:28
  13.9 1.1 %collective-permute-done.1.after.refs_6_ = bf16[8,7296]{1,0:T(8,128)(2,1)S(1)} collective-permute-done((bf16[8,7296]{1,0:T(8,128)(2,1)S(1)}, bf16[8,7296]{1,0:T(8,128)(2,1)S(1)}, u32[]{:S(2)}, u32[]{:S(2)}) %collective-permute-start.1) | collective-permute-done | bytes 116768 | tf_op jit(solution)/shard_map/ppermute | solution.py:28
  15.0 5.0 %collective-permute-done.3.refs_2_ = bf16[8,7296]{1,0:T(8,128)(2,1)S(1)} collective-permute-done((bf16[8,7296]{1,0:T(8,128)(2,1)S(1)}, bf16[8,7296]{1,0:T(8,128)(2,1)S(1)}, u32[]{:S(2)}, u32[]{:S(2)}) %collective-permute-start.3) | collective-permute-done | bytes 116768 | tf_op jit(solution)/shard_map/ppermute | solution.py:28
  20.0 0.8 %collective-permute-start.7 = (bf16[8,7296]{1,0:T(8,128)(2,1)S(1)}, bf16[8,7296]{1,0:T(8,128)(2,1)S(1)}, u32[]{:S(2)}, u32[]{:S(2)}) collective-permute-start(bf16[8,7296]{1,0:T(8,128)(2,1)S(1)} %collective-permute-done.1.after.refs_6_), channel_id=1, source_target_pairs={{0,2},{1,3},{2,0},{3,1},{4,6},{5,7},{6,4},{7,5},{8,10},{9,11},{10,... | collective-permute-start | bytes 350216 | tf_op jit(solution)/shard_map/ppermute | solution.py:37
  20.8 2.1 %collective-permute-done.5.refs_4_ = bf16[8,7296]{1,0:T(8,128)(2,1)S(1)} collective-permute-done((bf16[8,7296]{1,0:T(8,128)(2,1)S(1)}, bf16[8,7296]{1,0:T(8,128)(2,1)S(1)}, u32[]{:S(2)}, u32[]{:S(2)}) %collective-permute-start.5) | collective-permute-done | bytes 116768 | tf_op jit(solution)/shard_map/ppermute | solution.py:28
  22.9 1.5 %collective-permute-start.4 = (bf16[8,7296]{1,0:T(8,128)(2,1)S(1)}, bf16[8,7296]{1,0:T(8,128)(2,1)S(1)}, u32[]{:S(2)}, u32[]{:S(2)}) collective-permute-start(bf16[8,7296]{1,0:T(8,128)(2,1)S(1)} %collective-permute-done.3.refs_2_), channel_id=1, source_target_pairs={{0,2},{1,3},{2,0},{3,1},{4,6},{5,7},{6,4},{7,5},{8,10},{9,11},{10,... | collective-permute-start | bytes 350216 | tf_op jit(solution)/shard_map/ppermute | solution.py:37
  25.6 3.4 %collective-permute-done.4.refs_3_ = bf16[8,7296]{1,0:T(8,128)(2,1)S(1)} collective-permute-done((bf16[8,7296]{1,0:T(8,128)(2,1)S(1)}, bf16[8,7296]{1,0:T(8,128)(2,1)S(1)}, u32[]{:S(2)}, u32[]{:S(2)}) %collective-permute-start.4) | collective-permute-done | bytes 116768 | tf_op jit(solution)/shard_map/ppermute | solution.py:37
  29.0 1.2 %collective-permute-done.6.refs_5_ = bf16[8,7296]{1,0:T(8,128)(2,1)S(1)} collective-permute-done((bf16[8,7296]{1,0:T(8,128)(2,1)S(1)}, bf16[8,7296]{1,0:T(8,128)(2,1)S(1)}, u32[]{:S(2)}, u32[]{:S(2)}) %collective-permute-start.6) | collective-permute-done | bytes 116768 | tf_op jit(solution)/shard_map/ppermute | solution.py:37
  30.8 2.3 %copy-done = bf16[4,1024,576]{1,2,0:T(8,128)(2,1)S(1)} copy-done((bf16[4,1024,576]{1,2,0:T(8,128)(2,1)S(1)}, bf16[4,1024,576]{1,2,0:T(8,128)(2,1)}, u32[]{:S(2)}) %copy-start) | copy-done | bytes 4718616
  33.1 1.1 %copy-done.2 = bf16[4,128,576]{1,2,0:T(8,128)(2,1)S(1)} copy-done((bf16[4,128,576]{1,2,0:T(8,128)(2,1)S(1)}, bf16[4,128,576]{1,2,0:T(8,128)(2,1)}, u32[]{:S(2)}) %copy-start.2) | copy-done | bytes 589848
  36.2 6.7 %shard_map.123 = (bf16[4,128,512]{2,1,0:T(8,128)(2,1)}, bf16[128,512]{1,0:T(8,128)(2,1)S(1)}) custom-call(s32[1]{0:T(128)} %bitcast.place, s32[16]{0:T(128)S(1)} %copy-done.10, s32[64]{0:T(128)S(1)} %copy-done.12, bf16[4,576,128]{2,1,0:T(8,128)(2,1)S(1)} %bitcast.8, bf16[4,576]{1,0:T(4,128)(2,1)S(1)} %copy-done.8, ...), custom_call_target="tpu_custom_call" | custom-call | flops 1140850688 | bytes 4718592 | tf_op jit(solution)/shard_map/pallas_call | solution.py:135
  43.0 3.5 %shard_map.124 = (bf16[8,7168]{1,0:T(8,128)(2,1)S(1)}, bf16[8,7168]{1,0:T(8,128)(2,1)S(1)}, bf16[8,7168]{1,0:T(8,128)(2,1)S(1)}, bf16[8,7168]{1,0:T(8,128)(2,1)S...) custom-call(s32[1]{0:T(128)} %bitcast.place, ...), custom_call_target="tpu_custom_call" | custom-call | flops 704643072 | bytes 5505024 | tf_op jit(solution)/shard_map/pallas_call | solution.py:215
  49.6 1.6 %collective-permute-start.19 = (bf16[16,7168]{1,0:T(8,128)(2,1)S(1)}, bf16[16,7168]{1,0:T(8,128)(2,1)S(1)}, u32[]{:S(2)}, u32[]{:S(2)}) collective-permute-start(bf16[16,7168]{1,0:T(8,128)(2,1)S(1)} %get-tuple-element.25), channel_id=1, source_target_pairs={{0,1},{1,0},{2,3},{3,2},{4,5},{5,4},{6,7},{7,6},{8,9},{9,8},{10,11... | collective-permute-start | bytes 688136 | tf_op jit(solution)/shard_map/ppermute | solution.py:37
  51.8 1.4 %collective-permute-start.17 = (bf16[8,7168]{1,0:T(8,128)(2,1)S(1)}, bf16[8,7168]{1,0:T(8,128)(2,1)S(1)}, u32[]{:S(2)}, u32[]{:S(2)}) collective-permute-start(bf16[8,7168]{1,0:T(8,128)(2,1)S(1)} %add_convert_fusion.7), channel_id=1, source_target_pairs={{0,2},{1,3},{2,0},{3,1},{4,6},{5,7},{6,4},{7,5},{8,10},{9,11},{10,... | collective-permute-start | bytes 344072 | tf_op jit(solution)/shard_map/ppermute | solution.py:37
  54.0 1.4 %collective-permute-start.23 = (bf16[8,7168]{1,0:T(8,128)(2,1)S(1)}, bf16[8,7168]{1,0:T(8,128)(2,1)S(1)}, u32[]{:S(2)}, u32[]{:S(2)}) collective-permute-start(bf16[8,7168]{1,0:T(8,128)(2,1)S(1)} %add_convert_fusion.3), channel_id=1, source_target_pairs={{0,2},{1,3},{2,0},{3,1},{4,6},{5,7},{6,4},{7,5},{8,10},{9,11},{10,... | collective-permute-start | bytes 344072 | tf_op jit(solution)/shard_map/ppermute | solution.py:37
  56.2 3.0 %collective-permute-done.17 = bf16[8,7168]{1,0:T(8,128)(2,1)S(1)} collective-permute-done((bf16[8,7168]{1,0:T(8,128)(2,1)S(1)}, bf16[8,7168]{1,0:T(8,128)(2,1)S(1)}, u32[]{:S(2)}, u32[]{:S(2)}) %collective-permute-start.17) | collective-permute-done | bytes 114720 | tf_op jit(solution)/shard_map/ppermute | solution.py:37
  59.3 1.6 %collective-permute-start.18 = (bf16[8,7168]{1,0:T(8,128)(2,1)S(1)}, bf16[8,7168]{1,0:T(8,128)(2,1)S(1)}, u32[]{:S(2)}, u32[]{:S(2)}) collective-permute-start(bf16[8,7168]{1,0:T(8,128)(2,1)S(1)} %add_convert_fusion.6), channel_id=1, source_target_pairs={{0,12},{1,13},{2,14},{3,15},{4,0},{5,1},{6,2},{7,3},{8,4},{9,5},{1... | collective-permute-start | bytes 344072 | tf_op jit(solution)/shard_map/ppermute | solution.py:28
  60.8 0.9 %collective-permute-done.20 = bf16[8,7168]{1,0:T(8,128)(2,1)S(1)} collective-permute-done((bf16[8,7168]{1,0:T(8,128)(2,1)S(1)}, bf16[8,7168]{1,0:T(8,128)(2,1)S(1)}, u32[]{:S(2)}, u32[]{:S(2)}) %collective-permute-start.20) | collective-permute-done | bytes 114720 | tf_op jit(solution)/shard_map/ppermute | solution.py:37
  62.1 2.0 %collective-permute-done.23 = bf16[8,7168]{1,0:T(8,128)(2,1)S(1)} collective-permute-done((bf16[8,7168]{1,0:T(8,128)(2,1)S(1)}, bf16[8,7168]{1,0:T(8,128)(2,1)S(1)}, u32[]{:S(2)}, u32[]{:S(2)}) %collective-permute-start.23) | collective-permute-done | bytes 114720 | tf_op jit(solution)/shard_map/ppermute | solution.py:37
  65.7 5.6 %collective-permute-done.21 = bf16[8,7168]{1,0:T(8,128)(2,1)S(1)} collective-permute-done((bf16[8,7168]{1,0:T(8,128)(2,1)S(1)}, bf16[8,7168]{1,0:T(8,128)(2,1)S(1)}, u32[]{:S(2)}, u32[]{:S(2)}) %collective-permute-start.21) | collective-permute-done | bytes 114720 | tf_op jit(solution)/shard_map/ppermute | solution.py:28
  (73 shorter events, 13.8 us)
Async XLA Ops:
  6.3 8.7 %collective-permute-start.1 = (bf16[8,7296]{1,0:T(8,128)(2,1)S(1)}, bf16[8,7296]{1,0:T(8,128)(2,1)S(1)}, u32[]{:S(2)}, u32[]{:S(2)}) collective-permute-start(bf16[8,7296]{1,0:T(8,128)(2,1)S(1)} %get-tuple-element.19.refs_0_), channel_id=1, source_target_pairs={{0,12},{1,13},{2,14},{3,15},{4,0},{5,1},{6,2},{7,3},{8,4},{9,5},{1... | collective-permute-start | bytes 350216 | tf_op jit(solution)/shard_map/ppermute | solution.py:28
  11.4 13.6 %collective-permute-start = (bf16[592,128]{1,0:T(8,128)(2,1)S(1)}, bf16[592,128]{1,0:T(8,128)(2,1)S(1)}, u32[]{:S(2)}, u32[]{:S(2)}) collective-permute-start(bf16[592,128]{1,0:T(8,128)(2,1)S(1)} %get-tuple-element.18), channel_id=1, source_target_pairs={{0,15},{1,0},{2,1},{3,2},{4,3},{5,4},{6,5},{7,6},{8,7},{9,8},{10,9... | collective-permute-start | bytes 454664 | tf_op jit(solution)/shard_map/ppermute | solution.py:28
  12.0 8.0 %collective-permute-start.3 = (bf16[8,7296]{1,0:T(8,128)(2,1)S(1)}, bf16[8,7296]{1,0:T(8,128)(2,1)S(1)}, u32[]{:S(2)}, u32[]{:S(2)}) collective-permute-start(bf16[8,7296]{1,0:T(8,128)(2,1)S(1)} %get-tuple-element.19.refs_0_), channel_id=1, source_target_pairs={{0,4},{1,5},{2,6},{3,7},{4,8},{5,9},{6,10},{7,11},{8,12},{9,13},{1... | collective-permute-start | bytes 350216 | tf_op jit(solution)/shard_map/ppermute | solution.py:28
  13.5 9.4 %collective-permute-start.5 = (bf16[8,7296]{1,0:T(8,128)(2,1)S(1)}, bf16[8,7296]{1,0:T(8,128)(2,1)S(1)}, u32[]{:S(2)}, u32[]{:S(2)}) collective-permute-start(bf16[8,7296]{1,0:T(8,128)(2,1)S(1)} %get-tuple-element.19.refs_0_), channel_id=1, source_target_pairs={{0,8},{1,9},{2,10},{3,11},{4,12},{5,13},{6,14},{7,15},{8,0},{9,1},... | collective-permute-start | bytes 350216 | tf_op jit(solution)/shard_map/ppermute | solution.py:28
  13.5 10.9 %collective-permute-start.2 = (bf16[8,7296]{1,0:T(8,128)(2,1)S(1)}, bf16[8,7296]{1,0:T(8,128)(2,1)S(1)}, u32[]{:S(2)}, u32[]{:S(2)}) collective-permute-start(bf16[8,7296]{1,0:T(8,128)(2,1)S(1)} %get-tuple-element.19.refs_0_), channel_id=1, source_target_pairs={{0,2},{1,3},{2,0},{3,1},{4,6},{5,7},{6,4},{7,5},{8,10},{9,11},{10,... | collective-permute-start | bytes 350216 | tf_op jit(solution)/shard_map/ppermute | solution.py:37
  15.0 10.0 %collective-permute-start.8 = (bf16[8,7296]{1,0:T(8,128)(2,1)S(1)}, bf16[8,7296]{1,0:T(8,128)(2,1)S(1)}, u32[]{:S(2)}, u32[]{:S(2)}) collective-permute-start(bf16[8,7296]{1,0:T(8,128)(2,1)S(1)} %get-tuple-element.19.refs_0_), channel_id=1, source_target_pairs={{0,1},{1,0},{2,3},{3,2},{4,5},{5,4},{6,7},{7,6},{8,9},{9,8},{10,11... | collective-permute-start | bytes 350216 | tf_op jit(solution)/shard_map/ppermute | solution.py:37
  20.0 5.5 %collective-permute-start.7 = (bf16[8,7296]{1,0:T(8,128)(2,1)S(1)}, bf16[8,7296]{1,0:T(8,128)(2,1)S(1)}, u32[]{:S(2)}, u32[]{:S(2)}) collective-permute-start(bf16[8,7296]{1,0:T(8,128)(2,1)S(1)} %collective-permute-done.1.after.refs_6_), channel_id=1, source_target_pairs={{0,2},{1,3},{2,0},{3,1},{4,6},{5,7},{6,4},{7,5},{8,10},{9,11},{10,... | collective-permute-start | bytes 350216 | tf_op jit(solution)/shard_map/ppermute | solution.py:37
  22.9 6.0 %collective-permute-start.4 = (bf16[8,7296]{1,0:T(8,128)(2,1)S(1)}, bf16[8,7296]{1,0:T(8,128)(2,1)S(1)}, u32[]{:S(2)}, u32[]{:S(2)}) collective-permute-start(bf16[8,7296]{1,0:T(8,128)(2,1)S(1)} %collective-permute-done.3.refs_2_), channel_id=1, source_target_pairs={{0,2},{1,3},{2,0},{3,1},{4,6},{5,7},{6,4},{7,5},{8,10},{9,11},{10,... | collective-permute-start | bytes 350216 | tf_op jit(solution)/shard_map/ppermute | solution.py:37
  24.4 5.8 %collective-permute-start.6 = (bf16[8,7296]{1,0:T(8,128)(2,1)S(1)}, bf16[8,7296]{1,0:T(8,128)(2,1)S(1)}, u32[]{:S(2)}, u32[]{:S(2)}) collective-permute-start(bf16[8,7296]{1,0:T(8,128)(2,1)S(1)} %collective-permute-done.5.refs_4_), channel_id=1, source_target_pairs={{0,2},{1,3},{2,0},{3,1},{4,6},{5,7},{6,4},{7,5},{8,10},{9,11},{10,... | collective-permute-start | bytes 350216 | tf_op jit(solution)/shard_map/ppermute | solution.py:37
  25.0 5.2 %collective-permute-start.14 = (bf16[8,7296]{1,0:T(8,128)(2,1)S(1)}, bf16[8,7296]{1,0:T(8,128)(2,1)S(1)}, u32[]{:S(2)}, u32[]{:S(2)}) collective-permute-start(bf16[8,7296]{1,0:T(8,128)(2,1)S(1)} %collective-permute-done.1.after.refs_6_), channel_id=1, source_target_pairs={{0,1},{1,0},{2,3},{3,2},{4,5},{5,4},{6,7},{7,6},{8,9},{9,8},{10,11... | collective-permute-start | bytes 350216 | tf_op jit(solution)/shard_map/ppermute | solution.py:37
  25.0 5.7 %collective-permute-start.10 = (bf16[8,7296]{1,0:T(8,128)(2,1)S(1)}, bf16[8,7296]{1,0:T(8,128)(2,1)S(1)}, u32[]{:S(2)}, u32[]{:S(2)}) collective-permute-start(bf16[8,7296]{1,0:T(8,128)(2,1)S(1)} %collective-permute-done.3.refs_2_), channel_id=1, source_target_pairs={{0,1},{1,0},{2,3},{3,2},{4,5},{5,4},{6,7},{7,6},{8,9},{9,8},{10,11... | collective-permute-start | bytes 350216 | tf_op jit(solution)/shard_map/ppermute | solution.py:37
  25.5 17.4 %collective-permute-start.12 = (bf16[8,7296]{1,0:T(8,128)(2,1)S(1)}, bf16[8,7296]{1,0:T(8,128)(2,1)S(1)}, u32[]{:S(2)}, u32[]{:S(2)}) collective-permute-start(bf16[8,7296]{1,0:T(8,128)(2,1)S(1)} %collective-permute-done.5.refs_4_), channel_id=1, source_target_pairs={{0,1},{1,0},{2,3},{3,2},{4,5},{5,4},{6,7},{7,6},{8,9},{9,8},{10,11... | collective-permute-start | bytes 350216 | tf_op jit(solution)/shard_map/ppermute | solution.py:37
  29.0 14.0 %collective-permute-start.9 = (bf16[8,7296]{1,0:T(8,128)(2,1)S(1)}, bf16[8,7296]{1,0:T(8,128)(2,1)S(1)}, u32[]{:S(2)}, u32[]{:S(2)}) collective-permute-start(bf16[8,7296]{1,0:T(8,128)(2,1)S(1)} %collective-permute-done.2.refs_1_), channel_id=1, source_target_pairs={{0,1},{1,0},{2,3},{3,2},{4,5},{5,4},{6,7},{7,6},{8,9},{9,8},{10,11... | collective-permute-start | bytes 350216 | tf_op jit(solution)/shard_map/ppermute | solution.py:37
  30.2 12.7 %collective-permute-start.15 = (bf16[8,7296]{1,0:T(8,128)(2,1)S(1)}, bf16[8,7296]{1,0:T(8,128)(2,1)S(1)}, u32[]{:S(2)}, u32[]{:S(2)}) collective-permute-start(bf16[8,7296]{1,0:T(8,128)(2,1)S(1)} %collective-permute-done.7.refs_7_), channel_id=1, source_target_pairs={{0,1},{1,0},{2,3},{3,2},{4,5},{5,4},{6,7},{7,6},{8,9},{9,8},{10,11... | collective-permute-start | bytes 350216 | tf_op jit(solution)/shard_map/ppermute | solution.py:37
  30.2 12.7 %collective-permute-start.11 = (bf16[8,7296]{1,0:T(8,128)(2,1)S(1)}, bf16[8,7296]{1,0:T(8,128)(2,1)S(1)}, u32[]{:S(2)}, u32[]{:S(2)}) collective-permute-start(bf16[8,7296]{1,0:T(8,128)(2,1)S(1)} %collective-permute-done.4.refs_3_), channel_id=1, source_target_pairs={{0,1},{1,0},{2,3},{3,2},{4,5},{5,4},{6,7},{7,6},{8,9},{9,8},{10,11... | collective-permute-start | bytes 350216 | tf_op jit(solution)/shard_map/ppermute | solution.py:37
  30.7 12.2 %collective-permute-start.13 = (bf16[8,7296]{1,0:T(8,128)(2,1)S(1)}, bf16[8,7296]{1,0:T(8,128)(2,1)S(1)}, u32[]{:S(2)}, u32[]{:S(2)}) collective-permute-start(bf16[8,7296]{1,0:T(8,128)(2,1)S(1)} %collective-permute-done.6.refs_5_), channel_id=1, source_target_pairs={{0,1},{1,0},{2,3},{3,2},{4,5},{5,4},{6,7},{7,6},{8,9},{9,8},{10,11... | collective-permute-start | bytes 350216 | tf_op jit(solution)/shard_map/ppermute | solution.py:37
  49.5 14.7 %collective-permute-start.27 = (bf16[128,512]{1,0:T(8,128)(2,1)S(1)}, bf16[128,512]{1,0:T(8,128)(2,1)S(1)}, u32[]{:S(2)}, u32[]{:S(2)}) collective-permute-start(bf16[128,512]{1,0:T(8,128)(2,1)S(1)} %get-tuple-element.20.after), channel_id=1, source_target_pairs={{0,1},{1,2},{2,3},{3,4},{4,5},{5,6},{6,7},{7,8},{8,9},{9,10},{10,1... | collective-permute-start | bytes 393224 | tf_op jit(solution)/shard_map/ppermute | solution.py:28
  51.8 7.4 %collective-permute-start.17 = (bf16[8,7168]{1,0:T(8,128)(2,1)S(1)}, bf16[8,7168]{1,0:T(8,128)(2,1)S(1)}, u32[]{:S(2)}, u32[]{:S(2)}) collective-permute-start(bf16[8,7168]{1,0:T(8,128)(2,1)S(1)} %add_convert_fusion.7), channel_id=1, source_target_pairs={{0,2},{1,3},{2,0},{3,1},{4,6},{5,7},{6,4},{7,5},{8,10},{9,11},{10,... | collective-permute-start | bytes 344072 | tf_op jit(solution)/shard_map/ppermute | solution.py:37
  53.2 8.5 %collective-permute-start.20 = (bf16[8,7168]{1,0:T(8,128)(2,1)S(1)}, bf16[8,7168]{1,0:T(8,128)(2,1)S(1)}, u32[]{:S(2)}, u32[]{:S(2)}) collective-permute-start(bf16[8,7168]{1,0:T(8,128)(2,1)S(1)} %add_convert_fusion.5), channel_id=1, source_target_pairs={{0,2},{1,3},{2,0},{3,1},{4,6},{5,7},{6,4},{7,5},{8,10},{9,11},{10,... | collective-permute-start | bytes 344072 | tf_op jit(solution)/shard_map/ppermute | solution.py:37
  54.0 10.1 %collective-permute-start.23 = (bf16[8,7168]{1,0:T(8,128)(2,1)S(1)}, bf16[8,7168]{1,0:T(8,128)(2,1)S(1)}, u32[]{:S(2)}, u32[]{:S(2)}) collective-permute-start(bf16[8,7168]{1,0:T(8,128)(2,1)S(1)} %add_convert_fusion.3), channel_id=1, source_target_pairs={{0,2},{1,3},{2,0},{3,1},{4,6},{5,7},{6,4},{7,5},{8,10},{9,11},{10,... | collective-permute-start | bytes 344072 | tf_op jit(solution)/shard_map/ppermute | solution.py:37
  55.4 10.3 %collective-permute-start.26 = (bf16[8,7168]{1,0:T(8,128)(2,1)S(1)}, bf16[8,7168]{1,0:T(8,128)(2,1)S(1)}, u32[]{:S(2)}, u32[]{:S(2)}) collective-permute-start(bf16[8,7168]{1,0:T(8,128)(2,1)S(1)} %add_convert_fusion.1), channel_id=1, source_target_pairs={{0,2},{1,3},{2,0},{3,1},{4,6},{5,7},{6,4},{7,5},{8,10},{9,11},{10,... | collective-permute-start | bytes 344072 | tf_op jit(solution)/shard_map/ppermute | solution.py:37
  59.3 6.4 %collective-permute-start.18 = (bf16[8,7168]{1,0:T(8,128)(2,1)S(1)}, bf16[8,7168]{1,0:T(8,128)(2,1)S(1)}, u32[]{:S(2)}, u32[]{:S(2)}) collective-permute-start(bf16[8,7168]{1,0:T(8,128)(2,1)S(1)} %add_convert_fusion.6), channel_id=1, source_target_pairs={{0,12},{1,13},{2,14},{3,15},{4,0},{5,1},{6,2},{7,3},{8,4},{9,5},{1... | collective-permute-start | bytes 344072 | tf_op jit(solution)/shard_map/ppermute | solution.py:28
  61.7 9.5 %collective-permute-start.21 = (bf16[8,7168]{1,0:T(8,128)(2,1)S(1)}, bf16[8,7168]{1,0:T(8,128)(2,1)S(1)}, u32[]{:S(2)}, u32[]{:S(2)}) collective-permute-start(bf16[8,7168]{1,0:T(8,128)(2,1)S(1)} %add_convert_fusion.4), channel_id=1, source_target_pairs={{0,8},{1,9},{2,10},{3,11},{4,12},{5,13},{6,14},{7,15},{8,0},{9,1},... | collective-permute-start | bytes 344072 | tf_op jit(solution)/shard_map/ppermute | solution.py:28
  64.2 7.1 %collective-permute-start.24 = (bf16[8,7168]{1,0:T(8,128)(2,1)S(1)}, bf16[8,7168]{1,0:T(8,128)(2,1)S(1)}, u32[]{:S(2)}, u32[]{:S(2)}) collective-permute-start(bf16[8,7168]{1,0:T(8,128)(2,1)S(1)} %add_convert_fusion.2), channel_id=1, source_target_pairs={{0,4},{1,5},{2,6},{3,7},{4,8},{5,9},{6,10},{7,11},{8,12},{9,13},{1... | collective-permute-start | bytes 344072 | tf_op jit(solution)/shard_map/ppermute | solution.py:28
  (17 other events, 48.6 us)

commit v4 on v3

--- a/solution.py
+++ b/solution.py
@@ -18,7 +18,6 @@
 
 WHOLE = pl.BlockSpec(memory_space=pltpu.VMEM)
 SCALARS = pl.BlockSpec(memory_space=pltpu.SMEM)
-APART = pl.BlockSpec(memory_space=pl.ANY)
 MAIN = pl.BlockSpec(memory_space=pltpu.HBM)
 
 
@@ -37,19 +36,24 @@
     return lax.ppermute(value, axis, pairs)
 
 
-def prepare_body(groups, place, moved, hidden, ids, gates, query, own, rows, payload, sem):
-    leaving = moved[place[0]]
+def prepare_body(groups, place, moved, hidden, ids, gates, query, own, rows, payload, *scratch):
+    moves, sems = scratch
+    tokens, model_width = hidden.shape
     width = query.shape[1]
-    copy = pltpu.make_async_copy(query.at[leaving], payload.at[pl.ds(0, width)], sem)
+    fetch = pltpu.make_async_copy(moved, moves, sems.at[0])
+    fetch.start()
+    fetch.wait()
+    leaving = moves[place[0]]
+    copy = pltpu.make_async_copy(query.at[leaving], payload.at[pl.ds(0, width)], sems.at[1])
     copy.start()
-    tokens, model_width = hidden.shape
     rows[:, :model_width] = hidden[...]
+    chosen, weight = ids[...].T, gates[...].T
     lane = lax.broadcasted_iota(jnp.int32, (tokens, rows.shape[1] - model_width), 1)
     part = (lane >= groups).astype(jnp.int32) + (lane >= 2 * groups).astype(jnp.int32)
     group = lane - groups * part
     coefficient = jnp.zeros(lane.shape, jnp.float32)
-    for k in range(ids.shape[1]):
-        coefficient += jnp.where(ids[:, k : k + 1] == group, gates[:, k : k + 1], 0.0)
+    for k in range(chosen.shape[1]):
+        coefficient += jnp.where(chosen[:, k : k + 1] == group, weight[:, k : k + 1], 0.0)
     high = coefficient.astype(jnp.bfloat16).astype(jnp.float32)
     middle = (coefficient - high).astype(jnp.bfloat16).astype(jnp.float32)
     low = coefficient - high - middle
@@ -69,7 +73,7 @@
     copy.wait()
 
 
-def prepare(place, moved, hidden, ids, gates, query_t, own, groups):
+def prepare(place, moved, hidden, ids_t, gates_t, query_t, own, groups):
     tokens, model_width = hidden.shape
     requests, width, heads = query_t.shape
     tail = -(-3 * groups // LANES) * LANES
@@ -80,27 +84,40 @@
             jax.ShapeDtypeStruct((tokens, model_width + tail), jnp.bfloat16),
             jax.ShapeDtypeStruct((width + extra, heads), jnp.bfloat16),
         ],
-        in_specs=[SCALARS, SCALARS, WHOLE, WHOLE, WHOLE, MAIN, WHOLE],
+        in_specs=[SCALARS, MAIN, WHOLE, WHOLE, WHOLE, MAIN, WHOLE],
         out_specs=[WHOLE, WHOLE],
-        scratch_shapes=[pltpu.SemaphoreType.DMA],
-        compiler_params=pltpu.CompilerParams(vmem_limit_bytes=8 * MIB),
-    )(place, moved, hidden, ids, gates, query_t, own)
-
-
-def attend_body(place, moved, lengths, query, own, payload, cache, after, home, away, keys, sems):
+        scratch_shapes=[
+            pltpu.SMEM(moved.shape, moved.dtype),
+            pltpu.SemaphoreType.DMA((2,)),
+        ],
+        compiler_params=pltpu.CompilerParams(vmem_limit_bytes=60 * MIB),
+        cost_estimate=pl.CostEstimate(flops=0, bytes_accessed=0, transcendentals=0),
+    )(place, moved, hidden, ids_t, gates_t, query_t, own)
+
+
+def attend_body(place, moved, lengths, query, own, payload, cache, home, away, mark, *scratch):
+    moves, extents, asking, keys, sems = scratch
     requests, width, positions = cache.shape
+    fetches = [
+        pltpu.make_async_copy(moved, moves, sems.at[0]),
+        pltpu.make_async_copy(lengths, extents, sems.at[1]),
+        pltpu.make_async_copy(query, asking, sems.at[2]),
+    ]
     copies = [
-        pltpu.make_async_copy(cache.at[j], keys.at[j], sems.at[j]) for j in range(requests)
+        pltpu.make_async_copy(cache.at[j], keys.at[j], sems.at[3 + j]) for j in range(requests)
     ]
-    for copy in copies:
-        copy.start()
-    leaving = moved[place[0]]
+    for fetch in fetches + copies:
+        fetch.start()
+    for fetch in fetches:
+        fetch.wait()
+    leaving = moves[place[0]]
+    mark[...] = jnp.full(mark.shape, leaving, jnp.int32)
     tail = payload[width:, :].astype(jnp.float32)
     visiting = jnp.concatenate([tail[r : r + 1] for r in range(-(-width // LANES))], axis=1)
     visiting = visiting[:, :width]
     for j in range(requests):
         here = leaving == j
-        asked = jnp.where(here, payload[:width, :], query[j]).T
+        asked = jnp.where(here, payload[:width, :], asking[j]).T
         latent = jnp.where(here, visiting, own[j : j + 1, :].astype(jnp.float32))
         copies[j].wait()
         scores = jnp.dot(asked, keys[j], preferred_element_type=jnp.float32) * score_scale
@@ -108,7 +125,7 @@
             jnp.sum(asked.astype(jnp.float32) * latent, axis=1, keepdims=True) * score_scale
         )
         live = lax.broadcasted_iota(jnp.int32, scores.shape, 1)
-        scores = jnp.where(live < lengths[place[0] * requests + j], scores, -jnp.inf)
+        scores = jnp.where(live < extents[place[0] * requests + j], scores, -jnp.inf)
         top_score = jnp.maximum(jnp.max(scores, axis=1, keepdims=True), own_score)
         raised = jnp.exp(scores - top_score)
         raised_own = jnp.exp(own_score - top_score)
@@ -129,7 +146,7 @@
             away[...] = result
 
 
-def attend(place, moved, lengths, query_t, own, payload, cache_t, after):
+def attend(place, moved, lengths, query_t, own, payload, cache_t):
     requests, width, heads = query_t.shape
     positions = cache_t.shape[2]
     return pl.pallas_call(
@@ -137,23 +154,27 @@
         out_shape=[
             jax.ShapeDtypeStruct((requests, heads, NOPE), jnp.bfloat16),
             jax.ShapeDtypeStruct((heads, NOPE), jnp.bfloat16),
-        ],
-        in_specs=[SCALARS, SCALARS, SCALARS, WHOLE, WHOLE, WHOLE, MAIN, APART],
-        out_specs=[WHOLE, WHOLE],
+            jax.ShapeDtypeStruct((8, LANES), jnp.int32),
+        ],
+        in_specs=[SCALARS, MAIN, MAIN, MAIN, WHOLE, WHOLE, MAIN],
+        out_specs=[WHOLE, WHOLE, WHOLE],
         scratch_shapes=[
-            pltpu.VMEM((requests, width, positions), jnp.bfloat16),
-            pltpu.SemaphoreType.DMA((requests,)),
-        ],
-        compiler_params=pltpu.CompilerParams(vmem_limit_bytes=24 * MIB),
+            pltpu.SMEM(moved.shape, moved.dtype),
+            pltpu.SMEM(lengths.shape, lengths.dtype),
+            pltpu.VMEM(query_t.shape, query_t.dtype),
+            pltpu.VMEM(cache_t.shape, cache_t.dtype),
+            pltpu.SemaphoreType.DMA((3 + requests,)),
+        ],
+        compiler_params=pltpu.CompilerParams(vmem_limit_bytes=58 * MIB),
         cost_estimate=pl.CostEstimate(
             flops=2 * requests * heads * positions * (width + NOPE),
-            bytes_accessed=2 * requests * width * positions,
-            transcendentals=requests * heads * positions,
+            bytes_accessed=0,
+            transcendentals=0,
         ),
-    )(place, moved, lengths, query_t, own, payload, cache_t, after)
-
-
-def expert_body(count, groups, place, w_gate, w_up, w_down, after, *refs):
+    )(place, moved, lengths, query_t, own, payload, cache_t)
+
+
+def expert_body(count, groups, place, w_gate, w_up, w_down, *refs):
     blocks, outs = refs[:count], refs[count:-4]
     first, second, sems, last_sem = refs[-4:]
     keeps, sends = outs[: count // 2], outs[count // 2 :]
@@ -199,24 +220,28 @@
     for s in range(steps):
         at = slice(s * CHUNK, (s + 1) * CHUNK)
         part = jnp.dot(activated, second[:, at], preferred_element_type=jnp.float32) * scale
-        for i, send in enumerate(sends):
-            low = half + 2 * tokens * i
-            send[:, at] = part[low : low + 2 * tokens].astype(jnp.bfloat16)
+        low = half
+        for send in sends:
+            send[:, at] = part[low : low + send.shape[0]].astype(jnp.bfloat16)
+            low += send.shape[0]
         for i, keep in enumerate(keeps):
             keep[:, at] = part[tokens * i : tokens * (i + 1)].astype(jnp.bfloat16)
 
 
-def expert(place, w_gate, w_up, w_down, after, blocks, groups):
+def expert(place, w_gate, w_up, w_down, blocks, groups):
     count = len(blocks)
     tokens = blocks[0].shape[0]
     _, model_width, hidden = w_gate.shape
     keep = jax.ShapeDtypeStruct((tokens, model_width), jnp.bfloat16)
-    send = jax.ShapeDtypeStruct((2 * tokens, model_width), jnp.bfloat16)
+    sends = [
+        jax.ShapeDtypeStruct((size * tokens, model_width), jnp.bfloat16)
+        for size in (2, count // 2 - 2)
+    ]
     outs = pl.pallas_call(
         functools.partial(expert_body, count, groups),
-        out_shape=[keep] * (count // 2) + [send] * (count // 4),
-        in_specs=[SCALARS, MAIN, MAIN, MAIN, APART] + [WHOLE] * count,
-        out_specs=[WHOLE] * (count // 2 + count // 4),
+        out_shape=[keep] * (count // 2) + sends,
+        in_specs=[SCALARS, MAIN, MAIN, MAIN] + [WHOLE] * count,
+        out_specs=[WHOLE] * (count // 2 + 2),
         scratch_shapes=[
             pltpu.VMEM((model_width, 2 * hidden), jnp.bfloat16),
             pltpu.VMEM((hidden, model_width), jnp.bfloat16),
@@ -226,10 +251,10 @@
         compiler_params=pltpu.CompilerParams(vmem_limit_bytes=40 * MIB),
         cost_estimate=pl.CostEstimate(
             flops=6 * count * tokens * model_width * hidden,
-            bytes_accessed=6 * model_width * hidden,
-            transcendentals=count * tokens * hidden,
+            bytes_accessed=0,
+            transcendentals=0,
         ),
-    )(place, w_gate, w_up, w_down, after, *blocks)
+    )(place, w_gate, w_up, w_down, *blocks)
     return outs[: count // 2], outs[count // 2 :]
 
 
@@ -261,30 +286,50 @@
     cache_t = jnp.swapaxes(latent_cache, 1, 2)
 
     rows, payload = prepare(
-        place, moved_slot, hidden_rows, group_ids, route_gates, query_t, new_latent, groups
-    )
-
-    columns = [rows] + [rotated(rows, axis, r) for r in range(1, turns)]
-    across = [swapped(own, axis, 2) for own in columns]
-    near = [block for pair in zip(columns, across) for block in pair]
+        place, moved_slot, hidden_rows, group_ids.T, route_gates.T, query_t, new_latent, groups
+    )
+
+    visiting = shifted(payload, axis, -1)
+    columns = {r: rotated(rows, axis, r) for r in range(1, turns) if r != 2}
+    across = {0: swapped(rows, axis, 2)}
+
+    home, away, mark = attend(
+        place, moved_slot, cache_lengths, query_t, new_latent, visiting, cache_t
+    )
+    columns, across, away = lax.optimization_barrier((columns, across, away))
+    columns[0] = rows
+    returned = shifted(away, axis, 1)
+
+    order = list(range(turns))
+    if turns > 2:
+        columns[2] = rotated(columns[1], axis, 1)
+        order.remove(2)
+        order = [2] + order
+    for r in order[1:] + order[:1]:
+        if r:
+            across[r] = swapped(columns[r], axis, 2)
+    near = [block for r in order for block in (columns[r], across[r])]
     blocks = near + [swapped(block, axis, 1) for block in near]
 
-    visiting = shifted(payload, axis, -1)
-    home, away = attend(
-        place, moved_slot, cache_lengths, query_t, new_latent, visiting, cache_t, columns[-1]
-    )
-    returned = shifted(away, axis, 1)
-
-    keeps, sends = expert(place, w_gate, w_up, w_down, away, blocks, groups)
-    terms = []
-    for r in list(range(1, turns)) + [0]:
-        chip = swapped(sends[r], axis, 1)
-        crossed = swapped(added(keeps[2 * r + 1], chip[tokens:]), axis, 2)
-        both = [keeps[2 * r], chip[:tokens], crossed]
-        terms += both if r == 0 else [rotated(added(*both), axis, -r)]
+    keeps, sends = expert(place, w_gate, w_up, w_down, blocks, groups)
+    first, rest = (swapped(send, axis, 1) for send in sends)
+
+    def chip(i, m):
+        if i == 0:
+            return [keeps[m], first[m * tokens : (m + 1) * tokens]]
+        low = (2 * (i - 1) + m) * tokens
+        return [keeps[2 * i + m], rest[low : low + tokens]]
+
+    crossed = [swapped(added(*chip(i, 1)), axis, 2) for i in range(turns)]
+    sums = {r: chip(i, 0) + [crossed[i]] for i, r in enumerate(order)}
+    if turns > 2:
+        sums[1] = sums[1] + [rotated(added(*sums.pop(2)), axis, -1)]
+    terms = sums.pop(0)
+    for r in sums:
+        terms = terms + [rotated(added(*sums[r]), axis, -r)]
     moe_out = added(*terms)
-    leaving = lax.dynamic_index_in_dim(moved_slot, position, 0, keepdims=False)
-    attn_out = lax.dynamic_update_slice_in_dim(home, returned[None], leaving, 0)
+    slots = jnp.arange(home.shape[0], dtype=jnp.int32)[:, None, None]
+    attn_out = jnp.where(slots == mark[:1, :1][None], returned[None], home)
     return (moe_out, attn_out)
 
 

time: 72.4 us -> 65.7 us (0.907)
  local copies, waits for them, and re-layouts: 11.5 us -> 1.94 us
  Pallas kernels: 11 us -> 14.6 us
  between operations: 2.75 us -> 0.8 us
  other arithmetic: 1 us -> 2.57 us
  waiting for transfers between devices: 25 us -> 23.9 us
  starting transfers between devices: 20.7 us -> 21.7 us
    unnamed x28 -> x14, local copies, waits for them, and re-layouts: 10.2 us -> 0.68 us
    ppermute x8, starting transfers between devices: 9.42 us -> 12.8 us  [shifted(): return lax.ppermute(value, axis, pairs)]
    pallas_call x1, Pallas kernels: 0.82 us -> 3.35 us  [prepare(): pl.pallas_call(functools.partial(prepare_body, groups), out_shape=[jax.Sh...]
    ppermute x20 -> x18, starting transfers between devices: 11.3 us -> 8.95 us  [swapped(): return lax.ppermute(value, axis, pairs)]
    ppermute x8, waiting for transfers between devices: 13.8 us -> 12.4 us  [shifted(): return lax.ppermute(value, axis, pairs)]
    slice x0 -> x1, local copies, waits for them, and re-layouts: none -> 1.26 us  [per_device(): attn_out = jnp.where(slots == mark[:1, :1][None], returned[None], home)]
    pallas_call x1, Pallas kernels: 6.71 us -> 7.8 us  [attend(): pl.pallas_call(attend_body, out_shape=[jax.ShapeDtypeStruct((requests, he...]
    select_n x0 -> x1, other arithmetic: none -> 0.9 us  [per_device(): attn_out = jnp.where(slots == mark[:1, :1][None], returned[None], home)]
  transfers between devices with their start and end apart: 28 -> 26, of which waited for: 10 -> 11; matrix products, arithmetic and copies ran while one was open for 2% -> 5% of each run, Pallas kernels for 9% -> 12%
where the time goes in v4:
time: 65.7 us; the launch traced here: 65.5 us
  waiting for transfers between devices  23.9 us (36%)
  starting transfers between devices  21.7 us (33%)
  Pallas kernels  14.6 us (22%)
  other arithmetic  2.57 us (4%)
  local copies, waits for them, and re-layouts  1.94 us (3%)
  between operations  0.8 us (1%)
    ppermute x8, starting transfers between devices, shifted(): return lax.ppermute(value, axis, pairs)  12.8 us
    ppermute x8, waiting for transfers between devices, shifted(): return lax.ppermute(value, axis, pairs)  12.4 us
    ppermute x18, waiting for transfers between devices, swapped(): return lax.ppermute(value, axis, pairs)  11.5 us
    ppermute x18, starting transfers between devices, swapped(): return lax.ppermute(value, axis, pairs)  8.95 us
    pallas_call x1, Pallas kernels, attend(): pl.pallas_call(attend_body, out_shape=[jax.ShapeDtypeStruct((requests, he...  7.8 us
    pallas_call x1, Pallas kernels, expert(): pl.pallas_call(functools.partial(expert_body, count, groups), out_shape=[...  3.45 us
    pallas_call x1, Pallas kernels, prepare(): pl.pallas_call(functools.partial(prepare_body, groups), out_shape=[jax.Sh...  3.35 us
  transfers between devices with their start and end apart: 26, of which 11 were waited for; matrix products, arithmetic and copies ran while one was open for 5% of the time, Pallas kernels for 12%

profile of v4, /device:TPU:0, one launch (start us, length us, event | category | flops | bytes accessed | tf_op | source)
XLA Modules:
  0.0 65.5 jit_solution(16669883723870738158)
XLA Ops:
  0.6 3.3 %shard_map.122 = (bf16[8,7296]{1,0:T(8,128)(2,1)}, bf16[592,128]{1,0:T(8,128)(2,1)}) custom-call(s32[1]{0:T(128)} %bitcast.place, s32[16]{0:T(128)} %moved.3, bf16[8,7168]{1,0:T(8,128)(2,1)} %hidden.1, s32[2,8]{1,0:T(2,128)} %bitcast.9, f32[2,8]{1,0:T(2,128)} %bitcast.10, bf16[4,576,128]{2,1,0:T(8,128)(2,1)} %bitcast.7, bf16[4,576]{1,0:T(4,128)(2,1)} %own.3), custom_call_target="tpu_custom_call" | custom-call | tf_op jit(solution)/shard_map/pallas_call | solution.py:81
  4.0 5.5 %collective-permute-start.3 = (bf16[592,128]{1,0:T(8,128)(2,1)}, bf16[592,128]{1,0:T(8,128)(2,1)S(1)}, u32[]{:S(2)}, u32[]{:S(2)}) collective-permute-start(bf16[592,128]{1,0:T(8,128)(2,1)} %get-tuple-element.22), channel_id=1, source_target_pairs={{0,15},{1,0},{2,1},{3,2},{4,3},{5,4},{6,5},{7,6},{8,7},{9,8},{10,9... | collective-permute-start | bytes 454664 | tf_op jit(solution)/shard_map/ppermute | solution.py:27
  9.5 1.2 %collective-permute-start.1 = (bf16[8,7296]{1,0:T(8,128)(2,1)}, bf16[8,7296]{1,0:T(8,128)(2,1)S(1)}, u32[]{:S(2)}, u32[]{:S(2)}) collective-permute-start(bf16[8,7296]{1,0:T(8,128)(2,1)} %get-tuple-element.21.refs_2_), channel_id=1, source_target_pairs={{0,12},{1,13},{2,14},{3,15},{4,0},{5,1},{6,2},{7,3},{8,4},{9,5},{1... | collective-permute-start | bytes 350216 | tf_op jit(solution)/shard_map/ppermute | solution.py:27
  10.7 0.8 %collective-permute-start = (bf16[8,7296]{1,0:T(8,128)(2,1)}, bf16[8,7296]{1,0:T(8,128)(2,1)S(1)}, u32[]{:S(2)}, u32[]{:S(2)}) collective-permute-start(bf16[8,7296]{1,0:T(8,128)(2,1)} %get-tuple-element.21.refs_2_), channel_id=1, source_target_pairs={{0,4},{1,5},{2,6},{3,7},{4,8},{5,9},{6,10},{7,11},{8,12},{9,13},{1... | collective-permute-start | bytes 350216 | tf_op jit(solution)/shard_map/ppermute | solution.py:27
  11.5 2.3 %collective-permute-done.3.payload = bf16[592,128]{1,0:T(8,128)(2,1)S(1)} collective-permute-done((bf16[592,128]{1,0:T(8,128)(2,1)}, bf16[592,128]{1,0:T(8,128)(2,1)S(1)}, u32[]{:S(2)}, u32[]{:S(2)}) %collective-permute-start.3) | collective-permute-done | bytes 151584 | tf_op jit(solution)/shard_map/ppermute | solution.py:27
  14.5 7.8 %shard_map.123 = (bf16[4,128,512]{2,1,0:T(8,128)(2,1)}, bf16[128,512]{1,0:T(8,128)(2,1)}, s32[8,128]{1,0:T(8,128)}) custom-call(s32[1]{0:T(128)} %bitcast.place, s32[16]{0:T(128)} %moved.3, s32[64]{0:T(128)} %lengths.1, bf16[4,576,128]{2,1,0:T(8,128)(2,1)} %bitcast.8, bf16[4,576]{1,0:T(4,128)(2,1)} %own.3, bf16[592,128]{1,0:T(8,128)(2,1)} %copy-done.5, ...), custom_call_target="tpu_custom_call" | custom-call | flops 1140850688 | tf_op jit(solution)/shard_map/pallas_call | solution.py:152
  23.7 1.4 %collective-permute-start.6 = (bf16[8,7296]{1,0:T(8,128)(2,1)S(1)}, bf16[8,7296]{1,0:T(8,128)(2,1)S(1)}, u32[]{:S(2)}, u32[]{:S(2)}) collective-permute-start(bf16[8,7296]{1,0:T(8,128)(2,1)S(1)} %collective-permute-done.refs_4_), channel_id=1, source_target_pairs={{0,2},{1,3},{2,0},{3,1},{4,6},{5,7},{6,4},{7,5},{8,10},{9,11},{10,... | collective-permute-start | bytes 350216 | tf_op jit(solution)/shard_map/ppermute | solution.py:36
  25.0 4.0 %collective-permute-done.4.refs_0_ = bf16[8,7296]{1,0:T(8,128)(2,1)S(1)} collective-permute-done((bf16[8,7296]{1,0:T(8,128)(2,1)S(1)}, bf16[8,7296]{1,0:T(8,128)(2,1)S(1)}, u32[]{:S(2)}, u32[]{:S(2)}) %collective-permute-start.4) | collective-permute-done | bytes 116768 | tf_op jit(solution)/shard_map/ppermute | solution.py:27
  30.7 3.2 %collective-permute-done.5.refs_1_ = bf16[8,7296]{1,0:T(8,128)(2,1)S(1)} collective-permute-done((bf16[8,7296]{1,0:T(8,128)(2,1)S(1)}, bf16[8,7296]{1,0:T(8,128)(2,1)S(1)}, u32[]{:S(2)}, u32[]{:S(2)}) %collective-permute-start.5) | collective-permute-done | bytes 116768 | tf_op jit(solution)/shard_map/ppermute | solution.py:36
  33.9 1.3 %collective-permute-done.9.refs_9_ = bf16[8,7296]{1,0:T(8,128)(2,1)S(1)} collective-permute-done((bf16[8,7296]{1,0:T(8,128)(2,1)S(1)}, bf16[8,7296]{1,0:T(8,128)(2,1)S(1)}, u32[]{:S(2)}, u32[]{:S(2)}) %collective-permute-start.9) | collective-permute-done | bytes 116768 | tf_op jit(solution)/shard_map/ppermute | solution.py:36
  35.2 3.4 %shard_map.124 = (bf16[8,7168]{1,0:T(8,128)(2,1)S(1)}, bf16[8,7168]{1,0:T(8,128)(2,1)S(1)}, bf16[8,7168]{1,0:T(8,128)(2,1)S(1)}, bf16[8,7168]{1,0:T(8,128)(2,1)S...) custom-call(s32[1]{0:T(128)} %bitcast.place, ...), custom_call_target="tpu_custom_call" | custom-call | flops 704643072 | tf_op jit(solution)/shard_map/pallas_call | solution.py:240
  38.9 1.3 %collective-permute-done.19 = bf16[16,7168]{1,0:T(8,128)(2,1)S(1)} collective-permute-done((bf16[16,7168]{1,0:T(8,128)(2,1)S(1)}, bf16[16,7168]{1,0:T(8,128)(2,1)S(1)}, u32[]{:S(2)}, u32[]{:S(2)}) %collective-permute-start.19) | collective-permute-done | bytes 229408 | tf_op jit(solution)/shard_map/ppermute | solution.py:36
  40.3 1.2 %collective-permute-start.20 = (bf16[8,7168]{1,0:T(8,128)(2,1)S(1)}, bf16[8,7168]{1,0:T(8,128)(2,1)S(1)}, u32[]{:S(2)}, u32[]{:S(2)}) collective-permute-start(bf16[8,7168]{1,0:T(8,128)(2,1)S(1)} %add_convert_fusion.5), channel_id=1, source_target_pairs={{0,2},{1,3},{2,0},{3,1},{4,6},{5,7},{6,4},{7,5},{8,10},{9,11},{10,... | collective-permute-start | bytes 344072 | tf_op jit(solution)/shard_map/ppermute | solution.py:36
  41.4 4.1 %collective-permute-done.20 = bf16[8,7168]{1,0:T(8,128)(2,1)S(1)} collective-permute-done((bf16[8,7168]{1,0:T(8,128)(2,1)S(1)}, bf16[8,7168]{1,0:T(8,128)(2,1)S(1)}, u32[]{:S(2)}, u32[]{:S(2)}) %collective-permute-start.20) | collective-permute-done | bytes 114720 | tf_op jit(solution)/shard_map/ppermute | solution.py:36
  45.6 3.1 %collective-permute-start.21 = (bf16[8,7168]{1,0:T(8,128)(2,1)S(1)}, bf16[8,7168]{1,0:T(8,128)(2,1)S(1)}, u32[]{:S(2)}, u32[]{:S(2)}) collective-permute-start(bf16[8,7168]{1,0:T(8,128)(2,1)S(1)} %add_convert_fusion.4), channel_id=1, source_target_pairs={{0,12},{1,13},{2,14},{3,15},{4,0},{5,1},{6,2},{7,3},{8,4},{9,5},{1... | collective-permute-start | bytes 344072 | tf_op jit(solution)/shard_map/ppermute | solution.py:27
  48.8 1.8 %collective-permute-start.23 = (bf16[8,7168]{1,0:T(8,128)(2,1)S(1)}, bf16[8,7168]{1,0:T(8,128)(2,1)S(1)}, u32[]{:S(2)}, u32[]{:S(2)}) collective-permute-start(bf16[8,7168]{1,0:T(8,128)(2,1)S(1)} %get-tuple-element.41), channel_id=1, source_target_pairs={{0,2},{1,3},{2,0},{3,1},{4,6},{5,7},{6,4},{7,5},{8,10},{9,11},{10,... | collective-permute-start | bytes 344072 | tf_op jit(solution)/shard_map/ppermute | solution.py:36
  50.9 1.3 %slice.35 = s32[1,1]{1,0:T(1,128)} slice(s32[8,128]{1,0:T(8,128)} %get-tuple-element.37), slice={[0:1], [0:1]} | slice | bytes 8 | tf_op jit(solution)/shard_map/slice | solution.py:332
  52.8 1.8 %collective-permute-start.17 = (bf16[8,7168]{1,0:T(8,128)(2,1)S(1)}, bf16[8,7168]{1,0:T(8,128)(2,1)S(1)}, u32[]{:S(2)}, u32[]{:S(2)}) collective-permute-start(bf16[8,7168]{1,0:T(8,128)(2,1)S(1)} %get-tuple-element.40), channel_id=1, source_target_pairs={{0,2},{1,3},{2,0},{3,1},{4,6},{5,7},{6,4},{7,5},{8,10},{9,11},{10,... | collective-permute-start | bytes 344072 | tf_op jit(solution)/shard_map/ppermute | solution.py:36
  54.6 1.0 %collective-permute-done.18 = bf16[8,7168]{1,0:T(8,128)(2,1)S(1)} collective-permute-done((bf16[8,7168]{1,0:T(8,128)(2,1)S(1)}, bf16[8,7168]{1,0:T(8,128)(2,1)S(1)}, u32[]{:S(2)}, u32[]{:S(2)}) %collective-permute-start.18) | collective-permute-done | bytes 114720 | tf_op jit(solution)/shard_map/ppermute | solution.py:36
  55.7 1.7 %collective-permute-start.22 = (bf16[8,7168]{1,0:T(8,128)(2,1)S(1)}, bf16[8,7168]{1,0:T(8,128)(2,1)S(1)}, u32[]{:S(2)}, u32[]{:S(2)}) collective-permute-start(bf16[8,7168]{1,0:T(8,128)(2,1)S(1)} %get-tuple-element.43), channel_id=1, source_target_pairs={{0,12},{1,13},{2,14},{3,15},{4,0},{5,1},{6,2},{7,3},{8,4},{9,5},{1... | collective-permute-start | bytes 344072 | tf_op jit(solution)/shard_map/ppermute | solution.py:27
  57.8 1.6 %collective-permute-done.25 = bf16[128,512]{1,0:T(8,128)(2,1)S(1)} collective-permute-done((bf16[128,512]{1,0:T(8,128)(2,1)S(1)}, bf16[128,512]{1,0:T(8,128)(2,1)S(1)}, u32[]{:S(2)}, u32[]{:S(2)}) %collective-permute-start.25) | collective-permute-done | bytes 131104 | tf_op jit(solution)/shard_map/ppermute | solution.py:27
  59.4 0.9 %broadcast_select_fusion = bf16[4,128,512]{2,1,0:T(8,128)(2,1)} fusion(bf16[4,128,512]{2,1,0:T(8,128)(2,1)S(1)} %copy-done.4, pred[4]{0:T(512)(128)(4,1)S(1)} %iota_compare_fusion, bf16[128,512]{1,0:T(8,128)(2,1)S(1)} %collective-permute-done.25), kind=kLoop, calls=%fused_computation | loop fusion | flops 262144 | bytes 1179652 | tf_op jit(solution)/shard_map/jit(_where)/select_n | solution.py:332
  61.0 3.7 %collective-permute-done.24 = bf16[8,7168]{1,0:T(8,128)(2,1)S(1)} collective-permute-done((bf16[8,7168]{1,0:T(8,128)(2,1)S(1)}, bf16[8,7168]{1,0:T(8,128)(2,1)S(1)}, u32[]{:S(2)}, u32[]{:S(2)}) %collective-permute-start.24) | collective-permute-done | bytes 114720 | tf_op jit(solution)/shard_map/ppermute | solution.py:27
  64.7 0.7 %add_convert_fusion = bf16[8,7168]{1,0:T(8,128)(2,1)} fusion(bf16[8,7168]{1,0:T(8,128)(2,1)S(1)} %collective-permute-done.24, bf16[8,7168]{1,0:T(8,128)(2,1)S(1)} %collective-permute-done.22, bf16[8,7168]{1,0:T(8,128)(2,1)S(1)} %collective-permute-done.17, bf16[8,7168]{1,0:T(8,128)(2,1)S(1)} %get-tuple-element.27, bf16[48,7168]{1,0:T(8,128)(2,1)S(1)} %collective-permute-done.16), kind=kLoop, calls=%fused_computation.1 | loop fusion | flops 573440 | bytes 688128 | tf_op jit(solution)/shard_map/convert_element_type | solution.py:262
  (53 shorter events, 6.1 us)
Async XLA Ops:
  4.0 9.9 %collective-permute-start.3 = (bf16[592,128]{1,0:T(8,128)(2,1)}, bf16[592,128]{1,0:T(8,128)(2,1)S(1)}, u32[]{:S(2)}, u32[]{:S(2)}) collective-permute-start(bf16[592,128]{1,0:T(8,128)(2,1)} %get-tuple-element.22), channel_id=1, source_target_pairs={{0,15},{1,0},{2,1},{3,2},{4,3},{5,4},{6,5},{7,6},{8,7},{9,8},{10,9... | collective-permute-start | bytes 454664 | tf_op jit(solution)/shard_map/ppermute | solution.py:27
  9.5 12.8 %collective-permute-start.2 = (bf16[8,7296]{1,0:T(8,128)(2,1)}, bf16[8,7296]{1,0:T(8,128)(2,1)S(1)}, u32[]{:S(2)}, u32[]{:S(2)}) collective-permute-start(bf16[8,7296]{1,0:T(8,128)(2,1)} %get-tuple-element.21.refs_2_), channel_id=1, source_target_pairs={{0,2},{1,3},{2,0},{3,1},{4,6},{5,7},{6,4},{7,5},{8,10},{9,11},{10,... | collective-permute-start | bytes 350216 | tf_op jit(solution)/shard_map/ppermute | solution.py:36
  9.5 12.9 %collective-permute-start.1 = (bf16[8,7296]{1,0:T(8,128)(2,1)}, bf16[8,7296]{1,0:T(8,128)(2,1)S(1)}, u32[]{:S(2)}, u32[]{:S(2)}) collective-permute-start(bf16[8,7296]{1,0:T(8,128)(2,1)} %get-tuple-element.21.refs_2_), channel_id=1, source_target_pairs={{0,12},{1,13},{2,14},{3,15},{4,0},{5,1},{6,2},{7,3},{8,4},{9,5},{1... | collective-permute-start | bytes 350216 | tf_op jit(solution)/shard_map/ppermute | solution.py:27
  10.7 11.7 %collective-permute-start = (bf16[8,7296]{1,0:T(8,128)(2,1)}, bf16[8,7296]{1,0:T(8,128)(2,1)S(1)}, u32[]{:S(2)}, u32[]{:S(2)}) collective-permute-start(bf16[8,7296]{1,0:T(8,128)(2,1)} %get-tuple-element.21.refs_2_), channel_id=1, source_target_pairs={{0,4},{1,5},{2,6},{3,7},{4,8},{5,9},{6,10},{7,11},{8,12},{9,13},{1... | collective-permute-start | bytes 350216 | tf_op jit(solution)/shard_map/ppermute | solution.py:27
  11.5 12.2 %collective-permute-start.10 = (bf16[8,7296]{1,0:T(8,128)(2,1)}, bf16[8,7296]{1,0:T(8,128)(2,1)S(1)}, u32[]{:S(2)}, u32[]{:S(2)}) collective-permute-start(bf16[8,7296]{1,0:T(8,128)(2,1)} %get-tuple-element.21.refs_2_), channel_id=1, source_target_pairs={{0,1},{1,0},{2,3},{3,2},{4,5},{5,4},{6,7},{7,6},{8,9},{9,8},{10,11... | collective-permute-start | bytes 350216 | tf_op jit(solution)/shard_map/ppermute | solution.py:36
  22.4 6.7 %collective-permute-start.4 = (bf16[8,7296]{1,0:T(8,128)(2,1)S(1)}, bf16[8,7296]{1,0:T(8,128)(2,1)S(1)}, u32[]{:S(2)}, u32[]{:S(2)}) collective-permute-start(bf16[8,7296]{1,0:T(8,128)(2,1)S(1)} %collective-permute-done.refs_4_), channel_id=1, source_target_pairs={{0,4},{1,5},{2,6},{3,7},{4,8},{5,9},{6,10},{7,11},{8,12},{9,13},{1... | collective-permute-start | bytes 350216 | tf_op jit(solution)/shard_map/ppermute | solution.py:27
  22.4 6.6 %collective-permute-start.11 = (bf16[8,7296]{1,0:T(8,128)(2,1)S(1)}, bf16[8,7296]{1,0:T(8,128)(2,1)S(1)}, u32[]{:S(2)}, u32[]{:S(2)}) collective-permute-start(bf16[8,7296]{1,0:T(8,128)(2,1)S(1)} %collective-permute-done.2.refs_3_), channel_id=1, source_target_pairs={{0,1},{1,0},{2,3},{3,2},{4,5},{5,4},{6,7},{7,6},{8,9},{9,8},{10,11... | collective-permute-start | bytes 350216 | tf_op jit(solution)/shard_map/ppermute | solution.py:36
  22.5 7.1 %collective-permute-start.14 = (bf16[8,7296]{1,0:T(8,128)(2,1)S(1)}, bf16[8,7296]{1,0:T(8,128)(2,1)S(1)}, u32[]{:S(2)}, u32[]{:S(2)}) collective-permute-start(bf16[8,7296]{1,0:T(8,128)(2,1)S(1)} %collective-permute-done.1.refs_6_), channel_id=1, source_target_pairs={{0,1},{1,0},{2,3},{3,2},{4,5},{5,4},{6,7},{7,6},{8,9},{9,8},{10,11... | collective-permute-start | bytes 350216 | tf_op jit(solution)/shard_map/ppermute | solution.py:36
  23.0 6.7 %collective-permute-start.7 = (bf16[8,7296]{1,0:T(8,128)(2,1)S(1)}, bf16[8,7296]{1,0:T(8,128)(2,1)S(1)}, u32[]{:S(2)}, u32[]{:S(2)}) collective-permute-start(bf16[8,7296]{1,0:T(8,128)(2,1)S(1)} %collective-permute-done.1.refs_6_), channel_id=1, source_target_pairs={{0,2},{1,3},{2,0},{3,1},{4,6},{5,7},{6,4},{7,5},{8,10},{9,11},{10,... | collective-permute-start | bytes 350216 | tf_op jit(solution)/shard_map/ppermute | solution.py:36
  23.7 7.0 %collective-permute-start.6 = (bf16[8,7296]{1,0:T(8,128)(2,1)S(1)}, bf16[8,7296]{1,0:T(8,128)(2,1)S(1)}, u32[]{:S(2)}, u32[]{:S(2)}) collective-permute-start(bf16[8,7296]{1,0:T(8,128)(2,1)S(1)} %collective-permute-done.refs_4_), channel_id=1, source_target_pairs={{0,2},{1,3},{2,0},{3,1},{4,6},{5,7},{6,4},{7,5},{8,10},{9,11},{10,... | collective-permute-start | bytes 350216 | tf_op jit(solution)/shard_map/ppermute | solution.py:36
  29.0 4.8 %collective-permute-start.5 = (bf16[8,7296]{1,0:T(8,128)(2,1)S(1)}, bf16[8,7296]{1,0:T(8,128)(2,1)S(1)}, u32[]{:S(2)}, u32[]{:S(2)}) collective-permute-start(bf16[8,7296]{1,0:T(8,128)(2,1)S(1)} %collective-permute-done.4.refs_0_), channel_id=1, source_target_pairs={{0,2},{1,3},{2,0},{3,1},{4,6},{5,7},{6,4},{7,5},{8,10},{9,11},{10,... | collective-permute-start | bytes 350216 | tf_op jit(solution)/shard_map/ppermute | solution.py:36
  29.0 4.8 %collective-permute-start.12 = (bf16[8,7296]{1,0:T(8,128)(2,1)S(1)}, bf16[8,7296]{1,0:T(8,128)(2,1)S(1)}, u32[]{:S(2)}, u32[]{:S(2)}) collective-permute-start(bf16[8,7296]{1,0:T(8,128)(2,1)S(1)} %collective-permute-done.refs_4_), channel_id=1, source_target_pairs={{0,1},{1,0},{2,3},{3,2},{4,5},{5,4},{6,7},{7,6},{8,9},{9,8},{10,11... | collective-permute-start | bytes 350216 | tf_op jit(solution)/shard_map/ppermute | solution.py:36
  29.6 4.3 %collective-permute-start.8 = (bf16[8,7296]{1,0:T(8,128)(2,1)S(1)}, bf16[8,7296]{1,0:T(8,128)(2,1)S(1)}, u32[]{:S(2)}, u32[]{:S(2)}) collective-permute-start(bf16[8,7296]{1,0:T(8,128)(2,1)S(1)} %collective-permute-done.4.refs_0_), channel_id=1, source_target_pairs={{0,1},{1,0},{2,3},{3,2},{4,5},{5,4},{6,7},{7,6},{8,9},{9,8},{10,11... | collective-permute-start | bytes 350216 | tf_op jit(solution)/shard_map/ppermute | solution.py:36
  29.7 4.2 %collective-permute-start.15 = (bf16[8,7296]{1,0:T(8,128)(2,1)S(1)}, bf16[8,7296]{1,0:T(8,128)(2,1)S(1)}, u32[]{:S(2)}, u32[]{:S(2)}) collective-permute-start(bf16[8,7296]{1,0:T(8,128)(2,1)S(1)} %collective-permute-done.7.refs_7_), channel_id=1, source_target_pairs={{0,1},{1,0},{2,3},{3,2},{4,5},{5,4},{6,7},{7,6},{8,9},{9,8},{10,11... | collective-permute-start | bytes 350216 | tf_op jit(solution)/shard_map/ppermute | solution.py:36
  30.7 3.2 %collective-permute-start.13 = (bf16[8,7296]{1,0:T(8,128)(2,1)S(1)}, bf16[8,7296]{1,0:T(8,128)(2,1)S(1)}, u32[]{:S(2)}, u32[]{:S(2)}) collective-permute-start(bf16[8,7296]{1,0:T(8,128)(2,1)S(1)} %collective-permute-done.6.refs_5_), channel_id=1, source_target_pairs={{0,1},{1,0},{2,3},{3,2},{4,5},{5,4},{6,7},{7,6},{8,9},{9,8},{10,11... | collective-permute-start | bytes 350216 | tf_op jit(solution)/shard_map/ppermute | solution.py:36
  40.3 5.3 %collective-permute-start.20 = (bf16[8,7168]{1,0:T(8,128)(2,1)S(1)}, bf16[8,7168]{1,0:T(8,128)(2,1)S(1)}, u32[]{:S(2)}, u32[]{:S(2)}) collective-permute-start(bf16[8,7168]{1,0:T(8,128)(2,1)S(1)} %add_convert_fusion.5), channel_id=1, source_target_pairs={{0,2},{1,3},{2,0},{3,1},{4,6},{5,7},{6,4},{7,5},{8,10},{9,11},{10,... | collective-permute-start | bytes 344072 | tf_op jit(solution)/shard_map/ppermute | solution.py:36
  41.4 7.2 %collective-permute-start.16 = (bf16[48,7168]{1,0:T(8,128)(2,1)S(1)}, bf16[48,7168]{1,0:T(8,128)(2,1)S(1)}, u32[]{:S(2)}, u32[]{:S(2)}) collective-permute-start(bf16[48,7168]{1,0:T(8,128)(2,1)S(1)} %get-tuple-element.28), channel_id=1, source_target_pairs={{0,1},{1,0},{2,3},{3,2},{4,5},{5,4},{6,7},{7,6},{8,9},{9,8},{10,11... | collective-permute-start | bytes 2064392 | tf_op jit(solution)/shard_map/ppermute | solution.py:36
  45.6 9.1 %collective-permute-start.21 = (bf16[8,7168]{1,0:T(8,128)(2,1)S(1)}, bf16[8,7168]{1,0:T(8,128)(2,1)S(1)}, u32[]{:S(2)}, u32[]{:S(2)}) collective-permute-start(bf16[8,7168]{1,0:T(8,128)(2,1)S(1)} %add_convert_fusion.4), channel_id=1, source_target_pairs={{0,12},{1,13},{2,14},{3,15},{4,0},{5,1},{6,2},{7,3},{8,4},{9,5},{1... | collective-permute-start | bytes 344072 | tf_op jit(solution)/shard_map/ppermute | solution.py:27
  48.8 5.9 %collective-permute-start.23 = (bf16[8,7168]{1,0:T(8,128)(2,1)S(1)}, bf16[8,7168]{1,0:T(8,128)(2,1)S(1)}, u32[]{:S(2)}, u32[]{:S(2)}) collective-permute-start(bf16[8,7168]{1,0:T(8,128)(2,1)S(1)} %get-tuple-element.41), channel_id=1, source_target_pairs={{0,2},{1,3},{2,0},{3,1},{4,6},{5,7},{6,4},{7,5},{8,10},{9,11},{10,... | collective-permute-start | bytes 344072 | tf_op jit(solution)/shard_map/ppermute | solution.py:36
  50.6 5.0 %collective-permute-start.18 = (bf16[8,7168]{1,0:T(8,128)(2,1)S(1)}, bf16[8,7168]{1,0:T(8,128)(2,1)S(1)}, u32[]{:S(2)}, u32[]{:S(2)}) collective-permute-start(bf16[8,7168]{1,0:T(8,128)(2,1)S(1)} %get-tuple-element.42), channel_id=1, source_target_pairs={{0,2},{1,3},{2,0},{3,1},{4,6},{5,7},{6,4},{7,5},{8,10},{9,11},{10,... | collective-permute-start | bytes 344072 | tf_op jit(solution)/shard_map/ppermute | solution.py:36
  52.1 7.3 %collective-permute-start.25 = (bf16[128,512]{1,0:T(8,128)(2,1)S(1)}, bf16[128,512]{1,0:T(8,128)(2,1)S(1)}, u32[]{:S(2)}, u32[]{:S(2)}) collective-permute-start(bf16[128,512]{1,0:T(8,128)(2,1)S(1)} %copy-done.6), channel_id=1, source_target_pairs={{0,1},{1,2},{2,3},{3,4},{4,5},{5,6},{6,7},{7,8},{8,9},{9,10},{10,1... | collective-permute-start | bytes 393224 | tf_op jit(solution)/shard_map/ppermute | solution.py:27
  52.8 7.5 %collective-permute-start.17 = (bf16[8,7168]{1,0:T(8,128)(2,1)S(1)}, bf16[8,7168]{1,0:T(8,128)(2,1)S(1)}, u32[]{:S(2)}, u32[]{:S(2)}) collective-permute-start(bf16[8,7168]{1,0:T(8,128)(2,1)S(1)} %get-tuple-element.40), channel_id=1, source_target_pairs={{0,2},{1,3},{2,0},{3,1},{4,6},{5,7},{6,4},{7,5},{8,10},{9,11},{10,... | collective-permute-start | bytes 344072 | tf_op jit(solution)/shard_map/ppermute | solution.py:36
  55.7 5.3 %collective-permute-start.22 = (bf16[8,7168]{1,0:T(8,128)(2,1)S(1)}, bf16[8,7168]{1,0:T(8,128)(2,1)S(1)}, u32[]{:S(2)}, u32[]{:S(2)}) collective-permute-start(bf16[8,7168]{1,0:T(8,128)(2,1)S(1)} %get-tuple-element.43), channel_id=1, source_target_pairs={{0,12},{1,13},{2,14},{3,15},{4,0},{5,1},{6,2},{7,3},{8,4},{9,5},{1... | collective-permute-start | bytes 344072 | tf_op jit(solution)/shard_map/ppermute | solution.py:27
  57.4 7.3 %collective-permute-start.24 = (bf16[8,7168]{1,0:T(8,128)(2,1)S(1)}, bf16[8,7168]{1,0:T(8,128)(2,1)S(1)}, u32[]{:S(2)}, u32[]{:S(2)}) collective-permute-start(bf16[8,7168]{1,0:T(8,128)(2,1)S(1)} %get-tuple-element.44), channel_id=1, source_target_pairs={{0,4},{1,5},{2,6},{3,7},{4,8},{5,9},{6,10},{7,11},{8,12},{9,13},{1... | collective-permute-start | bytes 344072 | tf_op jit(solution)/shard_map/ppermute | solution.py:27
  (9 other events, 134.3 us)

commit v5 on v4

--- a/solution.py
+++ b/solution.py
@@ -36,16 +36,9 @@
     return lax.ppermute(value, axis, pairs)
 
 
-def prepare_body(groups, place, moved, hidden, ids, gates, query, own, rows, payload, *scratch):
-    moves, sems = scratch
+def prepare_body(groups, place, moved, hidden, ids, gates, query, own, rows, payload):
     tokens, model_width = hidden.shape
-    width = query.shape[1]
-    fetch = pltpu.make_async_copy(moved, moves, sems.at[0])
-    fetch.start()
-    fetch.wait()
-    leaving = moves[place[0]]
-    copy = pltpu.make_async_copy(query.at[leaving], payload.at[pl.ds(0, width)], sems.at[1])
-    copy.start()
+    requests, width, _ = query.shape
     rows[:, :model_width] = hidden[...]
     chosen, weight = ids[...].T, gates[...].T
     lane = lax.broadcasted_iota(jnp.int32, (tokens, rows.shape[1] - model_width), 1)
@@ -59,6 +52,8 @@
     low = coefficient - high - middle
     pieces = jnp.where(part == 0, high, jnp.where(part == 1, middle, low))
     rows[:, model_width:] = jnp.where(lane < 3 * groups, pieces, 0.0).astype(jnp.bfloat16)
+    leaving = moved[place[0]]
+    payload[:width, :] = query[leaving]
     slots = lax.broadcasted_iota(jnp.int32, own.shape, 0)
     latent = jnp.sum(
         jnp.where(slots == leaving, own[...].astype(jnp.float32), 0.0), axis=0, keepdims=True
@@ -70,7 +65,6 @@
     for r in range(latent.shape[1] // LANES):
         block = jnp.where(row == r, latent[:, r * LANES : (r + 1) * LANES], block)
     payload[width:, :] = block.astype(jnp.bfloat16)
-    copy.wait()
 
 
 def prepare(place, moved, hidden, ids_t, gates_t, query_t, own, groups):
@@ -84,12 +78,8 @@
             jax.ShapeDtypeStruct((tokens, model_width + tail), jnp.bfloat16),
             jax.ShapeDtypeStruct((width + extra, heads), jnp.bfloat16),
         ],
-        in_specs=[SCALARS, MAIN, WHOLE, WHOLE, WHOLE, MAIN, WHOLE],
+        in_specs=[SCALARS, SCALARS] + [WHOLE] * 5,
         out_specs=[WHOLE, WHOLE],
-        scratch_shapes=[
-            pltpu.SMEM(moved.shape, moved.dtype),
-            pltpu.SemaphoreType.DMA((2,)),
-        ],
         compiler_params=pltpu.CompilerParams(vmem_limit_bytes=60 * MIB),
         cost_estimate=pl.CostEstimate(flops=0, bytes_accessed=0, transcendentals=0),
     )(place, moved, hidden, ids_t, gates_t, query_t, own)
@@ -174,40 +164,22 @@
     )(place, moved, lengths, query_t, own, payload, cache_t)
 
 
-def expert_body(count, groups, place, w_gate, w_up, w_down, *refs):
-    blocks, outs = refs[:count], refs[count:-4]
-    first, second, sems, last_sem = refs[-4:]
-    keeps, sends = outs[: count // 2], outs[count // 2 :]
+def expert_body(count, groups, sizes, place, w_gate, w_up, w_down, *refs):
+    blocks, outs = refs[:count], refs[count:]
     model_width = w_gate.shape[1]
-    hidden = w_gate.shape[2]
     steps = model_width // CHUNK
-    copies = []
-    for s in range(steps):
-        at = pl.ds(s * CHUNK, CHUNK)
-        copies.append(
-            [
-                pltpu.make_async_copy(w_gate.at[0, at], first.at[at, :hidden], sems.at[2 * s]),
-                pltpu.make_async_copy(w_up.at[0, at], first.at[at, hidden:], sems.at[2 * s + 1]),
-            ]
-        )
-    for pair in copies:
-        for copy in pair:
-            copy.start()
-    last = pltpu.make_async_copy(w_down.at[0], second, last_sem)
-    last.start()
 
     def joined(at):
         return jnp.concatenate([block[:, at].astype(jnp.float32) for block in blocks], axis=0)
 
-    total = None
+    gate = up = None
     for s in range(steps):
         at = slice(s * CHUNK, (s + 1) * CHUNK)
         rows = joined(at).astype(jnp.bfloat16)
-        for copy in copies[s]:
-            copy.wait()
-        term = jnp.dot(rows, first[at, :], preferred_element_type=jnp.float32)
-        total = term if total is None else total + term
-    gate, up = total[:, :hidden], total[:, hidden:]
+        gate_term = jnp.dot(rows, w_gate[0, at, :], preferred_element_type=jnp.float32)
+        up_term = jnp.dot(rows, w_up[0, at, :], preferred_element_type=jnp.float32)
+        gate = gate_term if gate is None else gate + gate_term
+        up = up_term if up is None else up + up_term
     activated = (gate / (1.0 + jnp.exp(-gate)) * up).astype(jnp.bfloat16)
     parts = joined(slice(model_width, blocks[0].shape[1]))
     lane = lax.broadcasted_iota(jnp.int32, parts.shape, 1)
@@ -215,47 +187,33 @@
     picked = (lane == mine) | (lane == mine + groups) | (lane == mine + 2 * groups)
     scale = jnp.sum(jnp.where(picked, parts, 0.0), axis=1, keepdims=True)
     tokens = blocks[0].shape[0]
-    half = count // 2 * tokens
-    last.wait()
     for s in range(steps):
         at = slice(s * CHUNK, (s + 1) * CHUNK)
-        part = jnp.dot(activated, second[:, at], preferred_element_type=jnp.float32) * scale
-        low = half
-        for send in sends:
-            send[:, at] = part[low : low + send.shape[0]].astype(jnp.bfloat16)
-            low += send.shape[0]
-        for i, keep in enumerate(keeps):
-            keep[:, at] = part[tokens * i : tokens * (i + 1)].astype(jnp.bfloat16)
-
-
-def expert(place, w_gate, w_up, w_down, blocks, groups):
+        part = jnp.dot(activated, w_down[0, :, at], preferred_element_type=jnp.float32) * scale
+        low = 0
+        for size, out in zip(sizes, outs):
+            out[:, at] = part[low : low + size * tokens].astype(jnp.bfloat16)
+            low += size * tokens
+
+
+def expert(place, w_gate, w_up, w_down, blocks, groups, sizes):
     count = len(blocks)
     tokens = blocks[0].shape[0]
     _, model_width, hidden = w_gate.shape
-    keep = jax.ShapeDtypeStruct((tokens, model_width), jnp.bfloat16)
-    sends = [
-        jax.ShapeDtypeStruct((size * tokens, model_width), jnp.bfloat16)
-        for size in (2, count // 2 - 2)
-    ]
-    outs = pl.pallas_call(
-        functools.partial(expert_body, count, groups),
-        out_shape=[keep] * (count // 2) + sends,
-        in_specs=[SCALARS, MAIN, MAIN, MAIN] + [WHOLE] * count,
-        out_specs=[WHOLE] * (count // 2 + 2),
-        scratch_shapes=[
-            pltpu.VMEM((model_width, 2 * hidden), jnp.bfloat16),
-            pltpu.VMEM((hidden, model_width), jnp.bfloat16),
-            pltpu.SemaphoreType.DMA((2 * (model_width // CHUNK),)),
-            pltpu.SemaphoreType.DMA,
+    return pl.pallas_call(
+        functools.partial(expert_body, count, groups, sizes),
+        out_shape=[
+            jax.ShapeDtypeStruct((size * tokens, model_width), jnp.bfloat16) for size in sizes
         ],
+        in_specs=[SCALARS] + [WHOLE] * (3 + count),
+        out_specs=[WHOLE] * len(sizes),
         compiler_params=pltpu.CompilerParams(vmem_limit_bytes=40 * MIB),
         cost_estimate=pl.CostEstimate(
             flops=6 * count * tokens * model_width * hidden,
-            bytes_accessed=0,
+            bytes_accessed=6 * model_width * hidden,
             transcendentals=0,
         ),
     )(place, w_gate, w_up, w_down, *blocks)
-    return outs[: count // 2], outs[count // 2 :]
 
 
 def added(*terms):
@@ -289,41 +247,53 @@
         place, moved_slot, hidden_rows, group_ids.T, route_gates.T, query_t, new_latent, groups
     )
 
-    visiting = shifted(payload, axis, -1)
     columns = {r: rotated(rows, axis, r) for r in range(1, turns) if r != 2}
     across = {0: swapped(rows, axis, 2)}
-
-    home, away, mark = attend(
-        place, moved_slot, cache_lengths, query_t, new_latent, visiting, cache_t
-    )
-    columns, across, away = lax.optimization_barrier((columns, across, away))
-    columns[0] = rows
-    returned = shifted(away, axis, 1)
-
     order = list(range(turns))
     if turns > 2:
         columns[2] = rotated(columns[1], axis, 1)
-        order.remove(2)
-        order = [2] + order
-    for r in order[1:] + order[:1]:
-        if r:
-            across[r] = swapped(columns[r], axis, 2)
-    near = [block for r in order for block in (columns[r], across[r])]
+        order = [2, 1] + order[3:] + [0]
+    for r in order[1:-1]:
+        across[r] = swapped(columns[r], axis, 2)
+
+    visiting = shifted(payload, axis, -1)
+    early = {r: columns.pop(r) for r in order[1:-1]}
+    visiting, early = lax.optimization_barrier((visiting, early))
+    home, away, mark = attend(
+        place, moved_slot, cache_lengths, query_t, new_latent, visiting, cache_t
+    )
+    columns, across, away = lax.optimization_barrier((columns, across, away))
+    columns.update(early)
+    columns[0] = rows
+    for r in order[:1]:
+        across[r] = swapped(columns[r], axis, 2)
+    returned = shifted(away, axis, 1)
+
+    batches = [order[: turns // 2], order[turns // 2 :]]
+    near = []
+    for batch in batches:
+        near += [across[r] for r in batch] + [columns[r] for r in batch]
     blocks = near + [swapped(block, axis, 1) for block in near]
-
-    keeps, sends = expert(place, w_gate, w_up, w_down, blocks, groups)
-    first, rest = (swapped(send, axis, 1) for send in sends)
-
-    def chip(i, m):
-        if i == 0:
-            return [keeps[m], first[m * tokens : (m + 1) * tokens]]
-        low = (2 * (i - 1) + m) * tokens
-        return [keeps[2 * i + m], rest[low : low + tokens]]
-
-    crossed = [swapped(added(*chip(i, 1)), axis, 2) for i in range(turns)]
-    sums = {r: chip(i, 0) + [crossed[i]] for i, r in enumerate(order)}
-    if turns > 2:
-        sums[1] = sums[1] + [rotated(added(*sums.pop(2)), axis, -1)]
+    sizes = []
+    for batch in batches:
+        sizes += [len(batch)] + [1] * len(batch)
+    outs = expert(
+        place, w_gate, w_up, w_down, blocks, groups, sizes + [2 * len(b) for b in batches]
+    )
+
+    sends = [swapped(send, axis, 1) for send in outs[-2:]]
+    sums = {}
+    crossed = None
+    for batch, chip in zip(batches, sends):
+        mine, outs = outs[: 1 + len(batch)], outs[1 + len(batch) :]
+        split = len(batch) * tokens
+        crossing = added(mine[0], chip[:split])
+        if crossed is not None:
+            crossing, crossed = lax.optimization_barrier((crossing, crossed))
+        crossed = swapped(crossing, axis, 2)
+        for i, r in enumerate(batch):
+            at = slice(i * tokens, (i + 1) * tokens)
+            sums[r] = [mine[1 + i], chip[split:][at], crossed[at]]
     terms = sums.pop(0)
     for r in sums:
         terms = terms + [rotated(added(*sums[r]), axis, -r)]

time: 65.7 us -> 63.9 us (0.973)
  waiting for transfers between devices: 23.9 us -> 26.1 us
  Pallas kernels: 14.6 us -> 12.5 us
  starting transfers between devices: 21.7 us -> 19.8 us
    ppermute x18 -> x16, waiting for transfers between devices: 11.5 us -> 14.8 us  [swapped(): return lax.ppermute(value, axis, pairs)]
    ppermute x18 -> x16, starting transfers between devices: 8.95 us -> 6.22 us  [swapped(): return lax.ppermute(value, axis, pairs)]
    pallas_call x1, Pallas kernels: 3.35 us -> 2.03 us  [prepare(): pl.pallas_call(functools.partial(prepare_body, groups), out_shape=[jax.Sh...]
    ppermute x8, waiting for transfers between devices: 12.4 us -> 11.3 us  [shifted(): return lax.ppermute(value, axis, pairs)]
    ppermute x8, starting transfers between devices: 12.8 us -> 13.6 us  [shifted(): return lax.ppermute(value, axis, pairs)]
    pallas_call x1, Pallas kernels: 3.45 us -> 2.69 us  [expert(): pl.pallas_call(functools.partial(expert_body, count, groups, sizes), out_...]
  transfers between devices with their start and end apart: 26 -> 24, of which waited for: 11 -> 9; matrix products, arithmetic and copies ran while one was open for 5% -> 5% of each run, Pallas kernels for 12% -> 12%
where the time goes in v5:
time: 63.9 us; the launch traced here: 63.7 us
  waiting for transfers between devices  26.1 us (41%)
  starting transfers between devices  19.8 us (31%)
  Pallas kernels  12.5 us (20%)
  other arithmetic  2.5 us (4%)
  local copies, waits for them, and re-layouts  1.9 us (3%)
  between operations  0.78 us (1%)
    ppermute x16, waiting for transfers between devices, swapped(): return lax.ppermute(value, axis, pairs)  14.8 us
    ppermute x8, starting transfers between devices, shifted(): return lax.ppermute(value, axis, pairs)  13.6 us
    ppermute x8, waiting for transfers between devices, shifted(): return lax.ppermute(value, axis, pairs)  11.3 us
    pallas_call x1, Pallas kernels, attend(): pl.pallas_call(attend_body, out_shape=[jax.ShapeDtypeStruct((requests, he...  7.8 us
    ppermute x16, starting transfers between devices, swapped(): return lax.ppermute(value, axis, pairs)  6.22 us
    pallas_call x1, Pallas kernels, expert(): pl.pallas_call(functools.partial(expert_body, count, groups, sizes), out_...  2.69 us
    pallas_call x1, Pallas kernels, prepare(): pl.pallas_call(functools.partial(prepare_body, groups), out_shape=[jax.Sh...  2.03 us
  transfers between devices with their start and end apart: 24, of which 9 were waited for; matrix products, arithmetic and copies ran while one was open for 5% of the time, Pallas kernels for 12%

profile of v5, /device:TPU:0, one launch (start us, length us, event | category | flops | bytes accessed | tf_op | source)
XLA Modules:
  0.0 63.7 jit_solution(12462760451976688796)
XLA Ops:
  0.6 2.0 %shard_map.122 = (bf16[8,7296]{1,0:T(8,128)(2,1)}, bf16[592,128]{1,0:T(8,128)(2,1)}) custom-call(s32[1]{0:T(128)} %bitcast.place, s32[16]{0:T(128)} %moved.3, bf16[8,7168]{1,0:T(8,128)(2,1)} %hidden.1, s32[2,8]{1,0:T(2,128)} %bitcast.9, f32[2,8]{1,0:T(2,128)} %bitcast.10, bf16[4,576,128]{2,1,0:T(8,128)(2,1)} %bitcast.7, bf16[4,576]{1,0:T(4,128)(2,1)} %own.3), custom_call_target="tpu_custom_call" | custom-call | tf_op jit(solution)/shard_map/pallas_call | solution.py:75
  2.7 5.4 %collective-permute-start.6 = (bf16[592,128]{1,0:T(8,128)(2,1)}, bf16[592,128]{1,0:T(8,128)(2,1)S(1)}, u32[]{:S(2)}, u32[]{:S(2)}) collective-permute-start(bf16[592,128]{1,0:T(8,128)(2,1)} %get-tuple-element.25), channel_id=1, source_target_pairs={{0,15},{1,0},{2,1},{3,2},{4,3},{5,4},{6,5},{7,6},{8,7},{9,8},{10,9... | collective-permute-start | bytes 454664 | tf_op jit(solution)/shard_map/ppermute | solution.py:27
  8.6 1.6 %collective-permute-start = (bf16[8,7296]{1,0:T(8,128)(2,1)}, bf16[8,7296]{1,0:T(8,128)(2,1)S(1)}, u32[]{:S(2)}, u32[]{:S(2)}) collective-permute-start(bf16[8,7296]{1,0:T(8,128)(2,1)} %get-tuple-element.24.refs_7_), channel_id=1, source_target_pairs={{0,4},{1,5},{2,6},{3,7},{4,8},{5,9},{6,10},{7,11},{8,12},{9,13},{1... | collective-permute-start | bytes 350216 | tf_op jit(solution)/shard_map/ppermute | solution.py:27
  10.2 3.9 %collective-permute-done.4.refs_6_ = bf16[8,7296]{1,0:T(8,128)(2,1)S(1)} collective-permute-done((bf16[8,7296]{1,0:T(8,128)(2,1)}, bf16[8,7296]{1,0:T(8,128)(2,1)S(1)}, u32[]{:S(2)}, u32[]{:S(2)}) %collective-permute-start.4) | collective-permute-done | bytes 116768 | tf_op jit(solution)/shard_map/ppermute | solution.py:27
  14.0 2.1 %collective-permute-done.refs_3_ = bf16[8,7296]{1,0:T(8,128)(2,1)S(1)} collective-permute-done((bf16[8,7296]{1,0:T(8,128)(2,1)}, bf16[8,7296]{1,0:T(8,128)(2,1)S(1)}, u32[]{:S(2)}, u32[]{:S(2)}) %collective-permute-start) | collective-permute-done | bytes 116768 | tf_op jit(solution)/shard_map/ppermute | solution.py:27
  16.6 1.1 %collective-permute-start.1 = (bf16[8,7296]{1,0:T(8,128)(2,1)S(1)}, bf16[8,7296]{1,0:T(8,128)(2,1)}, u32[]{:S(2)}, u32[]{:S(2)}) collective-permute-start(bf16[8,7296]{1,0:T(8,128)(2,1)S(1)} %collective-permute-done.refs_3_), channel_id=1, source_target_pairs={{0,4},{1,5},{2,6},{3,7},{4,8},{5,9},{6,10},{7,11},{8,12},{9,13},{1... | collective-permute-start | bytes 350216 | tf_op jit(solution)/shard_map/ppermute | solution.py:27
  17.7 0.6 %copy-done.5 = bf16[592,128]{1,0:T(8,128)(2,1)} copy-done((bf16[592,128]{1,0:T(8,128)(2,1)}, bf16[592,128]{1,0:T(8,128)(2,1)S(1)}, u32[]{:S(2)}) %copy-start.5) | copy-done | bytes 151576
  18.3 7.8 %shard_map.123 = (bf16[4,128,512]{2,1,0:T(8,128)(2,1)}, bf16[128,512]{1,0:T(8,128)(2,1)}, s32[8,128]{1,0:T(8,128)}) custom-call(s32[1]{0:T(128)} %bitcast.place, s32[16]{0:T(128)} %moved.3, s32[64]{0:T(128)} %lengths.1, bf16[4,576,128]{2,1,0:T(8,128)(2,1)} %bitcast.8, bf16[4,576]{1,0:T(4,128)(2,1)} %own.3, bf16[592,128]{1,0:T(8,128)(2,1)} %copy-done.5, ...), custom_call_target="tpu_custom_call" | custom-call | flops 1140850688 | tf_op jit(solution)/shard_map/pallas_call | solution.py:142
  26.7 2.1 %collective-permute-start.7 = (bf16[8,7296]{1,0:T(8,128)(2,1)}, bf16[8,7296]{1,0:T(8,128)(2,1)S(1)}, u32[]{:S(2)}, u32[]{:S(2)}) collective-permute-start(bf16[8,7296]{1,0:T(8,128)(2,1)} %collective-permute-done.1.refs_2_), channel_id=1, source_target_pairs={{0,2},{1,3},{2,0},{3,1},{4,6},{5,7},{6,4},{7,5},{8,10},{9,11},{10,... | collective-permute-start | bytes 350216 | tf_op jit(solution)/shard_map/ppermute | solution.py:36
  29.9 2.6 %collective-permute-done.7.refs_0_ = bf16[8,7296]{1,0:T(8,128)(2,1)S(1)} collective-permute-done((bf16[8,7296]{1,0:T(8,128)(2,1)}, bf16[8,7296]{1,0:T(8,128)(2,1)S(1)}, u32[]{:S(2)}, u32[]{:S(2)}) %collective-permute-start.7) | collective-permute-done | bytes 116768 | tf_op jit(solution)/shard_map/ppermute | solution.py:36
  32.5 1.3 %collective-permute-done.8.refs_8_ = bf16[8,7296]{1,0:T(8,128)(2,1)S(1)} collective-permute-done((bf16[8,7296]{1,0:T(8,128)(2,1)S(1)}, bf16[8,7296]{1,0:T(8,128)(2,1)S(1)}, u32[]{:S(2)}, u32[]{:S(2)}) %collective-permute-start.8) | collective-permute-done | bytes 116768 | tf_op jit(solution)/shard_map/ppermute | solution.py:36
  33.8 2.7 %shard_map.124 = (bf16[16,7168]{1,0:T(8,128)(2,1)S(1)}, bf16[8,7168]{1,0:T(8,128)(2,1)S(1)}, bf16[8,7168]{1,0:T(8,128)(2,1)S(1)}, bf16[16,7168]{1,0:T(8,128)(2,1...) custom-call(s32[1]{0:T(128)} %bitcast.place, ...), custom_call_target="tpu_custom_call" | custom-call | flops 704643072 | bytes 5505024 | tf_op jit(solution)/shard_map/pallas_call | solution.py:203
  36.8 1.2 %slice.51 = s32[1,1]{1,0:T(1,128)} slice(s32[8,128]{1,0:T(8,128)} %get-tuple-element.43), slice={[0:1], [0:1]} | slice | bytes 8 | tf_op jit(solution)/shard_map/slice | solution.py:302
  38.0 0.6 iota_compare_fusion
  39.0 1.5 %collective-permute-start.16 = (bf16[32,7168]{1,0:T(8,128)(2,1)S(1)}, bf16[32,7168]{1,0:T(8,128)(2,1)S(1)}, u32[]{:S(2)}, u32[]{:S(2)}) collective-permute-start(bf16[32,7168]{1,0:T(8,128)(2,1)S(1)} %get-tuple-element.35), channel_id=1, source_target_pairs={{0,1},{1,0},{2,3},{3,2},{4,5},{5,4},{6,7},{7,6},{8,9},{9,8},{10,11... | collective-permute-start | bytes 1376264 | tf_op jit(solution)/shard_map/ppermute | solution.py:36
  41.0 1.0 %collective-permute-done.16 = bf16[32,7168]{1,0:T(8,128)(2,1)S(1)} collective-permute-done((bf16[32,7168]{1,0:T(8,128)(2,1)S(1)}, bf16[32,7168]{1,0:T(8,128)(2,1)S(1)}, u32[]{:S(2)}, u32[]{:S(2)}) %collective-permute-start.16) | collective-permute-done | bytes 458784 | tf_op jit(solution)/shard_map/ppermute | solution.py:36
  42.0 7.5 %collective-permute-done.18 = bf16[16,7168]{1,0:T(8,128)(2,1)S(1)} collective-permute-done((bf16[16,7168]{1,0:T(8,128)(2,1)S(1)}, bf16[16,7168]{1,0:T(8,128)(2,1)S(1)}, u32[]{:S(2)}, u32[]{:S(2)}) %collective-permute-start.18) | collective-permute-done | bytes 229408 | tf_op jit(solution)/shard_map/ppermute | solution.py:36
  49.7 2.0 %collective-permute-start.20 = (bf16[8,7168]{1,0:T(8,128)(2,1)S(1)}, bf16[8,7168]{1,0:T(8,128)(2,1)S(1)}, u32[]{:S(2)}, u32[]{:S(2)}) collective-permute-start(bf16[8,7168]{1,0:T(8,128)(2,1)S(1)} %get-tuple-element.46), channel_id=1, source_target_pairs={{0,8},{1,9},{2,10},{3,11},{4,12},{5,13},{6,14},{7,15},{8,0},{9,1},... | collective-permute-start | bytes 344072 | tf_op jit(solution)/shard_map/ppermute | solution.py:27
  51.7 2.2 %collective-permute-start.21 = (bf16[8,7168]{1,0:T(8,128)(2,1)S(1)}, bf16[8,7168]{1,0:T(8,128)(2,1)S(1)}, u32[]{:S(2)}, u32[]{:S(2)}) collective-permute-start(bf16[8,7168]{1,0:T(8,128)(2,1)S(1)} %get-tuple-element.47), channel_id=1, source_target_pairs={{0,12},{1,13},{2,14},{3,15},{4,0},{5,1},{6,2},{7,3},{8,4},{9,5},{1... | collective-permute-start | bytes 344072 | tf_op jit(solution)/shard_map/ppermute | solution.py:27
  53.9 2.4 %collective-permute-done.19 = bf16[16,7168]{1,0:T(8,128)(2,1)S(1)} collective-permute-done((bf16[16,7168]{1,0:T(8,128)(2,1)S(1)}, bf16[16,7168]{1,0:T(8,128)(2,1)S(1)}, u32[]{:S(2)}, u32[]{:S(2)}) %collective-permute-start.19) | collective-permute-done | bytes 229408 | tf_op jit(solution)/shard_map/ppermute | solution.py:36
  56.7 0.9 %broadcast_select_fusion = bf16[4,128,512]{2,1,0:T(8,128)(2,1)} fusion(bf16[4,128,512]{2,1,0:T(8,128)(2,1)S(1)} %copy-done.4, pred[4]{0:T(512)(128)(4,1)S(1)} %iota_compare_fusion, bf16[128,512]{1,0:T(8,128)(2,1)S(1)} %collective-permute-done.23), kind=kLoop, calls=%fused_computation | loop fusion | flops 262144 | bytes 1179652 | tf_op jit(solution)/shard_map/jit(_where)/select_n | solution.py:302
  57.6 0.7 %collective-permute-done.20 = bf16[8,7168]{1,0:T(8,128)(2,1)S(1)} collective-permute-done((bf16[8,7168]{1,0:T(8,128)(2,1)S(1)}, bf16[8,7168]{1,0:T(8,128)(2,1)S(1)}, u32[]{:S(2)}, u32[]{:S(2)}) %collective-permute-start.20) | collective-permute-done | bytes 114720 | tf_op jit(solution)/shard_map/ppermute | solution.py:27
  58.3 4.6 %collective-permute-done.22 = bf16[8,7168]{1,0:T(8,128)(2,1)S(1)} collective-permute-done((bf16[8,7168]{1,0:T(8,128)(2,1)S(1)}, bf16[8,7168]{1,0:T(8,128)(2,1)S(1)}, u32[]{:S(2)}, u32[]{:S(2)}) %collective-permute-start.22) | collective-permute-done | bytes 114720 | tf_op jit(solution)/shard_map/ppermute | solution.py:27
  62.9 0.7 %add_convert_fusion.2 = bf16[8,7168]{1,0:T(8,128)(2,1)} fusion(bf16[8,7168]{1,0:T(8,128)(2,1)S(1)} %collective-permute-done.22, bf16[8,7168]{1,0:T(8,128)(2,1)S(1)} %collective-permute-done.21, bf16[8,7168]{1,0:T(8,128)(2,1)S(1)} %collective-permute-done.20, bf16[8,7168]{1,0:T(8,128)(2,1)S(1)} %get-tuple-element.34, ...), kind=kLoop, calls=%fused_computation.3 | loop fusion | flops 688128 | bytes 802816 | tf_op jit(solution)/shard_map/convert_element_type | solution.py:220
  (49 shorter events, 4.2 us)
Async XLA Ops:
  2.7 15.0 %collective-permute-start.6 = (bf16[592,128]{1,0:T(8,128)(2,1)}, bf16[592,128]{1,0:T(8,128)(2,1)S(1)}, u32[]{:S(2)}, u32[]{:S(2)}) collective-permute-start(bf16[592,128]{1,0:T(8,128)(2,1)} %get-tuple-element.25), channel_id=1, source_target_pairs={{0,15},{1,0},{2,1},{3,2},{4,3},{5,4},{6,5},{7,6},{8,7},{9,8},{10,9... | collective-permute-start | bytes 454664 | tf_op jit(solution)/shard_map/ppermute | solution.py:27
  8.1 5.9 %collective-permute-start.4 = (bf16[8,7296]{1,0:T(8,128)(2,1)}, bf16[8,7296]{1,0:T(8,128)(2,1)S(1)}, u32[]{:S(2)}, u32[]{:S(2)}) collective-permute-start(bf16[8,7296]{1,0:T(8,128)(2,1)} %get-tuple-element.24.refs_7_), channel_id=1, source_target_pairs={{0,12},{1,13},{2,14},{3,15},{4,0},{5,1},{6,2},{7,3},{8,4},{9,5},{1... | collective-permute-start | bytes 350216 | tf_op jit(solution)/shard_map/ppermute | solution.py:27
  8.6 7.6 %collective-permute-start = (bf16[8,7296]{1,0:T(8,128)(2,1)}, bf16[8,7296]{1,0:T(8,128)(2,1)S(1)}, u32[]{:S(2)}, u32[]{:S(2)}) collective-permute-start(bf16[8,7296]{1,0:T(8,128)(2,1)} %get-tuple-element.24.refs_7_), channel_id=1, source_target_pairs={{0,4},{1,5},{2,6},{3,7},{4,8},{5,9},{6,10},{7,11},{8,12},{9,13},{1... | collective-permute-start | bytes 350216 | tf_op jit(solution)/shard_map/ppermute | solution.py:27
  10.2 16.0 %collective-permute-start.2 = (bf16[8,7296]{1,0:T(8,128)(2,1)}, bf16[8,7296]{1,0:T(8,128)(2,1)S(1)}, u32[]{:S(2)}, u32[]{:S(2)}) collective-permute-start(bf16[8,7296]{1,0:T(8,128)(2,1)} %get-tuple-element.24.refs_7_), channel_id=1, source_target_pairs={{0,2},{1,3},{2,0},{3,1},{4,6},{5,7},{6,4},{7,5},{8,10},{9,11},{10,... | collective-permute-start | bytes 350216 | tf_op jit(solution)/shard_map/ppermute | solution.py:36
  14.0 12.2 %collective-permute-start.5 = (bf16[8,7296]{1,0:T(8,128)(2,1)S(1)}, bf16[8,7296]{1,0:T(8,128)(2,1)S(1)}, u32[]{:S(2)}, u32[]{:S(2)}) collective-permute-start(bf16[8,7296]{1,0:T(8,128)(2,1)S(1)} %collective-permute-done.4.refs_6_), channel_id=1, source_target_pairs={{0,2},{1,3},{2,0},{3,1},{4,6},{5,7},{6,4},{7,5},{8,10},{9,11},{10,... | collective-permute-start | bytes 350216 | tf_op jit(solution)/shard_map/ppermute | solution.py:36
  16.1 10.6 %collective-permute-start.3 = (bf16[8,7296]{1,0:T(8,128)(2,1)S(1)}, bf16[8,7296]{1,0:T(8,128)(2,1)S(1)}, u32[]{:S(2)}, u32[]{:S(2)}) collective-permute-start(bf16[8,7296]{1,0:T(8,128)(2,1)S(1)} %collective-permute-done.refs_3_), channel_id=1, source_target_pairs={{0,2},{1,3},{2,0},{3,1},{4,6},{5,7},{6,4},{7,5},{8,10},{9,11},{10,... | collective-permute-start | bytes 350216 | tf_op jit(solution)/shard_map/ppermute | solution.py:36
  16.6 10.2 %collective-permute-start.1 = (bf16[8,7296]{1,0:T(8,128)(2,1)S(1)}, bf16[8,7296]{1,0:T(8,128)(2,1)}, u32[]{:S(2)}, u32[]{:S(2)}) collective-permute-start(bf16[8,7296]{1,0:T(8,128)(2,1)S(1)} %collective-permute-done.refs_3_), channel_id=1, source_target_pairs={{0,4},{1,5},{2,6},{3,7},{4,8},{5,9},{6,10},{7,11},{8,12},{9,13},{1... | collective-permute-start | bytes 350216 | tf_op jit(solution)/shard_map/ppermute | solution.py:27
  17.7 11.2 %collective-permute-start.15 = (bf16[8,7296]{1,0:T(8,128)(2,1)}, bf16[8,7296]{1,0:T(8,128)(2,1)}, u32[]{:S(2)}, u32[]{:S(2)}) collective-permute-start(bf16[8,7296]{1,0:T(8,128)(2,1)} %get-tuple-element.24.refs_7_), channel_id=1, source_target_pairs={{0,1},{1,0},{2,3},{3,2},{4,5},{5,4},{6,7},{7,6},{8,9},{9,8},{10,11... | collective-permute-start | bytes 350216 | tf_op jit(solution)/shard_map/ppermute | solution.py:36
  26.2 3.2 %collective-permute-start.11 = (bf16[8,7296]{1,0:T(8,128)(2,1)S(1)}, bf16[8,7296]{1,0:T(8,128)(2,1)S(1)}, u32[]{:S(2)}, u32[]{:S(2)}) collective-permute-start(bf16[8,7296]{1,0:T(8,128)(2,1)S(1)} %collective-permute-done.refs_3_), channel_id=1, source_target_pairs={{0,1},{1,0},{2,3},{3,2},{4,5},{5,4},{6,7},{7,6},{8,9},{9,8},{10,11... | collective-permute-start | bytes 350216 | tf_op jit(solution)/shard_map/ppermute | solution.py:36
  26.2 3.2 %collective-permute-start.14 = (bf16[8,7296]{1,0:T(8,128)(2,1)S(1)}, bf16[8,7296]{1,0:T(8,128)(2,1)S(1)}, u32[]{:S(2)}, u32[]{:S(2)}) collective-permute-start(bf16[8,7296]{1,0:T(8,128)(2,1)S(1)} %collective-permute-done.4.refs_6_), channel_id=1, source_target_pairs={{0,1},{1,0},{2,3},{3,2},{4,5},{5,4},{6,7},{7,6},{8,9},{9,8},{10,11... | collective-permute-start | bytes 350216 | tf_op jit(solution)/shard_map/ppermute | solution.py:36
  26.7 5.7 %collective-permute-start.7 = (bf16[8,7296]{1,0:T(8,128)(2,1)}, bf16[8,7296]{1,0:T(8,128)(2,1)S(1)}, u32[]{:S(2)}, u32[]{:S(2)}) collective-permute-start(bf16[8,7296]{1,0:T(8,128)(2,1)} %collective-permute-done.1.refs_2_), channel_id=1, source_target_pairs={{0,2},{1,3},{2,0},{3,1},{4,6},{5,7},{6,4},{7,5},{8,10},{9,11},{10,... | collective-permute-start | bytes 350216 | tf_op jit(solution)/shard_map/ppermute | solution.py:36
  28.8 3.7 %collective-permute-start.10 = (bf16[8,7296]{1,0:T(8,128)(2,1)}, bf16[8,7296]{1,0:T(8,128)(2,1)S(1)}, u32[]{:S(2)}, u32[]{:S(2)}) collective-permute-start(bf16[8,7296]{1,0:T(8,128)(2,1)} %collective-permute-done.1.refs_2_), channel_id=1, source_target_pairs={{0,1},{1,0},{2,3},{3,2},{4,5},{5,4},{6,7},{7,6},{8,9},{9,8},{10,11... | collective-permute-start | bytes 350216 | tf_op jit(solution)/shard_map/ppermute | solution.py:36
  28.8 3.6 %collective-permute-start.9 = (bf16[8,7296]{1,0:T(8,128)(2,1)S(1)}, bf16[8,7296]{1,0:T(8,128)(2,1)S(1)}, u32[]{:S(2)}, u32[]{:S(2)}) collective-permute-start(bf16[8,7296]{1,0:T(8,128)(2,1)S(1)} %collective-permute-done.3.refs_1_), channel_id=1, source_target_pairs={{0,1},{1,0},{2,3},{3,2},{4,5},{5,4},{6,7},{7,6},{8,9},{9,8},{10,11... | collective-permute-start | bytes 350216 | tf_op jit(solution)/shard_map/ppermute | solution.py:36
  29.4 3.1 %collective-permute-start.12 = (bf16[8,7296]{1,0:T(8,128)(2,1)S(1)}, bf16[8,7296]{1,0:T(8,128)(2,1)S(1)}, u32[]{:S(2)}, u32[]{:S(2)}) collective-permute-start(bf16[8,7296]{1,0:T(8,128)(2,1)S(1)} %collective-permute-done.5.refs_4_), channel_id=1, source_target_pairs={{0,1},{1,0},{2,3},{3,2},{4,5},{5,4},{6,7},{7,6},{8,9},{9,8},{10,11... | collective-permute-start | bytes 350216 | tf_op jit(solution)/shard_map/ppermute | solution.py:36
  29.4 3.1 %collective-permute-start.13 = (bf16[8,7296]{1,0:T(8,128)(2,1)S(1)}, bf16[8,7296]{1,0:T(8,128)(2,1)S(1)}, u32[]{:S(2)}, u32[]{:S(2)}) collective-permute-start(bf16[8,7296]{1,0:T(8,128)(2,1)S(1)} %collective-permute-done.2.refs_5_), channel_id=1, source_target_pairs={{0,1},{1,0},{2,3},{3,2},{4,5},{5,4},{6,7},{7,6},{8,9},{9,8},{10,11... | collective-permute-start | bytes 350216 | tf_op jit(solution)/shard_map/ppermute | solution.py:36
  32.5 1.3 %collective-permute-start.8 = (bf16[8,7296]{1,0:T(8,128)(2,1)S(1)}, bf16[8,7296]{1,0:T(8,128)(2,1)S(1)}, u32[]{:S(2)}, u32[]{:S(2)}) collective-permute-start(bf16[8,7296]{1,0:T(8,128)(2,1)S(1)} %collective-permute-done.7.refs_0_), channel_id=1, source_target_pairs={{0,1},{1,0},{2,3},{3,2},{4,5},{5,4},{6,7},{7,6},{8,9},{9,8},{10,11... | collective-permute-start | bytes 350216 | tf_op jit(solution)/shard_map/ppermute | solution.py:36
  36.5 4.0 %collective-permute-start.17 = (bf16[32,7168]{1,0:T(8,128)(2,1)S(1)}, bf16[32,7168]{1,0:T(8,128)(2,1)S(1)}, u32[]{:S(2)}, u32[]{:S(2)}) collective-permute-start(bf16[32,7168]{1,0:T(8,128)(2,1)S(1)} %get-tuple-element.38), channel_id=1, source_target_pairs={{0,1},{1,0},{2,3},{3,2},{4,5},{5,4},{6,7},{7,6},{8,9},{9,8},{10,11... | collective-permute-start | bytes 1376264 | tf_op jit(solution)/shard_map/ppermute | solution.py:36
  38.6 18.1 %collective-permute-start.23 = (bf16[128,512]{1,0:T(8,128)(2,1)S(1)}, bf16[128,512]{1,0:T(8,128)(2,1)S(1)}, u32[]{:S(2)}, u32[]{:S(2)}) collective-permute-start(bf16[128,512]{1,0:T(8,128)(2,1)S(1)} %copy-done.6), channel_id=1, source_target_pairs={{0,1},{1,2},{2,3},{3,4},{4,5},{5,6},{6,7},{7,8},{8,9},{9,10},{10,1... | collective-permute-start | bytes 393224 | tf_op jit(solution)/shard_map/ppermute | solution.py:27
  39.0 2.9 %collective-permute-start.16 = (bf16[32,7168]{1,0:T(8,128)(2,1)S(1)}, bf16[32,7168]{1,0:T(8,128)(2,1)S(1)}, u32[]{:S(2)}, u32[]{:S(2)}) collective-permute-start(bf16[32,7168]{1,0:T(8,128)(2,1)S(1)} %get-tuple-element.35), channel_id=1, source_target_pairs={{0,1},{1,0},{2,3},{3,2},{4,5},{5,4},{6,7},{7,6},{8,9},{9,8},{10,11... | collective-permute-start | bytes 1376264 | tf_op jit(solution)/shard_map/ppermute | solution.py:36
  40.6 9.0 %collective-permute-start.18 = (bf16[16,7168]{1,0:T(8,128)(2,1)S(1)}, bf16[16,7168]{1,0:T(8,128)(2,1)S(1)}, u32[]{:S(2)}, u32[]{:S(2)}) collective-permute-start(bf16[16,7168]{1,0:T(8,128)(2,1)S(1)} %add_convert_fusion), channel_id=1, source_target_pairs={{0,2},{1,3},{2,0},{3,1},{4,6},{5,7},{6,4},{7,5},{8,10},{9,11},{10,... | collective-permute-start | bytes 688136 | tf_op jit(solution)/shard_map/ppermute | solution.py:36
  49.6 6.7 %collective-permute-start.19 = (bf16[16,7168]{1,0:T(8,128)(2,1)S(1)}, bf16[16,7168]{1,0:T(8,128)(2,1)S(1)}, u32[]{:S(2)}, u32[]{:S(2)}) collective-permute-start(bf16[16,7168]{1,0:T(8,128)(2,1)S(1)} %add_convert_fusion.1), channel_id=1, source_target_pairs={{0,2},{1,3},{2,0},{3,1},{4,6},{5,7},{6,4},{7,5},{8,10},{9,11},{10,... | collective-permute-start | bytes 688136 | tf_op jit(solution)/shard_map/ppermute | solution.py:36
  49.7 8.7 %collective-permute-start.20 = (bf16[8,7168]{1,0:T(8,128)(2,1)S(1)}, bf16[8,7168]{1,0:T(8,128)(2,1)S(1)}, u32[]{:S(2)}, u32[]{:S(2)}) collective-permute-start(bf16[8,7168]{1,0:T(8,128)(2,1)S(1)} %get-tuple-element.46), channel_id=1, source_target_pairs={{0,8},{1,9},{2,10},{3,11},{4,12},{5,13},{6,14},{7,15},{8,0},{9,1},... | collective-permute-start | bytes 344072 | tf_op jit(solution)/shard_map/ppermute | solution.py:27
  51.7 6.7 %collective-permute-start.21 = (bf16[8,7168]{1,0:T(8,128)(2,1)S(1)}, bf16[8,7168]{1,0:T(8,128)(2,1)S(1)}, u32[]{:S(2)}, u32[]{:S(2)}) collective-permute-start(bf16[8,7168]{1,0:T(8,128)(2,1)S(1)} %get-tuple-element.47), channel_id=1, source_target_pairs={{0,12},{1,13},{2,14},{3,15},{4,0},{5,1},{6,2},{7,3},{8,4},{9,5},{1... | collective-permute-start | bytes 344072 | tf_op jit(solution)/shard_map/ppermute | solution.py:27
  56.3 6.6 %collective-permute-start.22 = (bf16[8,7168]{1,0:T(8,128)(2,1)S(1)}, bf16[8,7168]{1,0:T(8,128)(2,1)S(1)}, u32[]{:S(2)}, u32[]{:S(2)}) collective-permute-start(bf16[8,7168]{1,0:T(8,128)(2,1)S(1)} %add_convert_fusion.3), channel_id=1, source_target_pairs={{0,4},{1,5},{2,6},{3,7},{4,8},{5,9},{6,10},{7,11},{8,12},{9,13},{1... | collective-permute-start | bytes 344072 | tf_op jit(solution)/shard_map/ppermute | solution.py:27
  (7 other events, 112.3 us)

commit v6 on v5

--- a/solution.py
+++ b/solution.py
@@ -85,37 +85,44 @@
     )(place, moved, hidden, ids_t, gates_t, query_t, own)
 
 
-def attend_body(place, moved, lengths, query, own, payload, cache, home, away, mark, *scratch):
-    moves, extents, asking, keys, sems = scratch
+def attend_body(ranks, visits, place, moved, lengths, query, own, cache, *refs):
+    if visits:
+        payload, home, away, asking, keys, sems = refs
+    else:
+        home, asking, keys, sems = refs
     requests, width, positions = cache.shape
-    fetches = [
-        pltpu.make_async_copy(moved, moves, sems.at[0]),
-        pltpu.make_async_copy(lengths, extents, sems.at[1]),
-        pltpu.make_async_copy(query, asking, sems.at[2]),
-    ]
-    copies = [
-        pltpu.make_async_copy(cache.at[j], keys.at[j], sems.at[3 + j]) for j in range(requests)
-    ]
-    for fetch in fetches + copies:
-        fetch.start()
-    for fetch in fetches:
-        fetch.wait()
-    leaving = moves[place[0]]
-    mark[...] = jnp.full(mark.shape, leaving, jnp.int32)
-    tail = payload[width:, :].astype(jnp.float32)
-    visiting = jnp.concatenate([tail[r : r + 1] for r in range(-(-width // LANES))], axis=1)
-    visiting = visiting[:, :width]
-    for j in range(requests):
-        here = leaving == j
-        asked = jnp.where(here, payload[:width, :], asking[j]).T
-        latent = jnp.where(here, visiting, own[j : j + 1, :].astype(jnp.float32))
-        copies[j].wait()
-        scores = jnp.dot(asked, keys[j], preferred_element_type=jnp.float32) * score_scale
+    leaving = moved[place[0]]
+    slots = [rank + (leaving <= rank).astype(jnp.int32) for rank in ranks]
+    copies = []
+    for i, slot in enumerate(slots):
+        pltpu.make_async_copy(query.at[slot], asking.at[i], sems.at[2 * i]).start()
+        pltpu.make_async_copy(cache.at[slot], keys.at[i], sems.at[2 * i + 1]).start()
+    if visits:
+        last = len(slots)
+        slots.append(leaving)
+        pltpu.make_async_copy(cache.at[leaving], keys.at[last], sems.at[2 * last + 1]).start()
+    which = lax.broadcasted_iota(jnp.int32, own.shape, 0)
+    own_rows = own[...].astype(jnp.float32)
+    work = []
+    for i, slot in enumerate(slots):
+        if i < len(ranks):
+            pltpu.make_async_copy(query.at[slot], asking.at[i], sems.at[2 * i]).wait()
+            asked = asking[i].T
+            latent = jnp.sum(jnp.where(which == slot, own_rows, 0.0), axis=0, keepdims=True)
+        else:
+            asked = payload[:width, :].T
+            tail = payload[width:, :].astype(jnp.float32)
+            pieces = [tail[r : r + 1] for r in range(-(-width // LANES))]
+            latent = jnp.concatenate(pieces, axis=1)[:, :width]
+        pltpu.make_async_copy(cache.at[slot], keys.at[i], sems.at[2 * i + 1]).wait()
+        scores = jnp.dot(asked, keys[i], preferred_element_type=jnp.float32) * score_scale
         own_score = (
             jnp.sum(asked.astype(jnp.float32) * latent, axis=1, keepdims=True) * score_scale
         )
+        work.append((slot, scores, own_score, latent))
+    for i, (slot, scores, own_score, latent) in enumerate(work):
         live = lax.broadcasted_iota(jnp.int32, scores.shape, 1)
-        scores = jnp.where(live < extents[place[0] * requests + j], scores, -jnp.inf)
+        scores = jnp.where(live < lengths[place[0] * requests + slot], scores, -jnp.inf)
         top_score = jnp.maximum(jnp.max(scores, axis=1, keepdims=True), own_score)
         raised = jnp.exp(scores - top_score)
         raised_own = jnp.exp(own_score - top_score)
@@ -124,44 +131,64 @@
         weight_own = (raised_own * share).astype(jnp.bfloat16).astype(jnp.float32)
         mixed = lax.dot_general(
             weights,
-            keys[j, :NOPE],
+            keys[i, :NOPE],
             (((1,), (1,)), ((), ())),
             preferred_element_type=jnp.float32,
         )
         result = (mixed + weight_own * latent[:, :NOPE]).astype(jnp.bfloat16)
-        home[j] = result
-
-        @pl.when(here)
-        def _():
+        if i < len(ranks):
+            home[i] = result
+        else:
             away[...] = result
 
 
-def attend(place, moved, lengths, query_t, own, payload, cache_t):
+def attend(ranks, place, moved, lengths, query_t, own, cache_t, payload=None):
     requests, width, heads = query_t.shape
     positions = cache_t.shape[2]
+    visits = payload is not None
+    count = len(ranks) + int(visits)
+    one = jax.ShapeDtypeStruct((heads, NOPE), jnp.bfloat16)
+    many = jax.ShapeDtypeStruct((len(ranks), heads, NOPE), jnp.bfloat16)
+    extra = [payload] if visits else []
     return pl.pallas_call(
-        attend_body,
-        out_shape=[
-            jax.ShapeDtypeStruct((requests, heads, NOPE), jnp.bfloat16),
-            jax.ShapeDtypeStruct((heads, NOPE), jnp.bfloat16),
-            jax.ShapeDtypeStruct((8, LANES), jnp.int32),
-        ],
-        in_specs=[SCALARS, MAIN, MAIN, MAIN, WHOLE, WHOLE, MAIN],
-        out_specs=[WHOLE, WHOLE, WHOLE],
+        functools.partial(attend_body, ranks, visits),
+        out_shape=[many] + [one] * len(extra),
+        in_specs=[SCALARS] * 3 + [MAIN, WHOLE, MAIN] + [WHOLE] * len(extra),
+        out_specs=[WHOLE] * (1 + len(extra)),
         scratch_shapes=[
-            pltpu.SMEM(moved.shape, moved.dtype),
-            pltpu.SMEM(lengths.shape, lengths.dtype),
-            pltpu.VMEM(query_t.shape, query_t.dtype),
-            pltpu.VMEM(cache_t.shape, cache_t.dtype),
-            pltpu.SemaphoreType.DMA((3 + requests,)),
+            pltpu.VMEM((len(ranks), width, heads), jnp.bfloat16),
+            pltpu.VMEM((count, width, positions), jnp.bfloat16),
+            pltpu.SemaphoreType.DMA((2 * count,)),
         ],
         compiler_params=pltpu.CompilerParams(vmem_limit_bytes=58 * MIB),
         cost_estimate=pl.CostEstimate(
-            flops=2 * requests * heads * positions * (width + NOPE),
+            flops=2 * count * heads * positions * (width + NOPE),
             bytes_accessed=0,
             transcendentals=0,
         ),
-    )(place, moved, lengths, query_t, own, payload, cache_t)
+    )(place, moved, lengths, query_t, own, cache_t, *extra)
+
+
+def settle_body(place, moved, first, second, returned, out):
+    leaving = moved[place[0]]
+    stay = [first[i] for i in range(first.shape[0])] + [second[i] for i in range(second.shape[0])]
+    for j in range(out.shape[0]):
+        below = stay[max(j - 1, 0)]
+        same = stay[min(j, len(stay) - 1)]
+        here = jnp.where(leaving < j, below, same)
+        out[j] = jnp.where(leaving == j, returned[...], here)
+
+
+def settle(place, moved, first, second, returned):
+    count = first.shape[0] + second.shape[0] + 1
+    return pl.pallas_call(
+        settle_body,
+        out_shape=jax.ShapeDtypeStruct((count,) + returned.shape, returned.dtype),
+        in_specs=[SCALARS, SCALARS] + [WHOLE] * 3,
+        out_specs=WHOLE,
+        compiler_params=pltpu.CompilerParams(vmem_limit_bytes=40 * MIB),
+        cost_estimate=pl.CostEstimate(flops=0, bytes_accessed=0, transcendentals=0),
+    )(place, moved, first, second, returned)
 
 
 def expert_body(count, groups, sizes, place, w_gate, w_up, w_down, *refs):
@@ -238,6 +265,7 @@
     turns = ranks // 4
     groups = ranks // SPLIT
     tokens = hidden_rows.shape[0]
+    requests = latent_cache.shape[0]
     position = lax.axis_index(axis)
     place = position[None]
     query_t = jnp.swapaxes(queries, 1, 2)
@@ -247,59 +275,69 @@
         place, moved_slot, hidden_rows, group_ids.T, route_gates.T, query_t, new_latent, groups
     )
 
+    visiting = shifted(payload, axis, -1)
     columns = {r: rotated(rows, axis, r) for r in range(1, turns) if r != 2}
     across = {0: swapped(rows, axis, 2)}
-    order = list(range(turns))
+
+    half = requests // 2
+    scalars = (place, moved_slot, cache_lengths)
+    new_here, _ = lax.optimization_barrier((new_latent, rows))
+    (first,) = attend(tuple(range(half)), *scalars, query_t, new_here, cache_t)
+    columns, across, visiting, first = lax.optimization_barrier((columns, across, visiting, first))
+    late = {}
     if turns > 2:
-        columns[2] = rotated(columns[1], axis, 1)
-        order = [2, 1] + order[3:] + [0]
-    for r in order[1:-1]:
-        across[r] = swapped(columns[r], axis, 2)
-
-    visiting = shifted(payload, axis, -1)
-    early = {r: columns.pop(r) for r in order[1:-1]}
-    visiting, early = lax.optimization_barrier((visiting, early))
-    home, away, mark = attend(
-        place, moved_slot, cache_lengths, query_t, new_latent, visiting, cache_t
-    )
-    columns, across, away = lax.optimization_barrier((columns, across, away))
-    columns.update(early)
+        late[2] = rotated(columns[1], axis, 1)
+    crossing = {r: swapped(columns[r], axis, 2) for r in columns}
+
+    second, away = attend(
+        tuple(range(half, requests - 1)), *scalars, query_t, new_latent, cache_t, visiting
+    )
+    late, crossing, away = lax.optimization_barrier((late, crossing, away))
+    across.update(crossing)
     columns[0] = rows
-    for r in order[:1]:
-        across[r] = swapped(columns[r], axis, 2)
     returned = shifted(away, axis, 1)
-
-    batches = [order[: turns // 2], order[turns // 2 :]]
-    near = []
-    for batch in batches:
-        near += [across[r] for r in batch] + [columns[r] for r in batch]
-    blocks = near + [swapped(block, axis, 1) for block in near]
-    sizes = []
-    for batch in batches:
-        sizes += [len(batch)] + [1] * len(batch)
-    outs = expert(
-        place, w_gate, w_up, w_down, blocks, groups, sizes + [2 * len(b) for b in batches]
-    )
-
-    sends = [swapped(send, axis, 1) for send in outs[-2:]]
+    late_across = {r: swapped(late[r], axis, 2) for r in late}
+
     sums = {}
-    crossed = None
-    for batch, chip in zip(batches, sends):
-        mine, outs = outs[: 1 + len(batch)], outs[1 + len(batch) :]
-        split = len(batch) * tokens
-        crossing = added(mine[0], chip[:split])
-        if crossed is not None:
-            crossing, crossed = lax.optimization_barrier((crossing, crossed))
-        crossed = swapped(crossing, axis, 2)
-        for i, r in enumerate(batch):
-            at = slice(i * tokens, (i + 1) * tokens)
-            sums[r] = [mine[1 + i], chip[split:][at], crossed[at]]
+    latest = []
+
+    def sent(outs, batches):
+        for i, batch in enumerate(batches):
+            mine, outs = outs[: 1 + len(batch)], outs[1 + len(batch) :]
+            send = outs[sum(1 + len(b) for b in batches[i + 1 :]) + i]
+            if latest:
+                _, send = lax.optimization_barrier((latest[0], send))
+            chip = swapped(send, axis, 1)
+            split = len(batch) * tokens
+            leaves = added(mine[0], chip[:split])
+            if batch == [0]:
+                _, leaves = lax.optimization_barrier((latest[1], leaves))
+            crossed = swapped(leaves, axis, 2)
+            if not latest:
+                latest.extend([leaves, crossed])
+            for k, r in enumerate(batch):
+                at = slice(k * tokens, (k + 1) * tokens)
+                sums[r] = [mine[1 + k], chip[split:][at], crossed[at]]
+
+    def through_experts(batches, columns, across):
+        near, sizes = [], []
+        for batch in batches:
+            near += [across[r] for r in batch] + [columns[r] for r in batch]
+            sizes += [len(batch)] + [1] * len(batch)
+        blocks = near + [swapped(block, axis, 1) for block in near]
+        if latest:
+            _, blocks = lax.optimization_barrier((latest[1], blocks))
+        sizes += [2 * len(batch) for batch in batches]
+        sent(expert(place, w_gate, w_up, w_down, blocks, groups, sizes), batches)
+
+    through_experts([sorted(crossing), [0]], columns, across)
+    if late:
+        through_experts([sorted(late)], late, late_across)
     terms = sums.pop(0)
     for r in sums:
         terms = terms + [rotated(added(*sums[r]), axis, -r)]
     moe_out = added(*terms)
-    slots = jnp.arange(home.shape[0], dtype=jnp.int32)[:, None, None]
-    attn_out = jnp.where(slots == mark[:1, :1][None], returned[None], home)
+    attn_out = settle(place, moved_slot, first, second, returned)
     return (moe_out, attn_out)
 
 

time: 63.9 us -> 60.2 us (0.942)
  waiting for transfers between devices: 26.1 us -> 19.7 us
  Pallas kernels: 12.5 us -> 15.7 us
  starting transfers between devices: 19.8 us -> 22.7 us
  local copies, waits for them, and re-layouts: 1.9 us -> 0.04 us
  other arithmetic: 2.5 us -> 0.99 us
    ppermute x8, waiting for transfers between devices: 11.3 us -> 7.56 us  [shifted(): return lax.ppermute(value, axis, pairs)]
    ppermute x16 -> x18, waiting for transfers between devices: 14.8 us -> 12.1 us  [swapped(): return lax.ppermute(value, axis, pairs)]
    pallas_call x1 -> x3, Pallas kernels: 7.8 us -> 10.4 us  [the longest x2 9.01 us: attend(): pl.pallas_call(functools.partial(attend_body, ranks, visits), out_shape=[...]
    ppermute x8, starting transfers between devices: 13.6 us -> 15.7 us  [shifted(): return lax.ppermute(value, axis, pairs)]
    slice x1 -> x0, local copies, waits for them, and re-layouts: 1.23 us -> none  [per_device(): attn_out = jnp.where(slots == mark[:1, :1][None], returned[None], home)]
    select_n x1 -> x0, other arithmetic: 0.9 us -> none  [per_device(): attn_out = jnp.where(slots == mark[:1, :1][None], returned[None], home)]
    ppermute x16 -> x18, starting transfers between devices: 6.22 us -> 7.03 us  [swapped(): return lax.ppermute(value, axis, pairs)]
    pallas_call x1 -> x2, Pallas kernels: 2.69 us -> 3.38 us  [expert(): pl.pallas_call(functools.partial(expert_body, count, groups, sizes), out_...]
  transfers between devices with their start and end apart: 24 -> 26, of which waited for: 9 -> 12; matrix products, arithmetic and copies ran while one was open for 5% -> 0% of each run, Pallas kernels for 12% -> 19%
where the time goes in v6:
time: 60.2 us; the launch traced here: 59.9 us
  starting transfers between devices  22.7 us (38%)
  waiting for transfers between devices  19.7 us (33%)
  Pallas kernels  15.7 us (26%)
  other arithmetic  0.99 us (2%)
  between operations  0.81 us (1%)
    ppermute x8, starting transfers between devices, shifted(): return lax.ppermute(value, axis, pairs)  15.7 us
    ppermute x18, waiting for transfers between devices, swapped(): return lax.ppermute(value, axis, pairs)  12.1 us
    pallas_call x2, Pallas kernels, attend(): pl.pallas_call(functools.partial(attend_body, ranks, visits), out_shape=[...  9.01 us
    ppermute x8, waiting for transfers between devices, shifted(): return lax.ppermute(value, axis, pairs)  7.56 us
    ppermute x18, starting transfers between devices, swapped(): return lax.ppermute(value, axis, pairs)  7.03 us
    pallas_call x2, Pallas kernels, expert(): pl.pallas_call(functools.partial(expert_body, count, groups, sizes), out_...  3.38 us
    pallas_call x1, Pallas kernels, prepare(): pl.pallas_call(functools.partial(prepare_body, groups), out_shape=[jax.Sh...  1.9 us
    pallas_call x1, Pallas kernels, settle(): pl.pallas_call(settle_body, out_shape=jax.ShapeDtypeStruct((count,) + ret...  1.39 us
  transfers between devices with their start and end apart: 26, of which 12 were waited for; matrix products, arithmetic and copies ran while one was open for 0% of the time, Pallas kernels for 19%

profile of v6, /device:TPU:0, one launch (start us, length us, event | category | flops | bytes accessed | tf_op | source)
XLA Modules:
  0.0 59.9 jit_solution(414093947918049253)
XLA Ops:
  0.6 1.9 %shard_map.122 = (bf16[8,7296]{1,0:T(8,128)(2,1)}, bf16[592,128]{1,0:T(8,128)(2,1)}) custom-call(s32[1]{0:T(128)} %bitcast.place, s32[16]{0:T(128)} %moved.7, bf16[8,7168]{1,0:T(8,128)(2,1)} %hidden.1, s32[2,8]{1,0:T(2,128)} %bitcast.10, f32[2,8]{1,0:T(2,128)} %bitcast.11, bf16[4,576,128]{2,1,0:T(8,128)(2,1)} %bitcast.7, bf16[4,576]{1,0:T(4,128)(2,1)} %own.4), custom_call_target="tpu_custom_call" | custom-call | tf_op jit(solution)/shard_map/pallas_call | solution.py:75
  2.5 5.4 %collective-permute-start.3 = (bf16[592,128]{1,0:T(8,128)(2,1)}, bf16[592,128]{1,0:T(8,128)(2,1)}, u32[]{:S(2)}, u32[]{:S(2)}) collective-permute-start(bf16[592,128]{1,0:T(8,128)(2,1)} %get-tuple-element.34), channel_id=1, source_target_pairs={{0,15},{1,0},{2,1},{3,2},{4,3},{5,4},{6,5},{7,6},{8,7},{9,8},{10,9... | collective-permute-start | bytes 454664 | tf_op jit(solution)/shard_map/ppermute | solution.py:27
  8.0 1.1 %collective-permute-start.1 = (bf16[8,7296]{1,0:T(8,128)(2,1)}, bf16[8,7296]{1,0:T(8,128)(2,1)S(1)}, u32[]{:S(2)}, u32[]{:S(2)}) collective-permute-start(bf16[8,7296]{1,0:T(8,128)(2,1)} %get-tuple-element.33.refs_5_), channel_id=1, source_target_pairs={{0,12},{1,13},{2,14},{3,15},{4,0},{5,1},{6,2},{7,3},{8,4},{9,5},{1... | collective-permute-start | bytes 350216 | tf_op jit(solution)/shard_map/ppermute | solution.py:27
  9.1 0.9 %collective-permute-start = (bf16[8,7296]{1,0:T(8,128)(2,1)}, bf16[8,7296]{1,0:T(8,128)(2,1)S(1)}, u32[]{:S(2)}, u32[]{:S(2)}) collective-permute-start(bf16[8,7296]{1,0:T(8,128)(2,1)} %get-tuple-element.33.refs_5_), channel_id=1, source_target_pairs={{0,4},{1,5},{2,6},{3,7},{4,8},{5,9},{6,10},{7,11},{8,12},{9,13},{1... | collective-permute-start | bytes 350216 | tf_op jit(solution)/shard_map/ppermute | solution.py:27
  10.0 4.5 %shard_map.123.first = bf16[2,128,512]{2,1,0:T(8,128)(2,1)} custom-call(s32[1]{0:T(128)} %bitcast.place, s32[16]{0:T(128)} %moved.7, s32[64]{0:T(128)} %lengths.3, bf16[4,576,128]{2,1,0:T(8,128)(2,1)} %bitcast.8, bf16[4,576]{1,0:T(4,128)(2,1)} %own.4, bf16[4,576,1024]{2,1,0:T(8,128)(2,1)} %bitcast.5), custom_call_target="tpu_custom_call" | custom-call | flops 570425344 | tf_op jit(solution)/shard_map/pallas_call | solution.py:153
  14.8 2.0 %collective-permute-done.refs_2_ = bf16[8,7296]{1,0:T(8,128)(2,1)S(1)} collective-permute-done((bf16[8,7296]{1,0:T(8,128)(2,1)}, bf16[8,7296]{1,0:T(8,128)(2,1)S(1)}, u32[]{:S(2)}, u32[]{:S(2)}) %collective-permute-start) | collective-permute-done | bytes 116768 | tf_op jit(solution)/shard_map/ppermute | solution.py:27
  16.8 0.7 %collective-permute-start.6 = (bf16[8,7296]{1,0:T(8,128)(2,1)S(1)}, bf16[8,7296]{1,0:T(8,128)(2,1)S(1)}, u32[]{:S(2)}, u32[]{:S(2)}) collective-permute-start(bf16[8,7296]{1,0:T(8,128)(2,1)S(1)} %collective-permute-done.1.refs_3_), channel_id=1, source_target_pairs={{0,2},{1,3},{2,0},{3,1},{4,6},{5,7},{6,4},{7,5},{8,10},{9,11},{10,... | collective-permute-start | bytes 350216 | tf_op jit(solution)/shard_map/ppermute | solution.py:36
  17.5 1.3 %collective-permute-start.5 = (bf16[8,7296]{1,0:T(8,128)(2,1)S(1)}, bf16[8,7296]{1,0:T(8,128)(2,1)}, u32[]{:S(2)}, u32[]{:S(2)}) collective-permute-start(bf16[8,7296]{1,0:T(8,128)(2,1)S(1)} %collective-permute-done.refs_2_), channel_id=1, source_target_pairs={{0,2},{1,3},{2,0},{3,1},{4,6},{5,7},{6,4},{7,5},{8,10},{9,11},{10,... | collective-permute-start | bytes 350216 | tf_op jit(solution)/shard_map/ppermute | solution.py:36
  18.8 1.6 %collective-permute-start.4 = (bf16[8,7296]{1,0:T(8,128)(2,1)S(1)}, bf16[8,7296]{1,0:T(8,128)(2,1)S(1)}, u32[]{:S(2)}, u32[]{:S(2)}) collective-permute-start(bf16[8,7296]{1,0:T(8,128)(2,1)S(1)} %collective-permute-done.refs_2_), channel_id=1, source_target_pairs={{0,4},{1,5},{2,6},{3,7},{4,8},{5,9},{6,10},{7,11},{8,12},{9,13},{1... | collective-permute-start | bytes 350216 | tf_op jit(solution)/shard_map/ppermute | solution.py:27
  21.0 4.5 %shard_map.124 = (bf16[1,128,512]{2,1,0:T(8,128)(2,1)}, bf16[128,512]{1,0:T(8,128)(2,1)}) custom-call(s32[1]{0:T(128)} %bitcast.place, s32[16]{0:T(128)} %moved.7, s32[64]{0:T(128)} %lengths.3, bf16[4,576,128]{2,1,0:T(8,128)(2,1)} %bitcast.9, bf16[4,576]{1,0:T(4,128)(2,1)} %own.4, bf16[4,576,1024]{2,1,0:T(8,128)(2,1)} %bitcast.6, ...), custom_call_target="tpu_custom_call" | custom-call | flops 570425344 | tf_op jit(solution)/shard_map/pallas_call | solution.py:153
  27.6 2.4 %shard_map.125 = (bf16[16,7168]{1,0:T(8,128)(2,1)S(1)}, bf16[8,7168]{1,0:T(8,128)(2,1)S(1)}, bf16[8,7168]{1,0:T(8,128)(2,1)S(1)}, bf16[8,7168]{1,0:T(8,128)(2,1)...) custom-call(s32[1]{0:T(128)} %bitcast.place, ...), custom_call_target="tpu_custom_call" | custom-call | flops 528482304 | bytes 5505024 | tf_op jit(solution)/shard_map/pallas_call | solution.py:230
  30.5 1.4 %collective-permute-done.13 = bf16[32,7168]{1,0:T(8,128)(2,1)S(1)} collective-permute-done((bf16[32,7168]{1,0:T(8,128)(2,1)S(1)}, bf16[32,7168]{1,0:T(8,128)(2,1)S(1)}, u32[]{:S(2)}, u32[]{:S(2)}) %collective-permute-start.13) | collective-permute-done | bytes 458784 | tf_op jit(solution)/shard_map/ppermute | solution.py:36
  33.0 3.4 %collective-permute-done.19.refs_0_ = bf16[8,7296]{1,0:T(8,128)(2,1)S(1)} collective-permute-done((bf16[8,7296]{1,0:T(8,128)(2,1)S(1)}, bf16[8,7296]{1,0:T(8,128)(2,1)S(1)}, u32[]{:S(2)}, u32[]{:S(2)}) %collective-permute-start.19) | collective-permute-done | bytes 116768 | tf_op jit(solution)/shard_map/ppermute | solution.py:36
  36.9 0.8 %collective-permute-done.20.refs_2_ = bf16[8,7296]{1,0:T(8,128)(2,1)S(1)} collective-permute-done((bf16[8,7296]{1,0:T(8,128)(2,1)S(1)}, bf16[8,7296]{1,0:T(8,128)(2,1)S(1)}, u32[]{:S(2)}, u32[]{:S(2)}) %collective-permute-start.20) | collective-permute-done | bytes 116768 | tf_op jit(solution)/shard_map/ppermute | solution.py:36
  37.7 2.9 %collective-permute-done.15 = bf16[16,7168]{1,0:T(8,128)(2,1)S(1)} collective-permute-done((bf16[16,7168]{1,0:T(8,128)(2,1)S(1)}, bf16[16,7168]{1,0:T(8,128)(2,1)S(1)}, u32[]{:S(2)}, u32[]{:S(2)}) %collective-permute-start.15) | collective-permute-done | bytes 229408 | tf_op jit(solution)/shard_map/ppermute | solution.py:36
  40.6 1.0 %shard_map.126 = (bf16[8,7168]{1,0:T(8,128)(2,1)S(1)}, bf16[8,7168]{1,0:T(8,128)(2,1)S(1)}, bf16[16,7168]{1,0:T(8,128)(2,1)S(1)}) custom-call(s32[1]{0:T(128)} %bitcast.place, bf16[1,7168,128]{2,1,0:T(8,128)(2,1)S(1)} %copy-done, bf16[1,7168,128]{2,1,0:T(8,128)(2,1)S(1)} %copy-done.1, bf16[1,128,7168]{2,1,0:T(8,128)(2,1)S(1)} %copy-done.2, ...), custom_call_target="tpu_custom_call" | custom-call | flops 176160768 | bytes 5505024 | tf_op jit(solution)/shard_map/pallas_call | solution.py:230
  41.7 0.9 %collective-permute-start.16 = (bf16[8,7168]{1,0:T(8,128)(2,1)S(1)}, bf16[8,7168]{1,0:T(8,128)(2,1)S(1)}, u32[]{:S(2)}, u32[]{:S(2)}) collective-permute-start(bf16[8,7168]{1,0:T(8,128)(2,1)S(1)} %add_convert_fusion.6), channel_id=1, source_target_pairs={{0,2},{1,3},{2,0},{3,1},{4,6},{5,7},{6,4},{7,5},{8,10},{9,11},{10,... | collective-permute-start | bytes 344072 | tf_op jit(solution)/shard_map/ppermute | solution.py:36
  43.2 0.9 %collective-permute-start.23 = (bf16[8,7168]{1,0:T(8,128)(2,1)S(1)}, bf16[8,7168]{1,0:T(8,128)(2,1)S(1)}, u32[]{:S(2)}, u32[]{:S(2)}) collective-permute-start(bf16[8,7168]{1,0:T(8,128)(2,1)S(1)} %add_convert_fusion.3), channel_id=1, source_target_pairs={{0,2},{1,3},{2,0},{3,1},{4,6},{5,7},{6,4},{7,5},{8,10},{9,11},{10,... | collective-permute-start | bytes 344072 | tf_op jit(solution)/shard_map/ppermute | solution.py:36
  44.2 3.5 %collective-permute-start.17 = (bf16[8,7168]{1,0:T(8,128)(2,1)S(1)}, bf16[8,7168]{1,0:T(8,128)(2,1)S(1)}, u32[]{:S(2)}, u32[]{:S(2)}) collective-permute-start(bf16[8,7168]{1,0:T(8,128)(2,1)S(1)} %get-tuple-element.64), channel_id=1, source_target_pairs={{0,12},{1,13},{2,14},{3,15},{4,0},{5,1},{6,2},{7,3},{8,4},{9,5},{1... | collective-permute-start | bytes 344072 | tf_op jit(solution)/shard_map/ppermute | solution.py:27
  47.7 2.1 %collective-permute-done.23 = bf16[8,7168]{1,0:T(8,128)(2,1)S(1)} collective-permute-done((bf16[8,7168]{1,0:T(8,128)(2,1)S(1)}, bf16[8,7168]{1,0:T(8,128)(2,1)S(1)}, u32[]{:S(2)}, u32[]{:S(2)}) %collective-permute-start.23) | collective-permute-done | bytes 114720 | tf_op jit(solution)/shard_map/ppermute | solution.py:36
  49.9 2.6 %collective-permute-start.24 = (bf16[8,7168]{1,0:T(8,128)(2,1)S(1)}, bf16[8,7168]{1,0:T(8,128)(2,1)S(1)}, u32[]{:S(2)}, u32[]{:S(2)}) collective-permute-start(bf16[8,7168]{1,0:T(8,128)(2,1)S(1)} %add_convert_fusion.2), channel_id=1, source_target_pairs={{0,8},{1,9},{2,10},{3,11},{4,12},{5,13},{6,14},{7,15},{8,0},{9,1},... | collective-permute-start | bytes 344072 | tf_op jit(solution)/shard_map/ppermute | solution.py:27
  52.5 1.4 %shard_map.127 = bf16[4,128,512]{2,1,0:T(8,128)(2,1)} custom-call(s32[1]{0:T(128)} %bitcast.place, s32[16]{0:T(128)S(1)} %copy-done.6, bf16[2,128,512]{2,1,0:T(8,128)(2,1)S(1)} %copy-done.3, bf16[1,128,512]{2,1,0:T(8,128)(2,1)S(1)} %copy-done.4, bf16[128,512]{1,0:T(8,128)(2,1)S(1)} %collective-permute-done.25.returned), custom_call_target="tpu_custom_call" | custom-call | tf_op jit(solution)/shard_map/pallas_call | solution.py:184
  54.6 4.6 %collective-permute-done.24 = bf16[8,7168]{1,0:T(8,128)(2,1)S(1)} collective-permute-done((bf16[8,7168]{1,0:T(8,128)(2,1)S(1)}, bf16[8,7168]{1,0:T(8,128)(2,1)S(1)}, u32[]{:S(2)}, u32[]{:S(2)}) %collective-permute-start.24) | collective-permute-done | bytes 114720 | tf_op jit(solution)/shard_map/ppermute | solution.py:27
  59.2 0.7 %add_convert_fusion.1 = bf16[8,7168]{1,0:T(8,128)(2,1)} fusion(bf16[8,7168]{1,0:T(8,128)(2,1)S(1)} %collective-permute-done.24, bf16[8,7168]{1,0:T(8,128)(2,1)S(1)} %collective-permute-done.18, bf16[8,7168]{1,0:T(8,128)(2,1)S(1)} %collective-permute-done.17, bf16[8,7168]{1,0:T(8,128)(2,1)S(1)} %collective-permute-done.16, ...), kind=kLoop, calls=%fused_computation.1 | loop fusion | flops 688128 | bytes 802816 | tf_op jit(solution)/shard_map/convert_element_type | solution.py:247
  (56 shorter events, 6.5 us)
Async XLA Ops:
  2.5 14.3 %collective-permute-start.3 = (bf16[592,128]{1,0:T(8,128)(2,1)}, bf16[592,128]{1,0:T(8,128)(2,1)}, u32[]{:S(2)}, u32[]{:S(2)}) collective-permute-start(bf16[592,128]{1,0:T(8,128)(2,1)} %get-tuple-element.34), channel_id=1, source_target_pairs={{0,15},{1,0},{2,1},{3,2},{4,3},{5,4},{6,5},{7,6},{8,7},{9,8},{10,9... | collective-permute-start | bytes 454664 | tf_op jit(solution)/shard_map/ppermute | solution.py:27
  8.0 6.6 %collective-permute-start.2 = (bf16[8,7296]{1,0:T(8,128)(2,1)}, bf16[8,7296]{1,0:T(8,128)(2,1)S(1)}, u32[]{:S(2)}, u32[]{:S(2)}) collective-permute-start(bf16[8,7296]{1,0:T(8,128)(2,1)} %get-tuple-element.33.refs_5_), channel_id=1, source_target_pairs={{0,2},{1,3},{2,0},{3,1},{4,6},{5,7},{6,4},{7,5},{8,10},{9,11},{10,... | collective-permute-start | bytes 350216 | tf_op jit(solution)/shard_map/ppermute | solution.py:36
  8.0 6.8 %collective-permute-start.1 = (bf16[8,7296]{1,0:T(8,128)(2,1)}, bf16[8,7296]{1,0:T(8,128)(2,1)S(1)}, u32[]{:S(2)}, u32[]{:S(2)}) collective-permute-start(bf16[8,7296]{1,0:T(8,128)(2,1)} %get-tuple-element.33.refs_5_), channel_id=1, source_target_pairs={{0,12},{1,13},{2,14},{3,15},{4,0},{5,1},{6,2},{7,3},{8,4},{9,5},{1... | collective-permute-start | bytes 350216 | tf_op jit(solution)/shard_map/ppermute | solution.py:27
  9.1 7.7 %collective-permute-start = (bf16[8,7296]{1,0:T(8,128)(2,1)}, bf16[8,7296]{1,0:T(8,128)(2,1)S(1)}, u32[]{:S(2)}, u32[]{:S(2)}) collective-permute-start(bf16[8,7296]{1,0:T(8,128)(2,1)} %get-tuple-element.33.refs_5_), channel_id=1, source_target_pairs={{0,4},{1,5},{2,6},{3,7},{4,8},{5,9},{6,10},{7,11},{8,12},{9,13},{1... | collective-permute-start | bytes 350216 | tf_op jit(solution)/shard_map/ppermute | solution.py:27
  16.8 8.7 %collective-permute-start.6 = (bf16[8,7296]{1,0:T(8,128)(2,1)S(1)}, bf16[8,7296]{1,0:T(8,128)(2,1)S(1)}, u32[]{:S(2)}, u32[]{:S(2)}) collective-permute-start(bf16[8,7296]{1,0:T(8,128)(2,1)S(1)} %collective-permute-done.1.refs_3_), channel_id=1, source_target_pairs={{0,2},{1,3},{2,0},{3,1},{4,6},{5,7},{6,4},{7,5},{8,10},{9,11},{10,... | collective-permute-start | bytes 350216 | tf_op jit(solution)/shard_map/ppermute | solution.py:36
  17.5 8.0 %collective-permute-start.5 = (bf16[8,7296]{1,0:T(8,128)(2,1)S(1)}, bf16[8,7296]{1,0:T(8,128)(2,1)}, u32[]{:S(2)}, u32[]{:S(2)}) collective-permute-start(bf16[8,7296]{1,0:T(8,128)(2,1)S(1)} %collective-permute-done.refs_2_), channel_id=1, source_target_pairs={{0,2},{1,3},{2,0},{3,1},{4,6},{5,7},{6,4},{7,5},{8,10},{9,11},{10,... | collective-permute-start | bytes 350216 | tf_op jit(solution)/shard_map/ppermute | solution.py:36
  18.8 7.2 %collective-permute-start.4 = (bf16[8,7296]{1,0:T(8,128)(2,1)S(1)}, bf16[8,7296]{1,0:T(8,128)(2,1)S(1)}, u32[]{:S(2)}, u32[]{:S(2)}) collective-permute-start(bf16[8,7296]{1,0:T(8,128)(2,1)S(1)} %collective-permute-done.refs_2_), channel_id=1, source_target_pairs={{0,4},{1,5},{2,6},{3,7},{4,8},{5,9},{6,10},{7,11},{8,12},{9,13},{1... | collective-permute-start | bytes 350216 | tf_op jit(solution)/shard_map/ppermute | solution.py:27
  20.5 5.7 %collective-permute-start.12 = (bf16[8,7296]{1,0:T(8,128)(2,1)S(1)}, bf16[8,7296]{1,0:T(8,128)(2,1)}, u32[]{:S(2)}, u32[]{:S(2)}) collective-permute-start(bf16[8,7296]{1,0:T(8,128)(2,1)S(1)} %copy-done.5), channel_id=1, source_target_pairs={{0,1},{1,0},{2,3},{3,2},{4,5},{5,4},{6,7},{7,6},{8,9},{9,8},{10,11... | collective-permute-start | bytes 350216 | tf_op jit(solution)/shard_map/ppermute | solution.py:36
  20.5 6.6 %collective-permute-start.10 = (bf16[8,7296]{1,0:T(8,128)(2,1)S(1)}, bf16[8,7296]{1,0:T(8,128)(2,1)}, u32[]{:S(2)}, u32[]{:S(2)}) collective-permute-start(bf16[8,7296]{1,0:T(8,128)(2,1)S(1)} %collective-permute-done.1.refs_3_), channel_id=1, source_target_pairs={{0,1},{1,0},{2,3},{3,2},{4,5},{5,4},{6,7},{7,6},{8,9},{9,8},{10,11... | collective-permute-start | bytes 350216 | tf_op jit(solution)/shard_map/ppermute | solution.py:36
  25.5 1.6 %collective-permute-start.9 = (bf16[8,7296]{1,0:T(8,128)(2,1)S(1)}, bf16[8,7296]{1,0:T(8,128)(2,1)S(1)}, u32[]{:S(2)}, u32[]{:S(2)}) collective-permute-start(bf16[8,7296]{1,0:T(8,128)(2,1)S(1)} %collective-permute-done.refs_2_), channel_id=1, source_target_pairs={{0,1},{1,0},{2,3},{3,2},{4,5},{5,4},{6,7},{7,6},{8,9},{9,8},{10,11... | collective-permute-start | bytes 350216 | tf_op jit(solution)/shard_map/ppermute | solution.py:36
  25.6 1.5 %collective-permute-start.11 = (bf16[8,7296]{1,0:T(8,128)(2,1)S(1)}, bf16[8,7296]{1,0:T(8,128)(2,1)S(1)}, u32[]{:S(2)}, u32[]{:S(2)}) collective-permute-start(bf16[8,7296]{1,0:T(8,128)(2,1)S(1)} %collective-permute-done.2.refs_4_), channel_id=1, source_target_pairs={{0,1},{1,0},{2,3},{3,2},{4,5},{5,4},{6,7},{7,6},{8,9},{9,8},{10,11... | collective-permute-start | bytes 350216 | tf_op jit(solution)/shard_map/ppermute | solution.py:36
  26.1 1.5 %collective-permute-start.7 = (bf16[8,7296]{1,0:T(8,128)(2,1)}, bf16[8,7296]{1,0:T(8,128)(2,1)S(1)}, u32[]{:S(2)}, u32[]{:S(2)}) collective-permute-start(bf16[8,7296]{1,0:T(8,128)(2,1)} %collective-permute-done.5.refs_0_), channel_id=1, source_target_pairs={{0,1},{1,0},{2,3},{3,2},{4,5},{5,4},{6,7},{7,6},{8,9},{9,8},{10,11... | collective-permute-start | bytes 350216 | tf_op jit(solution)/shard_map/ppermute | solution.py:36
  30.0 1.9 %collective-permute-start.13 = (bf16[32,7168]{1,0:T(8,128)(2,1)S(1)}, bf16[32,7168]{1,0:T(8,128)(2,1)S(1)}, u32[]{:S(2)}, u32[]{:S(2)}) collective-permute-start(bf16[32,7168]{1,0:T(8,128)(2,1)S(1)} %get-tuple-element.45), channel_id=1, source_target_pairs={{0,1},{1,0},{2,3},{3,2},{4,5},{5,4},{6,7},{7,6},{8,9},{9,8},{10,11... | collective-permute-start | bytes 1376264 | tf_op jit(solution)/shard_map/ppermute | solution.py:36
  30.4 6.0 %collective-permute-start.19 = (bf16[8,7296]{1,0:T(8,128)(2,1)S(1)}, bf16[8,7296]{1,0:T(8,128)(2,1)S(1)}, u32[]{:S(2)}, u32[]{:S(2)}) collective-permute-start(bf16[8,7296]{1,0:T(8,128)(2,1)S(1)} %collective-permute-done.4.refs_1_), channel_id=1, source_target_pairs={{0,2},{1,3},{2,0},{3,1},{4,6},{5,7},{6,4},{7,5},{8,10},{9,11},{10,... | collective-permute-start | bytes 350216 | tf_op jit(solution)/shard_map/ppermute | solution.py:36
  32.0 8.6 %collective-permute-start.15 = (bf16[16,7168]{1,0:T(8,128)(2,1)S(1)}, bf16[16,7168]{1,0:T(8,128)(2,1)S(1)}, u32[]{:S(2)}, u32[]{:S(2)}) collective-permute-start(bf16[16,7168]{1,0:T(8,128)(2,1)S(1)} %add_convert_fusion), channel_id=1, source_target_pairs={{0,2},{1,3},{2,0},{3,1},{4,6},{5,7},{6,4},{7,5},{8,10},{9,11},{10,... | collective-permute-start | bytes 688136 | tf_op jit(solution)/shard_map/ppermute | solution.py:36
  32.5 9.2 %collective-permute-start.14 = (bf16[16,7168]{1,0:T(8,128)(2,1)S(1)}, bf16[16,7168]{1,0:T(8,128)(2,1)S(1)}, u32[]{:S(2)}, u32[]{:S(2)}) collective-permute-start(bf16[16,7168]{1,0:T(8,128)(2,1)S(1)} %get-tuple-element.47), channel_id=1, source_target_pairs={{0,1},{1,0},{2,3},{3,2},{4,5},{5,4},{6,7},{7,6},{8,9},{9,8},{10,11... | collective-permute-start | bytes 688136 | tf_op jit(solution)/shard_map/ppermute | solution.py:36
  32.5 4.4 %collective-permute-start.21 = (bf16[8,7296]{1,0:T(8,128)(2,1)S(1)}, bf16[8,7296]{1,0:T(8,128)(2,1)S(1)}, u32[]{:S(2)}, u32[]{:S(2)}) collective-permute-start(bf16[8,7296]{1,0:T(8,128)(2,1)S(1)} %collective-permute-done.4.refs_1_), channel_id=1, source_target_pairs={{0,1},{1,0},{2,3},{3,2},{4,5},{5,4},{6,7},{7,6},{8,9},{9,8},{10,11... | collective-permute-start | bytes 350216 | tf_op jit(solution)/shard_map/ppermute | solution.py:36
  36.4 16.0 %collective-permute-start.25 = (bf16[128,512]{1,0:T(8,128)(2,1)S(1)}, bf16[128,512]{1,0:T(8,128)(2,1)S(1)}, u32[]{:S(2)}, u32[]{:S(2)}) collective-permute-start(bf16[128,512]{1,0:T(8,128)(2,1)S(1)} %copy-done.7), channel_id=1, source_target_pairs={{0,1},{1,2},{2,3},{3,4},{4,5},{5,6},{6,7},{7,8},{8,9},{9,10},{10,1... | collective-permute-start | bytes 393224 | tf_op jit(solution)/shard_map/ppermute | solution.py:27
  41.6 1.6 %collective-permute-start.22 = (bf16[16,7168]{1,0:T(8,128)(2,1)S(1)}, bf16[16,7168]{1,0:T(8,128)(2,1)S(1)}, u32[]{:S(2)}, u32[]{:S(2)}) collective-permute-start(bf16[16,7168]{1,0:T(8,128)(2,1)S(1)} %get-tuple-element.59), channel_id=1, source_target_pairs={{0,1},{1,0},{2,3},{3,2},{4,5},{5,4},{6,7},{7,6},{8,9},{9,8},{10,11... | collective-permute-start | bytes 688136 | tf_op jit(solution)/shard_map/ppermute | solution.py:36
  41.7 12.1 %collective-permute-start.16 = (bf16[8,7168]{1,0:T(8,128)(2,1)S(1)}, bf16[8,7168]{1,0:T(8,128)(2,1)S(1)}, u32[]{:S(2)}, u32[]{:S(2)}) collective-permute-start(bf16[8,7168]{1,0:T(8,128)(2,1)S(1)} %add_convert_fusion.6), channel_id=1, source_target_pairs={{0,2},{1,3},{2,0},{3,1},{4,6},{5,7},{6,4},{7,5},{8,10},{9,11},{10,... | collective-permute-start | bytes 344072 | tf_op jit(solution)/shard_map/ppermute | solution.py:36
  43.2 6.6 %collective-permute-start.23 = (bf16[8,7168]{1,0:T(8,128)(2,1)S(1)}, bf16[8,7168]{1,0:T(8,128)(2,1)S(1)}, u32[]{:S(2)}, u32[]{:S(2)}) collective-permute-start(bf16[8,7168]{1,0:T(8,128)(2,1)S(1)} %add_convert_fusion.3), channel_id=1, source_target_pairs={{0,2},{1,3},{2,0},{3,1},{4,6},{5,7},{6,4},{7,5},{8,10},{9,11},{10,... | collective-permute-start | bytes 344072 | tf_op jit(solution)/shard_map/ppermute | solution.py:36
  44.2 9.7 %collective-permute-start.17 = (bf16[8,7168]{1,0:T(8,128)(2,1)S(1)}, bf16[8,7168]{1,0:T(8,128)(2,1)S(1)}, u32[]{:S(2)}, u32[]{:S(2)}) collective-permute-start(bf16[8,7168]{1,0:T(8,128)(2,1)S(1)} %get-tuple-element.64), channel_id=1, source_target_pairs={{0,12},{1,13},{2,14},{3,15},{4,0},{5,1},{6,2},{7,3},{8,4},{9,5},{1... | collective-permute-start | bytes 344072 | tf_op jit(solution)/shard_map/ppermute | solution.py:27
  47.7 6.9 %collective-permute-start.18 = (bf16[8,7168]{1,0:T(8,128)(2,1)S(1)}, bf16[8,7168]{1,0:T(8,128)(2,1)S(1)}, u32[]{:S(2)}, u32[]{:S(2)}) collective-permute-start(bf16[8,7168]{1,0:T(8,128)(2,1)S(1)} %get-tuple-element.65), channel_id=1, source_target_pairs={{0,4},{1,5},{2,6},{3,7},{4,8},{5,9},{6,10},{7,11},{8,12},{9,13},{1... | collective-permute-start | bytes 344072 | tf_op jit(solution)/shard_map/ppermute | solution.py:27
  49.9 9.3 %collective-permute-start.24 = (bf16[8,7168]{1,0:T(8,128)(2,1)S(1)}, bf16[8,7168]{1,0:T(8,128)(2,1)S(1)}, u32[]{:S(2)}, u32[]{:S(2)}) collective-permute-start(bf16[8,7168]{1,0:T(8,128)(2,1)S(1)} %add_convert_fusion.2), channel_id=1, source_target_pairs={{0,8},{1,9},{2,10},{3,11},{4,12},{5,13},{6,14},{7,15},{8,0},{9,1},... | collective-permute-start | bytes 344072 | tf_op jit(solution)/shard_map/ppermute | solution.py:27
  (10 other events, 99.8 us)

commit v7 on v6

--- a/solution.py
+++ b/solution.py
@@ -294,50 +294,43 @@
     )
     late, crossing, away = lax.optimization_barrier((late, crossing, away))
     across.update(crossing)
+    across.update({r: swapped(late[r], axis, 2) for r in late})
     columns[0] = rows
-    returned = shifted(away, axis, 1)
-    late_across = {r: swapped(late[r], axis, 2) for r in late}
+    columns.update(late)
+
+    batches = [sorted(late)] * bool(late) + [sorted(crossing), [0]]
+    near, sizes = [], []
+    for batch in batches:
+        near += [across[r] for r in batch] + [columns[r] for r in batch]
+        sizes += [len(batch)] + [1] * len(batch)
+    others = [swapped(block, axis, 1) for block in near]
+    sizes += [2 * len(batch) for batch in batches]
+    outs = expert(place, w_gate, w_up, w_down, near + others, groups, sizes)
+    sends = list(outs[len(outs) - len(batches) :])
+    sends[0] = swapped(sends[0], axis, 1)
 
     sums = {}
-    latest = []
-
-    def sent(outs, batches):
-        for i, batch in enumerate(batches):
-            mine, outs = outs[: 1 + len(batch)], outs[1 + len(batch) :]
-            send = outs[sum(1 + len(b) for b in batches[i + 1 :]) + i]
-            if latest:
-                _, send = lax.optimization_barrier((latest[0], send))
-            chip = swapped(send, axis, 1)
-            split = len(batch) * tokens
-            leaves = added(mine[0], chip[:split])
-            if batch == [0]:
-                _, leaves = lax.optimization_barrier((latest[1], leaves))
-            crossed = swapped(leaves, axis, 2)
-            if not latest:
-                latest.extend([leaves, crossed])
-            for k, r in enumerate(batch):
-                at = slice(k * tokens, (k + 1) * tokens)
-                sums[r] = [mine[1 + k], chip[split:][at], crossed[at]]
-
-    def through_experts(batches, columns, across):
-        near, sizes = [], []
-        for batch in batches:
-            near += [across[r] for r in batch] + [columns[r] for r in batch]
-            sizes += [len(batch)] + [1] * len(batch)
-        blocks = near + [swapped(block, axis, 1) for block in near]
-        if latest:
-            _, blocks = lax.optimization_barrier((latest[1], blocks))
-        sizes += [2 * len(batch) for batch in batches]
-        sent(expert(place, w_gate, w_up, w_down, blocks, groups, sizes), batches)
-
-    through_experts([sorted(crossing), [0]], columns, across)
-    if late:
-        through_experts([sorted(late)], late, late_across)
+    for i, batch in enumerate(batches):
+        mine, outs = outs[: 1 + len(batch)], outs[1 + len(batch) :]
+        split = len(batch) * tokens
+        chip = sends[i]
+        if i:
+            _, chip = lax.optimization_barrier((leaves, chip))
+            chip = swapped(chip, axis, 1)
+        leaves = added(mine[0], chip[:split])
+        crossed = swapped(leaves, axis, 2)
+        if batch == batches[-2]:
+            crossed, away = lax.optimization_barrier((crossed, away))
+        for k, r in enumerate(batch):
+            at = slice(k * tokens, (k + 1) * tokens)
+            sums[r] = [mine[1 + k], chip[split:][at], crossed[at]]
     terms = sums.pop(0)
     for r in sums:
         terms = terms + [rotated(added(*sums[r]), axis, -r)]
+    returned = shifted(away, axis, 1)
+    attn_out = settle(place, moved_slot, first, second, returned)
+    _, terms = lax.optimization_barrier((attn_out, terms))
     moe_out = added(*terms)
-    attn_out = settle(place, moved_slot, first, second, returned)
     return (moe_out, attn_out)
 
 

time: 60.2 us -> 62.9 us (1.045)
  waiting for transfers between devices: 19.7 us -> 24.2 us
  starting transfers between devices: 22.7 us -> 21.5 us
    ppermute x18, waiting for transfers between devices: 12.1 us -> 17.5 us  [swapped(): return lax.ppermute(value, axis, pairs)]
    ppermute x8, starting transfers between devices: 15.7 us -> 14.2 us  [shifted(): return lax.ppermute(value, axis, pairs)]
    ppermute x8, waiting for transfers between devices: 7.56 us -> 6.69 us  [shifted(): return lax.ppermute(value, axis, pairs)]
    pallas_call x2 -> x1, Pallas kernels: 3.38 us -> 2.76 us  [expert(): pl.pallas_call(functools.partial(expert_body, count, groups, sizes), out_...]
  transfers between devices with their start and end apart: 26 -> 26, of which waited for: 12 -> 10; matrix products, arithmetic and copies ran while one was open for 0% -> 0% of each run, Pallas kernels for 19% -> 17%
where the time goes in v7:
time: 62.9 us; the launch traced here: 62.6 us
  waiting for transfers between devices  24.2 us (38%)
  starting transfers between devices  21.5 us (34%)
  Pallas kernels  15.1 us (24%)
  other arithmetic  1.01 us (2%)
  between operations  0.83 us (1%)
    ppermute x18, waiting for transfers between devices, swapped(): return lax.ppermute(value, axis, pairs)  17.5 us
    ppermute x8, starting transfers between devices, shifted(): return lax.ppermute(value, axis, pairs)  14.2 us
    pallas_call x2, Pallas kernels, attend(): pl.pallas_call(functools.partial(attend_body, ranks, visits), out_shape=[...  9.02 us
    ppermute x18, starting transfers between devices, swapped(): return lax.ppermute(value, axis, pairs)  7.32 us
    ppermute x8, waiting for transfers between devices, shifted(): return lax.ppermute(value, axis, pairs)  6.69 us
    pallas_call x1, Pallas kernels, expert(): pl.pallas_call(functools.partial(expert_body, count, groups, sizes), out_...  2.76 us
    pallas_call x1, Pallas kernels, prepare(): pl.pallas_call(functools.partial(prepare_body, groups), out_shape=[jax.Sh...  1.91 us
    pallas_call x1, Pallas kernels, settle(): pl.pallas_call(settle_body, out_shape=jax.ShapeDtypeStruct((count,) + ret...  1.39 us
  transfers between devices with their start and end apart: 26, of which 10 were waited for; matrix products, arithmetic and copies ran while one was open for 0% of the time, Pallas kernels for 17%

profile of v7, /device:TPU:0, one launch (start us, length us, event | category | flops | bytes accessed | tf_op | source)
XLA Modules:
  0.0 62.6 jit_solution(14737258432269765851)
XLA Ops:
  0.6 1.9 %shard_map.122 = (bf16[8,7296]{1,0:T(8,128)(2,1)}, bf16[592,128]{1,0:T(8,128)(2,1)}) custom-call(s32[1]{0:T(128)} %bitcast.place, s32[16]{0:T(128)} %moved.7, bf16[8,7168]{1,0:T(8,128)(2,1)} %hidden.1, s32[2,8]{1,0:T(2,128)} %bitcast.10, f32[2,8]{1,0:T(2,128)} %bitcast.11, bf16[4,576,128]{2,1,0:T(8,128)(2,1)} %bitcast.7, bf16[4,576]{1,0:T(4,128)(2,1)} %own.4), custom_call_target="tpu_custom_call" | custom-call | tf_op jit(solution)/shard_map/pallas_call | solution.py:75
  2.5 5.4 %collective-permute-start.3 = (bf16[592,128]{1,0:T(8,128)(2,1)}, bf16[592,128]{1,0:T(8,128)(2,1)}, u32[]{:S(2)}, u32[]{:S(2)}) collective-permute-start(bf16[592,128]{1,0:T(8,128)(2,1)} %get-tuple-element.37), channel_id=1, source_target_pairs={{0,15},{1,0},{2,1},{3,2},{4,3},{5,4},{6,5},{7,6},{8,7},{9,8},{10,9... | collective-permute-start | bytes 454664 | tf_op jit(solution)/shard_map/ppermute | solution.py:27
  8.0 1.1 %collective-permute-start.1 = (bf16[8,7296]{1,0:T(8,128)(2,1)}, bf16[8,7296]{1,0:T(8,128)(2,1)S(1)}, u32[]{:S(2)}, u32[]{:S(2)}) collective-permute-start(bf16[8,7296]{1,0:T(8,128)(2,1)} %get-tuple-element.36.refs_7_), channel_id=1, source_target_pairs={{0,12},{1,13},{2,14},{3,15},{4,0},{5,1},{6,2},{7,3},{8,4},{9,5},{1... | collective-permute-start | bytes 350216 | tf_op jit(solution)/shard_map/ppermute | solution.py:27
  9.1 0.9 %collective-permute-start = (bf16[8,7296]{1,0:T(8,128)(2,1)}, bf16[8,7296]{1,0:T(8,128)(2,1)S(1)}, u32[]{:S(2)}, u32[]{:S(2)}) collective-permute-start(bf16[8,7296]{1,0:T(8,128)(2,1)} %get-tuple-element.36.refs_7_), channel_id=1, source_target_pairs={{0,4},{1,5},{2,6},{3,7},{4,8},{5,9},{6,10},{7,11},{8,12},{9,13},{1... | collective-permute-start | bytes 350216 | tf_op jit(solution)/shard_map/ppermute | solution.py:27
  10.0 4.5 %shard_map.123.first = bf16[2,128,512]{2,1,0:T(8,128)(2,1)} custom-call(s32[1]{0:T(128)} %bitcast.place, s32[16]{0:T(128)} %moved.7, s32[64]{0:T(128)} %lengths.3, bf16[4,576,128]{2,1,0:T(8,128)(2,1)} %bitcast.8, bf16[4,576]{1,0:T(4,128)(2,1)} %own.4, bf16[4,576,1024]{2,1,0:T(8,128)(2,1)} %bitcast.5), custom_call_target="tpu_custom_call" | custom-call | flops 570425344 | tf_op jit(solution)/shard_map/pallas_call | solution.py:153
  14.8 2.0 %collective-permute-done.refs_4_ = bf16[8,7296]{1,0:T(8,128)(2,1)S(1)} collective-permute-done((bf16[8,7296]{1,0:T(8,128)(2,1)}, bf16[8,7296]{1,0:T(8,128)(2,1)S(1)}, u32[]{:S(2)}, u32[]{:S(2)}) %collective-permute-start) | collective-permute-done | bytes 116768 | tf_op jit(solution)/shard_map/ppermute | solution.py:27
  16.8 0.7 %collective-permute-start.6 = (bf16[8,7296]{1,0:T(8,128)(2,1)S(1)}, bf16[8,7296]{1,0:T(8,128)(2,1)S(1)}, u32[]{:S(2)}, u32[]{:S(2)}) collective-permute-start(bf16[8,7296]{1,0:T(8,128)(2,1)S(1)} %collective-permute-done.1.refs_5_), channel_id=1, source_target_pairs={{0,2},{1,3},{2,0},{3,1},{4,6},{5,7},{6,4},{7,5},{8,10},{9,11},{10,... | collective-permute-start | bytes 350216 | tf_op jit(solution)/shard_map/ppermute | solution.py:36
  17.6 1.3 %collective-permute-start.5 = (bf16[8,7296]{1,0:T(8,128)(2,1)S(1)}, bf16[8,7296]{1,0:T(8,128)(2,1)S(1)}, u32[]{:S(2)}, u32[]{:S(2)}) collective-permute-start(bf16[8,7296]{1,0:T(8,128)(2,1)S(1)} %collective-permute-done.refs_4_), channel_id=1, source_target_pairs={{0,2},{1,3},{2,0},{3,1},{4,6},{5,7},{6,4},{7,5},{8,10},{9,11},{10,... | collective-permute-start | bytes 350216 | tf_op jit(solution)/shard_map/ppermute | solution.py:36
  18.8 1.6 %collective-permute-start.4 = (bf16[8,7296]{1,0:T(8,128)(2,1)S(1)}, bf16[8,7296]{1,0:T(8,128)(2,1)}, u32[]{:S(2)}, u32[]{:S(2)}) collective-permute-start(bf16[8,7296]{1,0:T(8,128)(2,1)S(1)} %collective-permute-done.refs_4_), channel_id=1, source_target_pairs={{0,4},{1,5},{2,6},{3,7},{4,8},{5,9},{6,10},{7,11},{8,12},{9,13},{1... | collective-permute-start | bytes 350216 | tf_op jit(solution)/shard_map/ppermute | solution.py:27
  21.0 4.5 %shard_map.124 = (bf16[1,128,512]{2,1,0:T(8,128)(2,1)}, bf16[128,512]{1,0:T(8,128)(2,1)}) custom-call(s32[1]{0:T(128)} %bitcast.place, s32[16]{0:T(128)} %moved.7, s32[64]{0:T(128)} %lengths.3, bf16[4,576,128]{2,1,0:T(8,128)(2,1)} %bitcast.9, bf16[4,576]{1,0:T(4,128)(2,1)} %own.4, bf16[4,576,1024]{2,1,0:T(8,128)(2,1)} %bitcast.6, ...), custom_call_target="tpu_custom_call" | custom-call | flops 570425344 | tf_op jit(solution)/shard_map/pallas_call | solution.py:153
  27.4 4.0 %collective-permute-done.7.refs_0_ = bf16[8,7296]{1,0:T(8,128)(2,1)S(1)} collective-permute-done((bf16[8,7296]{1,0:T(8,128)(2,1)}, bf16[8,7296]{1,0:T(8,128)(2,1)S(1)}, u32[]{:S(2)}, u32[]{:S(2)}) %collective-permute-start.7) | collective-permute-done | bytes 116768 | tf_op jit(solution)/shard_map/ppermute | solution.py:36
  31.4 1.3 %collective-permute-done.8.refs_8_ = bf16[8,7296]{1,0:T(8,128)(2,1)S(1)} collective-permute-done((bf16[8,7296]{1,0:T(8,128)(2,1)S(1)}, bf16[8,7296]{1,0:T(8,128)(2,1)S(1)}, u32[]{:S(2)}, u32[]{:S(2)}) %collective-permute-start.8) | collective-permute-done | bytes 116768 | tf_op jit(solution)/shard_map/ppermute | solution.py:36
  32.7 2.8 %shard_map.125 = (bf16[8,7168]{1,0:T(8,128)(2,1)S(1)}, bf16[8,7168]{1,0:T(8,128)(2,1)S(1)}, bf16[16,7168]{1,0:T(8,128)(2,1)S(1)}, bf16[8,7168]{1,0:T(8,128)(2,1)...) custom-call(s32[1]{0:T(128)} %bitcast.place, ...), custom_call_target="tpu_custom_call" | custom-call | flops 704643072 | bytes 5505024 | tf_op jit(solution)/shard_map/pallas_call | solution.py:230
  35.7 1.4 %collective-permute-done.16 = bf16[16,7168]{1,0:T(8,128)(2,1)S(1)} collective-permute-done((bf16[16,7168]{1,0:T(8,128)(2,1)S(1)}, bf16[16,7168]{1,0:T(8,128)(2,1)S(1)}, u32[]{:S(2)}, u32[]{:S(2)}) %collective-permute-start.16) | collective-permute-done | bytes 229408 | tf_op jit(solution)/shard_map/ppermute | solution.py:36
  37.6 1.4 %collective-permute-done.17 = bf16[32,7168]{1,0:T(8,128)(2,1)S(1)} collective-permute-done((bf16[32,7168]{1,0:T(8,128)(2,1)S(1)}, bf16[32,7168]{1,0:T(8,128)(2,1)S(1)}, u32[]{:S(2)}, u32[]{:S(2)}) %collective-permute-start.17) | collective-permute-done | bytes 458784 | tf_op jit(solution)/shard_map/ppermute | solution.py:36
  39.3 3.5 %collective-permute-done.22 = bf16[8,7168]{1,0:T(8,128)(2,1)S(1)} collective-permute-done((bf16[8,7168]{1,0:T(8,128)(2,1)S(1)}, bf16[8,7168]{1,0:T(8,128)(2,1)S(1)}, u32[]{:S(2)}, u32[]{:S(2)}) %collective-permute-start.22) | collective-permute-done | bytes 114720 | tf_op jit(solution)/shard_map/ppermute | solution.py:36
  42.8 1.2 %collective-permute-start.23 = (bf16[8,7168]{1,0:T(8,128)(2,1)S(1)}, bf16[8,7168]{1,0:T(8,128)(2,1)S(1)}, u32[]{:S(2)}, u32[]{:S(2)}) collective-permute-start(bf16[8,7168]{1,0:T(8,128)(2,1)S(1)} %add_convert_fusion.4), channel_id=1, source_target_pairs={{0,8},{1,9},{2,10},{3,11},{4,12},{5,13},{6,14},{7,15},{8,0},{9,1},... | collective-permute-start | bytes 344072 | tf_op jit(solution)/shard_map/ppermute | solution.py:27
  44.3 1.8 %collective-permute-start.21 = (bf16[8,7168]{1,0:T(8,128)(2,1)S(1)}, bf16[8,7168]{1,0:T(8,128)(2,1)S(1)}, u32[]{:S(2)}, u32[]{:S(2)}) collective-permute-start(bf16[8,7168]{1,0:T(8,128)(2,1)S(1)} %add_convert_fusion.5), channel_id=1, source_target_pairs={{0,2},{1,3},{2,0},{3,1},{4,6},{5,7},{6,4},{7,5},{8,10},{9,11},{10,... | collective-permute-start | bytes 344072 | tf_op jit(solution)/shard_map/ppermute | solution.py:36
  46.1 5.9 %collective-permute-done.18 = bf16[16,7168]{1,0:T(8,128)(2,1)S(1)} collective-permute-done((bf16[16,7168]{1,0:T(8,128)(2,1)S(1)}, bf16[16,7168]{1,0:T(8,128)(2,1)S(1)}, u32[]{:S(2)}, u32[]{:S(2)}) %collective-permute-start.18) | collective-permute-done | bytes 229408 | tf_op jit(solution)/shard_map/ppermute | solution.py:36
  52.1 1.7 %collective-permute-start.25 = (bf16[8,7168]{1,0:T(8,128)(2,1)S(1)}, bf16[8,7168]{1,0:T(8,128)(2,1)S(1)}, u32[]{:S(2)}, u32[]{:S(2)}) collective-permute-start(bf16[8,7168]{1,0:T(8,128)(2,1)S(1)} %get-tuple-element.70), channel_id=1, source_target_pairs={{0,4},{1,5},{2,6},{3,7},{4,8},{5,9},{6,10},{7,11},{8,12},{9,13},{1... | collective-permute-start | bytes 344072 | tf_op jit(solution)/shard_map/ppermute | solution.py:27
  53.8 2.2 %collective-permute-start.24 = (bf16[8,7168]{1,0:T(8,128)(2,1)S(1)}, bf16[8,7168]{1,0:T(8,128)(2,1)S(1)}, u32[]{:S(2)}, u32[]{:S(2)}) collective-permute-start(bf16[8,7168]{1,0:T(8,128)(2,1)S(1)} %get-tuple-element.71), channel_id=1, source_target_pairs={{0,12},{1,13},{2,14},{3,15},{4,0},{5,1},{6,2},{7,3},{8,4},{9,5},{1... | collective-permute-start | bytes 344072 | tf_op jit(solution)/shard_map/ppermute | solution.py:27
  56.0 4.5 %collective-permute-done.19.returned = bf16[128,512]{1,0:T(8,128)(2,1)S(1)} collective-permute-done((bf16[128,512]{1,0:T(8,128)(2,1)S(1)}, bf16[128,512]{1,0:T(8,128)(2,1)S(1)}, u32[]{:S(2)}, u32[]{:S(2)}) %collective-permute-start.19) | collective-permute-done | bytes 131104 | tf_op jit(solution)/shard_map/ppermute | solution.py:27
  60.5 1.4 %shard_map.126 = bf16[4,128,512]{2,1,0:T(8,128)(2,1)} custom-call(s32[1]{0:T(128)} %bitcast.place, s32[16]{0:T(128)S(1)} %copy-done.6, bf16[2,128,512]{2,1,0:T(8,128)(2,1)S(1)} %copy-done.3, bf16[1,128,512]{2,1,0:T(8,128)(2,1)S(1)} %copy-done.4, bf16[128,512]{1,0:T(8,128)(2,1)S(1)} %collective-permute-done.19.returned), custom_call_target="tpu_custom_call" | custom-call | tf_op jit(solution)/shard_map/pallas_call | solution.py:184
  61.9 0.7 %add_convert_fusion.1 = bf16[8,7168]{1,0:T(8,128)(2,1)} fusion(bf16[8,7168]{1,0:T(8,128)(2,1)S(1)} %collective-permute-done.25, bf16[8,7168]{1,0:T(8,128)(2,1)S(1)} %collective-permute-done.24, bf16[8,7168]{1,0:T(8,128)(2,1)S(1)} %collective-permute-done.23, bf16[8,7168]{1,0:T(8,128)(2,1)S(1)} %collective-permute-done.21, bf16[8,7168]{1,0:T(8,128)(2,1)S(1)} %slice.42, ...), kind=kLoop, calls=%fused_computation.1 | loop fusion | flops 688128 | bytes 802816 | tf_op jit(solution)/shard_map/convert_element_type | solution.py:247
  (56 shorter events, 4.1 us)
Async XLA Ops:
  2.5 14.3 %collective-permute-start.3 = (bf16[592,128]{1,0:T(8,128)(2,1)}, bf16[592,128]{1,0:T(8,128)(2,1)}, u32[]{:S(2)}, u32[]{:S(2)}) collective-permute-start(bf16[592,128]{1,0:T(8,128)(2,1)} %get-tuple-element.37), channel_id=1, source_target_pairs={{0,15},{1,0},{2,1},{3,2},{4,3},{5,4},{6,5},{7,6},{8,7},{9,8},{10,9... | collective-permute-start | bytes 454664 | tf_op jit(solution)/shard_map/ppermute | solution.py:27
  8.0 6.6 %collective-permute-start.2 = (bf16[8,7296]{1,0:T(8,128)(2,1)}, bf16[8,7296]{1,0:T(8,128)(2,1)S(1)}, u32[]{:S(2)}, u32[]{:S(2)}) collective-permute-start(bf16[8,7296]{1,0:T(8,128)(2,1)} %get-tuple-element.36.refs_7_), channel_id=1, source_target_pairs={{0,2},{1,3},{2,0},{3,1},{4,6},{5,7},{6,4},{7,5},{8,10},{9,11},{10,... | collective-permute-start | bytes 350216 | tf_op jit(solution)/shard_map/ppermute | solution.py:36
  8.0 6.8 %collective-permute-start.1 = (bf16[8,7296]{1,0:T(8,128)(2,1)}, bf16[8,7296]{1,0:T(8,128)(2,1)S(1)}, u32[]{:S(2)}, u32[]{:S(2)}) collective-permute-start(bf16[8,7296]{1,0:T(8,128)(2,1)} %get-tuple-element.36.refs_7_), channel_id=1, source_target_pairs={{0,12},{1,13},{2,14},{3,15},{4,0},{5,1},{6,2},{7,3},{8,4},{9,5},{1... | collective-permute-start | bytes 350216 | tf_op jit(solution)/shard_map/ppermute | solution.py:27
  9.1 7.7 %collective-permute-start = (bf16[8,7296]{1,0:T(8,128)(2,1)}, bf16[8,7296]{1,0:T(8,128)(2,1)S(1)}, u32[]{:S(2)}, u32[]{:S(2)}) collective-permute-start(bf16[8,7296]{1,0:T(8,128)(2,1)} %get-tuple-element.36.refs_7_), channel_id=1, source_target_pairs={{0,4},{1,5},{2,6},{3,7},{4,8},{5,9},{6,10},{7,11},{8,12},{9,13},{1... | collective-permute-start | bytes 350216 | tf_op jit(solution)/shard_map/ppermute | solution.py:27
  16.8 8.7 %collective-permute-start.6 = (bf16[8,7296]{1,0:T(8,128)(2,1)S(1)}, bf16[8,7296]{1,0:T(8,128)(2,1)S(1)}, u32[]{:S(2)}, u32[]{:S(2)}) collective-permute-start(bf16[8,7296]{1,0:T(8,128)(2,1)S(1)} %collective-permute-done.1.refs_5_), channel_id=1, source_target_pairs={{0,2},{1,3},{2,0},{3,1},{4,6},{5,7},{6,4},{7,5},{8,10},{9,11},{10,... | collective-permute-start | bytes 350216 | tf_op jit(solution)/shard_map/ppermute | solution.py:36
  17.6 8.0 %collective-permute-start.5 = (bf16[8,7296]{1,0:T(8,128)(2,1)S(1)}, bf16[8,7296]{1,0:T(8,128)(2,1)S(1)}, u32[]{:S(2)}, u32[]{:S(2)}) collective-permute-start(bf16[8,7296]{1,0:T(8,128)(2,1)S(1)} %collective-permute-done.refs_4_), channel_id=1, source_target_pairs={{0,2},{1,3},{2,0},{3,1},{4,6},{5,7},{6,4},{7,5},{8,10},{9,11},{10,... | collective-permute-start | bytes 350216 | tf_op jit(solution)/shard_map/ppermute | solution.py:36
  18.8 6.7 %collective-permute-start.4 = (bf16[8,7296]{1,0:T(8,128)(2,1)S(1)}, bf16[8,7296]{1,0:T(8,128)(2,1)}, u32[]{:S(2)}, u32[]{:S(2)}) collective-permute-start(bf16[8,7296]{1,0:T(8,128)(2,1)S(1)} %collective-permute-done.refs_4_), channel_id=1, source_target_pairs={{0,4},{1,5},{2,6},{3,7},{4,8},{5,9},{6,10},{7,11},{8,12},{9,13},{1... | collective-permute-start | bytes 350216 | tf_op jit(solution)/shard_map/ppermute | solution.py:27
  20.5 5.8 %collective-permute-start.15 = (bf16[8,7296]{1,0:T(8,128)(2,1)S(1)}, bf16[8,7296]{1,0:T(8,128)(2,1)}, u32[]{:S(2)}, u32[]{:S(2)}) collective-permute-start(bf16[8,7296]{1,0:T(8,128)(2,1)S(1)} %copy-done.5), channel_id=1, source_target_pairs={{0,1},{1,0},{2,3},{3,2},{4,5},{5,4},{6,7},{7,6},{8,9},{9,8},{10,11... | collective-permute-start | bytes 350216 | tf_op jit(solution)/shard_map/ppermute | solution.py:36
  20.5 6.6 %collective-permute-start.13 = (bf16[8,7296]{1,0:T(8,128)(2,1)S(1)}, bf16[8,7296]{1,0:T(8,128)(2,1)}, u32[]{:S(2)}, u32[]{:S(2)}) collective-permute-start(bf16[8,7296]{1,0:T(8,128)(2,1)S(1)} %collective-permute-done.1.refs_5_), channel_id=1, source_target_pairs={{0,1},{1,0},{2,3},{3,2},{4,5},{5,4},{6,7},{7,6},{8,9},{9,8},{10,11... | collective-permute-start | bytes 350216 | tf_op jit(solution)/shard_map/ppermute | solution.py:36
  25.6 5.8 %collective-permute-start.7 = (bf16[8,7296]{1,0:T(8,128)(2,1)}, bf16[8,7296]{1,0:T(8,128)(2,1)S(1)}, u32[]{:S(2)}, u32[]{:S(2)}) collective-permute-start(bf16[8,7296]{1,0:T(8,128)(2,1)} %collective-permute-done.4.refs_1_), channel_id=1, source_target_pairs={{0,2},{1,3},{2,0},{3,1},{4,6},{5,7},{6,4},{7,5},{8,10},{9,11},{10,... | collective-permute-start | bytes 350216 | tf_op jit(solution)/shard_map/ppermute | solution.py:36
  26.3 5.1 %collective-permute-start.12 = (bf16[8,7296]{1,0:T(8,128)(2,1)S(1)}, bf16[8,7296]{1,0:T(8,128)(2,1)S(1)}, u32[]{:S(2)}, u32[]{:S(2)}) collective-permute-start(bf16[8,7296]{1,0:T(8,128)(2,1)S(1)} %collective-permute-done.refs_4_), channel_id=1, source_target_pairs={{0,1},{1,0},{2,3},{3,2},{4,5},{5,4},{6,7},{7,6},{8,9},{9,8},{10,11... | collective-permute-start | bytes 350216 | tf_op jit(solution)/shard_map/ppermute | solution.py:36
  26.3 5.1 %collective-permute-start.9 = (bf16[8,7296]{1,0:T(8,128)(2,1)}, bf16[8,7296]{1,0:T(8,128)(2,1)S(1)}, u32[]{:S(2)}, u32[]{:S(2)}) collective-permute-start(bf16[8,7296]{1,0:T(8,128)(2,1)} %collective-permute-done.4.refs_1_), channel_id=1, source_target_pairs={{0,1},{1,0},{2,3},{3,2},{4,5},{5,4},{6,7},{7,6},{8,9},{9,8},{10,11... | collective-permute-start | bytes 350216 | tf_op jit(solution)/shard_map/ppermute | solution.py:36
  26.9 4.5 %collective-permute-start.10 = (bf16[8,7296]{1,0:T(8,128)(2,1)S(1)}, bf16[8,7296]{1,0:T(8,128)(2,1)S(1)}, u32[]{:S(2)}, u32[]{:S(2)}) collective-permute-start(bf16[8,7296]{1,0:T(8,128)(2,1)S(1)} %collective-permute-done.5.refs_2_), channel_id=1, source_target_pairs={{0,1},{1,0},{2,3},{3,2},{4,5},{5,4},{6,7},{7,6},{8,9},{9,8},{10,11... | collective-permute-start | bytes 350216 | tf_op jit(solution)/shard_map/ppermute | solution.py:36
  27.0 4.4 %collective-permute-start.11 = (bf16[8,7296]{1,0:T(8,128)(2,1)S(1)}, bf16[8,7296]{1,0:T(8,128)(2,1)S(1)}, u32[]{:S(2)}, u32[]{:S(2)}) collective-permute-start(bf16[8,7296]{1,0:T(8,128)(2,1)S(1)} %collective-permute-done.6.refs_3_), channel_id=1, source_target_pairs={{0,1},{1,0},{2,3},{3,2},{4,5},{5,4},{6,7},{7,6},{8,9},{9,8},{10,11... | collective-permute-start | bytes 350216 | tf_op jit(solution)/shard_map/ppermute | solution.py:36
  35.5 1.6 %collective-permute-start.16 = (bf16[16,7168]{1,0:T(8,128)(2,1)S(1)}, bf16[16,7168]{1,0:T(8,128)(2,1)S(1)}, u32[]{:S(2)}, u32[]{:S(2)}) collective-permute-start(bf16[16,7168]{1,0:T(8,128)(2,1)S(1)} %get-tuple-element.51), channel_id=1, source_target_pairs={{0,1},{1,0},{2,3},{3,2},{4,5},{5,4},{6,7},{7,6},{8,9},{9,8},{10,11... | collective-permute-start | bytes 688136 | tf_op jit(solution)/shard_map/ppermute | solution.py:36
  37.1 1.9 %collective-permute-start.17 = (bf16[32,7168]{1,0:T(8,128)(2,1)S(1)}, bf16[32,7168]{1,0:T(8,128)(2,1)S(1)}, u32[]{:S(2)}, u32[]{:S(2)}) collective-permute-start(bf16[32,7168]{1,0:T(8,128)(2,1)S(1)} %get-tuple-element.53), channel_id=1, source_target_pairs={{0,1},{1,0},{2,3},{3,2},{4,5},{5,4},{6,7},{7,6},{8,9},{9,8},{10,11... | collective-permute-start | bytes 1376264 | tf_op jit(solution)/shard_map/ppermute | solution.py:36
  37.3 5.4 %collective-permute-start.22 = (bf16[8,7168]{1,0:T(8,128)(2,1)S(1)}, bf16[8,7168]{1,0:T(8,128)(2,1)S(1)}, u32[]{:S(2)}, u32[]{:S(2)}) collective-permute-start(bf16[8,7168]{1,0:T(8,128)(2,1)S(1)} %add_convert_fusion.6), channel_id=1, source_target_pairs={{0,2},{1,3},{2,0},{3,1},{4,6},{5,7},{6,4},{7,5},{8,10},{9,11},{10,... | collective-permute-start | bytes 344072 | tf_op jit(solution)/shard_map/ppermute | solution.py:36
  39.1 5.2 %collective-permute-start.20 = (bf16[16,7168]{1,0:T(8,128)(2,1)S(1)}, bf16[16,7168]{1,0:T(8,128)(2,1)S(1)}, u32[]{:S(2)}, u32[]{:S(2)}) collective-permute-start(bf16[16,7168]{1,0:T(8,128)(2,1)S(1)} %get-tuple-element.58), channel_id=1, source_target_pairs={{0,1},{1,0},{2,3},{3,2},{4,5},{5,4},{6,7},{7,6},{8,9},{9,8},{10,11... | collective-permute-start | bytes 688136 | tf_op jit(solution)/shard_map/ppermute | solution.py:36
  42.8 19.1 %collective-permute-start.23 = (bf16[8,7168]{1,0:T(8,128)(2,1)S(1)}, bf16[8,7168]{1,0:T(8,128)(2,1)S(1)}, u32[]{:S(2)}, u32[]{:S(2)}) collective-permute-start(bf16[8,7168]{1,0:T(8,128)(2,1)S(1)} %add_convert_fusion.4), channel_id=1, source_target_pairs={{0,8},{1,9},{2,10},{3,11},{4,12},{5,13},{6,14},{7,15},{8,0},{9,1},... | collective-permute-start | bytes 344072 | tf_op jit(solution)/shard_map/ppermute | solution.py:27
  44.0 8.0 %collective-permute-start.18 = (bf16[16,7168]{1,0:T(8,128)(2,1)S(1)}, bf16[16,7168]{1,0:T(8,128)(2,1)S(1)}, u32[]{:S(2)}, u32[]{:S(2)}) collective-permute-start(bf16[16,7168]{1,0:T(8,128)(2,1)S(1)} %add_convert_fusion), channel_id=1, source_target_pairs={{0,2},{1,3},{2,0},{3,1},{4,6},{5,7},{6,4},{7,5},{8,10},{9,11},{10,... | collective-permute-start | bytes 688136 | tf_op jit(solution)/shard_map/ppermute | solution.py:36
  44.3 17.6 %collective-permute-start.21 = (bf16[8,7168]{1,0:T(8,128)(2,1)S(1)}, bf16[8,7168]{1,0:T(8,128)(2,1)S(1)}, u32[]{:S(2)}, u32[]{:S(2)}) collective-permute-start(bf16[8,7168]{1,0:T(8,128)(2,1)S(1)} %add_convert_fusion.5), channel_id=1, source_target_pairs={{0,2},{1,3},{2,0},{3,1},{4,6},{5,7},{6,4},{7,5},{8,10},{9,11},{10,... | collective-permute-start | bytes 344072 | tf_op jit(solution)/shard_map/ppermute | solution.py:36
  52.0 8.5 %collective-permute-start.19 = (bf16[128,512]{1,0:T(8,128)(2,1)S(1)}, bf16[128,512]{1,0:T(8,128)(2,1)S(1)}, u32[]{:S(2)}, u32[]{:S(2)}) collective-permute-start(bf16[128,512]{1,0:T(8,128)(2,1)S(1)} %copy-done.7), channel_id=1, source_target_pairs={{0,1},{1,2},{2,3},{3,4},{4,5},{5,6},{6,7},{7,8},{8,9},{9,10},{10,1... | collective-permute-start | bytes 393224 | tf_op jit(solution)/shard_map/ppermute | solution.py:27
  52.1 9.8 %collective-permute-start.25 = (bf16[8,7168]{1,0:T(8,128)(2,1)S(1)}, bf16[8,7168]{1,0:T(8,128)(2,1)S(1)}, u32[]{:S(2)}, u32[]{:S(2)}) collective-permute-start(bf16[8,7168]{1,0:T(8,128)(2,1)S(1)} %get-tuple-element.70), channel_id=1, source_target_pairs={{0,4},{1,5},{2,6},{3,7},{4,8},{5,9},{6,10},{7,11},{8,12},{9,13},{1... | collective-permute-start | bytes 344072 | tf_op jit(solution)/shard_map/ppermute | solution.py:27
  53.8 8.1 %collective-permute-start.24 = (bf16[8,7168]{1,0:T(8,128)(2,1)S(1)}, bf16[8,7168]{1,0:T(8,128)(2,1)S(1)}, u32[]{:S(2)}, u32[]{:S(2)}) collective-permute-start(bf16[8,7168]{1,0:T(8,128)(2,1)S(1)} %get-tuple-element.71), channel_id=1, source_target_pairs={{0,12},{1,13},{2,14},{3,15},{4,0},{5,1},{6,2},{7,3},{8,4},{9,5},{1... | collective-permute-start | bytes 344072 | tf_op jit(solution)/shard_map/ppermute | solution.py:27
  (10 other events, 163.5 us)

commit v8 on v7

--- a/solution.py
+++ b/solution.py
@@ -83,6 +83,12 @@
         compiler_params=pltpu.CompilerParams(vmem_limit_bytes=60 * MIB),
         cost_estimate=pl.CostEstimate(flops=0, bytes_accessed=0, transcendentals=0),
     )(place, moved, hidden, ids_t, gates_t, query_t, own)
+
+
+def crossed(value, axis, steps):
+    count = lax.axis_size(axis)
+    pairs = [(source, ((source + 4 * steps) % count) ^ 2) for source in range(count)]
+    return lax.ppermute(value, axis, pairs)
 
 
 def attend_body(ranks, visits, place, moved, lengths, query, own, cache, *refs):
@@ -276,58 +282,53 @@
     )
 
     visiting = shifted(payload, axis, -1)
-    columns = {r: rotated(rows, axis, r) for r in range(1, turns) if r != 2}
+    far = [2] if turns > 2 else []
+    columns = {r: rotated(rows, axis, r) for r in far}
     across = {0: swapped(rows, axis, 2)}
 
     half = requests // 2
     scalars = (place, moved_slot, cache_lengths)
     new_here, _ = lax.optimization_barrier((new_latent, rows))
     (first,) = attend(tuple(range(half)), *scalars, query_t, new_here, cache_t)
-    columns, across, visiting, first = lax.optimization_barrier((columns, across, visiting, first))
-    late = {}
-    if turns > 2:
-        late[2] = rotated(columns[1], axis, 1)
-    crossing = {r: swapped(columns[r], axis, 2) for r in columns}
-
+    rows_then, first = lax.optimization_barrier((rows, first))
+    straight = [r for r in range(1, turns) if r not in far]
+    direct = {r: (crossed(rows_then, axis, r), rotated(rows_then, axis, r)) for r in straight}
+
+    columns, visiting = lax.optimization_barrier((columns, visiting))
+    across.update({r: swapped(columns[r], axis, 2) for r in far})
     second, away = attend(
         tuple(range(half, requests - 1)), *scalars, query_t, new_latent, cache_t, visiting
     )
-    late, crossing, away = lax.optimization_barrier((late, crossing, away))
-    across.update(crossing)
-    across.update({r: swapped(late[r], axis, 2) for r in late})
+    returned = shifted(away, axis, 1)
     columns[0] = rows
-    columns.update(late)
-
-    batches = [sorted(late)] * bool(late) + [sorted(crossing), [0]]
-    near, sizes = [], []
-    for batch in batches:
-        near += [across[r] for r in batch] + [columns[r] for r in batch]
-        sizes += [len(batch)] + [1] * len(batch)
-    others = [swapped(block, axis, 1) for block in near]
-    sizes += [2 * len(batch) for batch in batches]
-    outs = expert(place, w_gate, w_up, w_down, near + others, groups, sizes)
-    sends = list(outs[len(outs) - len(batches) :])
-    sends[0] = swapped(sends[0], axis, 1)
-
-    sums = {}
-    for i, batch in enumerate(batches):
-        mine, outs = outs[: 1 + len(batch)], outs[1 + len(batch) :]
-        split = len(batch) * tokens
-        chip = sends[i]
-        if i:
-            _, chip = lax.optimization_barrier((leaves, chip))
-            chip = swapped(chip, axis, 1)
-        leaves = added(mine[0], chip[:split])
-        crossed = swapped(leaves, axis, 2)
-        if batch == batches[-2]:
-            crossed, away = lax.optimization_barrier((crossed, away))
-        for k, r in enumerate(batch):
-            at = slice(k * tokens, (k + 1) * tokens)
-            sums[r] = [mine[1 + k], chip[split:][at], crossed[at]]
-    terms = sums.pop(0)
-    for r in sums:
-        terms = terms + [rotated(added(*sums[r]), axis, -r)]
-    returned = shifted(away, axis, 1)
+    pairs = {r: (across[r], columns[r]) for r in columns}
+    pairs, direct, _ = lax.optimization_barrier((pairs, direct, away))
+    pairs.update(direct)
+
+    order = far + straight + [0]
+    near = [block for r in order for block in pairs[r]]
+    blocks = near + [swapped(block, axis, 1) for block in near]
+    ahead = 2 * len(far)
+    sizes = [1] * len(near) + [size for size in (ahead, len(near) - ahead) if size]
+    outs = expert(place, w_gate, w_up, w_down, blocks, groups, sizes)
+    chips = [swapped(send, axis, 1) for send in outs[len(near) :]]
+    chip_blocks = []
+    for chip in chips:
+        chip_blocks += [chip[i : i + tokens] for i in range(0, chip.shape[0], tokens)]
+
+    halves = [[outs[i], chip_blocks[i]] for i in range(len(near))]
+    sums = {r: (halves[2 * i], halves[2 * i + 1]) for i, r in enumerate(order)}
+    over = {r: swapped(added(*sums[r][0]), axis, 2) for r in far}
+    terms = sums[0][1]
+    for r in straight:
+        terms = terms + [
+            crossed(added(*sums[r][0]), axis, -r),
+            rotated(added(*sums[r][1]), axis, -r),
+        ]
+    over, terms = lax.optimization_barrier((over, terms))
+    terms = terms + [swapped(added(*sums[0][0]), axis, 2)]
+    for r in far:
+        terms = terms + [rotated(added(*sums[r][1], over[r]), axis, -r)]
     attn_out = settle(place, moved_slot, first, second, returned)
     _, terms = lax.optimization_barrier((attn_out, terms))
     moe_out = added(*terms)

time: 62.9 us -> 61.5 us (0.978)
  waiting for transfers between devices: 24.2 us -> 20 us
  starting transfers between devices: 21.5 us -> 24.4 us
    ppermute x18 -> x14, waiting for transfers between devices: 17.5 us -> 3.03 us  [swapped(): return lax.ppermute(value, axis, pairs)]
    ppermute x0 -> x4, waiting for transfers between devices: none -> 7.76 us  [crossed(): return lax.ppermute(value, axis, pairs)]
    ppermute x0 -> x4, starting transfers between devices: none -> 7.73 us  [crossed(): return lax.ppermute(value, axis, pairs)]
    ppermute x8, starting transfers between devices: 14.2 us -> 11.3 us  [shifted(): return lax.ppermute(value, axis, pairs)]
    ppermute x8, waiting for transfers between devices: 6.69 us -> 9.18 us  [shifted(): return lax.ppermute(value, axis, pairs)]
    ppermute x18 -> x14, starting transfers between devices: 7.32 us -> 5.34 us  [swapped(): return lax.ppermute(value, axis, pairs)]
  transfers between devices with their start and end apart: 26 -> 26, of which waited for: 10 -> 13; matrix products, arithmetic and copies ran while one was open for 0% -> 0% of each run, Pallas kernels for 17% -> 17%
where the time goes in v8:
time: 61.5 us; the launch traced here: 61.3 us
  starting transfers between devices  24.4 us (40%)
  waiting for transfers between devices  20 us (33%)
  Pallas kernels  15 us (24%)
  other arithmetic  0.98 us (2%)
  between operations  0.82 us (1%)
    ppermute x8, starting transfers between devices, shifted(): return lax.ppermute(value, axis, pairs)  11.3 us
    ppermute x8, waiting for transfers between devices, shifted(): return lax.ppermute(value, axis, pairs)  9.18 us
    pallas_call x2, Pallas kernels, attend(): pl.pallas_call(functools.partial(attend_body, ranks, visits), out_shape=[...  9.02 us
    ppermute x4, waiting for transfers between devices, crossed(): return lax.ppermute(value, axis, pairs)  7.76 us
    ppermute x4, starting transfers between devices, crossed(): return lax.ppermute(value, axis, pairs)  7.73 us
    ppermute x14, starting transfers between devices, swapped(): return lax.ppermute(value, axis, pairs)  5.34 us
    ppermute x14, waiting for transfers between devices, swapped(): return lax.ppermute(value, axis, pairs)  3.03 us
    pallas_call x1, Pallas kernels, expert(): pl.pallas_call(functools.partial(expert_body, count, groups, sizes), out_...  2.71 us
  transfers between devices with their start and end apart: 26, of which 13 were waited for; matrix products, arithmetic and copies ran while one was open for 0% of the time, Pallas kernels for 17%

profile of v8, /device:TPU:0, one launch (start us, length us, event | category | flops | bytes accessed | tf_op | source)
XLA Modules:
  0.0 61.3 jit_solution(7369945046069593039)
XLA Ops:
  0.6 1.9 %shard_map.122 = (bf16[8,7296]{1,0:T(8,128)(2,1)}, bf16[592,128]{1,0:T(8,128)(2,1)}) custom-call(s32[1]{0:T(128)} %bitcast.place, s32[16]{0:T(128)} %moved.7, bf16[8,7168]{1,0:T(8,128)(2,1)} %hidden.1, s32[2,8]{1,0:T(2,128)} %bitcast.10, f32[2,8]{1,0:T(2,128)} %bitcast.11, bf16[4,576,128]{2,1,0:T(8,128)(2,1)} %bitcast.7, bf16[4,576]{1,0:T(4,128)(2,1)} %own.4), custom_call_target="tpu_custom_call" | custom-call | tf_op jit(solution)/shard_map/pallas_call | solution.py:75
  2.5 5.4 %collective-permute-start.1 = (bf16[592,128]{1,0:T(8,128)(2,1)}, bf16[592,128]{1,0:T(8,128)(2,1)}, u32[]{:S(2)}, u32[]{:S(2)}) collective-permute-start(bf16[592,128]{1,0:T(8,128)(2,1)} %get-tuple-element.47), channel_id=1, source_target_pairs={{0,15},{1,0},{2,1},{3,2},{4,3},{5,4},{6,5},{7,6},{8,7},{9,8},{10,9... | collective-permute-start | bytes 454664 | tf_op jit(solution)/shard_map/ppermute | solution.py:27
  8.1 4.5 %shard_map.123.first = bf16[2,128,512]{2,1,0:T(8,128)(2,1)} custom-call(s32[1]{0:T(128)} %bitcast.place, s32[16]{0:T(128)} %moved.7, s32[64]{0:T(128)} %lengths.3, bf16[4,576,128]{2,1,0:T(8,128)(2,1)} %bitcast.8, bf16[4,576]{1,0:T(4,128)(2,1)} %own.4, bf16[4,576,1024]{2,1,0:T(8,128)(2,1)} %bitcast.5), custom_call_target="tpu_custom_call" | custom-call | flops 570425344 | tf_op jit(solution)/shard_map/pallas_call | solution.py:159
  12.7 1.4 %collective-permute-start.8 = (bf16[8,7296]{1,0:T(8,128)(2,1)S(1)}, bf16[8,7296]{1,0:T(8,128)(2,1)S(1)}, u32[]{:S(2)}, u32[]{:S(2)}) collective-permute-start(bf16[8,7296]{1,0:T(8,128)(2,1)S(1)} %copy-done.5), channel_id=1, source_target_pairs={{0,12},{1,13},{2,14},{3,15},{4,0},{5,1},{6,2},{7,3},{8,4},{9,5},{1... | collective-permute-start | bytes 350216 | tf_op jit(solution)/shard_map/ppermute | solution.py:27
  14.1 4.4 %collective-permute-start.7 = (bf16[8,7296]{1,0:T(8,128)(2,1)S(1)}, bf16[8,7296]{1,0:T(8,128)(2,1)S(1)}, u32[]{:S(2)}, u32[]{:S(2)}) collective-permute-start(bf16[8,7296]{1,0:T(8,128)(2,1)S(1)} %copy-done.5), channel_id=1, source_target_pairs={{0,14},{1,15},{2,12},{3,13},{4,2},{5,3},{6,0},{7,1},{8,6},{9,7},{1... | collective-permute-start | bytes 350216 | tf_op jit(solution)/shard_map/ppermute | solution.py:91
  18.6 1.0 %collective-permute-start.4 = (bf16[8,7296]{1,0:T(8,128)(2,1)S(1)}, bf16[8,7296]{1,0:T(8,128)(2,1)}, u32[]{:S(2)}, u32[]{:S(2)}) collective-permute-start(bf16[8,7296]{1,0:T(8,128)(2,1)S(1)} %collective-permute-done.refs_1_), channel_id=1, source_target_pairs={{0,2},{1,3},{2,0},{3,1},{4,6},{5,7},{6,4},{7,5},{8,10},{9,11},{10,... | collective-permute-start | bytes 350216 | tf_op jit(solution)/shard_map/ppermute | solution.py:36
  19.6 4.5 %shard_map.124 = (bf16[1,128,512]{2,1,0:T(8,128)(2,1)}, bf16[128,512]{1,0:T(8,128)(2,1)}) custom-call(s32[1]{0:T(128)} %bitcast.place, s32[16]{0:T(128)} %moved.7, s32[64]{0:T(128)} %lengths.3, bf16[4,576,128]{2,1,0:T(8,128)(2,1)} %bitcast.9, bf16[4,576]{1,0:T(4,128)(2,1)} %own.4, bf16[4,576,1024]{2,1,0:T(8,128)(2,1)} %bitcast.6, ...), custom_call_target="tpu_custom_call" | custom-call | flops 570425344 | tf_op jit(solution)/shard_map/pallas_call | solution.py:159
  24.1 1.0 %collective-permute-done.6.refs_3_ = bf16[8,7296]{1,0:T(8,128)(2,1)S(1)} collective-permute-done((bf16[8,7296]{1,0:T(8,128)(2,1)S(1)}, bf16[8,7296]{1,0:T(8,128)(2,1)S(1)}, u32[]{:S(2)}, u32[]{:S(2)}) %collective-permute-start.6) | collective-permute-done | bytes 116768 | tf_op jit(solution)/shard_map/ppermute | solution.py:27
  25.1 2.1 %collective-permute-done.5.refs_2_ = bf16[8,7296]{1,0:T(8,128)(2,1)} collective-permute-done((bf16[8,7296]{1,0:T(8,128)(2,1)S(1)}, bf16[8,7296]{1,0:T(8,128)(2,1)}, u32[]{:S(2)}, u32[]{:S(2)}) %collective-permute-start.5) | collective-permute-done | bytes 116768 | tf_op jit(solution)/shard_map/ppermute | solution.py:91
  30.8 2.7 %shard_map.126 = (bf16[8,7168]{1,0:T(8,128)(2,1)S(1)}, bf16[8,7168]{1,0:T(8,128)(2,1)S(1)}, bf16[8,7168]{1,0:T(8,128)(2,1)S(1)}, bf16[8,7168]{1,0:T(8,128)(2,1)S...) custom-call(s32[1]{0:T(128)} %bitcast.place, ...), custom_call_target="tpu_custom_call" | custom-call | flops 704643072 | bytes 5505024 | tf_op jit(solution)/shard_map/pallas_call | solution.py:236
  34.1 1.0 %collective-permute-done.17 = bf16[16,7168]{1,0:T(8,128)(2,1)S(1)} collective-permute-done((bf16[16,7168]{1,0:T(8,128)(2,1)S(1)}, bf16[16,7168]{1,0:T(8,128)(2,1)S(1)}, u32[]{:S(2)}, u32[]{:S(2)}) %collective-permute-start.17) | collective-permute-done | bytes 229408 | tf_op jit(solution)/shard_map/ppermute | solution.py:36
  36.2 1.3 %collective-permute-start.23 = (bf16[8,7168]{1,0:T(8,128)(2,1)S(1)}, bf16[8,7168]{1,0:T(8,128)(2,1)S(1)}, u32[]{:S(2)}, u32[]{:S(2)}) collective-permute-start(bf16[8,7168]{1,0:T(8,128)(2,1)S(1)} %get-tuple-element.87), channel_id=1, source_target_pairs={{0,4},{1,5},{2,6},{3,7},{4,8},{5,9},{6,10},{7,11},{8,12},{9,13},{1... | collective-permute-start | bytes 344072 | tf_op jit(solution)/shard_map/ppermute | solution.py:27
  37.5 1.9 %collective-permute-start.22 = (bf16[8,7168]{1,0:T(8,128)(2,1)S(1)}, bf16[8,7168]{1,0:T(8,128)(2,1)S(1)}, u32[]{:S(2)}, u32[]{:S(2)}) collective-permute-start(bf16[8,7168]{1,0:T(8,128)(2,1)S(1)} %get-tuple-element.88), channel_id=1, source_target_pairs={{0,6},{1,7},{2,4},{3,5},{4,10},{5,11},{6,8},{7,9},{8,14},{9,15},{1... | collective-permute-start | bytes 344072 | tf_op jit(solution)/shard_map/ppermute | solution.py:91
  39.4 2.2 %collective-permute-start.21 = (bf16[8,7168]{1,0:T(8,128)(2,1)S(1)}, bf16[8,7168]{1,0:T(8,128)(2,1)S(1)}, u32[]{:S(2)}, u32[]{:S(2)}) collective-permute-start(bf16[8,7168]{1,0:T(8,128)(2,1)S(1)} %get-tuple-element.89), channel_id=1, source_target_pairs={{0,12},{1,13},{2,14},{3,15},{4,0},{5,1},{6,2},{7,3},{8,4},{9,5},{1... | collective-permute-start | bytes 344072 | tf_op jit(solution)/shard_map/ppermute | solution.py:27
  41.6 1.4 %collective-permute-start.20 = (bf16[8,7168]{1,0:T(8,128)(2,1)S(1)}, bf16[8,7168]{1,0:T(8,128)(2,1)S(1)}, u32[]{:S(2)}, u32[]{:S(2)}) collective-permute-start(bf16[8,7168]{1,0:T(8,128)(2,1)S(1)} %get-tuple-element.90), channel_id=1, source_target_pairs={{0,14},{1,15},{2,12},{3,13},{4,2},{5,3},{6,0},{7,1},{8,6},{9,7},{1... | collective-permute-start | bytes 344072 | tf_op jit(solution)/shard_map/ppermute | solution.py:91
  43.1 1.1 %collective-permute-done.23 = bf16[8,7168]{1,0:T(8,128)(2,1)S(1)} collective-permute-done((bf16[8,7168]{1,0:T(8,128)(2,1)S(1)}, bf16[8,7168]{1,0:T(8,128)(2,1)S(1)}, u32[]{:S(2)}, u32[]{:S(2)}) %collective-permute-start.23) | collective-permute-done | bytes 114720 | tf_op jit(solution)/shard_map/ppermute | solution.py:27
  44.2 1.2 %collective-permute-start.24 = (bf16[8,7168]{1,0:T(8,128)(2,1)S(1)}, bf16[8,7168]{1,0:T(8,128)(2,1)S(1)}, u32[]{:S(2)}, u32[]{:S(2)}) collective-permute-start(bf16[8,7168]{1,0:T(8,128)(2,1)S(1)} %get-tuple-element.86), channel_id=1, source_target_pairs={{0,2},{1,3},{2,0},{3,1},{4,6},{5,7},{6,4},{7,5},{8,10},{9,11},{10,... | collective-permute-start | bytes 344072 | tf_op jit(solution)/shard_map/ppermute | solution.py:36
  45.4 1.8 %collective-permute-done.22 = bf16[8,7168]{1,0:T(8,128)(2,1)S(1)} collective-permute-done((bf16[8,7168]{1,0:T(8,128)(2,1)S(1)}, bf16[8,7168]{1,0:T(8,128)(2,1)S(1)}, u32[]{:S(2)}, u32[]{:S(2)}) %collective-permute-start.22) | collective-permute-done | bytes 114720 | tf_op jit(solution)/shard_map/ppermute | solution.py:91
  47.2 1.1 %collective-permute-done.21 = bf16[8,7168]{1,0:T(8,128)(2,1)S(1)} collective-permute-done((bf16[8,7168]{1,0:T(8,128)(2,1)S(1)}, bf16[8,7168]{1,0:T(8,128)(2,1)S(1)}, u32[]{:S(2)}, u32[]{:S(2)}) %collective-permute-start.21) | collective-permute-done | bytes 114720 | tf_op jit(solution)/shard_map/ppermute | solution.py:27
  48.3 3.8 %collective-permute-done.20 = bf16[8,7168]{1,0:T(8,128)(2,1)S(1)} collective-permute-done((bf16[8,7168]{1,0:T(8,128)(2,1)S(1)}, bf16[8,7168]{1,0:T(8,128)(2,1)S(1)}, u32[]{:S(2)}, u32[]{:S(2)}) %collective-permute-start.20) | collective-permute-done | bytes 114720 | tf_op jit(solution)/shard_map/ppermute | solution.py:91
  52.2 0.9 %collective-permute-start.25 = (bf16[8,7168]{1,0:T(8,128)(2,1)S(1)}, bf16[8,7168]{1,0:T(8,128)(2,1)S(1)}, u32[]{:S(2)}, u32[]{:S(2)}) collective-permute-start(bf16[8,7168]{1,0:T(8,128)(2,1)S(1)} %add_convert_fusion.1), channel_id=1, source_target_pairs={{0,8},{1,9},{2,10},{3,11},{4,12},{5,13},{6,14},{7,15},{8,0},{9,1},... | collective-permute-start | bytes 344072 | tf_op jit(solution)/shard_map/ppermute | solution.py:27
  53.1 1.4 %shard_map.125 = bf16[4,128,512]{2,1,0:T(8,128)(2,1)} custom-call(s32[1]{0:T(128)} %bitcast.place, s32[16]{0:T(128)S(1)} %copy-done.6, bf16[2,128,512]{2,1,0:T(8,128)(2,1)S(1)} %copy-done.3, bf16[1,128,512]{2,1,0:T(8,128)(2,1)S(1)} %copy-done.4, bf16[128,512]{1,0:T(8,128)(2,1)S(1)} %collective-permute-done.2.returned), custom_call_target="tpu_custom_call" | custom-call | tf_op jit(solution)/shard_map/pallas_call | solution.py:190
  54.5 6.0 %collective-permute-done.25 = bf16[8,7168]{1,0:T(8,128)(2,1)S(1)} collective-permute-done((bf16[8,7168]{1,0:T(8,128)(2,1)S(1)}, bf16[8,7168]{1,0:T(8,128)(2,1)S(1)}, u32[]{:S(2)}, u32[]{:S(2)}) %collective-permute-start.25) | collective-permute-done | bytes 114720 | tf_op jit(solution)/shard_map/ppermute | solution.py:27
  60.5 0.8 %add_convert_fusion = bf16[8,7168]{1,0:T(8,128)(2,1)} fusion(bf16[8,7168]{1,0:T(8,128)(2,1)S(1)} %collective-permute-done.25, bf16[8,7168]{1,0:T(8,128)(2,1)S(1)} %collective-permute-done.24, bf16[8,7168]{1,0:T(8,128)(2,1)S(1)} %collective-permute-done.23, bf16[8,7168]{1,0:T(8,128)(2,1)S(1)} %collective-permute-done.22, ...), kind=kLoop, calls=%fused_computation | loop fusion | flops 917504 | bytes 1032192 | tf_op jit(solution)/shard_map/convert_element_type | solution.py:253
  (54 shorter events, 5.6 us)
Async XLA Ops:
  2.5 15.9 %collective-permute-start.1 = (bf16[592,128]{1,0:T(8,128)(2,1)}, bf16[592,128]{1,0:T(8,128)(2,1)}, u32[]{:S(2)}, u32[]{:S(2)}) collective-permute-start(bf16[592,128]{1,0:T(8,128)(2,1)} %get-tuple-element.47), channel_id=1, source_target_pairs={{0,15},{1,0},{2,1},{3,2},{4,3},{5,4},{6,5},{7,6},{8,7},{9,8},{10,9... | collective-permute-start | bytes 454664 | tf_op jit(solution)/shard_map/ppermute | solution.py:27
  8.0 10.5 %collective-permute-start = (bf16[8,7296]{1,0:T(8,128)(2,1)}, bf16[8,7296]{1,0:T(8,128)(2,1)S(1)}, u32[]{:S(2)}, u32[]{:S(2)}) collective-permute-start(bf16[8,7296]{1,0:T(8,128)(2,1)} %get-tuple-element.60.refs_7_), channel_id=1, source_target_pairs={{0,8},{1,9},{2,10},{3,11},{4,12},{5,13},{6,14},{7,15},{8,0},{9,1},... | collective-permute-start | bytes 350216 | tf_op jit(solution)/shard_map/ppermute | solution.py:27
  8.0 10.6 %collective-permute-start.3 = (bf16[8,7296]{1,0:T(8,128)(2,1)}, bf16[8,7296]{1,0:T(8,128)(2,1)S(1)}, u32[]{:S(2)}, u32[]{:S(2)}) collective-permute-start(bf16[8,7296]{1,0:T(8,128)(2,1)} %get-tuple-element.60.refs_7_), channel_id=1, source_target_pairs={{0,2},{1,3},{2,0},{3,1},{4,6},{5,7},{6,4},{7,5},{8,10},{9,11},{10,... | collective-permute-start | bytes 350216 | tf_op jit(solution)/shard_map/ppermute | solution.py:36
  12.7 11.4 %collective-permute-start.8 = (bf16[8,7296]{1,0:T(8,128)(2,1)S(1)}, bf16[8,7296]{1,0:T(8,128)(2,1)S(1)}, u32[]{:S(2)}, u32[]{:S(2)}) collective-permute-start(bf16[8,7296]{1,0:T(8,128)(2,1)S(1)} %copy-done.5), channel_id=1, source_target_pairs={{0,12},{1,13},{2,14},{3,15},{4,0},{5,1},{6,2},{7,3},{8,4},{9,5},{1... | collective-permute-start | bytes 350216 | tf_op jit(solution)/shard_map/ppermute | solution.py:27
  14.1 10.0 %collective-permute-start.7 = (bf16[8,7296]{1,0:T(8,128)(2,1)S(1)}, bf16[8,7296]{1,0:T(8,128)(2,1)S(1)}, u32[]{:S(2)}, u32[]{:S(2)}) collective-permute-start(bf16[8,7296]{1,0:T(8,128)(2,1)S(1)} %copy-done.5), channel_id=1, source_target_pairs={{0,14},{1,15},{2,12},{3,13},{4,2},{5,3},{6,0},{7,1},{8,6},{9,7},{1... | collective-permute-start | bytes 350216 | tf_op jit(solution)/shard_map/ppermute | solution.py:91
  18.5 6.6 %collective-permute-start.6 = (bf16[8,7296]{1,0:T(8,128)(2,1)S(1)}, bf16[8,7296]{1,0:T(8,128)(2,1)S(1)}, u32[]{:S(2)}, u32[]{:S(2)}) collective-permute-start(bf16[8,7296]{1,0:T(8,128)(2,1)S(1)} %copy-done.5), channel_id=1, source_target_pairs={{0,4},{1,5},{2,6},{3,7},{4,8},{5,9},{6,10},{7,11},{8,12},{9,13},{1... | collective-permute-start | bytes 350216 | tf_op jit(solution)/shard_map/ppermute | solution.py:27
  18.5 8.7 %collective-permute-start.5 = (bf16[8,7296]{1,0:T(8,128)(2,1)S(1)}, bf16[8,7296]{1,0:T(8,128)(2,1)}, u32[]{:S(2)}, u32[]{:S(2)}) collective-permute-start(bf16[8,7296]{1,0:T(8,128)(2,1)S(1)} %copy-done.5), channel_id=1, source_target_pairs={{0,6},{1,7},{2,4},{3,5},{4,10},{5,11},{6,8},{7,9},{8,14},{9,15},{1... | collective-permute-start | bytes 350216 | tf_op jit(solution)/shard_map/ppermute | solution.py:91
  18.6 8.7 %collective-permute-start.4 = (bf16[8,7296]{1,0:T(8,128)(2,1)S(1)}, bf16[8,7296]{1,0:T(8,128)(2,1)}, u32[]{:S(2)}, u32[]{:S(2)}) collective-permute-start(bf16[8,7296]{1,0:T(8,128)(2,1)S(1)} %collective-permute-done.refs_1_), channel_id=1, source_target_pairs={{0,2},{1,3},{2,0},{3,1},{4,6},{5,7},{6,4},{7,5},{8,10},{9,11},{10,... | collective-permute-start | bytes 350216 | tf_op jit(solution)/shard_map/ppermute | solution.py:36
  27.2 1.7 %collective-permute-start.9 = (bf16[8,7296]{1,0:T(8,128)(2,1)}, bf16[8,7296]{1,0:T(8,128)(2,1)S(1)}, u32[]{:S(2)}, u32[]{:S(2)}) collective-permute-start(bf16[8,7296]{1,0:T(8,128)(2,1)} %collective-permute-done.4.refs_0_), channel_id=1, source_target_pairs={{0,1},{1,0},{2,3},{3,2},{4,5},{5,4},{6,7},{7,6},{8,9},{9,8},{10,11... | collective-permute-start | bytes 350216 | tf_op jit(solution)/shard_map/ppermute | solution.py:36
  27.2 1.8 %collective-permute-start.10 = (bf16[8,7296]{1,0:T(8,128)(2,1)S(1)}, bf16[8,7296]{1,0:T(8,128)(2,1)S(1)}, u32[]{:S(2)}, u32[]{:S(2)}) collective-permute-start(bf16[8,7296]{1,0:T(8,128)(2,1)S(1)} %collective-permute-done.refs_1_), channel_id=1, source_target_pairs={{0,1},{1,0},{2,3},{3,2},{4,5},{5,4},{6,7},{7,6},{8,9},{9,8},{10,11... | collective-permute-start | bytes 350216 | tf_op jit(solution)/shard_map/ppermute | solution.py:36
  27.8 1.7 %collective-permute-start.11 = (bf16[8,7296]{1,0:T(8,128)(2,1)}, bf16[8,7296]{1,0:T(8,128)(2,1)S(1)}, u32[]{:S(2)}, u32[]{:S(2)}) collective-permute-start(bf16[8,7296]{1,0:T(8,128)(2,1)} %collective-permute-done.5.refs_2_), channel_id=1, source_target_pairs={{0,1},{1,0},{2,3},{3,2},{4,5},{5,4},{6,7},{7,6},{8,9},{9,8},{10,11... | collective-permute-start | bytes 350216 | tf_op jit(solution)/shard_map/ppermute | solution.py:36
  27.8 1.8 %collective-permute-start.12 = (bf16[8,7296]{1,0:T(8,128)(2,1)S(1)}, bf16[8,7296]{1,0:T(8,128)(2,1)S(1)}, u32[]{:S(2)}, u32[]{:S(2)}) collective-permute-start(bf16[8,7296]{1,0:T(8,128)(2,1)S(1)} %collective-permute-done.6.refs_3_), channel_id=1, source_target_pairs={{0,1},{1,0},{2,3},{3,2},{4,5},{5,4},{6,7},{7,6},{8,9},{9,8},{10,11... | collective-permute-start | bytes 350216 | tf_op jit(solution)/shard_map/ppermute | solution.py:36
  29.0 1.4 %collective-permute-start.15 = (bf16[8,7296]{1,0:T(8,128)(2,1)S(1)}, bf16[8,7296]{1,0:T(8,128)(2,1)S(1)}, u32[]{:S(2)}, u32[]{:S(2)}) collective-permute-start(bf16[8,7296]{1,0:T(8,128)(2,1)S(1)} %collective-permute-done.3.refs_6_), channel_id=1, source_target_pairs={{0,1},{1,0},{2,3},{3,2},{4,5},{5,4},{6,7},{7,6},{8,9},{9,8},{10,11... | collective-permute-start | bytes 350216 | tf_op jit(solution)/shard_map/ppermute | solution.py:36
  29.4 1.3 %collective-permute-start.16 = (bf16[8,7296]{1,0:T(8,128)(2,1)S(1)}, bf16[8,7296]{1,0:T(8,128)(2,1)S(1)}, u32[]{:S(2)}, u32[]{:S(2)}) collective-permute-start(bf16[8,7296]{1,0:T(8,128)(2,1)S(1)} %copy-done.5), channel_id=1, source_target_pairs={{0,1},{1,0},{2,3},{3,2},{4,5},{5,4},{6,7},{7,6},{8,9},{9,8},{10,11... | collective-permute-start | bytes 350216 | tf_op jit(solution)/shard_map/ppermute | solution.py:36
  33.5 1.6 %collective-permute-start.17 = (bf16[16,7168]{1,0:T(8,128)(2,1)S(1)}, bf16[16,7168]{1,0:T(8,128)(2,1)S(1)}, u32[]{:S(2)}, u32[]{:S(2)}) collective-permute-start(bf16[16,7168]{1,0:T(8,128)(2,1)S(1)} %get-tuple-element.62), channel_id=1, source_target_pairs={{0,1},{1,0},{2,3},{3,2},{4,5},{5,4},{6,7},{7,6},{8,9},{9,8},{10,11... | collective-permute-start | bytes 688136 | tf_op jit(solution)/shard_map/ppermute | solution.py:36
  33.7 2.3 %collective-permute-start.19 = (bf16[48,7168]{1,0:T(8,128)(2,1)S(1)}, bf16[48,7168]{1,0:T(8,128)(2,1)S(1)}, u32[]{:S(2)}, u32[]{:S(2)}) collective-permute-start(bf16[48,7168]{1,0:T(8,128)(2,1)S(1)} %get-tuple-element.64), channel_id=1, source_target_pairs={{0,1},{1,0},{2,3},{3,2},{4,5},{5,4},{6,7},{7,6},{8,9},{9,8},{10,11... | collective-permute-start | bytes 2064392 | tf_op jit(solution)/shard_map/ppermute | solution.py:36
  35.1 7.9 %collective-permute-start.18 = (bf16[8,7168]{1,0:T(8,128)(2,1)S(1)}, bf16[8,7168]{1,0:T(8,128)(2,1)S(1)}, u32[]{:S(2)}, u32[]{:S(2)}) collective-permute-start(bf16[8,7168]{1,0:T(8,128)(2,1)S(1)} %add_convert_fusion.7), channel_id=1, source_target_pairs={{0,2},{1,3},{2,0},{3,1},{4,6},{5,7},{6,4},{7,5},{8,10},{9,11},{10,... | collective-permute-start | bytes 344072 | tf_op jit(solution)/shard_map/ppermute | solution.py:36
  36.2 8.0 %collective-permute-start.23 = (bf16[8,7168]{1,0:T(8,128)(2,1)S(1)}, bf16[8,7168]{1,0:T(8,128)(2,1)S(1)}, u32[]{:S(2)}, u32[]{:S(2)}) collective-permute-start(bf16[8,7168]{1,0:T(8,128)(2,1)S(1)} %get-tuple-element.87), channel_id=1, source_target_pairs={{0,4},{1,5},{2,6},{3,7},{4,8},{5,9},{6,10},{7,11},{8,12},{9,13},{1... | collective-permute-start | bytes 344072 | tf_op jit(solution)/shard_map/ppermute | solution.py:27
  37.5 9.7 %collective-permute-start.22 = (bf16[8,7168]{1,0:T(8,128)(2,1)S(1)}, bf16[8,7168]{1,0:T(8,128)(2,1)S(1)}, u32[]{:S(2)}, u32[]{:S(2)}) collective-permute-start(bf16[8,7168]{1,0:T(8,128)(2,1)S(1)} %get-tuple-element.88), channel_id=1, source_target_pairs={{0,6},{1,7},{2,4},{3,5},{4,10},{5,11},{6,8},{7,9},{8,14},{9,15},{1... | collective-permute-start | bytes 344072 | tf_op jit(solution)/shard_map/ppermute | solution.py:91
  39.4 8.9 %collective-permute-start.21 = (bf16[8,7168]{1,0:T(8,128)(2,1)S(1)}, bf16[8,7168]{1,0:T(8,128)(2,1)S(1)}, u32[]{:S(2)}, u32[]{:S(2)}) collective-permute-start(bf16[8,7168]{1,0:T(8,128)(2,1)S(1)} %get-tuple-element.89), channel_id=1, source_target_pairs={{0,12},{1,13},{2,14},{3,15},{4,0},{5,1},{6,2},{7,3},{8,4},{9,5},{1... | collective-permute-start | bytes 344072 | tf_op jit(solution)/shard_map/ppermute | solution.py:27
  41.6 10.5 %collective-permute-start.20 = (bf16[8,7168]{1,0:T(8,128)(2,1)S(1)}, bf16[8,7168]{1,0:T(8,128)(2,1)S(1)}, u32[]{:S(2)}, u32[]{:S(2)}) collective-permute-start(bf16[8,7168]{1,0:T(8,128)(2,1)S(1)} %get-tuple-element.90), channel_id=1, source_target_pairs={{0,14},{1,15},{2,12},{3,13},{4,2},{5,3},{6,0},{7,1},{8,6},{9,7},{1... | collective-permute-start | bytes 344072 | tf_op jit(solution)/shard_map/ppermute | solution.py:91
  43.0 10.0 %collective-permute-start.2 = (bf16[128,512]{1,0:T(8,128)(2,1)S(1)}, bf16[128,512]{1,0:T(8,128)(2,1)S(1)}, u32[]{:S(2)}, u32[]{:S(2)}) collective-permute-start(bf16[128,512]{1,0:T(8,128)(2,1)S(1)} %copy-done.7), channel_id=1, source_target_pairs={{0,1},{1,2},{2,3},{3,4},{4,5},{5,6},{6,7},{7,8},{8,9},{9,10},{10,1... | collective-permute-start | bytes 393224 | tf_op jit(solution)/shard_map/ppermute | solution.py:27
  44.2 10.3 %collective-permute-start.24 = (bf16[8,7168]{1,0:T(8,128)(2,1)S(1)}, bf16[8,7168]{1,0:T(8,128)(2,1)S(1)}, u32[]{:S(2)}, u32[]{:S(2)}) collective-permute-start(bf16[8,7168]{1,0:T(8,128)(2,1)S(1)} %get-tuple-element.86), channel_id=1, source_target_pairs={{0,2},{1,3},{2,0},{3,1},{4,6},{5,7},{6,4},{7,5},{8,10},{9,11},{10,... | collective-permute-start | bytes 344072 | tf_op jit(solution)/shard_map/ppermute | solution.py:36
  52.2 8.3 %collective-permute-start.25 = (bf16[8,7168]{1,0:T(8,128)(2,1)S(1)}, bf16[8,7168]{1,0:T(8,128)(2,1)S(1)}, u32[]{:S(2)}, u32[]{:S(2)}) collective-permute-start(bf16[8,7168]{1,0:T(8,128)(2,1)S(1)} %add_convert_fusion.1), channel_id=1, source_target_pairs={{0,8},{1,9},{2,10},{3,11},{4,12},{5,13},{6,14},{7,15},{8,0},{9,1},... | collective-permute-start | bytes 344072 | tf_op jit(solution)/shard_map/ppermute | solution.py:27
  (10 other events, 134.4 us)

commit v9 on v7

--- a/solution.py
+++ b/solution.py
@@ -276,7 +276,9 @@
     )
 
     visiting = shifted(payload, axis, -1)
-    columns = {r: rotated(rows, axis, r) for r in range(1, turns) if r != 2}
+    order = list(range(1, turns))
+    order = order[1:2] + order[:1] + order[2:]
+    columns = {r: rotated(rows, axis, r) for r in order}
     across = {0: swapped(rows, axis, 2)}
 
     half = requests // 2
@@ -284,46 +286,29 @@
     new_here, _ = lax.optimization_barrier((new_latent, rows))
     (first,) = attend(tuple(range(half)), *scalars, query_t, new_here, cache_t)
     columns, across, visiting, first = lax.optimization_barrier((columns, across, visiting, first))
-    late = {}
-    if turns > 2:
-        late[2] = rotated(columns[1], axis, 1)
-    crossing = {r: swapped(columns[r], axis, 2) for r in columns}
-
+
+    later = {r: swapped(columns[r], axis, 2) for r in order}
     second, away = attend(
         tuple(range(half, requests - 1)), *scalars, query_t, new_latent, cache_t, visiting
     )
-    late, crossing, away = lax.optimization_barrier((late, crossing, away))
-    across.update(crossing)
-    across.update({r: swapped(late[r], axis, 2) for r in late})
+    later, away = lax.optimization_barrier((later, away))
+    across.update(later)
     columns[0] = rows
-    columns.update(late)
-
-    batches = [sorted(late)] * bool(late) + [sorted(crossing), [0]]
-    near, sizes = [], []
-    for batch in batches:
-        near += [across[r] for r in batch] + [columns[r] for r in batch]
-        sizes += [len(batch)] + [1] * len(batch)
-    others = [swapped(block, axis, 1) for block in near]
-    sizes += [2 * len(batch) for batch in batches]
-    outs = expert(place, w_gate, w_up, w_down, near + others, groups, sizes)
-    sends = list(outs[len(outs) - len(batches) :])
-    sends[0] = swapped(sends[0], axis, 1)
+
+    order = order + [0]
+    near = [block for r in order for block in (across[r], columns[r])]
+    blocks = near + [swapped(block, axis, 1) for block in near]
+    sizes = [1] * len(near) + [2] * len(order)
+    outs = expert(place, w_gate, w_up, w_down, blocks, groups, sizes)
+    keeps, sends = outs[: len(near)], outs[len(near) :]
 
     sums = {}
-    for i, batch in enumerate(batches):
-        mine, outs = outs[: 1 + len(batch)], outs[1 + len(batch) :]
-        split = len(batch) * tokens
-        chip = sends[i]
-        if i:
-            _, chip = lax.optimization_barrier((leaves, chip))
-            chip = swapped(chip, axis, 1)
-        leaves = added(mine[0], chip[:split])
-        crossed = swapped(leaves, axis, 2)
-        if batch == batches[-2]:
-            crossed, away = lax.optimization_barrier((crossed, away))
-        for k, r in enumerate(batch):
-            at = slice(k * tokens, (k + 1) * tokens)
-            sums[r] = [mine[1 + k], chip[split:][at], crossed[at]]
+    for i, r in enumerate(order):
+        chip = swapped(sends[i], axis, 1)
+        over = swapped(added(keeps[2 * i], chip[:tokens]), axis, 2)
+        if i == len(order) - 2:
+            over, away = lax.optimization_barrier((over, away))
+        sums[r] = [keeps[2 * i + 1], chip[tokens:], over]
     terms = sums.pop(0)
     for r in sums:
         terms = terms + [rotated(added(*sums[r]), axis, -r)]

time: 62.9 us -> 60.6 us (0.963)
  waiting for transfers between devices: 24.2 us -> 19.6 us
  starting transfers between devices: 21.5 us -> 23.7 us
    ppermute x18 -> x20, waiting for transfers between devices: 17.5 us -> 10.5 us  [swapped(): return lax.ppermute(value, axis, pairs)]
    ppermute x8, waiting for transfers between devices: 6.69 us -> 9.16 us  [shifted(): return lax.ppermute(value, axis, pairs)]
    ppermute x18 -> x20, starting transfers between devices: 7.32 us -> 9.36 us  [swapped(): return lax.ppermute(value, axis, pairs)]
  transfers between devices with their start and end apart: 26 -> 28, of which waited for: 10 -> 13; matrix products, arithmetic and copies ran while one was open for 0% -> 0% of each run, Pallas kernels for 17% -> 17%
where the time goes in v9:
time: 60.6 us; the launch traced here: 60.4 us
  starting transfers between devices  23.7 us (39%)
  waiting for transfers between devices  19.6 us (32%)
  Pallas kernels  15.2 us (25%)
  other arithmetic  0.99 us (2%)
  between operations  0.82 us (1%)
    ppermute x8, starting transfers between devices, shifted(): return lax.ppermute(value, axis, pairs)  14.4 us
    ppermute x20, waiting for transfers between devices, swapped(): return lax.ppermute(value, axis, pairs)  10.5 us
    ppermute x20, starting transfers between devices, swapped(): return lax.ppermute(value, axis, pairs)  9.36 us
    ppermute x8, waiting for transfers between devices, shifted(): return lax.ppermute(value, axis, pairs)  9.16 us
    pallas_call x2, Pallas kernels, attend(): pl.pallas_call(functools.partial(attend_body, ranks, visits), out_shape=[...  9.02 us
    pallas_call x1, Pallas kernels, expert(): pl.pallas_call(functools.partial(expert_body, count, groups, sizes), out_...  2.88 us
    pallas_call x1, Pallas kernels, prepare(): pl.pallas_call(functools.partial(prepare_body, groups), out_shape=[jax.Sh...  1.9 us
    pallas_call x1, Pallas kernels, settle(): pl.pallas_call(settle_body, out_shape=jax.ShapeDtypeStruct((count,) + ret...  1.39 us
  transfers between devices with their start and end apart: 28, of which 13 were waited for; matrix products, arithmetic and copies ran while one was open for 0% of the time, Pallas kernels for 17%

profile of v9, /device:TPU:0, one launch (start us, length us, event | category | flops | bytes accessed | tf_op | source)
XLA Modules:
  0.0 60.4 jit_solution(16605909080637905529)
XLA Ops:
  0.6 1.9 %shard_map.122 = (bf16[8,7296]{1,0:T(8,128)(2,1)}, bf16[592,128]{1,0:T(8,128)(2,1)}) custom-call(s32[1]{0:T(128)} %bitcast.place, s32[16]{0:T(128)} %moved.7, bf16[8,7168]{1,0:T(8,128)(2,1)} %hidden.1, s32[2,8]{1,0:T(2,128)} %bitcast.10, f32[2,8]{1,0:T(2,128)} %bitcast.11, bf16[4,576,128]{2,1,0:T(8,128)(2,1)} %bitcast.7, bf16[4,576]{1,0:T(4,128)(2,1)} %own.4), custom_call_target="tpu_custom_call" | custom-call | tf_op jit(solution)/shard_map/pallas_call | solution.py:75
  2.5 5.4 %collective-permute-start.4 = (bf16[592,128]{1,0:T(8,128)(2,1)}, bf16[592,128]{1,0:T(8,128)(2,1)}, u32[]{:S(2)}, u32[]{:S(2)}) collective-permute-start(bf16[592,128]{1,0:T(8,128)(2,1)} %get-tuple-element.38), channel_id=1, source_target_pairs={{0,15},{1,0},{2,1},{3,2},{4,3},{5,4},{6,5},{7,6},{8,7},{9,8},{10,9... | collective-permute-start | bytes 454664 | tf_op jit(solution)/shard_map/ppermute | solution.py:27
  8.0 1.1 %collective-permute-start.2 = (bf16[8,7296]{1,0:T(8,128)(2,1)}, bf16[8,7296]{1,0:T(8,128)(2,1)S(1)}, u32[]{:S(2)}, u32[]{:S(2)}) collective-permute-start(bf16[8,7296]{1,0:T(8,128)(2,1)} %get-tuple-element.37.refs_7_), channel_id=1, source_target_pairs={{0,12},{1,13},{2,14},{3,15},{4,0},{5,1},{6,2},{7,3},{8,4},{9,5},{1... | collective-permute-start | bytes 350216 | tf_op jit(solution)/shard_map/ppermute | solution.py:27
  9.1 1.0 %collective-permute-start = (bf16[8,7296]{1,0:T(8,128)(2,1)}, bf16[8,7296]{1,0:T(8,128)(2,1)S(1)}, u32[]{:S(2)}, u32[]{:S(2)}) collective-permute-start(bf16[8,7296]{1,0:T(8,128)(2,1)} %get-tuple-element.37.refs_7_), channel_id=1, source_target_pairs={{0,4},{1,5},{2,6},{3,7},{4,8},{5,9},{6,10},{7,11},{8,12},{9,13},{1... | collective-permute-start | bytes 350216 | tf_op jit(solution)/shard_map/ppermute | solution.py:27
  10.1 4.5 %shard_map.123.first = bf16[2,128,512]{2,1,0:T(8,128)(2,1)} custom-call(s32[1]{0:T(128)} %bitcast.place, s32[16]{0:T(128)} %moved.7, s32[64]{0:T(128)} %lengths.3, bf16[4,576,128]{2,1,0:T(8,128)(2,1)} %bitcast.8, bf16[4,576]{1,0:T(4,128)(2,1)} %own.4, bf16[4,576,1024]{2,1,0:T(8,128)(2,1)} %bitcast.5), custom_call_target="tpu_custom_call" | custom-call | flops 570425344 | tf_op jit(solution)/shard_map/pallas_call | solution.py:153
  14.9 5.9 %collective-permute-done.1.refs_1_ = bf16[8,7296]{1,0:T(8,128)(2,1)S(1)} collective-permute-done((bf16[8,7296]{1,0:T(8,128)(2,1)}, bf16[8,7296]{1,0:T(8,128)(2,1)S(1)}, u32[]{:S(2)}, u32[]{:S(2)}) %collective-permute-start.1) | collective-permute-done | bytes 116768 | tf_op jit(solution)/shard_map/ppermute | solution.py:27
  20.8 2.0 %collective-permute-start.6 = (bf16[8,7296]{1,0:T(8,128)(2,1)S(1)}, bf16[8,7296]{1,0:T(8,128)(2,1)}, u32[]{:S(2)}, u32[]{:S(2)}) collective-permute-start(bf16[8,7296]{1,0:T(8,128)(2,1)S(1)} %collective-permute-done.1.refs_1_), channel_id=1, source_target_pairs={{0,2},{1,3},{2,0},{3,1},{4,6},{5,7},{6,4},{7,5},{8,10},{9,11},{10,... | collective-permute-start | bytes 350216 | tf_op jit(solution)/shard_map/ppermute | solution.py:36
  22.9 0.5 collective-permute-start.14
  23.4 3.5 %collective-permute-done.5.refs_2_ = bf16[8,7296]{1,0:T(8,128)(2,1)S(1)} collective-permute-done((bf16[8,7296]{1,0:T(8,128)(2,1)S(1)}, bf16[8,7296]{1,0:T(8,128)(2,1)S(1)}, u32[]{:S(2)}, u32[]{:S(2)}) %collective-permute-start.5) | collective-permute-done | bytes 116768 | tf_op jit(solution)/shard_map/ppermute | solution.py:36
  26.9 4.5 %shard_map.124 = (bf16[1,128,512]{2,1,0:T(8,128)(2,1)}, bf16[128,512]{1,0:T(8,128)(2,1)}) custom-call(s32[1]{0:T(128)} %bitcast.place, s32[16]{0:T(128)} %moved.7, s32[64]{0:T(128)} %lengths.3, bf16[4,576,128]{2,1,0:T(8,128)(2,1)} %bitcast.9, bf16[4,576]{1,0:T(4,128)(2,1)} %own.4, bf16[4,576,1024]{2,1,0:T(8,128)(2,1)} %bitcast.6, ...), custom_call_target="tpu_custom_call" | custom-call | flops 570425344 | tf_op jit(solution)/shard_map/pallas_call | solution.py:153
  31.4 0.6 collective-permute-start.9
  34.2 2.9 %shard_map.125 = (bf16[8,7168]{1,0:T(8,128)(2,1)S(1)}, bf16[8,7168]{1,0:T(8,128)(2,1)S(1)}, bf16[8,7168]{1,0:T(8,128)(2,1)S(1)}, bf16[8,7168]{1,0:T(8,128)(2,1)S...) custom-call(s32[1]{0:T(128)} %bitcast.place, ...), custom_call_target="tpu_custom_call" | custom-call | flops 704643072 | bytes 5505024 | tf_op jit(solution)/shard_map/pallas_call | solution.py:230
  38.2 0.5 collective-permute-done.16
  39.1 1.8 %collective-permute-start.20 = (bf16[8,7168]{1,0:T(8,128)(2,1)S(1)}, bf16[8,7168]{1,0:T(8,128)(2,1)S(1)}, u32[]{:S(2)}, u32[]{:S(2)}) collective-permute-start(bf16[8,7168]{1,0:T(8,128)(2,1)S(1)} %add_convert_fusion.6), channel_id=1, source_target_pairs={{0,2},{1,3},{2,0},{3,1},{4,6},{5,7},{6,4},{7,5},{8,10},{9,11},{10,... | collective-permute-start | bytes 344072 | tf_op jit(solution)/shard_map/ppermute | solution.py:36
  41.3 1.8 %collective-permute-start.25 = (bf16[8,7168]{1,0:T(8,128)(2,1)S(1)}, bf16[8,7168]{1,0:T(8,128)(2,1)S(1)}, u32[]{:S(2)}, u32[]{:S(2)}) collective-permute-start(bf16[8,7168]{1,0:T(8,128)(2,1)S(1)} %add_convert_fusion.3), channel_id=1, source_target_pairs={{0,2},{1,3},{2,0},{3,1},{4,6},{5,7},{6,4},{7,5},{8,10},{9,11},{10,... | collective-permute-start | bytes 344072 | tf_op jit(solution)/shard_map/ppermute | solution.py:36
  43.2 1.6 %collective-permute-done.17 = bf16[8,7168]{1,0:T(8,128)(2,1)S(1)} collective-permute-done((bf16[8,7168]{1,0:T(8,128)(2,1)S(1)}, bf16[8,7168]{1,0:T(8,128)(2,1)S(1)}, u32[]{:S(2)}, u32[]{:S(2)}) %collective-permute-start.17) | collective-permute-done | bytes 114720 | tf_op jit(solution)/shard_map/ppermute | solution.py:36
  44.8 1.4 %collective-permute-start.27 = (bf16[8,7168]{1,0:T(8,128)(2,1)S(1)}, bf16[8,7168]{1,0:T(8,128)(2,1)S(1)}, u32[]{:S(2)}, u32[]{:S(2)}) collective-permute-start(bf16[8,7168]{1,0:T(8,128)(2,1)S(1)} %add_convert_fusion.1), channel_id=1, source_target_pairs={{0,4},{1,5},{2,6},{3,7},{4,8},{5,9},{6,10},{7,11},{8,12},{9,13},{1... | collective-permute-start | bytes 344072 | tf_op jit(solution)/shard_map/ppermute | solution.py:27
  46.2 3.4 %collective-permute-done.22 = bf16[8,7168]{1,0:T(8,128)(2,1)S(1)} collective-permute-done((bf16[8,7168]{1,0:T(8,128)(2,1)S(1)}, bf16[8,7168]{1,0:T(8,128)(2,1)S(1)}, u32[]{:S(2)}, u32[]{:S(2)}) %collective-permute-start.22) | collective-permute-done | bytes 114720 | tf_op jit(solution)/shard_map/ppermute | solution.py:36
  49.7 4.7 %collective-permute-start.23 = (bf16[8,7168]{1,0:T(8,128)(2,1)S(1)}, bf16[8,7168]{1,0:T(8,128)(2,1)S(1)}, u32[]{:S(2)}, u32[]{:S(2)}) collective-permute-start(bf16[8,7168]{1,0:T(8,128)(2,1)S(1)} %add_convert_fusion.4), channel_id=1, source_target_pairs={{0,8},{1,9},{2,10},{3,11},{4,12},{5,13},{6,14},{7,15},{8,0},{9,1},... | collective-permute-start | bytes 344072 | tf_op jit(solution)/shard_map/ppermute | solution.py:27
  54.4 0.7 %collective-permute-start.26 = (bf16[8,7168]{1,0:T(8,128)(2,1)S(1)}, bf16[8,7168]{1,0:T(8,128)(2,1)S(1)}, u32[]{:S(2)}, u32[]{:S(2)}) collective-permute-start(bf16[8,7168]{1,0:T(8,128)(2,1)S(1)} %add_convert_fusion.2), channel_id=1, source_target_pairs={{0,12},{1,13},{2,14},{3,15},{4,0},{5,1},{6,2},{7,3},{8,4},{9,5},{1... | collective-permute-start | bytes 344072 | tf_op jit(solution)/shard_map/ppermute | solution.py:27
  55.2 1.4 %shard_map.126 = bf16[4,128,512]{2,1,0:T(8,128)(2,1)} custom-call(s32[1]{0:T(128)} %bitcast.place, s32[16]{0:T(128)S(1)} %copy-done.6, bf16[2,128,512]{2,1,0:T(8,128)(2,1)S(1)} %copy-done.3, bf16[1,128,512]{2,1,0:T(8,128)(2,1)S(1)} %copy-done.4, bf16[128,512]{1,0:T(8,128)(2,1)S(1)} %collective-permute-done.18.returned), custom_call_target="tpu_custom_call" | custom-call | tf_op jit(solution)/shard_map/pallas_call | solution.py:184
  56.6 2.2 %collective-permute-done.23 = bf16[8,7168]{1,0:T(8,128)(2,1)S(1)} collective-permute-done((bf16[8,7168]{1,0:T(8,128)(2,1)S(1)}, bf16[8,7168]{1,0:T(8,128)(2,1)S(1)}, u32[]{:S(2)}, u32[]{:S(2)}) %collective-permute-start.23) | collective-permute-done | bytes 114720 | tf_op jit(solution)/shard_map/ppermute | solution.py:27
  58.8 0.9 %collective-permute-done.26 = bf16[8,7168]{1,0:T(8,128)(2,1)S(1)} collective-permute-done((bf16[8,7168]{1,0:T(8,128)(2,1)S(1)}, bf16[8,7168]{1,0:T(8,128)(2,1)S(1)}, u32[]{:S(2)}, u32[]{:S(2)}) %collective-permute-start.26) | collective-permute-done | bytes 114720 | tf_op jit(solution)/shard_map/ppermute | solution.py:27
  59.7 0.7 %add_convert_fusion = bf16[8,7168]{1,0:T(8,128)(2,1)} fusion(bf16[8,7168]{1,0:T(8,128)(2,1)S(1)} %collective-permute-done.27, bf16[8,7168]{1,0:T(8,128)(2,1)S(1)} %collective-permute-done.26, bf16[8,7168]{1,0:T(8,128)(2,1)S(1)} %collective-permute-done.23, bf16[8,7168]{1,0:T(8,128)(2,1)S(1)} %collective-permute-done.20, bf16[8,7168]{1,0:T(8,128)(2,1)S(1)} %slice.33, ...), kind=kLoop, calls=%fused_computation | loop fusion | flops 688128 | bytes 802816 | tf_op jit(solution)/shard_map/convert_element_type | solution.py:247
  (62 shorter events, 4.6 us)
Async XLA Ops:
  2.5 18.3 %collective-permute-start.4 = (bf16[592,128]{1,0:T(8,128)(2,1)}, bf16[592,128]{1,0:T(8,128)(2,1)}, u32[]{:S(2)}, u32[]{:S(2)}) collective-permute-start(bf16[592,128]{1,0:T(8,128)(2,1)} %get-tuple-element.38), channel_id=1, source_target_pairs={{0,15},{1,0},{2,1},{3,2},{4,3},{5,4},{6,5},{7,6},{8,7},{9,8},{10,9... | collective-permute-start | bytes 454664 | tf_op jit(solution)/shard_map/ppermute | solution.py:27
  8.0 6.7 %collective-permute-start.3 = (bf16[8,7296]{1,0:T(8,128)(2,1)}, bf16[8,7296]{1,0:T(8,128)(2,1)S(1)}, u32[]{:S(2)}, u32[]{:S(2)}) collective-permute-start(bf16[8,7296]{1,0:T(8,128)(2,1)} %get-tuple-element.37.refs_7_), channel_id=1, source_target_pairs={{0,2},{1,3},{2,0},{3,1},{4,6},{5,7},{6,4},{7,5},{8,10},{9,11},{10,... | collective-permute-start | bytes 350216 | tf_op jit(solution)/shard_map/ppermute | solution.py:36
  8.0 6.9 %collective-permute-start.2 = (bf16[8,7296]{1,0:T(8,128)(2,1)}, bf16[8,7296]{1,0:T(8,128)(2,1)S(1)}, u32[]{:S(2)}, u32[]{:S(2)}) collective-permute-start(bf16[8,7296]{1,0:T(8,128)(2,1)} %get-tuple-element.37.refs_7_), channel_id=1, source_target_pairs={{0,12},{1,13},{2,14},{3,15},{4,0},{5,1},{6,2},{7,3},{8,4},{9,5},{1... | collective-permute-start | bytes 350216 | tf_op jit(solution)/shard_map/ppermute | solution.py:27
  9.1 11.7 %collective-permute-start.1 = (bf16[8,7296]{1,0:T(8,128)(2,1)}, bf16[8,7296]{1,0:T(8,128)(2,1)S(1)}, u32[]{:S(2)}, u32[]{:S(2)}) collective-permute-start(bf16[8,7296]{1,0:T(8,128)(2,1)} %get-tuple-element.37.refs_7_), channel_id=1, source_target_pairs={{0,8},{1,9},{2,10},{3,11},{4,12},{5,13},{6,14},{7,15},{8,0},{9,1},... | collective-permute-start | bytes 350216 | tf_op jit(solution)/shard_map/ppermute | solution.py:27
  9.1 11.7 %collective-permute-start = (bf16[8,7296]{1,0:T(8,128)(2,1)}, bf16[8,7296]{1,0:T(8,128)(2,1)S(1)}, u32[]{:S(2)}, u32[]{:S(2)}) collective-permute-start(bf16[8,7296]{1,0:T(8,128)(2,1)} %get-tuple-element.37.refs_7_), channel_id=1, source_target_pairs={{0,4},{1,5},{2,6},{3,7},{4,8},{5,9},{6,10},{7,11},{8,12},{9,13},{1... | collective-permute-start | bytes 350216 | tf_op jit(solution)/shard_map/ppermute | solution.py:27
  20.8 6.1 %collective-permute-start.5 = (bf16[8,7296]{1,0:T(8,128)(2,1)S(1)}, bf16[8,7296]{1,0:T(8,128)(2,1)S(1)}, u32[]{:S(2)}, u32[]{:S(2)}) collective-permute-start(bf16[8,7296]{1,0:T(8,128)(2,1)S(1)} %collective-permute-done.refs_3_), channel_id=1, source_target_pairs={{0,2},{1,3},{2,0},{3,1},{4,6},{5,7},{6,4},{7,5},{8,10},{9,11},{10,... | collective-permute-start | bytes 350216 | tf_op jit(solution)/shard_map/ppermute | solution.py:36
  20.8 10.6 %collective-permute-start.6 = (bf16[8,7296]{1,0:T(8,128)(2,1)S(1)}, bf16[8,7296]{1,0:T(8,128)(2,1)}, u32[]{:S(2)}, u32[]{:S(2)}) collective-permute-start(bf16[8,7296]{1,0:T(8,128)(2,1)S(1)} %collective-permute-done.1.refs_1_), channel_id=1, source_target_pairs={{0,2},{1,3},{2,0},{3,1},{4,6},{5,7},{6,4},{7,5},{8,10},{9,11},{10,... | collective-permute-start | bytes 350216 | tf_op jit(solution)/shard_map/ppermute | solution.py:36
  22.8 9.2 %collective-permute-start.7 = (bf16[8,7296]{1,0:T(8,128)(2,1)S(1)}, bf16[8,7296]{1,0:T(8,128)(2,1)}, u32[]{:S(2)}, u32[]{:S(2)}) collective-permute-start(bf16[8,7296]{1,0:T(8,128)(2,1)S(1)} %collective-permute-done.2.refs_5_), channel_id=1, source_target_pairs={{0,2},{1,3},{2,0},{3,1},{4,6},{5,7},{6,4},{7,5},{8,10},{9,11},{10,... | collective-permute-start | bytes 350216 | tf_op jit(solution)/shard_map/ppermute | solution.py:36
  22.9 9.2 %collective-permute-start.15 = (bf16[8,7296]{1,0:T(8,128)(2,1)S(1)}, bf16[8,7296]{1,0:T(8,128)(2,1)}, u32[]{:S(2)}, u32[]{:S(2)}) collective-permute-start(bf16[8,7296]{1,0:T(8,128)(2,1)S(1)} %copy-done.5), channel_id=1, source_target_pairs={{0,1},{1,0},{2,3},{3,2},{4,5},{5,4},{6,7},{7,6},{8,9},{9,8},{10,11... | collective-permute-start | bytes 350216 | tf_op jit(solution)/shard_map/ppermute | solution.py:36
  22.9 9.6 %collective-permute-start.14 = (bf16[8,7296]{1,0:T(8,128)(2,1)S(1)}, bf16[8,7296]{1,0:T(8,128)(2,1)}, u32[]{:S(2)}, u32[]{:S(2)}) collective-permute-start(bf16[8,7296]{1,0:T(8,128)(2,1)S(1)} %collective-permute-done.3.refs_6_), channel_id=1, source_target_pairs={{0,1},{1,0},{2,3},{3,2},{4,5},{5,4},{6,7},{7,6},{8,9},{9,8},{10,11... | collective-permute-start | bytes 350216 | tf_op jit(solution)/shard_map/ppermute | solution.py:36
  26.9 5.7 %collective-permute-start.11 = (bf16[8,7296]{1,0:T(8,128)(2,1)S(1)}, bf16[8,7296]{1,0:T(8,128)(2,1)}, u32[]{:S(2)}, u32[]{:S(2)}) collective-permute-start(bf16[8,7296]{1,0:T(8,128)(2,1)S(1)} %collective-permute-done.refs_3_), channel_id=1, source_target_pairs={{0,1},{1,0},{2,3},{3,2},{4,5},{5,4},{6,7},{7,6},{8,9},{9,8},{10,11... | collective-permute-start | bytes 350216 | tf_op jit(solution)/shard_map/ppermute | solution.py:36
  31.4 1.6 %collective-permute-start.9 = (bf16[8,7296]{1,0:T(8,128)(2,1)S(1)}, bf16[8,7296]{1,0:T(8,128)(2,1)S(1)}, u32[]{:S(2)}, u32[]{:S(2)}) collective-permute-start(bf16[8,7296]{1,0:T(8,128)(2,1)S(1)} %collective-permute-done.1.refs_1_), channel_id=1, source_target_pairs={{0,1},{1,0},{2,3},{3,2},{4,5},{5,4},{6,7},{7,6},{8,9},{9,8},{10,11... | collective-permute-start | bytes 350216 | tf_op jit(solution)/shard_map/ppermute | solution.py:36
  32.1 1.6 %collective-permute-start.8 = (bf16[8,7296]{1,0:T(8,128)(2,1)}, bf16[8,7296]{1,0:T(8,128)(2,1)S(1)}, u32[]{:S(2)}, u32[]{:S(2)}) collective-permute-start(bf16[8,7296]{1,0:T(8,128)(2,1)} %collective-permute-done.6.refs_0_), channel_id=1, source_target_pairs={{0,1},{1,0},{2,3},{3,2},{4,5},{5,4},{6,7},{7,6},{8,9},{9,8},{10,11... | collective-permute-start | bytes 350216 | tf_op jit(solution)/shard_map/ppermute | solution.py:36
  32.6 1.6 %collective-permute-start.12 = (bf16[8,7296]{1,0:T(8,128)(2,1)}, bf16[8,7296]{1,0:T(8,128)(2,1)S(1)}, u32[]{:S(2)}, u32[]{:S(2)}) collective-permute-start(bf16[8,7296]{1,0:T(8,128)(2,1)} %collective-permute-done.7.refs_4_), channel_id=1, source_target_pairs={{0,1},{1,0},{2,3},{3,2},{4,5},{5,4},{6,7},{7,6},{8,9},{9,8},{10,11... | collective-permute-start | bytes 350216 | tf_op jit(solution)/shard_map/ppermute | solution.py:36
  37.7 3.2 %collective-permute-start.21 = (bf16[16,7168]{1,0:T(8,128)(2,1)S(1)}, bf16[16,7168]{1,0:T(8,128)(2,1)S(1)}, u32[]{:S(2)}, u32[]{:S(2)}) collective-permute-start(bf16[16,7168]{1,0:T(8,128)(2,1)S(1)} %get-tuple-element.59), channel_id=1, source_target_pairs={{0,1},{1,0},{2,3},{3,2},{4,5},{5,4},{6,7},{7,6},{8,9},{9,8},{10,11... | collective-permute-start | bytes 688136 | tf_op jit(solution)/shard_map/ppermute | solution.py:36
  38.1 3.2 %collective-permute-start.24 = (bf16[16,7168]{1,0:T(8,128)(2,1)S(1)}, bf16[16,7168]{1,0:T(8,128)(2,1)S(1)}, u32[]{:S(2)}, u32[]{:S(2)}) collective-permute-start(bf16[16,7168]{1,0:T(8,128)(2,1)S(1)} %get-tuple-element.62), channel_id=1, source_target_pairs={{0,1},{1,0},{2,3},{3,2},{4,5},{5,4},{6,7},{7,6},{8,9},{9,8},{10,11... | collective-permute-start | bytes 688136 | tf_op jit(solution)/shard_map/ppermute | solution.py:36
  38.7 6.0 %collective-permute-start.17 = (bf16[8,7168]{1,0:T(8,128)(2,1)S(1)}, bf16[8,7168]{1,0:T(8,128)(2,1)S(1)}, u32[]{:S(2)}, u32[]{:S(2)}) collective-permute-start(bf16[8,7168]{1,0:T(8,128)(2,1)S(1)} %add_convert_fusion.7), channel_id=1, source_target_pairs={{0,2},{1,3},{2,0},{3,1},{4,6},{5,7},{6,4},{7,5},{8,10},{9,11},{10,... | collective-permute-start | bytes 344072 | tf_op jit(solution)/shard_map/ppermute | solution.py:36
  39.1 17.5 %collective-permute-start.20 = (bf16[8,7168]{1,0:T(8,128)(2,1)S(1)}, bf16[8,7168]{1,0:T(8,128)(2,1)S(1)}, u32[]{:S(2)}, u32[]{:S(2)}) collective-permute-start(bf16[8,7168]{1,0:T(8,128)(2,1)S(1)} %add_convert_fusion.6), channel_id=1, source_target_pairs={{0,2},{1,3},{2,0},{3,1},{4,6},{5,7},{6,4},{7,5},{8,10},{9,11},{10,... | collective-permute-start | bytes 344072 | tf_op jit(solution)/shard_map/ppermute | solution.py:36
  41.0 8.7 %collective-permute-start.22 = (bf16[8,7168]{1,0:T(8,128)(2,1)S(1)}, bf16[8,7168]{1,0:T(8,128)(2,1)S(1)}, u32[]{:S(2)}, u32[]{:S(2)}) collective-permute-start(bf16[8,7168]{1,0:T(8,128)(2,1)S(1)} %add_convert_fusion.5), channel_id=1, source_target_pairs={{0,2},{1,3},{2,0},{3,1},{4,6},{5,7},{6,4},{7,5},{8,10},{9,11},{10,... | collective-permute-start | bytes 344072 | tf_op jit(solution)/shard_map/ppermute | solution.py:36
  41.3 13.1 %collective-permute-start.25 = (bf16[8,7168]{1,0:T(8,128)(2,1)S(1)}, bf16[8,7168]{1,0:T(8,128)(2,1)S(1)}, u32[]{:S(2)}, u32[]{:S(2)}) collective-permute-start(bf16[8,7168]{1,0:T(8,128)(2,1)S(1)} %add_convert_fusion.3), channel_id=1, source_target_pairs={{0,2},{1,3},{2,0},{3,1},{4,6},{5,7},{6,4},{7,5},{8,10},{9,11},{10,... | collective-permute-start | bytes 344072 | tf_op jit(solution)/shard_map/ppermute | solution.py:36
  44.8 11.8 %collective-permute-start.27 = (bf16[8,7168]{1,0:T(8,128)(2,1)S(1)}, bf16[8,7168]{1,0:T(8,128)(2,1)S(1)}, u32[]{:S(2)}, u32[]{:S(2)}) collective-permute-start(bf16[8,7168]{1,0:T(8,128)(2,1)S(1)} %add_convert_fusion.1), channel_id=1, source_target_pairs={{0,4},{1,5},{2,6},{3,7},{4,8},{5,9},{6,10},{7,11},{8,12},{9,13},{1... | collective-permute-start | bytes 344072 | tf_op jit(solution)/shard_map/ppermute | solution.py:27
  46.2 8.9 %collective-permute-start.18 = (bf16[128,512]{1,0:T(8,128)(2,1)S(1)}, bf16[128,512]{1,0:T(8,128)(2,1)S(1)}, u32[]{:S(2)}, u32[]{:S(2)}) collective-permute-start(bf16[128,512]{1,0:T(8,128)(2,1)S(1)} %copy-done.7), channel_id=1, source_target_pairs={{0,1},{1,2},{2,3},{3,4},{4,5},{5,6},{6,7},{7,8},{8,9},{9,10},{10,1... | collective-permute-start | bytes 393224 | tf_op jit(solution)/shard_map/ppermute | solution.py:27
  49.7 9.1 %collective-permute-start.23 = (bf16[8,7168]{1,0:T(8,128)(2,1)S(1)}, bf16[8,7168]{1,0:T(8,128)(2,1)S(1)}, u32[]{:S(2)}, u32[]{:S(2)}) collective-permute-start(bf16[8,7168]{1,0:T(8,128)(2,1)S(1)} %add_convert_fusion.4), channel_id=1, source_target_pairs={{0,8},{1,9},{2,10},{3,11},{4,12},{5,13},{6,14},{7,15},{8,0},{9,1},... | collective-permute-start | bytes 344072 | tf_op jit(solution)/shard_map/ppermute | solution.py:27
  54.4 5.2 %collective-permute-start.26 = (bf16[8,7168]{1,0:T(8,128)(2,1)S(1)}, bf16[8,7168]{1,0:T(8,128)(2,1)S(1)}, u32[]{:S(2)}, u32[]{:S(2)}) collective-permute-start(bf16[8,7168]{1,0:T(8,128)(2,1)S(1)} %add_convert_fusion.2), channel_id=1, source_target_pairs={{0,12},{1,13},{2,14},{3,15},{4,0},{5,1},{6,2},{7,3},{8,4},{9,5},{1... | collective-permute-start | bytes 344072 | tf_op jit(solution)/shard_map/ppermute | solution.py:27
  (12 other events, 144.9 us)

commit v10 on v9

--- a/solution.py
+++ b/solution.py
@@ -169,26 +169,24 @@
     )(place, moved, lengths, query_t, own, cache_t, *extra)
 
 
-def settle_body(place, moved, first, second, returned, out):
+def settle_body(place, moved, stay, returned, out):
     leaving = moved[place[0]]
-    stay = [first[i] for i in range(first.shape[0])] + [second[i] for i in range(second.shape[0])]
     for j in range(out.shape[0]):
         below = stay[max(j - 1, 0)]
-        same = stay[min(j, len(stay) - 1)]
+        same = stay[min(j, stay.shape[0] - 1)]
         here = jnp.where(leaving < j, below, same)
         out[j] = jnp.where(leaving == j, returned[...], here)
 
 
-def settle(place, moved, first, second, returned):
-    count = first.shape[0] + second.shape[0] + 1
+def settle(place, moved, stay, returned):
     return pl.pallas_call(
         settle_body,
-        out_shape=jax.ShapeDtypeStruct((count,) + returned.shape, returned.dtype),
-        in_specs=[SCALARS, SCALARS] + [WHOLE] * 3,
+        out_shape=jax.ShapeDtypeStruct((stay.shape[0] + 1,) + returned.shape, returned.dtype),
+        in_specs=[SCALARS, SCALARS, WHOLE, WHOLE],
         out_specs=WHOLE,
         compiler_params=pltpu.CompilerParams(vmem_limit_bytes=40 * MIB),
         cost_estimate=pl.CostEstimate(flops=0, bytes_accessed=0, transcendentals=0),
-    )(place, moved, first, second, returned)
+    )(place, moved, stay, returned)
 
 
 def expert_body(count, groups, sizes, place, w_gate, w_up, w_down, *refs):
@@ -281,17 +279,18 @@
     columns = {r: rotated(rows, axis, r) for r in order}
     across = {0: swapped(rows, axis, 2)}
 
-    half = requests // 2
-    scalars = (place, moved_slot, cache_lengths)
-    new_here, _ = lax.optimization_barrier((new_latent, rows))
-    (first,) = attend(tuple(range(half)), *scalars, query_t, new_here, cache_t)
-    columns, across, visiting, first = lax.optimization_barrier((columns, across, visiting, first))
-
+    stay, away = attend(
+        tuple(range(requests - 1)),
+        place,
+        moved_slot,
+        cache_lengths,
+        query_t,
+        new_latent,
+        cache_t,
+        visiting,
+    )
+    columns, across, away = lax.optimization_barrier((columns, across, away))
     later = {r: swapped(columns[r], axis, 2) for r in order}
-    second, away = attend(
-        tuple(range(half, requests - 1)), *scalars, query_t, new_latent, cache_t, visiting
-    )
-    later, away = lax.optimization_barrier((later, away))
     across.update(later)
     columns[0] = rows
 
@@ -302,18 +301,20 @@
     outs = expert(place, w_gate, w_up, w_down, blocks, groups, sizes)
     keeps, sends = outs[: len(near)], outs[len(near) :]
 
-    sums = {}
-    for i, r in enumerate(order):
-        chip = swapped(sends[i], axis, 1)
-        over = swapped(added(keeps[2 * i], chip[:tokens]), axis, 2)
-        if i == len(order) - 2:
-            over, away = lax.optimization_barrier((over, away))
-        sums[r] = [keeps[2 * i + 1], chip[tokens:], over]
+    chips = [swapped(send, axis, 1) for send in sends]
+    leaves = [added(keeps[2 * i], chip[:tokens]) for i, chip in enumerate(chips)]
+    overs = [swapped(leaf, axis, 2) for leaf in leaves[:-1]]
+    overs[0], leaves[-1] = lax.optimization_barrier((overs[0], leaves[-1]))
+    overs[-1], away = lax.optimization_barrier((overs[-1], away))
+    overs.append(swapped(leaves[-1], axis, 2))
+    sums = {
+        r: [keeps[2 * i + 1], chips[i][tokens:], overs[i]] for i, r in enumerate(order)
+    }
     terms = sums.pop(0)
     for r in sums:
         terms = terms + [rotated(added(*sums[r]), axis, -r)]
     returned = shifted(away, axis, 1)
-    attn_out = settle(place, moved_slot, first, second, returned)
+    attn_out = settle(place, moved_slot, stay, returned)
     _, terms = lax.optimization_barrier((attn_out, terms))
     moe_out = added(*terms)
     return (moe_out, attn_out)

time: 60.6 us -> 56.1 us (0.926)
  the two profiles are of different devices: /device:TPU:0 before, /device:TPU:13 now
where the time goes in v10:
time: 56.1 us; the launch traced here: 55.9 us
  starting transfers between devices  29.3 us (52%)
  waiting for transfers between devices  13 us (23%)
  Pallas kernels  11.7 us (21%)
  other arithmetic  1 us (2%)
  between operations  0.8 us (1%)
    ppermute x20, starting transfers between devices, swapped(): return lax.ppermute(value, axis, pairs)  16.1 us
    ppermute x8, starting transfers between devices, shifted(): return lax.ppermute(value, axis, pairs)  13.2 us
    ppermute x8, waiting for transfers between devices, shifted(): return lax.ppermute(value, axis, pairs)  7.51 us
    pallas_call x1, Pallas kernels, attend(): pl.pallas_call(functools.partial(attend_body, ranks, visits), out_shape=[...  6.53 us
    ppermute x20, waiting for transfers between devices, swapped(): return lax.ppermute(value, axis, pairs)  5.48 us
    pallas_call x1, Pallas kernels, prepare(): pl.pallas_call(functools.partial(prepare_body, groups), out_shape=[jax.Sh...  2.05 us
    pallas_call x1, Pallas kernels, expert(): pl.pallas_call(functools.partial(expert_body, count, groups, sizes), out_...  1.73 us
    pallas_call x1, Pallas kernels, settle(): pl.pallas_call(settle_body, out_shape=jax.ShapeDtypeStruct((stay.shape[0]...  1.39 us
  transfers between devices with their start and end apart: 28, of which 10 were waited for; matrix products, arithmetic and copies ran while one was open for 0% of the time, Pallas kernels for 14%

profile of v10, /device:TPU:13, one launch (start us, length us, event | category | flops | bytes accessed | tf_op | source)
XLA Modules:
  0.0 55.9 jit_solution(18264193677977651033)
XLA Ops:
  0.6 2.0 %shard_map.122 = (bf16[8,7296]{1,0:T(8,128)(2,1)}, bf16[592,128]{1,0:T(8,128)(2,1)}) custom-call(s32[1]{0:T(128)} %bitcast.place, s32[16]{0:T(128)} %moved.5, bf16[8,7168]{1,0:T(8,128)(2,1)} %hidden.1, s32[2,8]{1,0:T(2,128)} %bitcast.8, f32[2,8]{1,0:T(2,128)} %bitcast.9, bf16[4,576,128]{2,1,0:T(8,128)(2,1)} %bitcast.6, bf16[4,576]{1,0:T(4,128)(2,1)} %own.3), custom_call_target="tpu_custom_call" | custom-call | tf_op jit(solution)/shard_map/pallas_call | solution.py:75
  3.6 2.5 %collective-permute-start.2 = (bf16[8,7296]{1,0:T(8,128)(2,1)}, bf16[8,7296]{1,0:T(8,128)(2,1)S(1)}, u32[]{:S(2)}, u32[]{:S(2)}) collective-permute-start(bf16[8,7296]{1,0:T(8,128)(2,1)} %get-tuple-element.35.refs_7_), channel_id=1, source_target_pairs={{0,8},{1,9},{2,10},{3,11},{4,12},{5,13},{6,14},{7,15},{8,0},{9,1},... | collective-permute-start | bytes 350216 | tf_op jit(solution)/shard_map/ppermute | solution.py:27
  6.1 2.2 %collective-permute-start.1 = (bf16[8,7296]{1,0:T(8,128)(2,1)}, bf16[8,7296]{1,0:T(8,128)(2,1)S(1)}, u32[]{:S(2)}, u32[]{:S(2)}) collective-permute-start(bf16[8,7296]{1,0:T(8,128)(2,1)} %get-tuple-element.35.refs_7_), channel_id=1, source_target_pairs={{0,4},{1,5},{2,6},{3,7},{4,8},{5,9},{6,10},{7,11},{8,12},{9,13},{1... | collective-permute-start | bytes 350216 | tf_op jit(solution)/shard_map/ppermute | solution.py:27
  8.3 1.4 %collective-permute-done.refs_0_ = bf16[592,128]{1,0:T(8,128)(2,1)S(1)} collective-permute-done((bf16[592,128]{1,0:T(8,128)(2,1)}, bf16[592,128]{1,0:T(8,128)(2,1)S(1)}, u32[]{:S(2)}, u32[]{:S(2)}) %collective-permute-start) | collective-permute-done | bytes 151584 | tf_op jit(solution)/shard_map/ppermute | solution.py:27
  10.3 6.5 %shard_map.123 = (bf16[3,128,512]{2,1,0:T(8,128)(2,1)}, bf16[128,512]{1,0:T(8,128)(2,1)}) custom-call(s32[1]{0:T(128)} %bitcast.place, s32[16]{0:T(128)} %moved.5, s32[64]{0:T(128)} %lengths.1, bf16[4,576,128]{2,1,0:T(8,128)(2,1)} %bitcast.7, bf16[4,576]{1,0:T(4,128)(2,1)} %own.3, bf16[4,576,1024]{2,1,0:T(8,128)(2,1)} %bitcast.5, bf16[592,128]{1,0:T(8,128)(2,1)} %copy-done.6), custom_call_target="tpu_custom_call" | custom-call | flops 1140850688 | tf_op jit(solution)/shard_map/pallas_call | solution.py:153
  17.6 2.6 %collective-permute-start.5 = (bf16[8,7296]{1,0:T(8,128)(2,1)S(1)}, bf16[8,7296]{1,0:T(8,128)(2,1)S(1)}, u32[]{:S(2)}, u32[]{:S(2)}) collective-permute-start(bf16[8,7296]{1,0:T(8,128)(2,1)S(1)} %collective-permute-done.2.refs_1_), channel_id=1, source_target_pairs={{0,2},{1,3},{2,0},{3,1},{4,6},{5,7},{6,4},{7,5},{8,10},{9,11},{10,... | collective-permute-start | bytes 350216 | tf_op jit(solution)/shard_map/ppermute | solution.py:36
  20.2 1.4 %collective-permute-start.7 = (bf16[8,7296]{1,0:T(8,128)(2,1)S(1)}, bf16[8,7296]{1,0:T(8,128)(2,1)S(1)}, u32[]{:S(2)}, u32[]{:S(2)}) collective-permute-start(bf16[8,7296]{1,0:T(8,128)(2,1)S(1)} %collective-permute-done.3.refs_5_), channel_id=1, source_target_pairs={{0,2},{1,3},{2,0},{3,1},{4,6},{5,7},{6,4},{7,5},{8,10},{9,11},{10,... | collective-permute-start | bytes 350216 | tf_op jit(solution)/shard_map/ppermute | solution.py:36
  21.7 1.3 %collective-permute-start.11 = (bf16[8,7296]{1,0:T(8,128)(2,1)S(1)}, bf16[8,7296]{1,0:T(8,128)(2,1)S(1)}, u32[]{:S(2)}, u32[]{:S(2)}) collective-permute-start(bf16[8,7296]{1,0:T(8,128)(2,1)S(1)} %collective-permute-done.1.refs_3_), channel_id=1, source_target_pairs={{0,1},{1,0},{2,3},{3,2},{4,5},{5,4},{6,7},{7,6},{8,9},{9,8},{10,11... | collective-permute-start | bytes 350216 | tf_op jit(solution)/shard_map/ppermute | solution.py:36
  23.3 1.7 %collective-permute-start.8 = (bf16[8,7296]{1,0:T(8,128)(2,1)S(1)}, bf16[8,7296]{1,0:T(8,128)(2,1)S(1)}, u32[]{:S(2)}, u32[]{:S(2)}) collective-permute-start(bf16[8,7296]{1,0:T(8,128)(2,1)S(1)} %collective-permute-done.5.refs_0_), channel_id=1, source_target_pairs={{0,1},{1,0},{2,3},{3,2},{4,5},{5,4},{6,7},{7,6},{8,9},{9,8},{10,11... | collective-permute-start | bytes 350216 | tf_op jit(solution)/shard_map/ppermute | solution.py:36
  25.8 1.7 %collective-permute-start.10 = (bf16[8,7296]{1,0:T(8,128)(2,1)S(1)}, bf16[8,7296]{1,0:T(8,128)(2,1)S(1)}, u32[]{:S(2)}, u32[]{:S(2)}) collective-permute-start(bf16[8,7296]{1,0:T(8,128)(2,1)S(1)} %collective-permute-done.6.refs_2_), channel_id=1, source_target_pairs={{0,1},{1,0},{2,3},{3,2},{4,5},{5,4},{6,7},{7,6},{8,9},{9,8},{10,11... | collective-permute-start | bytes 350216 | tf_op jit(solution)/shard_map/ppermute | solution.py:36
  28.3 1.0 %collective-permute-start.12 = (bf16[8,7296]{1,0:T(8,128)(2,1)S(1)}, bf16[8,7296]{1,0:T(8,128)(2,1)S(1)}, u32[]{:S(2)}, u32[]{:S(2)}) collective-permute-start(bf16[8,7296]{1,0:T(8,128)(2,1)S(1)} %collective-permute-done.7.refs_4_), channel_id=1, source_target_pairs={{0,1},{1,0},{2,3},{3,2},{4,5},{5,4},{6,7},{7,6},{8,9},{9,8},{10,11... | collective-permute-start | bytes 350216 | tf_op jit(solution)/shard_map/ppermute | solution.py:36
  29.4 0.9 %collective-permute-done.12.refs_12_ = bf16[8,7296]{1,0:T(8,128)(2,1)S(1)} collective-permute-done((bf16[8,7296]{1,0:T(8,128)(2,1)S(1)}, bf16[8,7296]{1,0:T(8,128)(2,1)S(1)}, u32[]{:S(2)}, u32[]{:S(2)}) %collective-permute-start.12) | collective-permute-done | bytes 116768 | tf_op jit(solution)/shard_map/ppermute | solution.py:36
  30.3 1.7 %shard_map.124 = (bf16[8,7168]{1,0:T(8,128)(2,1)S(1)}, bf16[8,7168]{1,0:T(8,128)(2,1)S(1)}, bf16[8,7168]{1,0:T(8,128)(2,1)S(1)}, bf16[8,7168]{1,0:T(8,128)(2,1)S...) custom-call(s32[1]{0:T(128)} %bitcast.place, ...), custom_call_target="tpu_custom_call" | custom-call | flops 704643072 | bytes 5505024 | tf_op jit(solution)/shard_map/pallas_call | solution.py:228
  33.7 1.5 %collective-permute-start.17 = (bf16[8,7168]{1,0:T(8,128)(2,1)S(1)}, bf16[8,7168]{1,0:T(8,128)(2,1)S(1)}, u32[]{:S(2)}, u32[]{:S(2)}) collective-permute-start(bf16[8,7168]{1,0:T(8,128)(2,1)S(1)} %add_convert_fusion.7), channel_id=1, source_target_pairs={{0,2},{1,3},{2,0},{3,1},{4,6},{5,7},{6,4},{7,5},{8,10},{9,11},{10,... | collective-permute-start | bytes 344072 | tf_op jit(solution)/shard_map/ppermute | solution.py:36
  36.0 0.9 %collective-permute-start.25 = (bf16[8,7168]{1,0:T(8,128)(2,1)S(1)}, bf16[8,7168]{1,0:T(8,128)(2,1)S(1)}, u32[]{:S(2)}, u32[]{:S(2)}) collective-permute-start(bf16[8,7168]{1,0:T(8,128)(2,1)S(1)} %add_convert_fusion.3), channel_id=1, source_target_pairs={{0,2},{1,3},{2,0},{3,1},{4,6},{5,7},{6,4},{7,5},{8,10},{9,11},{10,... | collective-permute-start | bytes 344072 | tf_op jit(solution)/shard_map/ppermute | solution.py:36
  36.9 1.2 %collective-permute-done.17 = bf16[8,7168]{1,0:T(8,128)(2,1)S(1)} collective-permute-done((bf16[8,7168]{1,0:T(8,128)(2,1)S(1)}, bf16[8,7168]{1,0:T(8,128)(2,1)S(1)}, u32[]{:S(2)}, u32[]{:S(2)}) %collective-permute-start.17) | collective-permute-done | bytes 114720 | tf_op jit(solution)/shard_map/ppermute | solution.py:36
  38.2 2.2 %collective-permute-start.27 = (bf16[8,7168]{1,0:T(8,128)(2,1)S(1)}, bf16[8,7168]{1,0:T(8,128)(2,1)S(1)}, u32[]{:S(2)}, u32[]{:S(2)}) collective-permute-start(bf16[8,7168]{1,0:T(8,128)(2,1)S(1)} %add_convert_fusion.1), channel_id=1, source_target_pairs={{0,4},{1,5},{2,6},{3,7},{4,8},{5,9},{6,10},{7,11},{8,12},{9,13},{1... | collective-permute-start | bytes 344072 | tf_op jit(solution)/shard_map/ppermute | solution.py:27
  40.3 3.1 %collective-permute-start.18 = (bf16[128,512]{1,0:T(8,128)(2,1)S(1)}, bf16[128,512]{1,0:T(8,128)(2,1)S(1)}, u32[]{:S(2)}, u32[]{:S(2)}) collective-permute-start(bf16[128,512]{1,0:T(8,128)(2,1)S(1)} %copy-done.7), channel_id=1, source_target_pairs={{0,1},{1,2},{2,3},{3,4},{4,5},{5,6},{6,7},{7,8},{8,9},{9,10},{10,1... | collective-permute-start | bytes 393224 | tf_op jit(solution)/shard_map/ppermute | solution.py:27
  44.0 1.2 %collective-permute-start.23 = (bf16[8,7168]{1,0:T(8,128)(2,1)S(1)}, bf16[8,7168]{1,0:T(8,128)(2,1)S(1)}, u32[]{:S(2)}, u32[]{:S(2)}) collective-permute-start(bf16[8,7168]{1,0:T(8,128)(2,1)S(1)} %add_convert_fusion.4), channel_id=1, source_target_pairs={{0,8},{1,9},{2,10},{3,11},{4,12},{5,13},{6,14},{7,15},{8,0},{9,1},... | collective-permute-start | bytes 344072 | tf_op jit(solution)/shard_map/ppermute | solution.py:27
  45.3 1.3 %collective-permute-start.26 = (bf16[8,7168]{1,0:T(8,128)(2,1)S(1)}, bf16[8,7168]{1,0:T(8,128)(2,1)S(1)}, u32[]{:S(2)}, u32[]{:S(2)}) collective-permute-start(bf16[8,7168]{1,0:T(8,128)(2,1)S(1)} %add_convert_fusion.2), channel_id=1, source_target_pairs={{0,12},{1,13},{2,14},{3,15},{4,0},{5,1},{6,2},{7,3},{8,4},{9,5},{1... | collective-permute-start | bytes 344072 | tf_op jit(solution)/shard_map/ppermute | solution.py:27
  46.7 1.4 %shard_map.125 = bf16[4,128,512]{2,1,0:T(8,128)(2,1)} custom-call(s32[1]{0:T(128)} %bitcast.place, s32[16]{0:T(128)S(1)} %copy-done.5, bf16[3,128,512]{2,1,0:T(8,128)(2,1)S(1)} %copy-done.3, bf16[128,512]{1,0:T(8,128)(2,1)S(1)} %collective-permute-done.18.returned), custom_call_target="tpu_custom_call" | custom-call | tf_op jit(solution)/shard_map/pallas_call | solution.py:182
  48.1 1.0 %collective-permute-done.22 = bf16[8,7168]{1,0:T(8,128)(2,1)S(1)} collective-permute-done((bf16[8,7168]{1,0:T(8,128)(2,1)S(1)}, bf16[8,7168]{1,0:T(8,128)(2,1)S(1)}, u32[]{:S(2)}, u32[]{:S(2)}) %collective-permute-start.22) | collective-permute-done | bytes 114720 | tf_op jit(solution)/shard_map/ppermute | solution.py:36
  49.1 3.0 %collective-permute-done.23 = bf16[8,7168]{1,0:T(8,128)(2,1)S(1)} collective-permute-done((bf16[8,7168]{1,0:T(8,128)(2,1)S(1)}, bf16[8,7168]{1,0:T(8,128)(2,1)S(1)}, u32[]{:S(2)}, u32[]{:S(2)}) %collective-permute-start.23) | collective-permute-done | bytes 114720 | tf_op jit(solution)/shard_map/ppermute | solution.py:27
  52.1 3.1 %collective-permute-done.26 = bf16[8,7168]{1,0:T(8,128)(2,1)S(1)} collective-permute-done((bf16[8,7168]{1,0:T(8,128)(2,1)S(1)}, bf16[8,7168]{1,0:T(8,128)(2,1)S(1)}, u32[]{:S(2)}, u32[]{:S(2)}) %collective-permute-start.26) | collective-permute-done | bytes 114720 | tf_op jit(solution)/shard_map/ppermute | solution.py:27
  (61 shorter events, 8.0 us)
Async XLA Ops:
  2.7 7.0 %collective-permute-start = (bf16[592,128]{1,0:T(8,128)(2,1)}, bf16[592,128]{1,0:T(8,128)(2,1)S(1)}, u32[]{:S(2)}, u32[]{:S(2)}) collective-permute-start(bf16[592,128]{1,0:T(8,128)(2,1)} %get-tuple-element.33), channel_id=1, source_target_pairs={{0,15},{1,0},{2,1},{3,2},{4,3},{5,4},{6,5},{7,6},{8,7},{9,8},{10,9... | collective-permute-start | bytes 454664 | tf_op jit(solution)/shard_map/ppermute | solution.py:27
  3.4 13.5 %collective-permute-start.4 = (bf16[8,7296]{1,0:T(8,128)(2,1)}, bf16[8,7296]{1,0:T(8,128)(2,1)S(1)}, u32[]{:S(2)}, u32[]{:S(2)}) collective-permute-start(bf16[8,7296]{1,0:T(8,128)(2,1)} %get-tuple-element.35.refs_7_), channel_id=1, source_target_pairs={{0,2},{1,3},{2,0},{3,1},{4,6},{5,7},{6,4},{7,5},{8,10},{9,11},{10,... | collective-permute-start | bytes 350216 | tf_op jit(solution)/shard_map/ppermute | solution.py:36
  3.6 13.3 %collective-permute-start.3 = (bf16[8,7296]{1,0:T(8,128)(2,1)}, bf16[8,7296]{1,0:T(8,128)(2,1)S(1)}, u32[]{:S(2)}, u32[]{:S(2)}) collective-permute-start(bf16[8,7296]{1,0:T(8,128)(2,1)} %get-tuple-element.35.refs_7_), channel_id=1, source_target_pairs={{0,12},{1,13},{2,14},{3,15},{4,0},{5,1},{6,2},{7,3},{8,4},{9,5},{1... | collective-permute-start | bytes 350216 | tf_op jit(solution)/shard_map/ppermute | solution.py:27
  3.6 13.3 %collective-permute-start.2 = (bf16[8,7296]{1,0:T(8,128)(2,1)}, bf16[8,7296]{1,0:T(8,128)(2,1)S(1)}, u32[]{:S(2)}, u32[]{:S(2)}) collective-permute-start(bf16[8,7296]{1,0:T(8,128)(2,1)} %get-tuple-element.35.refs_7_), channel_id=1, source_target_pairs={{0,8},{1,9},{2,10},{3,11},{4,12},{5,13},{6,14},{7,15},{8,0},{9,1},... | collective-permute-start | bytes 350216 | tf_op jit(solution)/shard_map/ppermute | solution.py:27
  6.1 10.8 %collective-permute-start.1 = (bf16[8,7296]{1,0:T(8,128)(2,1)}, bf16[8,7296]{1,0:T(8,128)(2,1)S(1)}, u32[]{:S(2)}, u32[]{:S(2)}) collective-permute-start(bf16[8,7296]{1,0:T(8,128)(2,1)} %get-tuple-element.35.refs_7_), channel_id=1, source_target_pairs={{0,4},{1,5},{2,6},{3,7},{4,8},{5,9},{6,10},{7,11},{8,12},{9,13},{1... | collective-permute-start | bytes 350216 | tf_op jit(solution)/shard_map/ppermute | solution.py:27
  9.7 10.6 %collective-permute-start.15 = (bf16[8,7296]{1,0:T(8,128)(2,1)}, bf16[8,7296]{1,0:T(8,128)(2,1)S(1)}, u32[]{:S(2)}, u32[]{:S(2)}) collective-permute-start(bf16[8,7296]{1,0:T(8,128)(2,1)} %get-tuple-element.35.refs_7_), channel_id=1, source_target_pairs={{0,1},{1,0},{2,3},{3,2},{4,5},{5,4},{6,7},{7,6},{8,9},{9,8},{10,11... | collective-permute-start | bytes 350216 | tf_op jit(solution)/shard_map/ppermute | solution.py:36
  16.9 4.8 %collective-permute-start.14 = (bf16[8,7296]{1,0:T(8,128)(2,1)S(1)}, bf16[8,7296]{1,0:T(8,128)(2,1)S(1)}, u32[]{:S(2)}, u32[]{:S(2)}) collective-permute-start(bf16[8,7296]{1,0:T(8,128)(2,1)S(1)} %collective-permute-done.4.refs_6_), channel_id=1, source_target_pairs={{0,1},{1,0},{2,3},{3,2},{4,5},{5,4},{6,7},{7,6},{8,9},{9,8},{10,11... | collective-permute-start | bytes 350216 | tf_op jit(solution)/shard_map/ppermute | solution.py:36
  17.6 5.5 %collective-permute-start.9 = (bf16[8,7296]{1,0:T(8,128)(2,1)S(1)}, bf16[8,7296]{1,0:T(8,128)(2,1)S(1)}, u32[]{:S(2)}, u32[]{:S(2)}) collective-permute-start(bf16[8,7296]{1,0:T(8,128)(2,1)S(1)} %collective-permute-done.2.refs_1_), channel_id=1, source_target_pairs={{0,1},{1,0},{2,3},{3,2},{4,5},{5,4},{6,7},{7,6},{8,9},{9,8},{10,11... | collective-permute-start | bytes 350216 | tf_op jit(solution)/shard_map/ppermute | solution.py:36
  17.6 5.7 %collective-permute-start.5 = (bf16[8,7296]{1,0:T(8,128)(2,1)S(1)}, bf16[8,7296]{1,0:T(8,128)(2,1)S(1)}, u32[]{:S(2)}, u32[]{:S(2)}) collective-permute-start(bf16[8,7296]{1,0:T(8,128)(2,1)S(1)} %collective-permute-done.2.refs_1_), channel_id=1, source_target_pairs={{0,2},{1,3},{2,0},{3,1},{4,6},{5,7},{6,4},{7,5},{8,10},{9,11},{10,... | collective-permute-start | bytes 350216 | tf_op jit(solution)/shard_map/ppermute | solution.py:36
  20.2 5.6 %collective-permute-start.6 = (bf16[8,7296]{1,0:T(8,128)(2,1)S(1)}, bf16[8,7296]{1,0:T(8,128)(2,1)S(1)}, u32[]{:S(2)}, u32[]{:S(2)}) collective-permute-start(bf16[8,7296]{1,0:T(8,128)(2,1)S(1)} %collective-permute-done.1.refs_3_), channel_id=1, source_target_pairs={{0,2},{1,3},{2,0},{3,1},{4,6},{5,7},{6,4},{7,5},{8,10},{9,11},{10,... | collective-permute-start | bytes 350216 | tf_op jit(solution)/shard_map/ppermute | solution.py:36
  20.2 8.1 %collective-permute-start.7 = (bf16[8,7296]{1,0:T(8,128)(2,1)S(1)}, bf16[8,7296]{1,0:T(8,128)(2,1)S(1)}, u32[]{:S(2)}, u32[]{:S(2)}) collective-permute-start(bf16[8,7296]{1,0:T(8,128)(2,1)S(1)} %collective-permute-done.3.refs_5_), channel_id=1, source_target_pairs={{0,2},{1,3},{2,0},{3,1},{4,6},{5,7},{6,4},{7,5},{8,10},{9,11},{10,... | collective-permute-start | bytes 350216 | tf_op jit(solution)/shard_map/ppermute | solution.py:36
  21.7 7.7 %collective-permute-start.11 = (bf16[8,7296]{1,0:T(8,128)(2,1)S(1)}, bf16[8,7296]{1,0:T(8,128)(2,1)S(1)}, u32[]{:S(2)}, u32[]{:S(2)}) collective-permute-start(bf16[8,7296]{1,0:T(8,128)(2,1)S(1)} %collective-permute-done.1.refs_3_), channel_id=1, source_target_pairs={{0,1},{1,0},{2,3},{3,2},{4,5},{5,4},{6,7},{7,6},{8,9},{9,8},{10,11... | collective-permute-start | bytes 350216 | tf_op jit(solution)/shard_map/ppermute | solution.py:36
  23.0 6.3 %collective-permute-start.13 = (bf16[8,7296]{1,0:T(8,128)(2,1)S(1)}, bf16[8,7296]{1,0:T(8,128)(2,1)S(1)}, u32[]{:S(2)}, u32[]{:S(2)}) collective-permute-start(bf16[8,7296]{1,0:T(8,128)(2,1)S(1)} %collective-permute-done.3.refs_5_), channel_id=1, source_target_pairs={{0,1},{1,0},{2,3},{3,2},{4,5},{5,4},{6,7},{7,6},{8,9},{9,8},{10,11... | collective-permute-start | bytes 350216 | tf_op jit(solution)/shard_map/ppermute | solution.py:36
  23.3 6.1 %collective-permute-start.8 = (bf16[8,7296]{1,0:T(8,128)(2,1)S(1)}, bf16[8,7296]{1,0:T(8,128)(2,1)S(1)}, u32[]{:S(2)}, u32[]{:S(2)}) collective-permute-start(bf16[8,7296]{1,0:T(8,128)(2,1)S(1)} %collective-permute-done.5.refs_0_), channel_id=1, source_target_pairs={{0,1},{1,0},{2,3},{3,2},{4,5},{5,4},{6,7},{7,6},{8,9},{9,8},{10,11... | collective-permute-start | bytes 350216 | tf_op jit(solution)/shard_map/ppermute | solution.py:36
  25.8 3.6 %collective-permute-start.10 = (bf16[8,7296]{1,0:T(8,128)(2,1)S(1)}, bf16[8,7296]{1,0:T(8,128)(2,1)S(1)}, u32[]{:S(2)}, u32[]{:S(2)}) collective-permute-start(bf16[8,7296]{1,0:T(8,128)(2,1)S(1)} %collective-permute-done.6.refs_2_), channel_id=1, source_target_pairs={{0,1},{1,0},{2,3},{3,2},{4,5},{5,4},{6,7},{7,6},{8,9},{9,8},{10,11... | collective-permute-start | bytes 350216 | tf_op jit(solution)/shard_map/ppermute | solution.py:36
  32.5 4.4 %collective-permute-start.19 = (bf16[16,7168]{1,0:T(8,128)(2,1)S(1)}, bf16[16,7168]{1,0:T(8,128)(2,1)S(1)}, u32[]{:S(2)}, u32[]{:S(2)}) collective-permute-start(bf16[16,7168]{1,0:T(8,128)(2,1)S(1)} %get-tuple-element.46), channel_id=1, source_target_pairs={{0,1},{1,0},{2,3},{3,2},{4,5},{5,4},{6,7},{7,6},{8,9},{9,8},{10,11... | collective-permute-start | bytes 688136 | tf_op jit(solution)/shard_map/ppermute | solution.py:36
  33.7 4.4 %collective-permute-start.17 = (bf16[8,7168]{1,0:T(8,128)(2,1)S(1)}, bf16[8,7168]{1,0:T(8,128)(2,1)S(1)}, u32[]{:S(2)}, u32[]{:S(2)}) collective-permute-start(bf16[8,7168]{1,0:T(8,128)(2,1)S(1)} %add_convert_fusion.7), channel_id=1, source_target_pairs={{0,2},{1,3},{2,0},{3,1},{4,6},{5,7},{6,4},{7,5},{8,10},{9,11},{10,... | collective-permute-start | bytes 344072 | tf_op jit(solution)/shard_map/ppermute | solution.py:36
  35.3 8.2 %collective-permute-start.21 = (bf16[8,7168]{1,0:T(8,128)(2,1)S(1)}, bf16[8,7168]{1,0:T(8,128)(2,1)S(1)}, u32[]{:S(2)}, u32[]{:S(2)}) collective-permute-start(bf16[8,7168]{1,0:T(8,128)(2,1)S(1)} %add_convert_fusion.6), channel_id=1, source_target_pairs={{0,2},{1,3},{2,0},{3,1},{4,6},{5,7},{6,4},{7,5},{8,10},{9,11},{10,... | collective-permute-start | bytes 344072 | tf_op jit(solution)/shard_map/ppermute | solution.py:36
  36.0 9.3 %collective-permute-start.25 = (bf16[8,7168]{1,0:T(8,128)(2,1)S(1)}, bf16[8,7168]{1,0:T(8,128)(2,1)S(1)}, u32[]{:S(2)}, u32[]{:S(2)}) collective-permute-start(bf16[8,7168]{1,0:T(8,128)(2,1)S(1)} %add_convert_fusion.3), channel_id=1, source_target_pairs={{0,2},{1,3},{2,0},{3,1},{4,6},{5,7},{6,4},{7,5},{8,10},{9,11},{10,... | collective-permute-start | bytes 344072 | tf_op jit(solution)/shard_map/ppermute | solution.py:36
  38.2 9.9 %collective-permute-start.27 = (bf16[8,7168]{1,0:T(8,128)(2,1)S(1)}, bf16[8,7168]{1,0:T(8,128)(2,1)S(1)}, u32[]{:S(2)}, u32[]{:S(2)}) collective-permute-start(bf16[8,7168]{1,0:T(8,128)(2,1)S(1)} %add_convert_fusion.1), channel_id=1, source_target_pairs={{0,4},{1,5},{2,6},{3,7},{4,8},{5,9},{6,10},{7,11},{8,12},{9,13},{1... | collective-permute-start | bytes 344072 | tf_op jit(solution)/shard_map/ppermute | solution.py:27
  40.3 6.3 %collective-permute-start.18 = (bf16[128,512]{1,0:T(8,128)(2,1)S(1)}, bf16[128,512]{1,0:T(8,128)(2,1)S(1)}, u32[]{:S(2)}, u32[]{:S(2)}) collective-permute-start(bf16[128,512]{1,0:T(8,128)(2,1)S(1)} %copy-done.7), channel_id=1, source_target_pairs={{0,1},{1,2},{2,3},{3,4},{4,5},{5,6},{6,7},{7,8},{8,9},{9,10},{10,1... | collective-permute-start | bytes 393224 | tf_op jit(solution)/shard_map/ppermute | solution.py:27
  43.5 5.6 %collective-permute-start.22 = (bf16[8,7168]{1,0:T(8,128)(2,1)S(1)}, bf16[8,7168]{1,0:T(8,128)(2,1)S(1)}, u32[]{:S(2)}, u32[]{:S(2)}) collective-permute-start(bf16[8,7168]{1,0:T(8,128)(2,1)S(1)} %add_convert_fusion.5), channel_id=1, source_target_pairs={{0,2},{1,3},{2,0},{3,1},{4,6},{5,7},{6,4},{7,5},{8,10},{9,11},{10,... | collective-permute-start | bytes 344072 | tf_op jit(solution)/shard_map/ppermute | solution.py:36
  44.0 8.1 %collective-permute-start.23 = (bf16[8,7168]{1,0:T(8,128)(2,1)S(1)}, bf16[8,7168]{1,0:T(8,128)(2,1)S(1)}, u32[]{:S(2)}, u32[]{:S(2)}) collective-permute-start(bf16[8,7168]{1,0:T(8,128)(2,1)S(1)} %add_convert_fusion.4), channel_id=1, source_target_pairs={{0,8},{1,9},{2,10},{3,11},{4,12},{5,13},{6,14},{7,15},{8,0},{9,1},... | collective-permute-start | bytes 344072 | tf_op jit(solution)/shard_map/ppermute | solution.py:27
  45.3 9.9 %collective-permute-start.26 = (bf16[8,7168]{1,0:T(8,128)(2,1)S(1)}, bf16[8,7168]{1,0:T(8,128)(2,1)S(1)}, u32[]{:S(2)}, u32[]{:S(2)}) collective-permute-start(bf16[8,7168]{1,0:T(8,128)(2,1)S(1)} %add_convert_fusion.2), channel_id=1, source_target_pairs={{0,12},{1,13},{2,14},{3,15},{4,0},{5,1},{6,2},{7,3},{8,4},{9,5},{1... | collective-permute-start | bytes 344072 | tf_op jit(solution)/shard_map/ppermute | solution.py:27
  (12 other events, 136.7 us)

commit v11 on v10

--- a/solution.py
+++ b/solution.py
@@ -83,6 +83,12 @@
         compiler_params=pltpu.CompilerParams(vmem_limit_bytes=60 * MIB),
         cost_estimate=pl.CostEstimate(flops=0, bytes_accessed=0, transcendentals=0),
     )(place, moved, hidden, ids_t, gates_t, query_t, own)
+
+
+def slanted(value, axis, steps):
+    count = lax.axis_size(axis)
+    pairs = [(source, ((source + 4 * steps) % count) ^ 2) for source in range(count)]
+    return lax.ppermute(value, axis, pairs)
 
 
 def attend_body(ranks, visits, place, moved, lengths, query, own, cache, *refs):
@@ -274,11 +280,9 @@
     )
 
     visiting = shifted(payload, axis, -1)
-    order = list(range(1, turns))
-    order = order[1:2] + order[:1] + order[2:]
-    columns = {r: rotated(rows, axis, r) for r in order}
+    far = list(range(2, turns))
+    columns = {r: rotated(rows, axis, r) for r in far}
     across = {0: swapped(rows, axis, 2)}
-
     stay, away = attend(
         tuple(range(requests - 1)),
         place,
@@ -289,12 +293,16 @@
         cache_t,
         visiting,
     )
-    columns, across, away = lax.optimization_barrier((columns, across, away))
-    later = {r: swapped(columns[r], axis, 2) for r in order}
-    across.update(later)
+    columns, across, rows_then, away = lax.optimization_barrier((columns, across, rows, away))
+
+    across.update({r: swapped(columns[r], axis, 2) for r in far})
+    across[1], columns[1] = slanted(rows_then, axis, 1), rotated(rows_then, axis, 1)
+    last = ({r: across.pop(r) for r in far + [1]}, columns.pop(1))
+    last, columns[1] = lax.optimization_barrier(last)
+    across.update(last)
     columns[0] = rows
 
-    order = order + [0]
+    order = far + [1, 0]
     near = [block for r in order for block in (across[r], columns[r])]
     blocks = near + [swapped(block, axis, 1) for block in near]
     sizes = [1] * len(near) + [2] * len(order)
@@ -303,16 +311,14 @@
 
     chips = [swapped(send, axis, 1) for send in sends]
     leaves = [added(keeps[2 * i], chip[:tokens]) for i, chip in enumerate(chips)]
-    overs = [swapped(leaf, axis, 2) for leaf in leaves[:-1]]
-    overs[0], leaves[-1] = lax.optimization_barrier((overs[0], leaves[-1]))
-    overs[-1], away = lax.optimization_barrier((overs[-1], away))
-    overs.append(swapped(leaves[-1], axis, 2))
-    sums = {
-        r: [keeps[2 * i + 1], chips[i][tokens:], overs[i]] for i, r in enumerate(order)
-    }
-    terms = sums.pop(0)
-    for r in sums:
-        terms = terms + [rotated(added(*sums[r]), axis, -r)]
+    rests = [[keeps[2 * i + 1], chip[tokens:]] for i, chip in enumerate(chips)]
+    overs = [swapped(leaf, axis, 2) for leaf in leaves[: len(far)]]
+    terms = [slanted(leaves[-2], axis, -1), rotated(added(*rests[-2]), axis, -1)]
+    overs[-1], terms = lax.optimization_barrier((overs[-1], terms))
+    overs[0], leaves[-1], away = lax.optimization_barrier((overs[0], leaves[-1], away))
+    terms = terms + rests[-1] + [swapped(leaves[-1], axis, 2)]
+    for r, rest, over in zip(far, rests, overs):
+        terms = terms + [rotated(added(*rest, over), axis, -r)]
     returned = shifted(away, axis, 1)
     attn_out = settle(place, moved_slot, stay, returned)
     _, terms = lax.optimization_barrier((attn_out, terms))

time: 56.1 us -> 56.9 us (1.014)
  the two profiles are of different devices: /device:TPU:13 before, /device:TPU:0 now
where the time goes in v11:
time: 56.9 us; the launch traced here: 56.8 us
  starting transfers between devices  21.5 us (38%)
  waiting for transfers between devices  21.1 us (37%)
  Pallas kernels  11.7 us (21%)
  other arithmetic  1 us (2%)
  between operations  0.8 us (1%)
  local copies, waits for them, and re-layouts  0.7 us (1%)
    ppermute x8, waiting for transfers between devices, shifted(): return lax.ppermute(value, axis, pairs)  13.2 us
    ppermute x8, starting transfers between devices, shifted(): return lax.ppermute(value, axis, pairs)  10.5 us
    ppermute x18, starting transfers between devices, swapped(): return lax.ppermute(value, axis, pairs)  8.79 us
    pallas_call x1, Pallas kernels, attend(): pl.pallas_call(functools.partial(attend_body, ranks, visits), out_shape=[...  6.54 us
    ppermute x18, waiting for transfers between devices, swapped(): return lax.ppermute(value, axis, pairs)  4.1 us
    ppermute x2, waiting for transfers between devices, slanted(): return lax.ppermute(value, axis, pairs)  3.82 us
    ppermute x2, starting transfers between devices, slanted(): return lax.ppermute(value, axis, pairs)  2.22 us
    pallas_call x1, Pallas kernels, prepare(): pl.pallas_call(functools.partial(prepare_body, groups), out_shape=[jax.Sh...  2.04 us
  transfers between devices with their start and end apart: 28, of which 14 were waited for; matrix products, arithmetic and copies ran while one was open for 0% of the time, Pallas kernels for 14%

profile of v11, /device:TPU:0, one launch (start us, length us, event | category | flops | bytes accessed | tf_op | source)
XLA Modules:
  0.0 56.8 jit_solution(10389099082146194463)
XLA Ops:
  0.6 2.0 %shard_map.122 = (bf16[8,7296]{1,0:T(8,128)(2,1)}, bf16[592,128]{1,0:T(8,128)(2,1)}) custom-call(s32[1]{0:T(128)} %bitcast.place, s32[16]{0:T(128)} %moved.5, bf16[8,7168]{1,0:T(8,128)(2,1)} %hidden.1, s32[2,8]{1,0:T(2,128)} %bitcast.8, f32[2,8]{1,0:T(2,128)} %bitcast.9, bf16[4,576,128]{2,1,0:T(8,128)(2,1)} %bitcast.6, bf16[4,576]{1,0:T(4,128)(2,1)} %own.3), custom_call_target="tpu_custom_call" | custom-call | tf_op jit(solution)/shard_map/pallas_call | solution.py:75
  2.7 5.4 %collective-permute-start = (bf16[592,128]{1,0:T(8,128)(2,1)}, bf16[592,128]{1,0:T(8,128)(2,1)S(1)}, u32[]{:S(2)}, u32[]{:S(2)}) collective-permute-start(bf16[592,128]{1,0:T(8,128)(2,1)} %get-tuple-element.40), channel_id=1, source_target_pairs={{0,15},{1,0},{2,1},{3,2},{4,3},{5,4},{6,5},{7,6},{8,7},{9,8},{10,9... | collective-permute-start | bytes 454664 | tf_op jit(solution)/shard_map/ppermute | solution.py:27
  8.1 1.1 %collective-permute-start.2 = (bf16[8,7296]{1,0:T(8,128)(2,1)}, bf16[8,7296]{1,0:T(8,128)(2,1)S(1)}, u32[]{:S(2)}, u32[]{:S(2)}) collective-permute-start(bf16[8,7296]{1,0:T(8,128)(2,1)} %get-tuple-element.44.refs_7_), channel_id=1, source_target_pairs={{0,12},{1,13},{2,14},{3,15},{4,0},{5,1},{6,2},{7,3},{8,4},{9,5},{1... | collective-permute-start | bytes 350216 | tf_op jit(solution)/shard_map/ppermute | solution.py:27
  9.3 3.3 %collective-permute-done.refs_0_ = bf16[592,128]{1,0:T(8,128)(2,1)S(1)} collective-permute-done((bf16[592,128]{1,0:T(8,128)(2,1)}, bf16[592,128]{1,0:T(8,128)(2,1)S(1)}, u32[]{:S(2)}, u32[]{:S(2)}) %collective-permute-start) | collective-permute-done | bytes 151584 | tf_op jit(solution)/shard_map/ppermute | solution.py:27
  12.5 0.7 %copy-done.6 = bf16[592,128]{1,0:T(8,128)(2,1)} copy-done((bf16[592,128]{1,0:T(8,128)(2,1)}, bf16[592,128]{1,0:T(8,128)(2,1)S(1)}, u32[]{:S(2)}) %copy-start.6) | copy-done | bytes 151576
  13.2 6.5 %shard_map.123 = (bf16[3,128,512]{2,1,0:T(8,128)(2,1)}, bf16[128,512]{1,0:T(8,128)(2,1)}) custom-call(s32[1]{0:T(128)} %bitcast.place, s32[16]{0:T(128)} %moved.5, s32[64]{0:T(128)} %lengths.1, bf16[4,576,128]{2,1,0:T(8,128)(2,1)} %bitcast.7, bf16[4,576]{1,0:T(4,128)(2,1)} %own.3, bf16[4,576,1024]{2,1,0:T(8,128)(2,1)} %bitcast.5, bf16[592,128]{1,0:T(8,128)(2,1)} %copy-done.6), custom_call_target="tpu_custom_call" | custom-call | flops 1140850688 | tf_op jit(solution)/shard_map/pallas_call | solution.py:159
  19.8 1.0 %collective-permute-start.4 = (bf16[8,7296]{1,0:T(8,128)(2,1)S(1)}, bf16[8,7296]{1,0:T(8,128)(2,1)S(1)}, u32[]{:S(2)}, u32[]{:S(2)}) collective-permute-start(bf16[8,7296]{1,0:T(8,128)(2,1)S(1)} %copy-done.4), channel_id=1, source_target_pairs={{0,6},{1,7},{2,4},{3,5},{4,10},{5,11},{6,8},{7,9},{8,14},{9,15},{1... | collective-permute-start | bytes 350216 | tf_op jit(solution)/shard_map/ppermute | solution.py:91
  20.9 0.7 %collective-permute-start.5 = (bf16[8,7296]{1,0:T(8,128)(2,1)S(1)}, bf16[8,7296]{1,0:T(8,128)(2,1)S(1)}, u32[]{:S(2)}, u32[]{:S(2)}) collective-permute-start(bf16[8,7296]{1,0:T(8,128)(2,1)S(1)} %collective-permute-done.1.refs_1_), channel_id=1, source_target_pairs={{0,2},{1,3},{2,0},{3,1},{4,6},{5,7},{6,4},{7,5},{8,10},{9,11},{10,... | collective-permute-start | bytes 350216 | tf_op jit(solution)/shard_map/ppermute | solution.py:36
  21.6 1.3 %collective-permute-start.6 = (bf16[8,7296]{1,0:T(8,128)(2,1)S(1)}, bf16[8,7296]{1,0:T(8,128)(2,1)S(1)}, u32[]{:S(2)}, u32[]{:S(2)}) collective-permute-start(bf16[8,7296]{1,0:T(8,128)(2,1)S(1)} %collective-permute-done.2.refs_3_), channel_id=1, source_target_pairs={{0,2},{1,3},{2,0},{3,1},{4,6},{5,7},{6,4},{7,5},{8,10},{9,11},{10,... | collective-permute-start | bytes 350216 | tf_op jit(solution)/shard_map/ppermute | solution.py:36
  23.3 4.1 %collective-permute-done.7.refs_5_ = bf16[8,7296]{1,0:T(8,128)(2,1)S(1)} collective-permute-done((bf16[8,7296]{1,0:T(8,128)(2,1)S(1)}, bf16[8,7296]{1,0:T(8,128)(2,1)S(1)}, u32[]{:S(2)}, u32[]{:S(2)}) %collective-permute-start.7) | collective-permute-done | bytes 116768 | tf_op jit(solution)/shard_map/ppermute | solution.py:27
  27.4 1.2 %collective-permute-done.4.refs_4_ = bf16[8,7296]{1,0:T(8,128)(2,1)S(1)} collective-permute-done((bf16[8,7296]{1,0:T(8,128)(2,1)S(1)}, bf16[8,7296]{1,0:T(8,128)(2,1)S(1)}, u32[]{:S(2)}, u32[]{:S(2)}) %collective-permute-start.4) | collective-permute-done | bytes 116768 | tf_op jit(solution)/shard_map/ppermute | solution.py:91
  28.6 0.6 %collective-permute-start.9 = (bf16[8,7296]{1,0:T(8,128)(2,1)S(1)}, bf16[8,7296]{1,0:T(8,128)(2,1)S(1)}, u32[]{:S(2)}, u32[]{:S(2)}) collective-permute-start(bf16[8,7296]{1,0:T(8,128)(2,1)S(1)} %collective-permute-done.1.refs_1_), channel_id=1, source_target_pairs={{0,1},{1,0},{2,3},{3,2},{4,5},{5,4},{6,7},{7,6},{8,9},{9,8},{10,11... | collective-permute-start | bytes 350216 | tf_op jit(solution)/shard_map/ppermute | solution.py:36
  29.6 2.3 %collective-permute-done.6.refs_2_ = bf16[8,7296]{1,0:T(8,128)(2,1)S(1)} collective-permute-done((bf16[8,7296]{1,0:T(8,128)(2,1)S(1)}, bf16[8,7296]{1,0:T(8,128)(2,1)S(1)}, u32[]{:S(2)}, u32[]{:S(2)}) %collective-permute-start.6) | collective-permute-done | bytes 116768 | tf_op jit(solution)/shard_map/ppermute | solution.py:36
  33.9 1.7 %shard_map.124 = (bf16[8,7168]{1,0:T(8,128)(2,1)S(1)}, bf16[8,7168]{1,0:T(8,128)(2,1)S(1)}, bf16[8,7168]{1,0:T(8,128)(2,1)S(1)}, bf16[8,7168]{1,0:T(8,128)(2,1)S...) custom-call(s32[1]{0:T(128)} %bitcast.place, ...), custom_call_target="tpu_custom_call" | custom-call | flops 704643072 | bytes 5505024 | tf_op jit(solution)/shard_map/pallas_call | solution.py:234
  37.9 1.5 %collective-permute-start.21 = (bf16[8,7168]{1,0:T(8,128)(2,1)S(1)}, bf16[8,7168]{1,0:T(8,128)(2,1)S(1)}, u32[]{:S(2)}, u32[]{:S(2)}) collective-permute-start(bf16[8,7168]{1,0:T(8,128)(2,1)S(1)} %add_convert_fusion.5), channel_id=1, source_target_pairs={{0,2},{1,3},{2,0},{3,1},{4,6},{5,7},{6,4},{7,5},{8,10},{9,11},{10,... | collective-permute-start | bytes 344072 | tf_op jit(solution)/shard_map/ppermute | solution.py:36
  39.5 2.4 %collective-permute-start.24 = (bf16[8,7168]{1,0:T(8,128)(2,1)S(1)}, bf16[8,7168]{1,0:T(8,128)(2,1)S(1)}, u32[]{:S(2)}, u32[]{:S(2)}) collective-permute-start(bf16[8,7168]{1,0:T(8,128)(2,1)S(1)} %get-tuple-element.78), channel_id=1, source_target_pairs={{0,12},{1,13},{2,14},{3,15},{4,0},{5,1},{6,2},{7,3},{8,4},{9,5},{1... | collective-permute-start | bytes 344072 | tf_op jit(solution)/shard_map/ppermute | solution.py:27
  41.9 1.2 %collective-permute-start.23 = (bf16[8,7168]{1,0:T(8,128)(2,1)S(1)}, bf16[8,7168]{1,0:T(8,128)(2,1)S(1)}, u32[]{:S(2)}, u32[]{:S(2)}) collective-permute-start(bf16[8,7168]{1,0:T(8,128)(2,1)S(1)} %get-tuple-element.79), channel_id=1, source_target_pairs={{0,14},{1,15},{2,12},{3,13},{4,2},{5,3},{6,0},{7,1},{8,6},{9,7},{1... | collective-permute-start | bytes 344072 | tf_op jit(solution)/shard_map/ppermute | solution.py:91
  43.3 1.3 %collective-permute-start.25 = (bf16[8,7168]{1,0:T(8,128)(2,1)S(1)}, bf16[8,7168]{1,0:T(8,128)(2,1)S(1)}, u32[]{:S(2)}, u32[]{:S(2)}) collective-permute-start(bf16[8,7168]{1,0:T(8,128)(2,1)S(1)} %add_convert_fusion.6), channel_id=1, source_target_pairs={{0,2},{1,3},{2,0},{3,1},{4,6},{5,7},{6,4},{7,5},{8,10},{9,11},{10,... | collective-permute-start | bytes 344072 | tf_op jit(solution)/shard_map/ppermute | solution.py:36
  44.6 1.4 %collective-permute-start.26 = (bf16[8,7168]{1,0:T(8,128)(2,1)S(1)}, bf16[8,7168]{1,0:T(8,128)(2,1)S(1)}, u32[]{:S(2)}, u32[]{:S(2)}) collective-permute-start(bf16[8,7168]{1,0:T(8,128)(2,1)S(1)} %add_convert_fusion.2), channel_id=1, source_target_pairs={{0,8},{1,9},{2,10},{3,11},{4,12},{5,13},{6,14},{7,15},{8,0},{9,1},... | collective-permute-start | bytes 344072 | tf_op jit(solution)/shard_map/ppermute | solution.py:27
  46.0 2.6 %collective-permute-done.23 = bf16[8,7168]{1,0:T(8,128)(2,1)S(1)} collective-permute-done((bf16[8,7168]{1,0:T(8,128)(2,1)S(1)}, bf16[8,7168]{1,0:T(8,128)(2,1)S(1)}, u32[]{:S(2)}, u32[]{:S(2)}) %collective-permute-start.23) | collective-permute-done | bytes 114720 | tf_op jit(solution)/shard_map/ppermute | solution.py:91
  48.8 4.3 %collective-permute-done.19.returned = bf16[128,512]{1,0:T(8,128)(2,1)S(1)} collective-permute-done((bf16[128,512]{1,0:T(8,128)(2,1)S(1)}, bf16[128,512]{1,0:T(8,128)(2,1)S(1)}, u32[]{:S(2)}, u32[]{:S(2)}) %collective-permute-start.19) | collective-permute-done | bytes 131104 | tf_op jit(solution)/shard_map/ppermute | solution.py:27
  53.1 1.4 %shard_map.125 = bf16[4,128,512]{2,1,0:T(8,128)(2,1)} custom-call(s32[1]{0:T(128)} %bitcast.place, s32[16]{0:T(128)S(1)} %copy-done.5, bf16[3,128,512]{2,1,0:T(8,128)(2,1)S(1)} %copy-done.3, bf16[128,512]{1,0:T(8,128)(2,1)S(1)} %collective-permute-done.19.returned), custom_call_target="tpu_custom_call" | custom-call | tf_op jit(solution)/shard_map/pallas_call | solution.py:188
  54.5 1.5 %collective-permute-done.27 = bf16[8,7168]{1,0:T(8,128)(2,1)S(1)} collective-permute-done((bf16[8,7168]{1,0:T(8,128)(2,1)S(1)}, bf16[8,7168]{1,0:T(8,128)(2,1)S(1)}, u32[]{:S(2)}, u32[]{:S(2)}) %collective-permute-start.27) | collective-permute-done | bytes 114720 | tf_op jit(solution)/shard_map/ppermute | solution.py:27
  56.0 0.8 %add_convert_fusion = bf16[8,7168]{1,0:T(8,128)(2,1)} fusion(bf16[8,7168]{1,0:T(8,128)(2,1)S(1)} %collective-permute-done.27, bf16[8,7168]{1,0:T(8,128)(2,1)S(1)} %collective-permute-done.26, bf16[8,7168]{1,0:T(8,128)(2,1)S(1)} %collective-permute-done.25, bf16[8,7168]{1,0:T(8,128)(2,1)S(1)} %slice.37, bf16[8,7168]{1,0:T(8,128)(2,1)S(1)} %get-tuple-element.73, ...), kind=kLoop, calls=%fused_computation | loop fusion | flops 802816 | bytes 917504 | tf_op jit(solution)/shard_map/convert_element_type | solution.py:251
  (60 shorter events, 5.6 us)
Async XLA Ops:
  2.7 9.8 %collective-permute-start = (bf16[592,128]{1,0:T(8,128)(2,1)}, bf16[592,128]{1,0:T(8,128)(2,1)S(1)}, u32[]{:S(2)}, u32[]{:S(2)}) collective-permute-start(bf16[592,128]{1,0:T(8,128)(2,1)} %get-tuple-element.40), channel_id=1, source_target_pairs={{0,15},{1,0},{2,1},{3,2},{4,3},{5,4},{6,5},{7,6},{8,7},{9,8},{10,9... | collective-permute-start | bytes 454664 | tf_op jit(solution)/shard_map/ppermute | solution.py:27
  8.1 11.6 %collective-permute-start.3 = (bf16[8,7296]{1,0:T(8,128)(2,1)}, bf16[8,7296]{1,0:T(8,128)(2,1)S(1)}, u32[]{:S(2)}, u32[]{:S(2)}) collective-permute-start(bf16[8,7296]{1,0:T(8,128)(2,1)} %get-tuple-element.44.refs_7_), channel_id=1, source_target_pairs={{0,2},{1,3},{2,0},{3,1},{4,6},{5,7},{6,4},{7,5},{8,10},{9,11},{10,... | collective-permute-start | bytes 350216 | tf_op jit(solution)/shard_map/ppermute | solution.py:36
  8.1 11.6 %collective-permute-start.2 = (bf16[8,7296]{1,0:T(8,128)(2,1)}, bf16[8,7296]{1,0:T(8,128)(2,1)S(1)}, u32[]{:S(2)}, u32[]{:S(2)}) collective-permute-start(bf16[8,7296]{1,0:T(8,128)(2,1)} %get-tuple-element.44.refs_7_), channel_id=1, source_target_pairs={{0,12},{1,13},{2,14},{3,15},{4,0},{5,1},{6,2},{7,3},{8,4},{9,5},{1... | collective-permute-start | bytes 350216 | tf_op jit(solution)/shard_map/ppermute | solution.py:27
  9.3 10.5 %collective-permute-start.1 = (bf16[8,7296]{1,0:T(8,128)(2,1)}, bf16[8,7296]{1,0:T(8,128)(2,1)S(1)}, u32[]{:S(2)}, u32[]{:S(2)}) collective-permute-start(bf16[8,7296]{1,0:T(8,128)(2,1)} %get-tuple-element.44.refs_7_), channel_id=1, source_target_pairs={{0,8},{1,9},{2,10},{3,11},{4,12},{5,13},{6,14},{7,15},{8,0},{9,1},... | collective-permute-start | bytes 350216 | tf_op jit(solution)/shard_map/ppermute | solution.py:27
  19.8 7.6 %collective-permute-start.7 = (bf16[8,7296]{1,0:T(8,128)(2,1)S(1)}, bf16[8,7296]{1,0:T(8,128)(2,1)S(1)}, u32[]{:S(2)}, u32[]{:S(2)}) collective-permute-start(bf16[8,7296]{1,0:T(8,128)(2,1)S(1)} %copy-done.4), channel_id=1, source_target_pairs={{0,4},{1,5},{2,6},{3,7},{4,8},{5,9},{6,10},{7,11},{8,12},{9,13},{1... | collective-permute-start | bytes 350216 | tf_op jit(solution)/shard_map/ppermute | solution.py:27
  19.8 8.8 %collective-permute-start.4 = (bf16[8,7296]{1,0:T(8,128)(2,1)S(1)}, bf16[8,7296]{1,0:T(8,128)(2,1)S(1)}, u32[]{:S(2)}, u32[]{:S(2)}) collective-permute-start(bf16[8,7296]{1,0:T(8,128)(2,1)S(1)} %copy-done.4), channel_id=1, source_target_pairs={{0,6},{1,7},{2,4},{3,5},{4,10},{5,11},{6,8},{7,9},{8,14},{9,15},{1... | collective-permute-start | bytes 350216 | tf_op jit(solution)/shard_map/ppermute | solution.py:91
  20.9 8.4 %collective-permute-start.5 = (bf16[8,7296]{1,0:T(8,128)(2,1)S(1)}, bf16[8,7296]{1,0:T(8,128)(2,1)S(1)}, u32[]{:S(2)}, u32[]{:S(2)}) collective-permute-start(bf16[8,7296]{1,0:T(8,128)(2,1)S(1)} %collective-permute-done.1.refs_1_), channel_id=1, source_target_pairs={{0,2},{1,3},{2,0},{3,1},{4,6},{5,7},{6,4},{7,5},{8,10},{9,11},{10,... | collective-permute-start | bytes 350216 | tf_op jit(solution)/shard_map/ppermute | solution.py:36
  21.6 10.3 %collective-permute-start.6 = (bf16[8,7296]{1,0:T(8,128)(2,1)S(1)}, bf16[8,7296]{1,0:T(8,128)(2,1)S(1)}, u32[]{:S(2)}, u32[]{:S(2)}) collective-permute-start(bf16[8,7296]{1,0:T(8,128)(2,1)S(1)} %collective-permute-done.2.refs_3_), channel_id=1, source_target_pairs={{0,2},{1,3},{2,0},{3,1},{4,6},{5,7},{6,4},{7,5},{8,10},{9,11},{10,... | collective-permute-start | bytes 350216 | tf_op jit(solution)/shard_map/ppermute | solution.py:36
  22.9 9.1 %collective-permute-start.15 = (bf16[8,7296]{1,0:T(8,128)(2,1)S(1)}, bf16[8,7296]{1,0:T(8,128)(2,1)S(1)}, u32[]{:S(2)}, u32[]{:S(2)}) collective-permute-start(bf16[8,7296]{1,0:T(8,128)(2,1)S(1)} %copy-done.4), channel_id=1, source_target_pairs={{0,1},{1,0},{2,3},{3,2},{4,5},{5,4},{6,7},{7,6},{8,9},{9,8},{10,11... | collective-permute-start | bytes 350216 | tf_op jit(solution)/shard_map/ppermute | solution.py:36
  27.4 5.0 %collective-permute-start.14 = (bf16[8,7296]{1,0:T(8,128)(2,1)S(1)}, bf16[8,7296]{1,0:T(8,128)(2,1)S(1)}, u32[]{:S(2)}, u32[]{:S(2)}) collective-permute-start(bf16[8,7296]{1,0:T(8,128)(2,1)S(1)} %collective-permute-done.3.refs_6_), channel_id=1, source_target_pairs={{0,1},{1,0},{2,3},{3,2},{4,5},{5,4},{6,7},{7,6},{8,9},{9,8},{10,11... | collective-permute-start | bytes 350216 | tf_op jit(solution)/shard_map/ppermute | solution.py:36
  28.6 3.9 %collective-permute-start.9 = (bf16[8,7296]{1,0:T(8,128)(2,1)S(1)}, bf16[8,7296]{1,0:T(8,128)(2,1)S(1)}, u32[]{:S(2)}, u32[]{:S(2)}) collective-permute-start(bf16[8,7296]{1,0:T(8,128)(2,1)S(1)} %collective-permute-done.1.refs_1_), channel_id=1, source_target_pairs={{0,1},{1,0},{2,3},{3,2},{4,5},{5,4},{6,7},{7,6},{8,9},{9,8},{10,11... | collective-permute-start | bytes 350216 | tf_op jit(solution)/shard_map/ppermute | solution.py:36
  29.3 3.6 %collective-permute-start.11 = (bf16[8,7296]{1,0:T(8,128)(2,1)S(1)}, bf16[8,7296]{1,0:T(8,128)(2,1)S(1)}, u32[]{:S(2)}, u32[]{:S(2)}) collective-permute-start(bf16[8,7296]{1,0:T(8,128)(2,1)S(1)} %collective-permute-done.2.refs_3_), channel_id=1, source_target_pairs={{0,1},{1,0},{2,3},{3,2},{4,5},{5,4},{6,7},{7,6},{8,9},{9,8},{10,11... | collective-permute-start | bytes 350216 | tf_op jit(solution)/shard_map/ppermute | solution.py:36
  35.7 1.6 %collective-permute-start.16 = (bf16[16,7168]{1,0:T(8,128)(2,1)S(1)}, bf16[16,7168]{1,0:T(8,128)(2,1)S(1)}, u32[]{:S(2)}, u32[]{:S(2)}) collective-permute-start(bf16[16,7168]{1,0:T(8,128)(2,1)S(1)} %get-tuple-element.53), channel_id=1, source_target_pairs={{0,1},{1,0},{2,3},{3,2},{4,5},{5,4},{6,7},{7,6},{8,9},{9,8},{10,11... | collective-permute-start | bytes 688136 | tf_op jit(solution)/shard_map/ppermute | solution.py:36
  36.1 7.0 %collective-permute-start.18 = (bf16[16,7168]{1,0:T(8,128)(2,1)S(1)}, bf16[16,7168]{1,0:T(8,128)(2,1)S(1)}, u32[]{:S(2)}, u32[]{:S(2)}) collective-permute-start(bf16[16,7168]{1,0:T(8,128)(2,1)S(1)} %get-tuple-element.55), channel_id=1, source_target_pairs={{0,1},{1,0},{2,3},{3,2},{4,5},{5,4},{6,7},{7,6},{8,9},{9,8},{10,11... | collective-permute-start | bytes 688136 | tf_op jit(solution)/shard_map/ppermute | solution.py:36
  36.2 1.7 %collective-permute-start.20 = (bf16[16,7168]{1,0:T(8,128)(2,1)S(1)}, bf16[16,7168]{1,0:T(8,128)(2,1)S(1)}, u32[]{:S(2)}, u32[]{:S(2)}) collective-permute-start(bf16[16,7168]{1,0:T(8,128)(2,1)S(1)} %get-tuple-element.59), channel_id=1, source_target_pairs={{0,1},{1,0},{2,3},{3,2},{4,5},{5,4},{6,7},{7,6},{8,9},{9,8},{10,11... | collective-permute-start | bytes 688136 | tf_op jit(solution)/shard_map/ppermute | solution.py:36
  36.6 2.9 %collective-permute-start.22 = (bf16[16,7168]{1,0:T(8,128)(2,1)S(1)}, bf16[16,7168]{1,0:T(8,128)(2,1)S(1)}, u32[]{:S(2)}, u32[]{:S(2)}) collective-permute-start(bf16[16,7168]{1,0:T(8,128)(2,1)S(1)} %get-tuple-element.61), channel_id=1, source_target_pairs={{0,1},{1,0},{2,3},{3,2},{4,5},{5,4},{6,7},{7,6},{8,9},{9,8},{10,11... | collective-permute-start | bytes 688136 | tf_op jit(solution)/shard_map/ppermute | solution.py:36
  37.3 6.0 %collective-permute-start.17 = (bf16[8,7168]{1,0:T(8,128)(2,1)S(1)}, bf16[8,7168]{1,0:T(8,128)(2,1)S(1)}, u32[]{:S(2)}, u32[]{:S(2)}) collective-permute-start(bf16[8,7168]{1,0:T(8,128)(2,1)S(1)} %add_convert_fusion.7), channel_id=1, source_target_pairs={{0,2},{1,3},{2,0},{3,1},{4,6},{5,7},{6,4},{7,5},{8,10},{9,11},{10,... | collective-permute-start | bytes 344072 | tf_op jit(solution)/shard_map/ppermute | solution.py:36
  37.9 8.1 %collective-permute-start.21 = (bf16[8,7168]{1,0:T(8,128)(2,1)S(1)}, bf16[8,7168]{1,0:T(8,128)(2,1)S(1)}, u32[]{:S(2)}, u32[]{:S(2)}) collective-permute-start(bf16[8,7168]{1,0:T(8,128)(2,1)S(1)} %add_convert_fusion.5), channel_id=1, source_target_pairs={{0,2},{1,3},{2,0},{3,1},{4,6},{5,7},{6,4},{7,5},{8,10},{9,11},{10,... | collective-permute-start | bytes 344072 | tf_op jit(solution)/shard_map/ppermute | solution.py:36
  39.5 6.5 %collective-permute-start.24 = (bf16[8,7168]{1,0:T(8,128)(2,1)S(1)}, bf16[8,7168]{1,0:T(8,128)(2,1)S(1)}, u32[]{:S(2)}, u32[]{:S(2)}) collective-permute-start(bf16[8,7168]{1,0:T(8,128)(2,1)S(1)} %get-tuple-element.78), channel_id=1, source_target_pairs={{0,12},{1,13},{2,14},{3,15},{4,0},{5,1},{6,2},{7,3},{8,4},{9,5},{1... | collective-permute-start | bytes 344072 | tf_op jit(solution)/shard_map/ppermute | solution.py:27
  41.9 6.8 %collective-permute-start.23 = (bf16[8,7168]{1,0:T(8,128)(2,1)S(1)}, bf16[8,7168]{1,0:T(8,128)(2,1)S(1)}, u32[]{:S(2)}, u32[]{:S(2)}) collective-permute-start(bf16[8,7168]{1,0:T(8,128)(2,1)S(1)} %get-tuple-element.79), channel_id=1, source_target_pairs={{0,14},{1,15},{2,12},{3,13},{4,2},{5,3},{6,0},{7,1},{8,6},{9,7},{1... | collective-permute-start | bytes 344072 | tf_op jit(solution)/shard_map/ppermute | solution.py:91
  43.3 11.2 %collective-permute-start.25 = (bf16[8,7168]{1,0:T(8,128)(2,1)S(1)}, bf16[8,7168]{1,0:T(8,128)(2,1)S(1)}, u32[]{:S(2)}, u32[]{:S(2)}) collective-permute-start(bf16[8,7168]{1,0:T(8,128)(2,1)S(1)} %add_convert_fusion.6), channel_id=1, source_target_pairs={{0,2},{1,3},{2,0},{3,1},{4,6},{5,7},{6,4},{7,5},{8,10},{9,11},{10,... | collective-permute-start | bytes 344072 | tf_op jit(solution)/shard_map/ppermute | solution.py:36
  44.6 9.9 %collective-permute-start.26 = (bf16[8,7168]{1,0:T(8,128)(2,1)S(1)}, bf16[8,7168]{1,0:T(8,128)(2,1)S(1)}, u32[]{:S(2)}, u32[]{:S(2)}) collective-permute-start(bf16[8,7168]{1,0:T(8,128)(2,1)S(1)} %add_convert_fusion.2), channel_id=1, source_target_pairs={{0,8},{1,9},{2,10},{3,11},{4,12},{5,13},{6,14},{7,15},{8,0},{9,1},... | collective-permute-start | bytes 344072 | tf_op jit(solution)/shard_map/ppermute | solution.py:27
  46.0 7.1 %collective-permute-start.19 = (bf16[128,512]{1,0:T(8,128)(2,1)S(1)}, bf16[128,512]{1,0:T(8,128)(2,1)S(1)}, u32[]{:S(2)}, u32[]{:S(2)}) collective-permute-start(bf16[128,512]{1,0:T(8,128)(2,1)S(1)} %copy-done.7), channel_id=1, source_target_pairs={{0,1},{1,2},{2,3},{3,4},{4,5},{5,6},{6,7},{7,8},{8,9},{9,10},{10,1... | collective-permute-start | bytes 393224 | tf_op jit(solution)/shard_map/ppermute | solution.py:27
  48.7 7.3 %collective-permute-start.27 = (bf16[8,7168]{1,0:T(8,128)(2,1)S(1)}, bf16[8,7168]{1,0:T(8,128)(2,1)S(1)}, u32[]{:S(2)}, u32[]{:S(2)}) collective-permute-start(bf16[8,7168]{1,0:T(8,128)(2,1)S(1)} %add_convert_fusion.1), channel_id=1, source_target_pairs={{0,4},{1,5},{2,6},{3,7},{4,8},{5,9},{6,10},{7,11},{8,12},{9,13},{1... | collective-permute-start | bytes 344072 | tf_op jit(solution)/shard_map/ppermute | solution.py:27
  (12 other events, 132.6 us)

commit v12 on v11

--- a/solution.py
+++ b/solution.py
@@ -311,15 +311,16 @@
 
     chips = [swapped(send, axis, 1) for send in sends]
     leaves = [added(keeps[2 * i], chip[:tokens]) for i, chip in enumerate(chips)]
+    leaves[0], away = lax.optimization_barrier((leaves[0], away))
     rests = [[keeps[2 * i + 1], chip[tokens:]] for i, chip in enumerate(chips)]
     overs = [swapped(leaf, axis, 2) for leaf in leaves[: len(far)]]
     terms = [slanted(leaves[-2], axis, -1), rotated(added(*rests[-2]), axis, -1)]
-    overs[-1], terms = lax.optimization_barrier((overs[-1], terms))
-    overs[0], leaves[-1], away = lax.optimization_barrier((overs[0], leaves[-1], away))
+    returned = shifted(away, axis, 1)
+    overs[-1], terms, returned = lax.optimization_barrier((overs[-1], terms, returned))
+    overs[0], leaves[-1] = lax.optimization_barrier((overs[0], leaves[-1]))
     terms = terms + rests[-1] + [swapped(leaves[-1], axis, 2)]
     for r, rest, over in zip(far, rests, overs):
         terms = terms + [rotated(added(*rest, over), axis, -r)]
-    returned = shifted(away, axis, 1)
     attn_out = settle(place, moved_slot, stay, returned)
     _, terms = lax.optimization_barrier((attn_out, terms))
     moe_out = added(*terms)

time: 56.9 us -> 62.5 us (1.098)
  waiting for transfers between devices: 21.1 us -> 27 us
    ppermute x18, waiting for transfers between devices: 4.1 us -> 12.8 us  [swapped(): return lax.ppermute(value, axis, pairs)]
    ppermute x2, waiting for transfers between devices: 3.82 us -> 1.23 us  [slanted(): return lax.ppermute(value, axis, pairs)]
    ppermute x18, starting transfers between devices: 8.79 us -> 6.75 us  [swapped(): return lax.ppermute(value, axis, pairs)]
    ppermute x8, starting transfers between devices: 10.5 us -> 12.2 us  [shifted(): return lax.ppermute(value, axis, pairs)]
  transfers between devices with their start and end apart: 28 -> 28, of which waited for: 14 -> 12; matrix products, arithmetic and copies ran while one was open for 0% -> 0% of each run, Pallas kernels for 14% -> 13%
where the time goes in v12:
time: 62.5 us; the launch traced here: 62.3 us
  waiting for transfers between devices  27 us (43%)
  starting transfers between devices  21.1 us (34%)
  Pallas kernels  11.7 us (19%)
  other arithmetic  1.02 us (2%)
  between operations  0.81 us (1%)
  local copies, waits for them, and re-layouts  0.69 us (1%)
    ppermute x8, waiting for transfers between devices, shifted(): return lax.ppermute(value, axis, pairs)  13.1 us
    ppermute x18, waiting for transfers between devices, swapped(): return lax.ppermute(value, axis, pairs)  12.8 us
    ppermute x8, starting transfers between devices, shifted(): return lax.ppermute(value, axis, pairs)  12.2 us
    ppermute x18, starting transfers between devices, swapped(): return lax.ppermute(value, axis, pairs)  6.75 us
    pallas_call x1, Pallas kernels, attend(): pl.pallas_call(functools.partial(attend_body, ranks, visits), out_shape=[...  6.54 us
    ppermute x2, starting transfers between devices, slanted(): return lax.ppermute(value, axis, pairs)  2.16 us
    pallas_call x1, Pallas kernels, prepare(): pl.pallas_call(functools.partial(prepare_body, groups), out_shape=[jax.Sh...  2.04 us
    pallas_call x1, Pallas kernels, expert(): pl.pallas_call(functools.partial(expert_body, count, groups, sizes), out_...  1.74 us
  transfers between devices with their start and end apart: 28, of which 12 were waited for; matrix products, arithmetic and copies ran while one was open for 0% of the time, Pallas kernels for 13%

profile of v12, /device:TPU:0, one launch (start us, length us, event | category | flops | bytes accessed | tf_op | source)
XLA Modules:
  0.0 62.3 jit_solution(4015013264669894359)
XLA Ops:
  0.6 2.0 %shard_map.122 = (bf16[8,7296]{1,0:T(8,128)(2,1)}, bf16[592,128]{1,0:T(8,128)(2,1)}) custom-call(s32[1]{0:T(128)} %bitcast.place, s32[16]{0:T(128)} %moved.5, bf16[8,7168]{1,0:T(8,128)(2,1)} %hidden.1, s32[2,8]{1,0:T(2,128)} %bitcast.8, f32[2,8]{1,0:T(2,128)} %bitcast.9, bf16[4,576,128]{2,1,0:T(8,128)(2,1)} %bitcast.6, bf16[4,576]{1,0:T(4,128)(2,1)} %own.3), custom_call_target="tpu_custom_call" | custom-call | tf_op jit(solution)/shard_map/pallas_call | solution.py:75
  2.7 5.4 %collective-permute-start = (bf16[592,128]{1,0:T(8,128)(2,1)}, bf16[592,128]{1,0:T(8,128)(2,1)S(1)}, u32[]{:S(2)}, u32[]{:S(2)}) collective-permute-start(bf16[592,128]{1,0:T(8,128)(2,1)} %get-tuple-element.42), channel_id=1, source_target_pairs={{0,15},{1,0},{2,1},{3,2},{4,3},{5,4},{6,5},{7,6},{8,7},{9,8},{10,9... | collective-permute-start | bytes 454664 | tf_op jit(solution)/shard_map/ppermute | solution.py:27
  8.1 1.1 %collective-permute-start.2 = (bf16[8,7296]{1,0:T(8,128)(2,1)}, bf16[8,7296]{1,0:T(8,128)(2,1)S(1)}, u32[]{:S(2)}, u32[]{:S(2)}) collective-permute-start(bf16[8,7296]{1,0:T(8,128)(2,1)} %get-tuple-element.46.refs_7_), channel_id=1, source_target_pairs={{0,12},{1,13},{2,14},{3,15},{4,0},{5,1},{6,2},{7,3},{8,4},{9,5},{1... | collective-permute-start | bytes 350216 | tf_op jit(solution)/shard_map/ppermute | solution.py:27
  9.3 3.3 %collective-permute-done.refs_0_ = bf16[592,128]{1,0:T(8,128)(2,1)S(1)} collective-permute-done((bf16[592,128]{1,0:T(8,128)(2,1)}, bf16[592,128]{1,0:T(8,128)(2,1)S(1)}, u32[]{:S(2)}, u32[]{:S(2)}) %collective-permute-start) | collective-permute-done | bytes 151584 | tf_op jit(solution)/shard_map/ppermute | solution.py:27
  12.5 0.7 %copy-done.6 = bf16[592,128]{1,0:T(8,128)(2,1)} copy-done((bf16[592,128]{1,0:T(8,128)(2,1)}, bf16[592,128]{1,0:T(8,128)(2,1)S(1)}, u32[]{:S(2)}) %copy-start.6) | copy-done | bytes 151576
  13.2 6.5 %shard_map.123 = (bf16[3,128,512]{2,1,0:T(8,128)(2,1)}, bf16[128,512]{1,0:T(8,128)(2,1)}) custom-call(s32[1]{0:T(128)} %bitcast.place, s32[16]{0:T(128)} %moved.5, s32[64]{0:T(128)} %lengths.1, bf16[4,576,128]{2,1,0:T(8,128)(2,1)} %bitcast.7, bf16[4,576]{1,0:T(4,128)(2,1)} %own.3, bf16[4,576,1024]{2,1,0:T(8,128)(2,1)} %bitcast.5, bf16[592,128]{1,0:T(8,128)(2,1)} %copy-done.6), custom_call_target="tpu_custom_call" | custom-call | flops 1140850688 | tf_op jit(solution)/shard_map/pallas_call | solution.py:159
  19.8 1.0 %collective-permute-start.4 = (bf16[8,7296]{1,0:T(8,128)(2,1)S(1)}, bf16[8,7296]{1,0:T(8,128)(2,1)S(1)}, u32[]{:S(2)}, u32[]{:S(2)}) collective-permute-start(bf16[8,7296]{1,0:T(8,128)(2,1)S(1)} %copy-done.4), channel_id=1, source_target_pairs={{0,6},{1,7},{2,4},{3,5},{4,10},{5,11},{6,8},{7,9},{8,14},{9,15},{1... | collective-permute-start | bytes 350216 | tf_op jit(solution)/shard_map/ppermute | solution.py:91
  20.9 0.7 %collective-permute-start.5 = (bf16[8,7296]{1,0:T(8,128)(2,1)S(1)}, bf16[8,7296]{1,0:T(8,128)(2,1)S(1)}, u32[]{:S(2)}, u32[]{:S(2)}) collective-permute-start(bf16[8,7296]{1,0:T(8,128)(2,1)S(1)} %collective-permute-done.1.refs_1_), channel_id=1, source_target_pairs={{0,2},{1,3},{2,0},{3,1},{4,6},{5,7},{6,4},{7,5},{8,10},{9,11},{10,... | collective-permute-start | bytes 350216 | tf_op jit(solution)/shard_map/ppermute | solution.py:36
  21.6 1.3 %collective-permute-start.6 = (bf16[8,7296]{1,0:T(8,128)(2,1)S(1)}, bf16[8,7296]{1,0:T(8,128)(2,1)S(1)}, u32[]{:S(2)}, u32[]{:S(2)}) collective-permute-start(bf16[8,7296]{1,0:T(8,128)(2,1)S(1)} %collective-permute-done.2.refs_3_), channel_id=1, source_target_pairs={{0,2},{1,3},{2,0},{3,1},{4,6},{5,7},{6,4},{7,5},{8,10},{9,11},{10,... | collective-permute-start | bytes 350216 | tf_op jit(solution)/shard_map/ppermute | solution.py:36
  23.4 4.1 %collective-permute-done.7.refs_5_ = bf16[8,7296]{1,0:T(8,128)(2,1)S(1)} collective-permute-done((bf16[8,7296]{1,0:T(8,128)(2,1)S(1)}, bf16[8,7296]{1,0:T(8,128)(2,1)S(1)}, u32[]{:S(2)}, u32[]{:S(2)}) %collective-permute-start.7) | collective-permute-done | bytes 116768 | tf_op jit(solution)/shard_map/ppermute | solution.py:27
  27.4 1.2 %collective-permute-done.4.refs_4_ = bf16[8,7296]{1,0:T(8,128)(2,1)S(1)} collective-permute-done((bf16[8,7296]{1,0:T(8,128)(2,1)S(1)}, bf16[8,7296]{1,0:T(8,128)(2,1)S(1)}, u32[]{:S(2)}, u32[]{:S(2)}) %collective-permute-start.4) | collective-permute-done | bytes 116768 | tf_op jit(solution)/shard_map/ppermute | solution.py:91
  28.6 0.6 %collective-permute-start.9 = (bf16[8,7296]{1,0:T(8,128)(2,1)S(1)}, bf16[8,7296]{1,0:T(8,128)(2,1)S(1)}, u32[]{:S(2)}, u32[]{:S(2)}) collective-permute-start(bf16[8,7296]{1,0:T(8,128)(2,1)S(1)} %collective-permute-done.1.refs_1_), channel_id=1, source_target_pairs={{0,1},{1,0},{2,3},{3,2},{4,5},{5,4},{6,7},{7,6},{8,9},{9,8},{10,11... | collective-permute-start | bytes 350216 | tf_op jit(solution)/shard_map/ppermute | solution.py:36
  29.6 2.3 %collective-permute-done.6.refs_2_ = bf16[8,7296]{1,0:T(8,128)(2,1)S(1)} collective-permute-done((bf16[8,7296]{1,0:T(8,128)(2,1)S(1)}, bf16[8,7296]{1,0:T(8,128)(2,1)S(1)}, u32[]{:S(2)}, u32[]{:S(2)}) %collective-permute-start.6) | collective-permute-done | bytes 116768 | tf_op jit(solution)/shard_map/ppermute | solution.py:36
  33.9 1.7 %shard_map.124 = (bf16[8,7168]{1,0:T(8,128)(2,1)S(1)}, bf16[8,7168]{1,0:T(8,128)(2,1)S(1)}, bf16[8,7168]{1,0:T(8,128)(2,1)S(1)}, bf16[8,7168]{1,0:T(8,128)(2,1)S...) custom-call(s32[1]{0:T(128)} %bitcast.place, ...), custom_call_target="tpu_custom_call" | custom-call | flops 704643072 | bytes 5505024 | tf_op jit(solution)/shard_map/pallas_call | solution.py:234
  36.8 0.5 collective-permute-done.16
  37.8 3.4 %collective-permute-start.20 = (bf16[8,7168]{1,0:T(8,128)(2,1)S(1)}, bf16[8,7168]{1,0:T(8,128)(2,1)S(1)}, u32[]{:S(2)}, u32[]{:S(2)}) collective-permute-start(bf16[8,7168]{1,0:T(8,128)(2,1)S(1)} %get-tuple-element.82), channel_id=1, source_target_pairs={{0,12},{1,13},{2,14},{3,15},{4,0},{5,1},{6,2},{7,3},{8,4},{9,5},{1... | collective-permute-start | bytes 344072 | tf_op jit(solution)/shard_map/ppermute | solution.py:27
  41.2 1.1 %collective-permute-start.19 = (bf16[8,7168]{1,0:T(8,128)(2,1)S(1)}, bf16[8,7168]{1,0:T(8,128)(2,1)S(1)}, u32[]{:S(2)}, u32[]{:S(2)}) collective-permute-start(bf16[8,7168]{1,0:T(8,128)(2,1)S(1)} %get-tuple-element.83), channel_id=1, source_target_pairs={{0,14},{1,15},{2,12},{3,13},{4,2},{5,3},{6,0},{7,1},{8,6},{9,7},{1... | collective-permute-start | bytes 344072 | tf_op jit(solution)/shard_map/ppermute | solution.py:91
  42.4 0.7 %collective-permute-start.24 = (bf16[8,7168]{1,0:T(8,128)(2,1)S(1)}, bf16[8,7168]{1,0:T(8,128)(2,1)S(1)}, u32[]{:S(2)}, u32[]{:S(2)}) collective-permute-start(bf16[8,7168]{1,0:T(8,128)(2,1)S(1)} %add_convert_fusion.4), channel_id=1, source_target_pairs={{0,2},{1,3},{2,0},{3,1},{4,6},{5,7},{6,4},{7,5},{8,10},{9,11},{10,... | collective-permute-start | bytes 344072 | tf_op jit(solution)/shard_map/ppermute | solution.py:36
  43.1 7.6 %collective-permute-done.24 = bf16[8,7168]{1,0:T(8,128)(2,1)S(1)} collective-permute-done((bf16[8,7168]{1,0:T(8,128)(2,1)S(1)}, bf16[8,7168]{1,0:T(8,128)(2,1)S(1)}, u32[]{:S(2)}, u32[]{:S(2)}) %collective-permute-start.24) | collective-permute-done | bytes 114720 | tf_op jit(solution)/shard_map/ppermute | solution.py:36
  51.3 1.8 %collective-permute-start.27 = (bf16[8,7168]{1,0:T(8,128)(2,1)S(1)}, bf16[8,7168]{1,0:T(8,128)(2,1)S(1)}, u32[]{:S(2)}, u32[]{:S(2)}) collective-permute-start(bf16[8,7168]{1,0:T(8,128)(2,1)S(1)} %add_convert_fusion.1), channel_id=1, source_target_pairs={{0,4},{1,5},{2,6},{3,7},{4,8},{5,9},{6,10},{7,11},{8,12},{9,13},{1... | collective-permute-start | bytes 344072 | tf_op jit(solution)/shard_map/ppermute | solution.py:27
  53.1 1.4 %shard_map.125 = bf16[4,128,512]{2,1,0:T(8,128)(2,1)} custom-call(s32[1]{0:T(128)} %bitcast.place, s32[16]{0:T(128)S(1)} %copy-done.5, bf16[3,128,512]{2,1,0:T(8,128)(2,1)S(1)} %copy-done.3, bf16[128,512]{1,0:T(8,128)(2,1)S(1)} %collective-permute-done.22.returned), custom_call_target="tpu_custom_call" | custom-call | tf_op jit(solution)/shard_map/pallas_call | solution.py:188
  54.5 1.4 %collective-permute-done.25 = bf16[8,7168]{1,0:T(8,128)(2,1)S(1)} collective-permute-done((bf16[8,7168]{1,0:T(8,128)(2,1)S(1)}, bf16[8,7168]{1,0:T(8,128)(2,1)S(1)}, u32[]{:S(2)}, u32[]{:S(2)}) %collective-permute-start.25) | collective-permute-done | bytes 114720 | tf_op jit(solution)/shard_map/ppermute | solution.py:36
  55.8 5.7 %collective-permute-done.26 = bf16[8,7168]{1,0:T(8,128)(2,1)S(1)} collective-permute-done((bf16[8,7168]{1,0:T(8,128)(2,1)S(1)}, bf16[8,7168]{1,0:T(8,128)(2,1)S(1)}, u32[]{:S(2)}, u32[]{:S(2)}) %collective-permute-start.26) | collective-permute-done | bytes 114720 | tf_op jit(solution)/shard_map/ppermute | solution.py:27
  61.6 0.8 %add_convert_fusion = bf16[8,7168]{1,0:T(8,128)(2,1)} fusion(bf16[8,7168]{1,0:T(8,128)(2,1)S(1)} %collective-permute-done.27, bf16[8,7168]{1,0:T(8,128)(2,1)S(1)} %collective-permute-done.26, bf16[8,7168]{1,0:T(8,128)(2,1)S(1)} %collective-permute-done.25, bf16[8,7168]{1,0:T(8,128)(2,1)S(1)} %slice.36, bf16[8,7168]{1,0:T(8,128)(2,1)S(1)} %get-tuple-element.77, ...), kind=kLoop, calls=%fused_computation | loop fusion | flops 802816 | bytes 917504 | tf_op jit(solution)/shard_map/convert_element_type | solution.py:251
  (60 shorter events, 5.1 us)
Async XLA Ops:
  2.7 9.8 %collective-permute-start = (bf16[592,128]{1,0:T(8,128)(2,1)}, bf16[592,128]{1,0:T(8,128)(2,1)S(1)}, u32[]{:S(2)}, u32[]{:S(2)}) collective-permute-start(bf16[592,128]{1,0:T(8,128)(2,1)} %get-tuple-element.42), channel_id=1, source_target_pairs={{0,15},{1,0},{2,1},{3,2},{4,3},{5,4},{6,5},{7,6},{8,7},{9,8},{10,9... | collective-permute-start | bytes 454664 | tf_op jit(solution)/shard_map/ppermute | solution.py:27
  8.1 11.6 %collective-permute-start.3 = (bf16[8,7296]{1,0:T(8,128)(2,1)}, bf16[8,7296]{1,0:T(8,128)(2,1)S(1)}, u32[]{:S(2)}, u32[]{:S(2)}) collective-permute-start(bf16[8,7296]{1,0:T(8,128)(2,1)} %get-tuple-element.46.refs_7_), channel_id=1, source_target_pairs={{0,2},{1,3},{2,0},{3,1},{4,6},{5,7},{6,4},{7,5},{8,10},{9,11},{10,... | collective-permute-start | bytes 350216 | tf_op jit(solution)/shard_map/ppermute | solution.py:36
  8.1 11.6 %collective-permute-start.2 = (bf16[8,7296]{1,0:T(8,128)(2,1)}, bf16[8,7296]{1,0:T(8,128)(2,1)S(1)}, u32[]{:S(2)}, u32[]{:S(2)}) collective-permute-start(bf16[8,7296]{1,0:T(8,128)(2,1)} %get-tuple-element.46.refs_7_), channel_id=1, source_target_pairs={{0,12},{1,13},{2,14},{3,15},{4,0},{5,1},{6,2},{7,3},{8,4},{9,5},{1... | collective-permute-start | bytes 350216 | tf_op jit(solution)/shard_map/ppermute | solution.py:27
  9.3 10.5 %collective-permute-start.1 = (bf16[8,7296]{1,0:T(8,128)(2,1)}, bf16[8,7296]{1,0:T(8,128)(2,1)S(1)}, u32[]{:S(2)}, u32[]{:S(2)}) collective-permute-start(bf16[8,7296]{1,0:T(8,128)(2,1)} %get-tuple-element.46.refs_7_), channel_id=1, source_target_pairs={{0,8},{1,9},{2,10},{3,11},{4,12},{5,13},{6,14},{7,15},{8,0},{9,1},... | collective-permute-start | bytes 350216 | tf_op jit(solution)/shard_map/ppermute | solution.py:27
  19.8 7.6 %collective-permute-start.7 = (bf16[8,7296]{1,0:T(8,128)(2,1)S(1)}, bf16[8,7296]{1,0:T(8,128)(2,1)S(1)}, u32[]{:S(2)}, u32[]{:S(2)}) collective-permute-start(bf16[8,7296]{1,0:T(8,128)(2,1)S(1)} %copy-done.4), channel_id=1, source_target_pairs={{0,4},{1,5},{2,6},{3,7},{4,8},{5,9},{6,10},{7,11},{8,12},{9,13},{1... | collective-permute-start | bytes 350216 | tf_op jit(solution)/shard_map/ppermute | solution.py:27
  19.8 8.8 %collective-permute-start.4 = (bf16[8,7296]{1,0:T(8,128)(2,1)S(1)}, bf16[8,7296]{1,0:T(8,128)(2,1)S(1)}, u32[]{:S(2)}, u32[]{:S(2)}) collective-permute-start(bf16[8,7296]{1,0:T(8,128)(2,1)S(1)} %copy-done.4), channel_id=1, source_target_pairs={{0,6},{1,7},{2,4},{3,5},{4,10},{5,11},{6,8},{7,9},{8,14},{9,15},{1... | collective-permute-start | bytes 350216 | tf_op jit(solution)/shard_map/ppermute | solution.py:91
  20.9 8.4 %collective-permute-start.5 = (bf16[8,7296]{1,0:T(8,128)(2,1)S(1)}, bf16[8,7296]{1,0:T(8,128)(2,1)S(1)}, u32[]{:S(2)}, u32[]{:S(2)}) collective-permute-start(bf16[8,7296]{1,0:T(8,128)(2,1)S(1)} %collective-permute-done.1.refs_1_), channel_id=1, source_target_pairs={{0,2},{1,3},{2,0},{3,1},{4,6},{5,7},{6,4},{7,5},{8,10},{9,11},{10,... | collective-permute-start | bytes 350216 | tf_op jit(solution)/shard_map/ppermute | solution.py:36
  21.6 10.3 %collective-permute-start.6 = (bf16[8,7296]{1,0:T(8,128)(2,1)S(1)}, bf16[8,7296]{1,0:T(8,128)(2,1)S(1)}, u32[]{:S(2)}, u32[]{:S(2)}) collective-permute-start(bf16[8,7296]{1,0:T(8,128)(2,1)S(1)} %collective-permute-done.2.refs_3_), channel_id=1, source_target_pairs={{0,2},{1,3},{2,0},{3,1},{4,6},{5,7},{6,4},{7,5},{8,10},{9,11},{10,... | collective-permute-start | bytes 350216 | tf_op jit(solution)/shard_map/ppermute | solution.py:36
  22.9 9.1 %collective-permute-start.15 = (bf16[8,7296]{1,0:T(8,128)(2,1)S(1)}, bf16[8,7296]{1,0:T(8,128)(2,1)S(1)}, u32[]{:S(2)}, u32[]{:S(2)}) collective-permute-start(bf16[8,7296]{1,0:T(8,128)(2,1)S(1)} %copy-done.4), channel_id=1, source_target_pairs={{0,1},{1,0},{2,3},{3,2},{4,5},{5,4},{6,7},{7,6},{8,9},{9,8},{10,11... | collective-permute-start | bytes 350216 | tf_op jit(solution)/shard_map/ppermute | solution.py:36
  27.4 5.0 %collective-permute-start.14 = (bf16[8,7296]{1,0:T(8,128)(2,1)S(1)}, bf16[8,7296]{1,0:T(8,128)(2,1)S(1)}, u32[]{:S(2)}, u32[]{:S(2)}) collective-permute-start(bf16[8,7296]{1,0:T(8,128)(2,1)S(1)} %collective-permute-done.3.refs_6_), channel_id=1, source_target_pairs={{0,1},{1,0},{2,3},{3,2},{4,5},{5,4},{6,7},{7,6},{8,9},{9,8},{10,11... | collective-permute-start | bytes 350216 | tf_op jit(solution)/shard_map/ppermute | solution.py:36
  28.6 3.9 %collective-permute-start.9 = (bf16[8,7296]{1,0:T(8,128)(2,1)S(1)}, bf16[8,7296]{1,0:T(8,128)(2,1)S(1)}, u32[]{:S(2)}, u32[]{:S(2)}) collective-permute-start(bf16[8,7296]{1,0:T(8,128)(2,1)S(1)} %collective-permute-done.1.refs_1_), channel_id=1, source_target_pairs={{0,1},{1,0},{2,3},{3,2},{4,5},{5,4},{6,7},{7,6},{8,9},{9,8},{10,11... | collective-permute-start | bytes 350216 | tf_op jit(solution)/shard_map/ppermute | solution.py:36
  29.3 3.6 %collective-permute-start.11 = (bf16[8,7296]{1,0:T(8,128)(2,1)S(1)}, bf16[8,7296]{1,0:T(8,128)(2,1)S(1)}, u32[]{:S(2)}, u32[]{:S(2)}) collective-permute-start(bf16[8,7296]{1,0:T(8,128)(2,1)S(1)} %collective-permute-done.2.refs_3_), channel_id=1, source_target_pairs={{0,1},{1,0},{2,3},{3,2},{4,5},{5,4},{6,7},{7,6},{8,9},{9,8},{10,11... | collective-permute-start | bytes 350216 | tf_op jit(solution)/shard_map/ppermute | solution.py:36
  35.7 1.6 %collective-permute-start.16 = (bf16[16,7168]{1,0:T(8,128)(2,1)S(1)}, bf16[16,7168]{1,0:T(8,128)(2,1)S(1)}, u32[]{:S(2)}, u32[]{:S(2)}) collective-permute-start(bf16[16,7168]{1,0:T(8,128)(2,1)S(1)} %get-tuple-element.55), channel_id=1, source_target_pairs={{0,1},{1,0},{2,3},{3,2},{4,5},{5,4},{6,7},{7,6},{8,9},{9,8},{10,11... | collective-permute-start | bytes 688136 | tf_op jit(solution)/shard_map/ppermute | solution.py:36
  36.1 1.6 %collective-permute-start.18 = (bf16[16,7168]{1,0:T(8,128)(2,1)S(1)}, bf16[16,7168]{1,0:T(8,128)(2,1)S(1)}, u32[]{:S(2)}, u32[]{:S(2)}) collective-permute-start(bf16[16,7168]{1,0:T(8,128)(2,1)S(1)} %get-tuple-element.57), channel_id=1, source_target_pairs={{0,1},{1,0},{2,3},{3,2},{4,5},{5,4},{6,7},{7,6},{8,9},{9,8},{10,11... | collective-permute-start | bytes 688136 | tf_op jit(solution)/shard_map/ppermute | solution.py:36
  36.2 6.1 %collective-permute-start.21 = (bf16[16,7168]{1,0:T(8,128)(2,1)S(1)}, bf16[16,7168]{1,0:T(8,128)(2,1)S(1)}, u32[]{:S(2)}, u32[]{:S(2)}) collective-permute-start(bf16[16,7168]{1,0:T(8,128)(2,1)S(1)} %get-tuple-element.60), channel_id=1, source_target_pairs={{0,1},{1,0},{2,3},{3,2},{4,5},{5,4},{6,7},{7,6},{8,9},{9,8},{10,11... | collective-permute-start | bytes 688136 | tf_op jit(solution)/shard_map/ppermute | solution.py:36
  36.6 6.5 %collective-permute-start.23 = (bf16[16,7168]{1,0:T(8,128)(2,1)S(1)}, bf16[16,7168]{1,0:T(8,128)(2,1)S(1)}, u32[]{:S(2)}, u32[]{:S(2)}) collective-permute-start(bf16[16,7168]{1,0:T(8,128)(2,1)S(1)} %get-tuple-element.67), channel_id=1, source_target_pairs={{0,1},{1,0},{2,3},{3,2},{4,5},{5,4},{6,7},{7,6},{8,9},{9,8},{10,11... | collective-permute-start | bytes 688136 | tf_op jit(solution)/shard_map/ppermute | solution.py:36
  37.3 13.6 %collective-permute-start.17 = (bf16[8,7168]{1,0:T(8,128)(2,1)S(1)}, bf16[8,7168]{1,0:T(8,128)(2,1)S(1)}, u32[]{:S(2)}, u32[]{:S(2)}) collective-permute-start(bf16[8,7168]{1,0:T(8,128)(2,1)S(1)} %add_convert_fusion.7), channel_id=1, source_target_pairs={{0,2},{1,3},{2,0},{3,1},{4,6},{5,7},{6,4},{7,5},{8,10},{9,11},{10,... | collective-permute-start | bytes 344072 | tf_op jit(solution)/shard_map/ppermute | solution.py:36
  37.8 13.4 %collective-permute-start.20 = (bf16[8,7168]{1,0:T(8,128)(2,1)S(1)}, bf16[8,7168]{1,0:T(8,128)(2,1)S(1)}, u32[]{:S(2)}, u32[]{:S(2)}) collective-permute-start(bf16[8,7168]{1,0:T(8,128)(2,1)S(1)} %get-tuple-element.82), channel_id=1, source_target_pairs={{0,12},{1,13},{2,14},{3,15},{4,0},{5,1},{6,2},{7,3},{8,4},{9,5},{1... | collective-permute-start | bytes 344072 | tf_op jit(solution)/shard_map/ppermute | solution.py:27
  41.2 10.0 %collective-permute-start.19 = (bf16[8,7168]{1,0:T(8,128)(2,1)S(1)}, bf16[8,7168]{1,0:T(8,128)(2,1)S(1)}, u32[]{:S(2)}, u32[]{:S(2)}) collective-permute-start(bf16[8,7168]{1,0:T(8,128)(2,1)S(1)} %get-tuple-element.83), channel_id=1, source_target_pairs={{0,14},{1,15},{2,12},{3,13},{4,2},{5,3},{6,0},{7,1},{8,6},{9,7},{1... | collective-permute-start | bytes 344072 | tf_op jit(solution)/shard_map/ppermute | solution.py:91
  42.4 8.4 %collective-permute-start.24 = (bf16[8,7168]{1,0:T(8,128)(2,1)S(1)}, bf16[8,7168]{1,0:T(8,128)(2,1)S(1)}, u32[]{:S(2)}, u32[]{:S(2)}) collective-permute-start(bf16[8,7168]{1,0:T(8,128)(2,1)S(1)} %add_convert_fusion.4), channel_id=1, source_target_pairs={{0,2},{1,3},{2,0},{3,1},{4,6},{5,7},{6,4},{7,5},{8,10},{9,11},{10,... | collective-permute-start | bytes 344072 | tf_op jit(solution)/shard_map/ppermute | solution.py:36
  43.1 8.1 %collective-permute-start.22 = (bf16[128,512]{1,0:T(8,128)(2,1)S(1)}, bf16[128,512]{1,0:T(8,128)(2,1)S(1)}, u32[]{:S(2)}, u32[]{:S(2)}) collective-permute-start(bf16[128,512]{1,0:T(8,128)(2,1)S(1)} %copy-done.7), channel_id=1, source_target_pairs={{0,1},{1,2},{2,3},{3,4},{4,5},{5,6},{6,7},{7,8},{8,9},{9,10},{10,1... | collective-permute-start | bytes 393224 | tf_op jit(solution)/shard_map/ppermute | solution.py:27
  50.8 5.1 %collective-permute-start.25 = (bf16[8,7168]{1,0:T(8,128)(2,1)S(1)}, bf16[8,7168]{1,0:T(8,128)(2,1)S(1)}, u32[]{:S(2)}, u32[]{:S(2)}) collective-permute-start(bf16[8,7168]{1,0:T(8,128)(2,1)S(1)} %add_convert_fusion.3), channel_id=1, source_target_pairs={{0,2},{1,3},{2,0},{3,1},{4,6},{5,7},{6,4},{7,5},{8,10},{9,11},{10,... | collective-permute-start | bytes 344072 | tf_op jit(solution)/shard_map/ppermute | solution.py:36
  50.8 10.7 %collective-permute-start.26 = (bf16[8,7168]{1,0:T(8,128)(2,1)S(1)}, bf16[8,7168]{1,0:T(8,128)(2,1)S(1)}, u32[]{:S(2)}, u32[]{:S(2)}) collective-permute-start(bf16[8,7168]{1,0:T(8,128)(2,1)S(1)} %add_convert_fusion.2), channel_id=1, source_target_pairs={{0,8},{1,9},{2,10},{3,11},{4,12},{5,13},{6,14},{7,15},{8,0},{9,1},... | collective-permute-start | bytes 344072 | tf_op jit(solution)/shard_map/ppermute | solution.py:27
  51.3 10.3 %collective-permute-start.27 = (bf16[8,7168]{1,0:T(8,128)(2,1)S(1)}, bf16[8,7168]{1,0:T(8,128)(2,1)S(1)}, u32[]{:S(2)}, u32[]{:S(2)}) collective-permute-start(bf16[8,7168]{1,0:T(8,128)(2,1)S(1)} %add_convert_fusion.1), channel_id=1, source_target_pairs={{0,4},{1,5},{2,6},{3,7},{4,8},{5,9},{6,10},{7,11},{8,12},{9,13},{1... | collective-permute-start | bytes 344072 | tf_op jit(solution)/shard_map/ppermute | solution.py:27
  (12 other events, 145.5 us)

commit v13 on v10

--- a/solution.py
+++ b/solution.py
@@ -279,6 +279,11 @@
     columns = {r: rotated(rows, axis, r) for r in order}
     across = {0: swapped(rows, axis, 2)}
 
+    lead = order[-1]
+    visiting, columns[lead] = lax.optimization_barrier((visiting, columns[lead]))
+    ahead = {lead: columns.pop(lead)}
+    crossing = swapped(ahead[lead], axis, 2)
+
     stay, away = attend(
         tuple(range(requests - 1)),
         place,
@@ -289,8 +294,12 @@
         cache_t,
         visiting,
     )
-    columns, across, away = lax.optimization_barrier((columns, across, away))
-    later = {r: swapped(columns[r], axis, 2) for r in order}
+    columns, across, crossing, away = lax.optimization_barrier(
+        (columns, across, crossing, away)
+    )
+    later = {r: swapped(columns[r], axis, 2) for r in columns}
+    columns.update(ahead)
+    across[lead] = crossing
     across.update(later)
     columns[0] = rows
 

time: 56.1 us -> 57.1 us (1.018)
  the two profiles are of different devices: /device:TPU:13 before, /device:TPU:0 now
where the time goes in v13:
time: 57.1 us; the launch traced here: 57 us
  starting transfers between devices  22.2 us (39%)
  waiting for transfers between devices  19.7 us (35%)
  Pallas kernels  12.6 us (22%)
  other arithmetic  1 us (2%)
  between operations  0.84 us (1%)
  local copies, waits for them, and re-layouts  0.62 us (1%)
    ppermute x8, starting transfers between devices, shifted(): return lax.ppermute(value, axis, pairs)  11.4 us
    ppermute x20, waiting for transfers between devices, swapped(): return lax.ppermute(value, axis, pairs)  11.2 us
    ppermute x20, starting transfers between devices, swapped(): return lax.ppermute(value, axis, pairs)  10.8 us
    ppermute x8, waiting for transfers between devices, shifted(): return lax.ppermute(value, axis, pairs)  8.53 us
    pallas_call x1, Pallas kernels, attend(): pl.pallas_call(functools.partial(attend_body, ranks, visits), out_shape=[...  6.53 us
    pallas_call x1, Pallas kernels, expert(): pl.pallas_call(functools.partial(expert_body, count, groups, sizes), out_...  2.65 us
    pallas_call x1, Pallas kernels, prepare(): pl.pallas_call(functools.partial(prepare_body, groups), out_shape=[jax.Sh...  2.05 us
    pallas_call x1, Pallas kernels, settle(): pl.pallas_call(settle_body, out_shape=jax.ShapeDtypeStruct((stay.shape[0]...  1.39 us
  transfers between devices with their start and end apart: 28, of which 8 were waited for; matrix products, arithmetic and copies ran while one was open for 0% of the time, Pallas kernels for 14%

profile of v13, /device:TPU:0, one launch (start us, length us, event | category | flops | bytes accessed | tf_op | source)
XLA Modules:
  0.0 57.0 jit_solution(13296564919634003289)
XLA Ops:
  0.6 2.0 %shard_map.122 = (bf16[8,7296]{1,0:T(8,128)(2,1)}, bf16[592,128]{1,0:T(8,128)(2,1)}) custom-call(s32[1]{0:T(128)} %bitcast.place, s32[16]{0:T(128)} %moved.5, bf16[8,7168]{1,0:T(8,128)(2,1)} %hidden.1, s32[2,8]{1,0:T(2,128)} %bitcast.8, f32[2,8]{1,0:T(2,128)} %bitcast.9, bf16[4,576,128]{2,1,0:T(8,128)(2,1)} %bitcast.6, bf16[4,576]{1,0:T(4,128)(2,1)} %own.3), custom_call_target="tpu_custom_call" | custom-call | tf_op jit(solution)/shard_map/pallas_call | solution.py:75
  2.7 5.4 %collective-permute-start = (bf16[592,128]{1,0:T(8,128)(2,1)}, bf16[592,128]{1,0:T(8,128)(2,1)S(1)}, u32[]{:S(2)}, u32[]{:S(2)}) collective-permute-start(bf16[592,128]{1,0:T(8,128)(2,1)} %get-tuple-element.35), channel_id=1, source_target_pairs={{0,15},{1,0},{2,1},{3,2},{4,3},{5,4},{6,5},{7,6},{8,7},{9,8},{10,9... | collective-permute-start | bytes 454664 | tf_op jit(solution)/shard_map/ppermute | solution.py:27
  8.6 0.7 %collective-permute-start.4 = (bf16[8,7296]{1,0:T(8,128)(2,1)}, bf16[8,7296]{1,0:T(8,128)(2,1)S(1)}, u32[]{:S(2)}, u32[]{:S(2)}) collective-permute-start(bf16[8,7296]{1,0:T(8,128)(2,1)} %get-tuple-element.36.refs_7_), channel_id=1, source_target_pairs={{0,2},{1,3},{2,0},{3,1},{4,6},{5,7},{6,4},{7,5},{8,10},{9,11},{10,... | collective-permute-start | bytes 350216 | tf_op jit(solution)/shard_map/ppermute | solution.py:36
  9.3 1.0 %collective-permute-start.2 = (bf16[8,7296]{1,0:T(8,128)(2,1)}, bf16[8,7296]{1,0:T(8,128)(2,1)S(1)}, u32[]{:S(2)}, u32[]{:S(2)}) collective-permute-start(bf16[8,7296]{1,0:T(8,128)(2,1)} %get-tuple-element.36.refs_7_), channel_id=1, source_target_pairs={{0,4},{1,5},{2,6},{3,7},{4,8},{5,9},{6,10},{7,11},{8,12},{9,13},{1... | collective-permute-start | bytes 350216 | tf_op jit(solution)/shard_map/ppermute | solution.py:27
  10.3 5.0 %collective-permute-done.1.refs_5_ = bf16[8,7296]{1,0:T(8,128)(2,1)S(1)} collective-permute-done((bf16[8,7296]{1,0:T(8,128)(2,1)}, bf16[8,7296]{1,0:T(8,128)(2,1)S(1)}, u32[]{:S(2)}, u32[]{:S(2)}) %collective-permute-start.1) | collective-permute-done | bytes 116768 | tf_op jit(solution)/shard_map/ppermute | solution.py:27
  15.4 0.6 %copy-done.6 = bf16[592,128]{1,0:T(8,128)(2,1)} copy-done((bf16[592,128]{1,0:T(8,128)(2,1)}, bf16[592,128]{1,0:T(8,128)(2,1)S(1)}, u32[]{:S(2)}) %copy-start.6) | copy-done | bytes 151576
  16.0 6.5 %shard_map.123 = (bf16[3,128,512]{2,1,0:T(8,128)(2,1)}, bf16[128,512]{1,0:T(8,128)(2,1)}) custom-call(s32[1]{0:T(128)} %bitcast.place, s32[16]{0:T(128)} %moved.5, s32[64]{0:T(128)} %lengths.1, bf16[4,576,128]{2,1,0:T(8,128)(2,1)} %bitcast.7, bf16[4,576]{1,0:T(4,128)(2,1)} %own.3, bf16[4,576,1024]{2,1,0:T(8,128)(2,1)} %bitcast.5, bf16[592,128]{1,0:T(8,128)(2,1)} %copy-done.6), custom_call_target="tpu_custom_call" | custom-call | flops 1140850688 | tf_op jit(solution)/shard_map/pallas_call | solution.py:153
  23.2 1.5 %collective-permute-start.6 = (bf16[8,7296]{1,0:T(8,128)(2,1)S(1)}, bf16[8,7296]{1,0:T(8,128)(2,1)S(1)}, u32[]{:S(2)}, u32[]{:S(2)}) collective-permute-start(bf16[8,7296]{1,0:T(8,128)(2,1)S(1)} %collective-permute-done.3.refs_1_), channel_id=1, source_target_pairs={{0,2},{1,3},{2,0},{3,1},{4,6},{5,7},{6,4},{7,5},{8,10},{9,11},{10,... | collective-permute-start | bytes 350216 | tf_op jit(solution)/shard_map/ppermute | solution.py:36
  24.6 0.6 collective-permute-start.7
  25.8 3.4 %collective-permute-done.6.refs_0_ = bf16[8,7296]{1,0:T(8,128)(2,1)S(1)} collective-permute-done((bf16[8,7296]{1,0:T(8,128)(2,1)S(1)}, bf16[8,7296]{1,0:T(8,128)(2,1)S(1)}, u32[]{:S(2)}, u32[]{:S(2)}) %collective-permute-start.6) | collective-permute-done | bytes 116768 | tf_op jit(solution)/shard_map/ppermute | solution.py:36
  29.2 1.7 %collective-permute-done.7.refs_2_ = bf16[8,7296]{1,0:T(8,128)(2,1)S(1)} collective-permute-done((bf16[8,7296]{1,0:T(8,128)(2,1)S(1)}, bf16[8,7296]{1,0:T(8,128)(2,1)S(1)}, u32[]{:S(2)}, u32[]{:S(2)}) %collective-permute-start.7) | collective-permute-done | bytes 116768 | tf_op jit(solution)/shard_map/ppermute | solution.py:36
  31.0 1.3 %collective-permute-done.10.refs_10_ = bf16[8,7296]{1,0:T(8,128)(2,1)S(1)} collective-permute-done((bf16[8,7296]{1,0:T(8,128)(2,1)S(1)}, bf16[8,7296]{1,0:T(8,128)(2,1)S(1)}, u32[]{:S(2)}, u32[]{:S(2)}) %collective-permute-start.10) | collective-permute-done | bytes 116768 | tf_op jit(solution)/shard_map/ppermute | solution.py:36
  32.3 2.7 %shard_map.124 = (bf16[8,7168]{1,0:T(8,128)(2,1)S(1)}, bf16[8,7168]{1,0:T(8,128)(2,1)S(1)}, bf16[8,7168]{1,0:T(8,128)(2,1)S(1)}, bf16[8,7168]{1,0:T(8,128)(2,1)S...) custom-call(s32[1]{0:T(128)} %bitcast.place, ...), custom_call_target="tpu_custom_call" | custom-call | flops 704643072 | bytes 5505024 | tf_op jit(solution)/shard_map/pallas_call | solution.py:228
  36.6 1.8 %collective-permute-start.17 = (bf16[8,7168]{1,0:T(8,128)(2,1)S(1)}, bf16[8,7168]{1,0:T(8,128)(2,1)S(1)}, u32[]{:S(2)}, u32[]{:S(2)}) collective-permute-start(bf16[8,7168]{1,0:T(8,128)(2,1)S(1)} %add_convert_fusion.7), channel_id=1, source_target_pairs={{0,2},{1,3},{2,0},{3,1},{4,6},{5,7},{6,4},{7,5},{8,10},{9,11},{10,... | collective-permute-start | bytes 344072 | tf_op jit(solution)/shard_map/ppermute | solution.py:36
  38.4 0.6 %collective-permute-start.21 = (bf16[8,7168]{1,0:T(8,128)(2,1)S(1)}, bf16[8,7168]{1,0:T(8,128)(2,1)S(1)}, u32[]{:S(2)}, u32[]{:S(2)}) collective-permute-start(bf16[8,7168]{1,0:T(8,128)(2,1)S(1)} %add_convert_fusion.6), channel_id=1, source_target_pairs={{0,2},{1,3},{2,0},{3,1},{4,6},{5,7},{6,4},{7,5},{8,10},{9,11},{10,... | collective-permute-start | bytes 344072 | tf_op jit(solution)/shard_map/ppermute | solution.py:36
  39.1 1.5 %collective-permute-start.25 = (bf16[8,7168]{1,0:T(8,128)(2,1)S(1)}, bf16[8,7168]{1,0:T(8,128)(2,1)S(1)}, u32[]{:S(2)}, u32[]{:S(2)}) collective-permute-start(bf16[8,7168]{1,0:T(8,128)(2,1)S(1)} %add_convert_fusion.3), channel_id=1, source_target_pairs={{0,2},{1,3},{2,0},{3,1},{4,6},{5,7},{6,4},{7,5},{8,10},{9,11},{10,... | collective-permute-start | bytes 344072 | tf_op jit(solution)/shard_map/ppermute | solution.py:36
  40.6 2.0 %collective-permute-done.17 = bf16[8,7168]{1,0:T(8,128)(2,1)S(1)} collective-permute-done((bf16[8,7168]{1,0:T(8,128)(2,1)S(1)}, bf16[8,7168]{1,0:T(8,128)(2,1)S(1)}, u32[]{:S(2)}, u32[]{:S(2)}) %collective-permute-start.17) | collective-permute-done | bytes 114720 | tf_op jit(solution)/shard_map/ppermute | solution.py:36
  42.8 2.3 %collective-permute-done.21 = bf16[8,7168]{1,0:T(8,128)(2,1)S(1)} collective-permute-done((bf16[8,7168]{1,0:T(8,128)(2,1)S(1)}, bf16[8,7168]{1,0:T(8,128)(2,1)S(1)}, u32[]{:S(2)}, u32[]{:S(2)}) %collective-permute-start.21) | collective-permute-done | bytes 114720 | tf_op jit(solution)/shard_map/ppermute | solution.py:36
  45.1 1.8 %collective-permute-start.22 = (bf16[8,7168]{1,0:T(8,128)(2,1)S(1)}, bf16[8,7168]{1,0:T(8,128)(2,1)S(1)}, u32[]{:S(2)}, u32[]{:S(2)}) collective-permute-start(bf16[8,7168]{1,0:T(8,128)(2,1)S(1)} %add_convert_fusion.5), channel_id=1, source_target_pairs={{0,2},{1,3},{2,0},{3,1},{4,6},{5,7},{6,4},{7,5},{8,10},{9,11},{10,... | collective-permute-start | bytes 344072 | tf_op jit(solution)/shard_map/ppermute | solution.py:36
  46.9 2.6 %collective-permute-start.23 = (bf16[8,7168]{1,0:T(8,128)(2,1)S(1)}, bf16[8,7168]{1,0:T(8,128)(2,1)S(1)}, u32[]{:S(2)}, u32[]{:S(2)}) collective-permute-start(bf16[8,7168]{1,0:T(8,128)(2,1)S(1)} %add_convert_fusion.4), channel_id=1, source_target_pairs={{0,8},{1,9},{2,10},{3,11},{4,12},{5,13},{6,14},{7,15},{8,0},{9,1},... | collective-permute-start | bytes 344072 | tf_op jit(solution)/shard_map/ppermute | solution.py:27
  49.5 1.8 %collective-permute-start.26 = (bf16[8,7168]{1,0:T(8,128)(2,1)S(1)}, bf16[8,7168]{1,0:T(8,128)(2,1)S(1)}, u32[]{:S(2)}, u32[]{:S(2)}) collective-permute-start(bf16[8,7168]{1,0:T(8,128)(2,1)S(1)} %add_convert_fusion.2), channel_id=1, source_target_pairs={{0,12},{1,13},{2,14},{3,15},{4,0},{5,1},{6,2},{7,3},{8,4},{9,5},{1... | collective-permute-start | bytes 344072 | tf_op jit(solution)/shard_map/ppermute | solution.py:27
  51.3 1.4 %shard_map.125 = bf16[4,128,512]{2,1,0:T(8,128)(2,1)} custom-call(s32[1]{0:T(128)} %bitcast.place, s32[16]{0:T(128)S(1)} %copy-done.5, bf16[3,128,512]{2,1,0:T(8,128)(2,1)S(1)} %copy-done.3, bf16[128,512]{1,0:T(8,128)(2,1)S(1)} %collective-permute-done.18.returned), custom_call_target="tpu_custom_call" | custom-call | tf_op jit(solution)/shard_map/pallas_call | solution.py:182
  52.7 3.5 %collective-permute-done.23 = bf16[8,7168]{1,0:T(8,128)(2,1)S(1)} collective-permute-done((bf16[8,7168]{1,0:T(8,128)(2,1)S(1)}, bf16[8,7168]{1,0:T(8,128)(2,1)S(1)}, u32[]{:S(2)}, u32[]{:S(2)}) %collective-permute-start.23) | collective-permute-done | bytes 114720 | tf_op jit(solution)/shard_map/ppermute | solution.py:27
  56.2 0.7 %add_convert_fusion = bf16[8,7168]{1,0:T(8,128)(2,1)} fusion(bf16[8,7168]{1,0:T(8,128)(2,1)S(1)} %collective-permute-done.27, bf16[8,7168]{1,0:T(8,128)(2,1)S(1)} %collective-permute-done.26, bf16[8,7168]{1,0:T(8,128)(2,1)S(1)} %collective-permute-done.23, bf16[8,7168]{1,0:T(8,128)(2,1)S(1)} %collective-permute-done.22, bf16[8,7168]{1,0:T(8,128)(2,1)S(1)} %slice.33, ...), kind=kLoop, calls=%fused_computation | loop fusion | flops 688128 | bytes 802816 | tf_op jit(solution)/shard_map/convert_element_type | solution.py:245
  (61 shorter events, 3.8 us)
Async XLA Ops:
  2.7 12.6 %collective-permute-start = (bf16[592,128]{1,0:T(8,128)(2,1)}, bf16[592,128]{1,0:T(8,128)(2,1)S(1)}, u32[]{:S(2)}, u32[]{:S(2)}) collective-permute-start(bf16[592,128]{1,0:T(8,128)(2,1)} %get-tuple-element.35), channel_id=1, source_target_pairs={{0,15},{1,0},{2,1},{3,2},{4,3},{5,4},{6,5},{7,6},{8,7},{9,8},{10,9... | collective-permute-start | bytes 454664 | tf_op jit(solution)/shard_map/ppermute | solution.py:27
  8.1 7.2 %collective-permute-start.1 = (bf16[8,7296]{1,0:T(8,128)(2,1)}, bf16[8,7296]{1,0:T(8,128)(2,1)S(1)}, u32[]{:S(2)}, u32[]{:S(2)}) collective-permute-start(bf16[8,7296]{1,0:T(8,128)(2,1)} %get-tuple-element.36.refs_7_), channel_id=1, source_target_pairs={{0,12},{1,13},{2,14},{3,15},{4,0},{5,1},{6,2},{7,3},{8,4},{9,5},{1... | collective-permute-start | bytes 350216 | tf_op jit(solution)/shard_map/ppermute | solution.py:27
  8.6 13.9 %collective-permute-start.4 = (bf16[8,7296]{1,0:T(8,128)(2,1)}, bf16[8,7296]{1,0:T(8,128)(2,1)S(1)}, u32[]{:S(2)}, u32[]{:S(2)}) collective-permute-start(bf16[8,7296]{1,0:T(8,128)(2,1)} %get-tuple-element.36.refs_7_), channel_id=1, source_target_pairs={{0,2},{1,3},{2,0},{3,1},{4,6},{5,7},{6,4},{7,5},{8,10},{9,11},{10,... | collective-permute-start | bytes 350216 | tf_op jit(solution)/shard_map/ppermute | solution.py:36
  9.3 13.3 %collective-permute-start.3 = (bf16[8,7296]{1,0:T(8,128)(2,1)}, bf16[8,7296]{1,0:T(8,128)(2,1)S(1)}, u32[]{:S(2)}, u32[]{:S(2)}) collective-permute-start(bf16[8,7296]{1,0:T(8,128)(2,1)} %get-tuple-element.36.refs_7_), channel_id=1, source_target_pairs={{0,8},{1,9},{2,10},{3,11},{4,12},{5,13},{6,14},{7,15},{8,0},{9,1},... | collective-permute-start | bytes 350216 | tf_op jit(solution)/shard_map/ppermute | solution.py:27
  9.3 13.3 %collective-permute-start.2 = (bf16[8,7296]{1,0:T(8,128)(2,1)}, bf16[8,7296]{1,0:T(8,128)(2,1)S(1)}, u32[]{:S(2)}, u32[]{:S(2)}) collective-permute-start(bf16[8,7296]{1,0:T(8,128)(2,1)} %get-tuple-element.36.refs_7_), channel_id=1, source_target_pairs={{0,4},{1,5},{2,6},{3,7},{4,8},{5,9},{6,10},{7,11},{8,12},{9,13},{1... | collective-permute-start | bytes 350216 | tf_op jit(solution)/shard_map/ppermute | solution.py:27
  15.3 7.3 %collective-permute-start.5 = (bf16[8,7296]{1,0:T(8,128)(2,1)S(1)}, bf16[8,7296]{1,0:T(8,128)(2,1)S(1)}, u32[]{:S(2)}, u32[]{:S(2)}) collective-permute-start(bf16[8,7296]{1,0:T(8,128)(2,1)S(1)} %collective-permute-done.1.refs_5_), channel_id=1, source_target_pairs={{0,2},{1,3},{2,0},{3,1},{4,6},{5,7},{6,4},{7,5},{8,10},{9,11},{10,... | collective-permute-start | bytes 350216 | tf_op jit(solution)/shard_map/ppermute | solution.py:36
  15.3 9.9 %collective-permute-start.15 = (bf16[8,7296]{1,0:T(8,128)(2,1)}, bf16[8,7296]{1,0:T(8,128)(2,1)}, u32[]{:S(2)}, u32[]{:S(2)}) collective-permute-start(bf16[8,7296]{1,0:T(8,128)(2,1)} %get-tuple-element.36.refs_7_), channel_id=1, source_target_pairs={{0,1},{1,0},{2,3},{3,2},{4,5},{5,4},{6,7},{7,6},{8,9},{9,8},{10,11... | collective-permute-start | bytes 350216 | tf_op jit(solution)/shard_map/ppermute | solution.py:36
  22.6 3.1 %collective-permute-start.12 = (bf16[8,7296]{1,0:T(8,128)(2,1)S(1)}, bf16[8,7296]{1,0:T(8,128)(2,1)S(1)}, u32[]{:S(2)}, u32[]{:S(2)}) collective-permute-start(bf16[8,7296]{1,0:T(8,128)(2,1)S(1)} %collective-permute-done.5.refs_4_), channel_id=1, source_target_pairs={{0,1},{1,0},{2,3},{3,2},{4,5},{5,4},{6,7},{7,6},{8,9},{9,8},{10,11... | collective-permute-start | bytes 350216 | tf_op jit(solution)/shard_map/ppermute | solution.py:36
  23.2 6.0 %collective-permute-start.6 = (bf16[8,7296]{1,0:T(8,128)(2,1)S(1)}, bf16[8,7296]{1,0:T(8,128)(2,1)S(1)}, u32[]{:S(2)}, u32[]{:S(2)}) collective-permute-start(bf16[8,7296]{1,0:T(8,128)(2,1)S(1)} %collective-permute-done.3.refs_1_), channel_id=1, source_target_pairs={{0,2},{1,3},{2,0},{3,1},{4,6},{5,7},{6,4},{7,5},{8,10},{9,11},{10,... | collective-permute-start | bytes 350216 | tf_op jit(solution)/shard_map/ppermute | solution.py:36
  24.6 6.3 %collective-permute-start.7 = (bf16[8,7296]{1,0:T(8,128)(2,1)S(1)}, bf16[8,7296]{1,0:T(8,128)(2,1)S(1)}, u32[]{:S(2)}, u32[]{:S(2)}) collective-permute-start(bf16[8,7296]{1,0:T(8,128)(2,1)S(1)} %collective-permute-done.2.refs_3_), channel_id=1, source_target_pairs={{0,2},{1,3},{2,0},{3,1},{4,6},{5,7},{6,4},{7,5},{8,10},{9,11},{10,... | collective-permute-start | bytes 350216 | tf_op jit(solution)/shard_map/ppermute | solution.py:36
  25.2 5.7 %collective-permute-start.9 = (bf16[8,7296]{1,0:T(8,128)(2,1)S(1)}, bf16[8,7296]{1,0:T(8,128)(2,1)S(1)}, u32[]{:S(2)}, u32[]{:S(2)}) collective-permute-start(bf16[8,7296]{1,0:T(8,128)(2,1)S(1)} %collective-permute-done.3.refs_1_), channel_id=1, source_target_pairs={{0,1},{1,0},{2,3},{3,2},{4,5},{5,4},{6,7},{7,6},{8,9},{9,8},{10,11... | collective-permute-start | bytes 350216 | tf_op jit(solution)/shard_map/ppermute | solution.py:36
  25.2 5.7 %collective-permute-start.11 = (bf16[8,7296]{1,0:T(8,128)(2,1)S(1)}, bf16[8,7296]{1,0:T(8,128)(2,1)S(1)}, u32[]{:S(2)}, u32[]{:S(2)}) collective-permute-start(bf16[8,7296]{1,0:T(8,128)(2,1)S(1)} %collective-permute-done.2.refs_3_), channel_id=1, source_target_pairs={{0,1},{1,0},{2,3},{3,2},{4,5},{5,4},{6,7},{7,6},{8,9},{9,8},{10,11... | collective-permute-start | bytes 350216 | tf_op jit(solution)/shard_map/ppermute | solution.py:36
  25.7 5.2 %collective-permute-start.14 = (bf16[8,7296]{1,0:T(8,128)(2,1)S(1)}, bf16[8,7296]{1,0:T(8,128)(2,1)S(1)}, u32[]{:S(2)}, u32[]{:S(2)}) collective-permute-start(bf16[8,7296]{1,0:T(8,128)(2,1)S(1)} %collective-permute-done.4.refs_6_), channel_id=1, source_target_pairs={{0,1},{1,0},{2,3},{3,2},{4,5},{5,4},{6,7},{7,6},{8,9},{9,8},{10,11... | collective-permute-start | bytes 350216 | tf_op jit(solution)/shard_map/ppermute | solution.py:36
  35.2 5.4 %collective-permute-start.19 = (bf16[16,7168]{1,0:T(8,128)(2,1)S(1)}, bf16[16,7168]{1,0:T(8,128)(2,1)S(1)}, u32[]{:S(2)}, u32[]{:S(2)}) collective-permute-start(bf16[16,7168]{1,0:T(8,128)(2,1)S(1)} %get-tuple-element.50), channel_id=1, source_target_pairs={{0,1},{1,0},{2,3},{3,2},{4,5},{5,4},{6,7},{7,6},{8,9},{9,8},{10,11... | collective-permute-start | bytes 688136 | tf_op jit(solution)/shard_map/ppermute | solution.py:36
  35.5 2.8 %collective-permute-start.20 = (bf16[16,7168]{1,0:T(8,128)(2,1)S(1)}, bf16[16,7168]{1,0:T(8,128)(2,1)S(1)}, u32[]{:S(2)}, u32[]{:S(2)}) collective-permute-start(bf16[16,7168]{1,0:T(8,128)(2,1)S(1)} %get-tuple-element.52), channel_id=1, source_target_pairs={{0,1},{1,0},{2,3},{3,2},{4,5},{5,4},{6,7},{7,6},{8,9},{9,8},{10,11... | collective-permute-start | bytes 688136 | tf_op jit(solution)/shard_map/ppermute | solution.py:36
  35.7 3.3 %collective-permute-start.24 = (bf16[16,7168]{1,0:T(8,128)(2,1)S(1)}, bf16[16,7168]{1,0:T(8,128)(2,1)S(1)}, u32[]{:S(2)}, u32[]{:S(2)}) collective-permute-start(bf16[16,7168]{1,0:T(8,128)(2,1)S(1)} %get-tuple-element.58), channel_id=1, source_target_pairs={{0,1},{1,0},{2,3},{3,2},{4,5},{5,4},{6,7},{7,6},{8,9},{9,8},{10,11... | collective-permute-start | bytes 688136 | tf_op jit(solution)/shard_map/ppermute | solution.py:36
  36.6 6.1 %collective-permute-start.17 = (bf16[8,7168]{1,0:T(8,128)(2,1)S(1)}, bf16[8,7168]{1,0:T(8,128)(2,1)S(1)}, u32[]{:S(2)}, u32[]{:S(2)}) collective-permute-start(bf16[8,7168]{1,0:T(8,128)(2,1)S(1)} %add_convert_fusion.7), channel_id=1, source_target_pairs={{0,2},{1,3},{2,0},{3,1},{4,6},{5,7},{6,4},{7,5},{8,10},{9,11},{10,... | collective-permute-start | bytes 344072 | tf_op jit(solution)/shard_map/ppermute | solution.py:36
  38.4 6.7 %collective-permute-start.21 = (bf16[8,7168]{1,0:T(8,128)(2,1)S(1)}, bf16[8,7168]{1,0:T(8,128)(2,1)S(1)}, u32[]{:S(2)}, u32[]{:S(2)}) collective-permute-start(bf16[8,7168]{1,0:T(8,128)(2,1)S(1)} %add_convert_fusion.6), channel_id=1, source_target_pairs={{0,2},{1,3},{2,0},{3,1},{4,6},{5,7},{6,4},{7,5},{8,10},{9,11},{10,... | collective-permute-start | bytes 344072 | tf_op jit(solution)/shard_map/ppermute | solution.py:36
  39.1 10.4 %collective-permute-start.25 = (bf16[8,7168]{1,0:T(8,128)(2,1)S(1)}, bf16[8,7168]{1,0:T(8,128)(2,1)S(1)}, u32[]{:S(2)}, u32[]{:S(2)}) collective-permute-start(bf16[8,7168]{1,0:T(8,128)(2,1)S(1)} %add_convert_fusion.3), channel_id=1, source_target_pairs={{0,2},{1,3},{2,0},{3,1},{4,6},{5,7},{6,4},{7,5},{8,10},{9,11},{10,... | collective-permute-start | bytes 344072 | tf_op jit(solution)/shard_map/ppermute | solution.py:36
  42.7 10.1 %collective-permute-start.27 = (bf16[8,7168]{1,0:T(8,128)(2,1)S(1)}, bf16[8,7168]{1,0:T(8,128)(2,1)S(1)}, u32[]{:S(2)}, u32[]{:S(2)}) collective-permute-start(bf16[8,7168]{1,0:T(8,128)(2,1)S(1)} %add_convert_fusion.1), channel_id=1, source_target_pairs={{0,4},{1,5},{2,6},{3,7},{4,8},{5,9},{6,10},{7,11},{8,12},{9,13},{1... | collective-permute-start | bytes 344072 | tf_op jit(solution)/shard_map/ppermute | solution.py:27
  42.8 8.6 %collective-permute-start.18 = (bf16[128,512]{1,0:T(8,128)(2,1)S(1)}, bf16[128,512]{1,0:T(8,128)(2,1)S(1)}, u32[]{:S(2)}, u32[]{:S(2)}) collective-permute-start(bf16[128,512]{1,0:T(8,128)(2,1)S(1)} %copy-done.7), channel_id=1, source_target_pairs={{0,1},{1,2},{2,3},{3,4},{4,5},{5,6},{6,7},{7,8},{8,9},{9,10},{10,1... | collective-permute-start | bytes 393224 | tf_op jit(solution)/shard_map/ppermute | solution.py:27
  45.1 7.7 %collective-permute-start.22 = (bf16[8,7168]{1,0:T(8,128)(2,1)S(1)}, bf16[8,7168]{1,0:T(8,128)(2,1)S(1)}, u32[]{:S(2)}, u32[]{:S(2)}) collective-permute-start(bf16[8,7168]{1,0:T(8,128)(2,1)S(1)} %add_convert_fusion.5), channel_id=1, source_target_pairs={{0,2},{1,3},{2,0},{3,1},{4,6},{5,7},{6,4},{7,5},{8,10},{9,11},{10,... | collective-permute-start | bytes 344072 | tf_op jit(solution)/shard_map/ppermute | solution.py:36
  46.9 9.4 %collective-permute-start.23 = (bf16[8,7168]{1,0:T(8,128)(2,1)S(1)}, bf16[8,7168]{1,0:T(8,128)(2,1)S(1)}, u32[]{:S(2)}, u32[]{:S(2)}) collective-permute-start(bf16[8,7168]{1,0:T(8,128)(2,1)S(1)} %add_convert_fusion.4), channel_id=1, source_target_pairs={{0,8},{1,9},{2,10},{3,11},{4,12},{5,13},{6,14},{7,15},{8,0},{9,1},... | collective-permute-start | bytes 344072 | tf_op jit(solution)/shard_map/ppermute | solution.py:27
  49.5 6.7 %collective-permute-start.26 = (bf16[8,7168]{1,0:T(8,128)(2,1)S(1)}, bf16[8,7168]{1,0:T(8,128)(2,1)S(1)}, u32[]{:S(2)}, u32[]{:S(2)}) collective-permute-start(bf16[8,7168]{1,0:T(8,128)(2,1)S(1)} %add_convert_fusion.2), channel_id=1, source_target_pairs={{0,12},{1,13},{2,14},{3,15},{4,0},{5,1},{6,2},{7,3},{8,4},{9,5},{1... | collective-permute-start | bytes 344072 | tf_op jit(solution)/shard_map/ppermute | solution.py:27
  (12 other events, 129.0 us)

commit v14 on v13

--- a/solution.py
+++ b/solution.py
@@ -160,7 +160,7 @@
             pltpu.VMEM((count, width, positions), jnp.bfloat16),
             pltpu.SemaphoreType.DMA((2 * count,)),
         ],
-        compiler_params=pltpu.CompilerParams(vmem_limit_bytes=58 * MIB),
+        compiler_params=pltpu.CompilerParams(vmem_limit_bytes=57 * MIB),
         cost_estimate=pl.CostEstimate(
             flops=2 * count * heads * positions * (width + NOPE),
             bytes_accessed=0,

time: 57.1 us -> 56.2 us (0.984)
  Pallas kernels: 12.6 us -> 11.7 us
    pallas_call x1, Pallas kernels: 2.65 us -> 1.74 us  [expert(): pl.pallas_call(functools.partial(expert_body, count, groups, sizes), out_...]
where the time goes in v14:
time: 56.2 us; the launch traced here: 56.1 us
  starting transfers between devices  22.2 us (40%)
  waiting for transfers between devices  19.7 us (35%)
  Pallas kernels  11.7 us (21%)
  other arithmetic  1.01 us (2%)
  between operations  0.84 us (1%)
  local copies, waits for them, and re-layouts  0.63 us (1%)
    ppermute x8, starting transfers between devices, shifted(): return lax.ppermute(value, axis, pairs)  11.4 us
    ppermute x20, waiting for transfers between devices, swapped(): return lax.ppermute(value, axis, pairs)  11.2 us
    ppermute x20, starting transfers between devices, swapped(): return lax.ppermute(value, axis, pairs)  10.8 us
    ppermute x8, waiting for transfers between devices, shifted(): return lax.ppermute(value, axis, pairs)  8.53 us
    pallas_call x1, Pallas kernels, attend(): pl.pallas_call(functools.partial(attend_body, ranks, visits), out_shape=[...  6.53 us
    pallas_call x1, Pallas kernels, prepare(): pl.pallas_call(functools.partial(prepare_body, groups), out_shape=[jax.Sh...  2.05 us
    pallas_call x1, Pallas kernels, expert(): pl.pallas_call(functools.partial(expert_body, count, groups, sizes), out_...  1.74 us
    pallas_call x1, Pallas kernels, settle(): pl.pallas_call(settle_body, out_shape=jax.ShapeDtypeStruct((stay.shape[0]...  1.39 us
  transfers between devices with their start and end apart: 28, of which 8 were waited for; matrix products, arithmetic and copies ran while one was open for 0% of the time, Pallas kernels for 14%

profile of v14, /device:TPU:0, one launch (start us, length us, event | category | flops | bytes accessed | tf_op | source)
XLA Modules:
  0.0 56.1 jit_solution(10860826888591559371)
XLA Ops:
  0.6 2.0 %shard_map.122 = (bf16[8,7296]{1,0:T(8,128)(2,1)}, bf16[592,128]{1,0:T(8,128)(2,1)}) custom-call(s32[1]{0:T(128)} %bitcast.place, s32[16]{0:T(128)} %moved.5, bf16[8,7168]{1,0:T(8,128)(2,1)} %hidden.1, s32[2,8]{1,0:T(2,128)} %bitcast.8, f32[2,8]{1,0:T(2,128)} %bitcast.9, bf16[4,576,128]{2,1,0:T(8,128)(2,1)} %bitcast.6, bf16[4,576]{1,0:T(4,128)(2,1)} %own.3), custom_call_target="tpu_custom_call" | custom-call | tf_op jit(solution)/shard_map/pallas_call | solution.py:75
  2.7 5.4 %collective-permute-start = (bf16[592,128]{1,0:T(8,128)(2,1)}, bf16[592,128]{1,0:T(8,128)(2,1)S(1)}, u32[]{:S(2)}, u32[]{:S(2)}) collective-permute-start(bf16[592,128]{1,0:T(8,128)(2,1)} %get-tuple-element.35), channel_id=1, source_target_pairs={{0,15},{1,0},{2,1},{3,2},{4,3},{5,4},{6,5},{7,6},{8,7},{9,8},{10,9... | collective-permute-start | bytes 454664 | tf_op jit(solution)/shard_map/ppermute | solution.py:27
  8.6 0.7 %collective-permute-start.4 = (bf16[8,7296]{1,0:T(8,128)(2,1)}, bf16[8,7296]{1,0:T(8,128)(2,1)S(1)}, u32[]{:S(2)}, u32[]{:S(2)}) collective-permute-start(bf16[8,7296]{1,0:T(8,128)(2,1)} %get-tuple-element.36.refs_7_), channel_id=1, source_target_pairs={{0,2},{1,3},{2,0},{3,1},{4,6},{5,7},{6,4},{7,5},{8,10},{9,11},{10,... | collective-permute-start | bytes 350216 | tf_op jit(solution)/shard_map/ppermute | solution.py:36
  9.3 1.0 %collective-permute-start.2 = (bf16[8,7296]{1,0:T(8,128)(2,1)}, bf16[8,7296]{1,0:T(8,128)(2,1)S(1)}, u32[]{:S(2)}, u32[]{:S(2)}) collective-permute-start(bf16[8,7296]{1,0:T(8,128)(2,1)} %get-tuple-element.36.refs_7_), channel_id=1, source_target_pairs={{0,4},{1,5},{2,6},{3,7},{4,8},{5,9},{6,10},{7,11},{8,12},{9,13},{1... | collective-permute-start | bytes 350216 | tf_op jit(solution)/shard_map/ppermute | solution.py:27
  10.3 5.0 %collective-permute-done.1.refs_5_ = bf16[8,7296]{1,0:T(8,128)(2,1)S(1)} collective-permute-done((bf16[8,7296]{1,0:T(8,128)(2,1)}, bf16[8,7296]{1,0:T(8,128)(2,1)S(1)}, u32[]{:S(2)}, u32[]{:S(2)}) %collective-permute-start.1) | collective-permute-done | bytes 116768 | tf_op jit(solution)/shard_map/ppermute | solution.py:27
  15.4 0.6 %copy-done.6 = bf16[592,128]{1,0:T(8,128)(2,1)} copy-done((bf16[592,128]{1,0:T(8,128)(2,1)}, bf16[592,128]{1,0:T(8,128)(2,1)S(1)}, u32[]{:S(2)}) %copy-start.6) | copy-done | bytes 151576
  16.0 6.5 %shard_map.123 = (bf16[3,128,512]{2,1,0:T(8,128)(2,1)}, bf16[128,512]{1,0:T(8,128)(2,1)}) custom-call(s32[1]{0:T(128)} %bitcast.place, s32[16]{0:T(128)} %moved.5, s32[64]{0:T(128)} %lengths.1, bf16[4,576,128]{2,1,0:T(8,128)(2,1)} %bitcast.7, bf16[4,576]{1,0:T(4,128)(2,1)} %own.3, bf16[4,576,1024]{2,1,0:T(8,128)(2,1)} %bitcast.5, bf16[592,128]{1,0:T(8,128)(2,1)} %copy-done.6), custom_call_target="tpu_custom_call" | custom-call | flops 1140850688 | tf_op jit(solution)/shard_map/pallas_call | solution.py:153
  23.2 1.5 %collective-permute-start.6 = (bf16[8,7296]{1,0:T(8,128)(2,1)S(1)}, bf16[8,7296]{1,0:T(8,128)(2,1)S(1)}, u32[]{:S(2)}, u32[]{:S(2)}) collective-permute-start(bf16[8,7296]{1,0:T(8,128)(2,1)S(1)} %collective-permute-done.3.refs_1_), channel_id=1, source_target_pairs={{0,2},{1,3},{2,0},{3,1},{4,6},{5,7},{6,4},{7,5},{8,10},{9,11},{10,... | collective-permute-start | bytes 350216 | tf_op jit(solution)/shard_map/ppermute | solution.py:36
  24.6 0.6 %collective-permute-start.7 = (bf16[8,7296]{1,0:T(8,128)(2,1)S(1)}, bf16[8,7296]{1,0:T(8,128)(2,1)S(1)}, u32[]{:S(2)}, u32[]{:S(2)}) collective-permute-start(bf16[8,7296]{1,0:T(8,128)(2,1)S(1)} %collective-permute-done.2.refs_3_), channel_id=1, source_target_pairs={{0,2},{1,3},{2,0},{3,1},{4,6},{5,7},{6,4},{7,5},{8,10},{9,11},{10,... | collective-permute-start | bytes 350216 | tf_op jit(solution)/shard_map/ppermute | solution.py:36
  25.8 3.4 %collective-permute-done.6.refs_0_ = bf16[8,7296]{1,0:T(8,128)(2,1)S(1)} collective-permute-done((bf16[8,7296]{1,0:T(8,128)(2,1)S(1)}, bf16[8,7296]{1,0:T(8,128)(2,1)S(1)}, u32[]{:S(2)}, u32[]{:S(2)}) %collective-permute-start.6) | collective-permute-done | bytes 116768 | tf_op jit(solution)/shard_map/ppermute | solution.py:36
  29.2 1.7 %collective-permute-done.7.refs_2_ = bf16[8,7296]{1,0:T(8,128)(2,1)S(1)} collective-permute-done((bf16[8,7296]{1,0:T(8,128)(2,1)S(1)}, bf16[8,7296]{1,0:T(8,128)(2,1)S(1)}, u32[]{:S(2)}, u32[]{:S(2)}) %collective-permute-start.7) | collective-permute-done | bytes 116768 | tf_op jit(solution)/shard_map/ppermute | solution.py:36
  31.0 1.3 %collective-permute-done.10.refs_10_ = bf16[8,7296]{1,0:T(8,128)(2,1)S(1)} collective-permute-done((bf16[8,7296]{1,0:T(8,128)(2,1)S(1)}, bf16[8,7296]{1,0:T(8,128)(2,1)S(1)}, u32[]{:S(2)}, u32[]{:S(2)}) %collective-permute-start.10) | collective-permute-done | bytes 116768 | tf_op jit(solution)/shard_map/ppermute | solution.py:36
  32.3 1.7 %shard_map.124 = (bf16[8,7168]{1,0:T(8,128)(2,1)S(1)}, bf16[8,7168]{1,0:T(8,128)(2,1)S(1)}, bf16[8,7168]{1,0:T(8,128)(2,1)S(1)}, bf16[8,7168]{1,0:T(8,128)(2,1)S...) custom-call(s32[1]{0:T(128)} %bitcast.place, ...), custom_call_target="tpu_custom_call" | custom-call | flops 704643072 | bytes 5505024 | tf_op jit(solution)/shard_map/pallas_call | solution.py:228
  35.6 1.8 %collective-permute-start.17 = (bf16[8,7168]{1,0:T(8,128)(2,1)S(1)}, bf16[8,7168]{1,0:T(8,128)(2,1)S(1)}, u32[]{:S(2)}, u32[]{:S(2)}) collective-permute-start(bf16[8,7168]{1,0:T(8,128)(2,1)S(1)} %add_convert_fusion.7), channel_id=1, source_target_pairs={{0,2},{1,3},{2,0},{3,1},{4,6},{5,7},{6,4},{7,5},{8,10},{9,11},{10,... | collective-permute-start | bytes 344072 | tf_op jit(solution)/shard_map/ppermute | solution.py:36
  37.5 0.6 %collective-permute-start.21 = (bf16[8,7168]{1,0:T(8,128)(2,1)S(1)}, bf16[8,7168]{1,0:T(8,128)(2,1)S(1)}, u32[]{:S(2)}, u32[]{:S(2)}) collective-permute-start(bf16[8,7168]{1,0:T(8,128)(2,1)S(1)} %add_convert_fusion.6), channel_id=1, source_target_pairs={{0,2},{1,3},{2,0},{3,1},{4,6},{5,7},{6,4},{7,5},{8,10},{9,11},{10,... | collective-permute-start | bytes 344072 | tf_op jit(solution)/shard_map/ppermute | solution.py:36
  38.1 1.5 %collective-permute-start.25 = (bf16[8,7168]{1,0:T(8,128)(2,1)S(1)}, bf16[8,7168]{1,0:T(8,128)(2,1)S(1)}, u32[]{:S(2)}, u32[]{:S(2)}) collective-permute-start(bf16[8,7168]{1,0:T(8,128)(2,1)S(1)} %add_convert_fusion.3), channel_id=1, source_target_pairs={{0,2},{1,3},{2,0},{3,1},{4,6},{5,7},{6,4},{7,5},{8,10},{9,11},{10,... | collective-permute-start | bytes 344072 | tf_op jit(solution)/shard_map/ppermute | solution.py:36
  39.7 2.0 %collective-permute-done.17 = bf16[8,7168]{1,0:T(8,128)(2,1)S(1)} collective-permute-done((bf16[8,7168]{1,0:T(8,128)(2,1)S(1)}, bf16[8,7168]{1,0:T(8,128)(2,1)S(1)}, u32[]{:S(2)}, u32[]{:S(2)}) %collective-permute-start.17) | collective-permute-done | bytes 114720 | tf_op jit(solution)/shard_map/ppermute | solution.py:36
  41.9 2.3 %collective-permute-done.21 = bf16[8,7168]{1,0:T(8,128)(2,1)S(1)} collective-permute-done((bf16[8,7168]{1,0:T(8,128)(2,1)S(1)}, bf16[8,7168]{1,0:T(8,128)(2,1)S(1)}, u32[]{:S(2)}, u32[]{:S(2)}) %collective-permute-start.21) | collective-permute-done | bytes 114720 | tf_op jit(solution)/shard_map/ppermute | solution.py:36
  44.2 1.8 %collective-permute-start.22 = (bf16[8,7168]{1,0:T(8,128)(2,1)S(1)}, bf16[8,7168]{1,0:T(8,128)(2,1)S(1)}, u32[]{:S(2)}, u32[]{:S(2)}) collective-permute-start(bf16[8,7168]{1,0:T(8,128)(2,1)S(1)} %add_convert_fusion.5), channel_id=1, source_target_pairs={{0,2},{1,3},{2,0},{3,1},{4,6},{5,7},{6,4},{7,5},{8,10},{9,11},{10,... | collective-permute-start | bytes 344072 | tf_op jit(solution)/shard_map/ppermute | solution.py:36
  46.0 2.6 %collective-permute-start.23 = (bf16[8,7168]{1,0:T(8,128)(2,1)S(1)}, bf16[8,7168]{1,0:T(8,128)(2,1)S(1)}, u32[]{:S(2)}, u32[]{:S(2)}) collective-permute-start(bf16[8,7168]{1,0:T(8,128)(2,1)S(1)} %add_convert_fusion.4), channel_id=1, source_target_pairs={{0,8},{1,9},{2,10},{3,11},{4,12},{5,13},{6,14},{7,15},{8,0},{9,1},... | collective-permute-start | bytes 344072 | tf_op jit(solution)/shard_map/ppermute | solution.py:27
  48.6 1.8 %collective-permute-start.26 = (bf16[8,7168]{1,0:T(8,128)(2,1)S(1)}, bf16[8,7168]{1,0:T(8,128)(2,1)S(1)}, u32[]{:S(2)}, u32[]{:S(2)}) collective-permute-start(bf16[8,7168]{1,0:T(8,128)(2,1)S(1)} %add_convert_fusion.2), channel_id=1, source_target_pairs={{0,12},{1,13},{2,14},{3,15},{4,0},{5,1},{6,2},{7,3},{8,4},{9,5},{1... | collective-permute-start | bytes 344072 | tf_op jit(solution)/shard_map/ppermute | solution.py:27
  50.4 1.4 %shard_map.125 = bf16[4,128,512]{2,1,0:T(8,128)(2,1)} custom-call(s32[1]{0:T(128)} %bitcast.place, s32[16]{0:T(128)S(1)} %copy-done.5, bf16[3,128,512]{2,1,0:T(8,128)(2,1)S(1)} %copy-done.3, bf16[128,512]{1,0:T(8,128)(2,1)S(1)} %collective-permute-done.18.returned), custom_call_target="tpu_custom_call" | custom-call | tf_op jit(solution)/shard_map/pallas_call | solution.py:182
  51.8 3.5 %collective-permute-done.23 = bf16[8,7168]{1,0:T(8,128)(2,1)S(1)} collective-permute-done((bf16[8,7168]{1,0:T(8,128)(2,1)S(1)}, bf16[8,7168]{1,0:T(8,128)(2,1)S(1)}, u32[]{:S(2)}, u32[]{:S(2)}) %collective-permute-start.23) | collective-permute-done | bytes 114720 | tf_op jit(solution)/shard_map/ppermute | solution.py:27
  55.3 0.7 %add_convert_fusion = bf16[8,7168]{1,0:T(8,128)(2,1)} fusion(bf16[8,7168]{1,0:T(8,128)(2,1)S(1)} %collective-permute-done.27, bf16[8,7168]{1,0:T(8,128)(2,1)S(1)} %collective-permute-done.26, bf16[8,7168]{1,0:T(8,128)(2,1)S(1)} %collective-permute-done.23, bf16[8,7168]{1,0:T(8,128)(2,1)S(1)} %collective-permute-done.22, bf16[8,7168]{1,0:T(8,128)(2,1)S(1)} %slice.33, ...), kind=kLoop, calls=%fused_computation | loop fusion | flops 688128 | bytes 802816 | tf_op jit(solution)/shard_map/convert_element_type | solution.py:245
  (61 shorter events, 3.8 us)
Async XLA Ops:
  2.7 12.6 %collective-permute-start = (bf16[592,128]{1,0:T(8,128)(2,1)}, bf16[592,128]{1,0:T(8,128)(2,1)S(1)}, u32[]{:S(2)}, u32[]{:S(2)}) collective-permute-start(bf16[592,128]{1,0:T(8,128)(2,1)} %get-tuple-element.35), channel_id=1, source_target_pairs={{0,15},{1,0},{2,1},{3,2},{4,3},{5,4},{6,5},{7,6},{8,7},{9,8},{10,9... | collective-permute-start | bytes 454664 | tf_op jit(solution)/shard_map/ppermute | solution.py:27
  8.1 7.2 %collective-permute-start.1 = (bf16[8,7296]{1,0:T(8,128)(2,1)}, bf16[8,7296]{1,0:T(8,128)(2,1)S(1)}, u32[]{:S(2)}, u32[]{:S(2)}) collective-permute-start(bf16[8,7296]{1,0:T(8,128)(2,1)} %get-tuple-element.36.refs_7_), channel_id=1, source_target_pairs={{0,12},{1,13},{2,14},{3,15},{4,0},{5,1},{6,2},{7,3},{8,4},{9,5},{1... | collective-permute-start | bytes 350216 | tf_op jit(solution)/shard_map/ppermute | solution.py:27
  8.6 13.9 %collective-permute-start.4 = (bf16[8,7296]{1,0:T(8,128)(2,1)}, bf16[8,7296]{1,0:T(8,128)(2,1)S(1)}, u32[]{:S(2)}, u32[]{:S(2)}) collective-permute-start(bf16[8,7296]{1,0:T(8,128)(2,1)} %get-tuple-element.36.refs_7_), channel_id=1, source_target_pairs={{0,2},{1,3},{2,0},{3,1},{4,6},{5,7},{6,4},{7,5},{8,10},{9,11},{10,... | collective-permute-start | bytes 350216 | tf_op jit(solution)/shard_map/ppermute | solution.py:36
  9.3 13.3 %collective-permute-start.3 = (bf16[8,7296]{1,0:T(8,128)(2,1)}, bf16[8,7296]{1,0:T(8,128)(2,1)S(1)}, u32[]{:S(2)}, u32[]{:S(2)}) collective-permute-start(bf16[8,7296]{1,0:T(8,128)(2,1)} %get-tuple-element.36.refs_7_), channel_id=1, source_target_pairs={{0,8},{1,9},{2,10},{3,11},{4,12},{5,13},{6,14},{7,15},{8,0},{9,1},... | collective-permute-start | bytes 350216 | tf_op jit(solution)/shard_map/ppermute | solution.py:27
  9.3 13.3 %collective-permute-start.2 = (bf16[8,7296]{1,0:T(8,128)(2,1)}, bf16[8,7296]{1,0:T(8,128)(2,1)S(1)}, u32[]{:S(2)}, u32[]{:S(2)}) collective-permute-start(bf16[8,7296]{1,0:T(8,128)(2,1)} %get-tuple-element.36.refs_7_), channel_id=1, source_target_pairs={{0,4},{1,5},{2,6},{3,7},{4,8},{5,9},{6,10},{7,11},{8,12},{9,13},{1... | collective-permute-start | bytes 350216 | tf_op jit(solution)/shard_map/ppermute | solution.py:27
  15.3 7.3 %collective-permute-start.5 = (bf16[8,7296]{1,0:T(8,128)(2,1)S(1)}, bf16[8,7296]{1,0:T(8,128)(2,1)S(1)}, u32[]{:S(2)}, u32[]{:S(2)}) collective-permute-start(bf16[8,7296]{1,0:T(8,128)(2,1)S(1)} %collective-permute-done.1.refs_5_), channel_id=1, source_target_pairs={{0,2},{1,3},{2,0},{3,1},{4,6},{5,7},{6,4},{7,5},{8,10},{9,11},{10,... | collective-permute-start | bytes 350216 | tf_op jit(solution)/shard_map/ppermute | solution.py:36
  15.3 9.9 %collective-permute-start.15 = (bf16[8,7296]{1,0:T(8,128)(2,1)}, bf16[8,7296]{1,0:T(8,128)(2,1)S(1)}, u32[]{:S(2)}, u32[]{:S(2)}) collective-permute-start(bf16[8,7296]{1,0:T(8,128)(2,1)} %get-tuple-element.36.refs_7_), channel_id=1, source_target_pairs={{0,1},{1,0},{2,3},{3,2},{4,5},{5,4},{6,7},{7,6},{8,9},{9,8},{10,11... | collective-permute-start | bytes 350216 | tf_op jit(solution)/shard_map/ppermute | solution.py:36
  22.6 3.1 %collective-permute-start.12 = (bf16[8,7296]{1,0:T(8,128)(2,1)S(1)}, bf16[8,7296]{1,0:T(8,128)(2,1)S(1)}, u32[]{:S(2)}, u32[]{:S(2)}) collective-permute-start(bf16[8,7296]{1,0:T(8,128)(2,1)S(1)} %collective-permute-done.5.refs_4_), channel_id=1, source_target_pairs={{0,1},{1,0},{2,3},{3,2},{4,5},{5,4},{6,7},{7,6},{8,9},{9,8},{10,11... | collective-permute-start | bytes 350216 | tf_op jit(solution)/shard_map/ppermute | solution.py:36
  23.2 6.0 %collective-permute-start.6 = (bf16[8,7296]{1,0:T(8,128)(2,1)S(1)}, bf16[8,7296]{1,0:T(8,128)(2,1)S(1)}, u32[]{:S(2)}, u32[]{:S(2)}) collective-permute-start(bf16[8,7296]{1,0:T(8,128)(2,1)S(1)} %collective-permute-done.3.refs_1_), channel_id=1, source_target_pairs={{0,2},{1,3},{2,0},{3,1},{4,6},{5,7},{6,4},{7,5},{8,10},{9,11},{10,... | collective-permute-start | bytes 350216 | tf_op jit(solution)/shard_map/ppermute | solution.py:36
  24.6 6.3 %collective-permute-start.7 = (bf16[8,7296]{1,0:T(8,128)(2,1)S(1)}, bf16[8,7296]{1,0:T(8,128)(2,1)S(1)}, u32[]{:S(2)}, u32[]{:S(2)}) collective-permute-start(bf16[8,7296]{1,0:T(8,128)(2,1)S(1)} %collective-permute-done.2.refs_3_), channel_id=1, source_target_pairs={{0,2},{1,3},{2,0},{3,1},{4,6},{5,7},{6,4},{7,5},{8,10},{9,11},{10,... | collective-permute-start | bytes 350216 | tf_op jit(solution)/shard_map/ppermute | solution.py:36
  25.2 5.7 %collective-permute-start.9 = (bf16[8,7296]{1,0:T(8,128)(2,1)S(1)}, bf16[8,7296]{1,0:T(8,128)(2,1)S(1)}, u32[]{:S(2)}, u32[]{:S(2)}) collective-permute-start(bf16[8,7296]{1,0:T(8,128)(2,1)S(1)} %collective-permute-done.3.refs_1_), channel_id=1, source_target_pairs={{0,1},{1,0},{2,3},{3,2},{4,5},{5,4},{6,7},{7,6},{8,9},{9,8},{10,11... | collective-permute-start | bytes 350216 | tf_op jit(solution)/shard_map/ppermute | solution.py:36
  25.2 5.7 %collective-permute-start.11 = (bf16[8,7296]{1,0:T(8,128)(2,1)S(1)}, bf16[8,7296]{1,0:T(8,128)(2,1)S(1)}, u32[]{:S(2)}, u32[]{:S(2)}) collective-permute-start(bf16[8,7296]{1,0:T(8,128)(2,1)S(1)} %collective-permute-done.2.refs_3_), channel_id=1, source_target_pairs={{0,1},{1,0},{2,3},{3,2},{4,5},{5,4},{6,7},{7,6},{8,9},{9,8},{10,11... | collective-permute-start | bytes 350216 | tf_op jit(solution)/shard_map/ppermute | solution.py:36
  25.7 5.2 %collective-permute-start.14 = (bf16[8,7296]{1,0:T(8,128)(2,1)S(1)}, bf16[8,7296]{1,0:T(8,128)(2,1)S(1)}, u32[]{:S(2)}, u32[]{:S(2)}) collective-permute-start(bf16[8,7296]{1,0:T(8,128)(2,1)S(1)} %collective-permute-done.4.refs_6_), channel_id=1, source_target_pairs={{0,1},{1,0},{2,3},{3,2},{4,5},{5,4},{6,7},{7,6},{8,9},{9,8},{10,11... | collective-permute-start | bytes 350216 | tf_op jit(solution)/shard_map/ppermute | solution.py:36
  34.3 5.4 %collective-permute-start.19 = (bf16[16,7168]{1,0:T(8,128)(2,1)S(1)}, bf16[16,7168]{1,0:T(8,128)(2,1)S(1)}, u32[]{:S(2)}, u32[]{:S(2)}) collective-permute-start(bf16[16,7168]{1,0:T(8,128)(2,1)S(1)} %get-tuple-element.50), channel_id=1, source_target_pairs={{0,1},{1,0},{2,3},{3,2},{4,5},{5,4},{6,7},{7,6},{8,9},{9,8},{10,11... | collective-permute-start | bytes 688136 | tf_op jit(solution)/shard_map/ppermute | solution.py:36
  34.6 2.8 %collective-permute-start.20 = (bf16[16,7168]{1,0:T(8,128)(2,1)S(1)}, bf16[16,7168]{1,0:T(8,128)(2,1)S(1)}, u32[]{:S(2)}, u32[]{:S(2)}) collective-permute-start(bf16[16,7168]{1,0:T(8,128)(2,1)S(1)} %get-tuple-element.52), channel_id=1, source_target_pairs={{0,1},{1,0},{2,3},{3,2},{4,5},{5,4},{6,7},{7,6},{8,9},{9,8},{10,11... | collective-permute-start | bytes 688136 | tf_op jit(solution)/shard_map/ppermute | solution.py:36
  34.8 3.4 %collective-permute-start.24 = (bf16[16,7168]{1,0:T(8,128)(2,1)S(1)}, bf16[16,7168]{1,0:T(8,128)(2,1)S(1)}, u32[]{:S(2)}, u32[]{:S(2)}) collective-permute-start(bf16[16,7168]{1,0:T(8,128)(2,1)S(1)} %get-tuple-element.58), channel_id=1, source_target_pairs={{0,1},{1,0},{2,3},{3,2},{4,5},{5,4},{6,7},{7,6},{8,9},{9,8},{10,11... | collective-permute-start | bytes 688136 | tf_op jit(solution)/shard_map/ppermute | solution.py:36
  35.6 6.1 %collective-permute-start.17 = (bf16[8,7168]{1,0:T(8,128)(2,1)S(1)}, bf16[8,7168]{1,0:T(8,128)(2,1)S(1)}, u32[]{:S(2)}, u32[]{:S(2)}) collective-permute-start(bf16[8,7168]{1,0:T(8,128)(2,1)S(1)} %add_convert_fusion.7), channel_id=1, source_target_pairs={{0,2},{1,3},{2,0},{3,1},{4,6},{5,7},{6,4},{7,5},{8,10},{9,11},{10,... | collective-permute-start | bytes 344072 | tf_op jit(solution)/shard_map/ppermute | solution.py:36
  37.5 6.7 %collective-permute-start.21 = (bf16[8,7168]{1,0:T(8,128)(2,1)S(1)}, bf16[8,7168]{1,0:T(8,128)(2,1)S(1)}, u32[]{:S(2)}, u32[]{:S(2)}) collective-permute-start(bf16[8,7168]{1,0:T(8,128)(2,1)S(1)} %add_convert_fusion.6), channel_id=1, source_target_pairs={{0,2},{1,3},{2,0},{3,1},{4,6},{5,7},{6,4},{7,5},{8,10},{9,11},{10,... | collective-permute-start | bytes 344072 | tf_op jit(solution)/shard_map/ppermute | solution.py:36
  38.1 10.4 %collective-permute-start.25 = (bf16[8,7168]{1,0:T(8,128)(2,1)S(1)}, bf16[8,7168]{1,0:T(8,128)(2,1)S(1)}, u32[]{:S(2)}, u32[]{:S(2)}) collective-permute-start(bf16[8,7168]{1,0:T(8,128)(2,1)S(1)} %add_convert_fusion.3), channel_id=1, source_target_pairs={{0,2},{1,3},{2,0},{3,1},{4,6},{5,7},{6,4},{7,5},{8,10},{9,11},{10,... | collective-permute-start | bytes 344072 | tf_op jit(solution)/shard_map/ppermute | solution.py:36
  41.7 10.1 %collective-permute-start.27 = (bf16[8,7168]{1,0:T(8,128)(2,1)S(1)}, bf16[8,7168]{1,0:T(8,128)(2,1)S(1)}, u32[]{:S(2)}, u32[]{:S(2)}) collective-permute-start(bf16[8,7168]{1,0:T(8,128)(2,1)S(1)} %add_convert_fusion.1), channel_id=1, source_target_pairs={{0,4},{1,5},{2,6},{3,7},{4,8},{5,9},{6,10},{7,11},{8,12},{9,13},{1... | collective-permute-start | bytes 344072 | tf_op jit(solution)/shard_map/ppermute | solution.py:27
  41.8 8.6 %collective-permute-start.18 = (bf16[128,512]{1,0:T(8,128)(2,1)S(1)}, bf16[128,512]{1,0:T(8,128)(2,1)S(1)}, u32[]{:S(2)}, u32[]{:S(2)}) collective-permute-start(bf16[128,512]{1,0:T(8,128)(2,1)S(1)} %copy-done.7), channel_id=1, source_target_pairs={{0,1},{1,2},{2,3},{3,4},{4,5},{5,6},{6,7},{7,8},{8,9},{9,10},{10,1... | collective-permute-start | bytes 393224 | tf_op jit(solution)/shard_map/ppermute | solution.py:27
  44.2 7.7 %collective-permute-start.22 = (bf16[8,7168]{1,0:T(8,128)(2,1)S(1)}, bf16[8,7168]{1,0:T(8,128)(2,1)S(1)}, u32[]{:S(2)}, u32[]{:S(2)}) collective-permute-start(bf16[8,7168]{1,0:T(8,128)(2,1)S(1)} %add_convert_fusion.5), channel_id=1, source_target_pairs={{0,2},{1,3},{2,0},{3,1},{4,6},{5,7},{6,4},{7,5},{8,10},{9,11},{10,... | collective-permute-start | bytes 344072 | tf_op jit(solution)/shard_map/ppermute | solution.py:36
  46.0 9.4 %collective-permute-start.23 = (bf16[8,7168]{1,0:T(8,128)(2,1)S(1)}, bf16[8,7168]{1,0:T(8,128)(2,1)S(1)}, u32[]{:S(2)}, u32[]{:S(2)}) collective-permute-start(bf16[8,7168]{1,0:T(8,128)(2,1)S(1)} %add_convert_fusion.4), channel_id=1, source_target_pairs={{0,8},{1,9},{2,10},{3,11},{4,12},{5,13},{6,14},{7,15},{8,0},{9,1},... | collective-permute-start | bytes 344072 | tf_op jit(solution)/shard_map/ppermute | solution.py:27
  48.6 6.7 %collective-permute-start.26 = (bf16[8,7168]{1,0:T(8,128)(2,1)S(1)}, bf16[8,7168]{1,0:T(8,128)(2,1)S(1)}, u32[]{:S(2)}, u32[]{:S(2)}) collective-permute-start(bf16[8,7168]{1,0:T(8,128)(2,1)S(1)} %add_convert_fusion.2), channel_id=1, source_target_pairs={{0,12},{1,13},{2,14},{3,15},{4,0},{5,1},{6,2},{7,3},{8,4},{9,5},{1... | collective-permute-start | bytes 344072 | tf_op jit(solution)/shard_map/ppermute | solution.py:27
  (12 other events, 129.1 us)

commit v15 on v14

--- a/solution.py
+++ b/solution.py
@@ -279,7 +279,7 @@
     columns = {r: rotated(rows, axis, r) for r in order}
     across = {0: swapped(rows, axis, 2)}
 
-    lead = order[-1]
+    lead = order[0]
     visiting, columns[lead] = lax.optimization_barrier((visiting, columns[lead]))
     ahead = {lead: columns.pop(lead)}
     crossing = swapped(ahead[lead], axis, 2)

time: 56.2 us -> 58.9 us (1.048)
  waiting for transfers between devices: 19.7 us -> 24.2 us
  starting transfers between devices: 22.2 us -> 20.4 us
    ppermute x8, waiting for transfers between devices: 8.53 us -> 13.1 us  [shifted(): return lax.ppermute(value, axis, pairs)]
    ppermute x8, starting transfers between devices: 11.4 us -> 10.2 us  [shifted(): return lax.ppermute(value, axis, pairs)]
  transfers between devices with their start and end apart: 28 -> 28, of which waited for: 8 -> 9; matrix products, arithmetic and copies ran while one was open for 0% -> 0% of each run, Pallas kernels for 14% -> 13%
where the time goes in v15:
time: 58.9 us; the launch traced here: 58.8 us
  waiting for transfers between devices  24.2 us (41%)
  starting transfers between devices  20.4 us (35%)
  Pallas kernels  11.7 us (20%)
  other arithmetic  0.99 us (2%)
  between operations  0.84 us (1%)
  local copies, waits for them, and re-layouts  0.62 us (1%)
    ppermute x8, waiting for transfers between devices, shifted(): return lax.ppermute(value, axis, pairs)  13.1 us
    ppermute x20, waiting for transfers between devices, swapped(): return lax.ppermute(value, axis, pairs)  11.1 us
    ppermute x20, starting transfers between devices, swapped(): return lax.ppermute(value, axis, pairs)  10.2 us
    ppermute x8, starting transfers between devices, shifted(): return lax.ppermute(value, axis, pairs)  10.2 us
    pallas_call x1, Pallas kernels, attend(): pl.pallas_call(functools.partial(attend_body, ranks, visits), out_shape=[...  6.53 us
    pallas_call x1, Pallas kernels, prepare(): pl.pallas_call(functools.partial(prepare_body, groups), out_shape=[jax.Sh...  2.05 us
    pallas_call x1, Pallas kernels, expert(): pl.pallas_call(functools.partial(expert_body, count, groups, sizes), out_...  1.73 us
    pallas_call x1, Pallas kernels, settle(): pl.pallas_call(settle_body, out_shape=jax.ShapeDtypeStruct((stay.shape[0]...  1.39 us
  transfers between devices with their start and end apart: 28, of which 9 were waited for; matrix products, arithmetic and copies ran while one was open for 0% of the time, Pallas kernels for 13%

profile of v15, /device:TPU:0, one launch (start us, length us, event | category | flops | bytes accessed | tf_op | source)
XLA Modules:
  0.0 58.8 jit_solution(1573084302542387907)
XLA Ops:
  0.6 2.0 %shard_map.122 = (bf16[8,7296]{1,0:T(8,128)(2,1)}, bf16[592,128]{1,0:T(8,128)(2,1)}) custom-call(s32[1]{0:T(128)} %bitcast.place, s32[16]{0:T(128)} %moved.5, bf16[8,7168]{1,0:T(8,128)(2,1)} %hidden.1, s32[2,8]{1,0:T(2,128)} %bitcast.8, f32[2,8]{1,0:T(2,128)} %bitcast.9, bf16[4,576,128]{2,1,0:T(8,128)(2,1)} %bitcast.6, bf16[4,576]{1,0:T(4,128)(2,1)} %own.3), custom_call_target="tpu_custom_call" | custom-call | tf_op jit(solution)/shard_map/pallas_call | solution.py:75
  2.7 5.4 %collective-permute-start = (bf16[592,128]{1,0:T(8,128)(2,1)}, bf16[592,128]{1,0:T(8,128)(2,1)S(1)}, u32[]{:S(2)}, u32[]{:S(2)}) collective-permute-start(bf16[592,128]{1,0:T(8,128)(2,1)} %get-tuple-element.35), channel_id=1, source_target_pairs={{0,15},{1,0},{2,1},{3,2},{4,3},{5,4},{6,5},{7,6},{8,7},{9,8},{10,9... | collective-permute-start | bytes 454664 | tf_op jit(solution)/shard_map/ppermute | solution.py:27
  8.3 1.3 %collective-permute-start.3 = (bf16[8,7296]{1,0:T(8,128)(2,1)}, bf16[8,7296]{1,0:T(8,128)(2,1)S(1)}, u32[]{:S(2)}, u32[]{:S(2)}) collective-permute-start(bf16[8,7296]{1,0:T(8,128)(2,1)} %get-tuple-element.36.refs_7_), channel_id=1, source_target_pairs={{0,12},{1,13},{2,14},{3,15},{4,0},{5,1},{6,2},{7,3},{8,4},{9,5},{1... | collective-permute-start | bytes 350216 | tf_op jit(solution)/shard_map/ppermute | solution.py:27
  9.6 0.7 %collective-permute-start.2 = (bf16[8,7296]{1,0:T(8,128)(2,1)}, bf16[8,7296]{1,0:T(8,128)(2,1)S(1)}, u32[]{:S(2)}, u32[]{:S(2)}) collective-permute-start(bf16[8,7296]{1,0:T(8,128)(2,1)} %get-tuple-element.36.refs_7_), channel_id=1, source_target_pairs={{0,4},{1,5},{2,6},{3,7},{4,8},{5,9},{6,10},{7,11},{8,12},{9,13},{1... | collective-permute-start | bytes 350216 | tf_op jit(solution)/shard_map/ppermute | solution.py:27
  10.3 8.4 %collective-permute-done.1.refs_1_ = bf16[8,7296]{1,0:T(8,128)(2,1)S(1)} collective-permute-done((bf16[8,7296]{1,0:T(8,128)(2,1)}, bf16[8,7296]{1,0:T(8,128)(2,1)S(1)}, u32[]{:S(2)}, u32[]{:S(2)}) %collective-permute-start.1) | collective-permute-done | bytes 116768 | tf_op jit(solution)/shard_map/ppermute | solution.py:27
  19.4 6.5 %shard_map.123 = (bf16[3,128,512]{2,1,0:T(8,128)(2,1)}, bf16[128,512]{1,0:T(8,128)(2,1)}) custom-call(s32[1]{0:T(128)} %bitcast.place, s32[16]{0:T(128)} %moved.5, s32[64]{0:T(128)} %lengths.1, bf16[4,576,128]{2,1,0:T(8,128)(2,1)} %bitcast.7, bf16[4,576]{1,0:T(4,128)(2,1)} %own.3, bf16[4,576,1024]{2,1,0:T(8,128)(2,1)} %bitcast.5, bf16[592,128]{1,0:T(8,128)(2,1)} %copy-done.6), custom_call_target="tpu_custom_call" | custom-call | flops 1140850688 | tf_op jit(solution)/shard_map/pallas_call | solution.py:153
  26.6 1.4 %collective-permute-start.6 = (bf16[8,7296]{1,0:T(8,128)(2,1)S(1)}, bf16[8,7296]{1,0:T(8,128)(2,1)S(1)}, u32[]{:S(2)}, u32[]{:S(2)}) collective-permute-start(bf16[8,7296]{1,0:T(8,128)(2,1)S(1)} %collective-permute-done.2.refs_3_), channel_id=1, source_target_pairs={{0,2},{1,3},{2,0},{3,1},{4,6},{5,7},{6,4},{7,5},{8,10},{9,11},{10,... | collective-permute-start | bytes 350216 | tf_op jit(solution)/shard_map/ppermute | solution.py:36
  28.1 0.6 collective-permute-start.7
  29.2 3.4 %collective-permute-done.6.refs_2_ = bf16[8,7296]{1,0:T(8,128)(2,1)S(1)} collective-permute-done((bf16[8,7296]{1,0:T(8,128)(2,1)S(1)}, bf16[8,7296]{1,0:T(8,128)(2,1)S(1)}, u32[]{:S(2)}, u32[]{:S(2)}) %collective-permute-start.6) | collective-permute-done | bytes 116768 | tf_op jit(solution)/shard_map/ppermute | solution.py:36
  32.6 1.7 %collective-permute-done.7.refs_4_ = bf16[8,7296]{1,0:T(8,128)(2,1)S(1)} collective-permute-done((bf16[8,7296]{1,0:T(8,128)(2,1)S(1)}, bf16[8,7296]{1,0:T(8,128)(2,1)S(1)}, u32[]{:S(2)}, u32[]{:S(2)}) %collective-permute-start.7) | collective-permute-done | bytes 116768 | tf_op jit(solution)/shard_map/ppermute | solution.py:36
  34.4 1.3 %collective-permute-done.12.refs_12_ = bf16[8,7296]{1,0:T(8,128)(2,1)S(1)} collective-permute-done((bf16[8,7296]{1,0:T(8,128)(2,1)S(1)}, bf16[8,7296]{1,0:T(8,128)(2,1)S(1)}, u32[]{:S(2)}, u32[]{:S(2)}) %collective-permute-start.12) | collective-permute-done | bytes 116768 | tf_op jit(solution)/shard_map/ppermute | solution.py:36
  35.7 1.7 %shard_map.124 = (bf16[8,7168]{1,0:T(8,128)(2,1)S(1)}, bf16[8,7168]{1,0:T(8,128)(2,1)S(1)}, bf16[8,7168]{1,0:T(8,128)(2,1)S(1)}, bf16[8,7168]{1,0:T(8,128)(2,1)S...) custom-call(s32[1]{0:T(128)} %bitcast.place, ...), custom_call_target="tpu_custom_call" | custom-call | flops 704643072 | bytes 5505024 | tf_op jit(solution)/shard_map/pallas_call | solution.py:228
  39.0 1.8 %collective-permute-start.17 = (bf16[8,7168]{1,0:T(8,128)(2,1)S(1)}, bf16[8,7168]{1,0:T(8,128)(2,1)S(1)}, u32[]{:S(2)}, u32[]{:S(2)}) collective-permute-start(bf16[8,7168]{1,0:T(8,128)(2,1)S(1)} %add_convert_fusion.7), channel_id=1, source_target_pairs={{0,2},{1,3},{2,0},{3,1},{4,6},{5,7},{6,4},{7,5},{8,10},{9,11},{10,... | collective-permute-start | bytes 344072 | tf_op jit(solution)/shard_map/ppermute | solution.py:36
  40.9 0.6 %collective-permute-start.21 = (bf16[8,7168]{1,0:T(8,128)(2,1)S(1)}, bf16[8,7168]{1,0:T(8,128)(2,1)S(1)}, u32[]{:S(2)}, u32[]{:S(2)}) collective-permute-start(bf16[8,7168]{1,0:T(8,128)(2,1)S(1)} %add_convert_fusion.6), channel_id=1, source_target_pairs={{0,2},{1,3},{2,0},{3,1},{4,6},{5,7},{6,4},{7,5},{8,10},{9,11},{10,... | collective-permute-start | bytes 344072 | tf_op jit(solution)/shard_map/ppermute | solution.py:36
  41.6 1.5 %collective-permute-start.25 = (bf16[8,7168]{1,0:T(8,128)(2,1)S(1)}, bf16[8,7168]{1,0:T(8,128)(2,1)S(1)}, u32[]{:S(2)}, u32[]{:S(2)}) collective-permute-start(bf16[8,7168]{1,0:T(8,128)(2,1)S(1)} %add_convert_fusion.3), channel_id=1, source_target_pairs={{0,2},{1,3},{2,0},{3,1},{4,6},{5,7},{6,4},{7,5},{8,10},{9,11},{10,... | collective-permute-start | bytes 344072 | tf_op jit(solution)/shard_map/ppermute | solution.py:36
  43.1 2.0 %collective-permute-done.17 = bf16[8,7168]{1,0:T(8,128)(2,1)S(1)} collective-permute-done((bf16[8,7168]{1,0:T(8,128)(2,1)S(1)}, bf16[8,7168]{1,0:T(8,128)(2,1)S(1)}, u32[]{:S(2)}, u32[]{:S(2)}) %collective-permute-start.17) | collective-permute-done | bytes 114720 | tf_op jit(solution)/shard_map/ppermute | solution.py:36
  45.3 2.3 %collective-permute-done.21 = bf16[8,7168]{1,0:T(8,128)(2,1)S(1)} collective-permute-done((bf16[8,7168]{1,0:T(8,128)(2,1)S(1)}, bf16[8,7168]{1,0:T(8,128)(2,1)S(1)}, u32[]{:S(2)}, u32[]{:S(2)}) %collective-permute-start.21) | collective-permute-done | bytes 114720 | tf_op jit(solution)/shard_map/ppermute | solution.py:36
  47.6 1.8 %collective-permute-start.22 = (bf16[8,7168]{1,0:T(8,128)(2,1)S(1)}, bf16[8,7168]{1,0:T(8,128)(2,1)S(1)}, u32[]{:S(2)}, u32[]{:S(2)}) collective-permute-start(bf16[8,7168]{1,0:T(8,128)(2,1)S(1)} %add_convert_fusion.5), channel_id=1, source_target_pairs={{0,2},{1,3},{2,0},{3,1},{4,6},{5,7},{6,4},{7,5},{8,10},{9,11},{10,... | collective-permute-start | bytes 344072 | tf_op jit(solution)/shard_map/ppermute | solution.py:36
  49.4 0.8 %collective-permute-start.23 = (bf16[8,7168]{1,0:T(8,128)(2,1)S(1)}, bf16[8,7168]{1,0:T(8,128)(2,1)S(1)}, u32[]{:S(2)}, u32[]{:S(2)}) collective-permute-start(bf16[8,7168]{1,0:T(8,128)(2,1)S(1)} %add_convert_fusion.4), channel_id=1, source_target_pairs={{0,8},{1,9},{2,10},{3,11},{4,12},{5,13},{6,14},{7,15},{8,0},{9,1},... | collective-permute-start | bytes 344072 | tf_op jit(solution)/shard_map/ppermute | solution.py:27
  50.2 1.8 %collective-permute-start.26 = (bf16[8,7168]{1,0:T(8,128)(2,1)S(1)}, bf16[8,7168]{1,0:T(8,128)(2,1)S(1)}, u32[]{:S(2)}, u32[]{:S(2)}) collective-permute-start(bf16[8,7168]{1,0:T(8,128)(2,1)S(1)} %add_convert_fusion.2), channel_id=1, source_target_pairs={{0,12},{1,13},{2,14},{3,15},{4,0},{5,1},{6,2},{7,3},{8,4},{9,5},{1... | collective-permute-start | bytes 344072 | tf_op jit(solution)/shard_map/ppermute | solution.py:27
  52.0 1.1 %collective-permute-done.18.returned = bf16[128,512]{1,0:T(8,128)(2,1)S(1)} collective-permute-done((bf16[128,512]{1,0:T(8,128)(2,1)S(1)}, bf16[128,512]{1,0:T(8,128)(2,1)S(1)}, u32[]{:S(2)}, u32[]{:S(2)}) %collective-permute-start.18) | collective-permute-done | bytes 131104 | tf_op jit(solution)/shard_map/ppermute | solution.py:27
  53.1 1.4 %shard_map.125 = bf16[4,128,512]{2,1,0:T(8,128)(2,1)} custom-call(s32[1]{0:T(128)} %bitcast.place, s32[16]{0:T(128)S(1)} %copy-done.5, bf16[3,128,512]{2,1,0:T(8,128)(2,1)S(1)} %copy-done.3, bf16[128,512]{1,0:T(8,128)(2,1)S(1)} %collective-permute-done.18.returned), custom_call_target="tpu_custom_call" | custom-call | tf_op jit(solution)/shard_map/pallas_call | solution.py:182
  54.5 3.5 %collective-permute-done.23 = bf16[8,7168]{1,0:T(8,128)(2,1)S(1)} collective-permute-done((bf16[8,7168]{1,0:T(8,128)(2,1)S(1)}, bf16[8,7168]{1,0:T(8,128)(2,1)S(1)}, u32[]{:S(2)}, u32[]{:S(2)}) %collective-permute-start.23) | collective-permute-done | bytes 114720 | tf_op jit(solution)/shard_map/ppermute | solution.py:27
  58.0 0.7 %add_convert_fusion = bf16[8,7168]{1,0:T(8,128)(2,1)} fusion(bf16[8,7168]{1,0:T(8,128)(2,1)S(1)} %collective-permute-done.27, bf16[8,7168]{1,0:T(8,128)(2,1)S(1)} %collective-permute-done.26, bf16[8,7168]{1,0:T(8,128)(2,1)S(1)} %collective-permute-done.23, bf16[8,7168]{1,0:T(8,128)(2,1)S(1)} %collective-permute-done.22, bf16[8,7168]{1,0:T(8,128)(2,1)S(1)} %slice.33, ...), kind=kLoop, calls=%fused_computation | loop fusion | flops 688128 | bytes 802816 | tf_op jit(solution)/shard_map/convert_element_type | solution.py:245
  (61 shorter events, 4.0 us)
Async XLA Ops:
  2.7 16.0 %collective-permute-start = (bf16[592,128]{1,0:T(8,128)(2,1)}, bf16[592,128]{1,0:T(8,128)(2,1)S(1)}, u32[]{:S(2)}, u32[]{:S(2)}) collective-permute-start(bf16[592,128]{1,0:T(8,128)(2,1)} %get-tuple-element.35), channel_id=1, source_target_pairs={{0,15},{1,0},{2,1},{3,2},{4,3},{5,4},{6,5},{7,6},{8,7},{9,8},{10,9... | collective-permute-start | bytes 454664 | tf_op jit(solution)/shard_map/ppermute | solution.py:27
  8.1 10.6 %collective-permute-start.1 = (bf16[8,7296]{1,0:T(8,128)(2,1)}, bf16[8,7296]{1,0:T(8,128)(2,1)S(1)}, u32[]{:S(2)}, u32[]{:S(2)}) collective-permute-start(bf16[8,7296]{1,0:T(8,128)(2,1)} %get-tuple-element.36.refs_7_), channel_id=1, source_target_pairs={{0,8},{1,9},{2,10},{3,11},{4,12},{5,13},{6,14},{7,15},{8,0},{9,1},... | collective-permute-start | bytes 350216 | tf_op jit(solution)/shard_map/ppermute | solution.py:27
  8.1 17.8 %collective-permute-start.4 = (bf16[8,7296]{1,0:T(8,128)(2,1)}, bf16[8,7296]{1,0:T(8,128)(2,1)S(1)}, u32[]{:S(2)}, u32[]{:S(2)}) collective-permute-start(bf16[8,7296]{1,0:T(8,128)(2,1)} %get-tuple-element.36.refs_7_), channel_id=1, source_target_pairs={{0,2},{1,3},{2,0},{3,1},{4,6},{5,7},{6,4},{7,5},{8,10},{9,11},{10,... | collective-permute-start | bytes 350216 | tf_op jit(solution)/shard_map/ppermute | solution.py:36
  8.3 17.8 %collective-permute-start.3 = (bf16[8,7296]{1,0:T(8,128)(2,1)}, bf16[8,7296]{1,0:T(8,128)(2,1)S(1)}, u32[]{:S(2)}, u32[]{:S(2)}) collective-permute-start(bf16[8,7296]{1,0:T(8,128)(2,1)} %get-tuple-element.36.refs_7_), channel_id=1, source_target_pairs={{0,12},{1,13},{2,14},{3,15},{4,0},{5,1},{6,2},{7,3},{8,4},{9,5},{1... | collective-permute-start | bytes 350216 | tf_op jit(solution)/shard_map/ppermute | solution.py:27
  9.6 16.4 %collective-permute-start.2 = (bf16[8,7296]{1,0:T(8,128)(2,1)}, bf16[8,7296]{1,0:T(8,128)(2,1)S(1)}, u32[]{:S(2)}, u32[]{:S(2)}) collective-permute-start(bf16[8,7296]{1,0:T(8,128)(2,1)} %get-tuple-element.36.refs_7_), channel_id=1, source_target_pairs={{0,4},{1,5},{2,6},{3,7},{4,8},{5,9},{6,10},{7,11},{8,12},{9,13},{1... | collective-permute-start | bytes 350216 | tf_op jit(solution)/shard_map/ppermute | solution.py:27
  18.7 7.3 %collective-permute-start.5 = (bf16[8,7296]{1,0:T(8,128)(2,1)S(1)}, bf16[8,7296]{1,0:T(8,128)(2,1)S(1)}, u32[]{:S(2)}, u32[]{:S(2)}) collective-permute-start(bf16[8,7296]{1,0:T(8,128)(2,1)S(1)} %collective-permute-done.1.refs_1_), channel_id=1, source_target_pairs={{0,2},{1,3},{2,0},{3,1},{4,6},{5,7},{6,4},{7,5},{8,10},{9,11},{10,... | collective-permute-start | bytes 350216 | tf_op jit(solution)/shard_map/ppermute | solution.py:36
  18.7 9.9 %collective-permute-start.15 = (bf16[8,7296]{1,0:T(8,128)(2,1)}, bf16[8,7296]{1,0:T(8,128)(2,1)S(1)}, u32[]{:S(2)}, u32[]{:S(2)}) collective-permute-start(bf16[8,7296]{1,0:T(8,128)(2,1)} %get-tuple-element.36.refs_7_), channel_id=1, source_target_pairs={{0,1},{1,0},{2,3},{3,2},{4,5},{5,4},{6,7},{7,6},{8,9},{9,8},{10,11... | collective-permute-start | bytes 350216 | tf_op jit(solution)/shard_map/ppermute | solution.py:36
  26.1 3.1 %collective-permute-start.8 = (bf16[8,7296]{1,0:T(8,128)(2,1)S(1)}, bf16[8,7296]{1,0:T(8,128)(2,1)S(1)}, u32[]{:S(2)}, u32[]{:S(2)}) collective-permute-start(bf16[8,7296]{1,0:T(8,128)(2,1)S(1)} %collective-permute-done.5.refs_0_), channel_id=1, source_target_pairs={{0,1},{1,0},{2,3},{3,2},{4,5},{5,4},{6,7},{7,6},{8,9},{9,8},{10,11... | collective-permute-start | bytes 350216 | tf_op jit(solution)/shard_map/ppermute | solution.py:36
  26.6 6.0 %collective-permute-start.6 = (bf16[8,7296]{1,0:T(8,128)(2,1)S(1)}, bf16[8,7296]{1,0:T(8,128)(2,1)S(1)}, u32[]{:S(2)}, u32[]{:S(2)}) collective-permute-start(bf16[8,7296]{1,0:T(8,128)(2,1)S(1)} %collective-permute-done.2.refs_3_), channel_id=1, source_target_pairs={{0,2},{1,3},{2,0},{3,1},{4,6},{5,7},{6,4},{7,5},{8,10},{9,11},{10,... | collective-permute-start | bytes 350216 | tf_op jit(solution)/shard_map/ppermute | solution.py:36
  28.1 6.3 %collective-permute-start.7 = (bf16[8,7296]{1,0:T(8,128)(2,1)S(1)}, bf16[8,7296]{1,0:T(8,128)(2,1)S(1)}, u32[]{:S(2)}, u32[]{:S(2)}) collective-permute-start(bf16[8,7296]{1,0:T(8,128)(2,1)S(1)} %collective-permute-done.3.refs_5_), channel_id=1, source_target_pairs={{0,2},{1,3},{2,0},{3,1},{4,6},{5,7},{6,4},{7,5},{8,10},{9,11},{10,... | collective-permute-start | bytes 350216 | tf_op jit(solution)/shard_map/ppermute | solution.py:36
  28.6 5.7 %collective-permute-start.11 = (bf16[8,7296]{1,0:T(8,128)(2,1)S(1)}, bf16[8,7296]{1,0:T(8,128)(2,1)S(1)}, u32[]{:S(2)}, u32[]{:S(2)}) collective-permute-start(bf16[8,7296]{1,0:T(8,128)(2,1)S(1)} %collective-permute-done.2.refs_3_), channel_id=1, source_target_pairs={{0,1},{1,0},{2,3},{3,2},{4,5},{5,4},{6,7},{7,6},{8,9},{9,8},{10,11... | collective-permute-start | bytes 350216 | tf_op jit(solution)/shard_map/ppermute | solution.py:36
  28.6 5.7 %collective-permute-start.13 = (bf16[8,7296]{1,0:T(8,128)(2,1)S(1)}, bf16[8,7296]{1,0:T(8,128)(2,1)S(1)}, u32[]{:S(2)}, u32[]{:S(2)}) collective-permute-start(bf16[8,7296]{1,0:T(8,128)(2,1)S(1)} %collective-permute-done.3.refs_5_), channel_id=1, source_target_pairs={{0,1},{1,0},{2,3},{3,2},{4,5},{5,4},{6,7},{7,6},{8,9},{9,8},{10,11... | collective-permute-start | bytes 350216 | tf_op jit(solution)/shard_map/ppermute | solution.py:36
  29.2 5.2 %collective-permute-start.14 = (bf16[8,7296]{1,0:T(8,128)(2,1)S(1)}, bf16[8,7296]{1,0:T(8,128)(2,1)S(1)}, u32[]{:S(2)}, u32[]{:S(2)}) collective-permute-start(bf16[8,7296]{1,0:T(8,128)(2,1)S(1)} %collective-permute-done.4.refs_6_), channel_id=1, source_target_pairs={{0,1},{1,0},{2,3},{3,2},{4,5},{5,4},{6,7},{7,6},{8,9},{9,8},{10,11... | collective-permute-start | bytes 350216 | tf_op jit(solution)/shard_map/ppermute | solution.py:36
  37.7 5.4 %collective-permute-start.19 = (bf16[16,7168]{1,0:T(8,128)(2,1)S(1)}, bf16[16,7168]{1,0:T(8,128)(2,1)S(1)}, u32[]{:S(2)}, u32[]{:S(2)}) collective-permute-start(bf16[16,7168]{1,0:T(8,128)(2,1)S(1)} %get-tuple-element.50), channel_id=1, source_target_pairs={{0,1},{1,0},{2,3},{3,2},{4,5},{5,4},{6,7},{7,6},{8,9},{9,8},{10,11... | collective-permute-start | bytes 688136 | tf_op jit(solution)/shard_map/ppermute | solution.py:36
  38.0 2.8 %collective-permute-start.20 = (bf16[16,7168]{1,0:T(8,128)(2,1)S(1)}, bf16[16,7168]{1,0:T(8,128)(2,1)S(1)}, u32[]{:S(2)}, u32[]{:S(2)}) collective-permute-start(bf16[16,7168]{1,0:T(8,128)(2,1)S(1)} %get-tuple-element.52), channel_id=1, source_target_pairs={{0,1},{1,0},{2,3},{3,2},{4,5},{5,4},{6,7},{7,6},{8,9},{9,8},{10,11... | collective-permute-start | bytes 688136 | tf_op jit(solution)/shard_map/ppermute | solution.py:36
  38.2 3.3 %collective-permute-start.24 = (bf16[16,7168]{1,0:T(8,128)(2,1)S(1)}, bf16[16,7168]{1,0:T(8,128)(2,1)S(1)}, u32[]{:S(2)}, u32[]{:S(2)}) collective-permute-start(bf16[16,7168]{1,0:T(8,128)(2,1)S(1)} %get-tuple-element.58), channel_id=1, source_target_pairs={{0,1},{1,0},{2,3},{3,2},{4,5},{5,4},{6,7},{7,6},{8,9},{9,8},{10,11... | collective-permute-start | bytes 688136 | tf_op jit(solution)/shard_map/ppermute | solution.py:36
  39.0 6.1 %collective-permute-start.17 = (bf16[8,7168]{1,0:T(8,128)(2,1)S(1)}, bf16[8,7168]{1,0:T(8,128)(2,1)S(1)}, u32[]{:S(2)}, u32[]{:S(2)}) collective-permute-start(bf16[8,7168]{1,0:T(8,128)(2,1)S(1)} %add_convert_fusion.7), channel_id=1, source_target_pairs={{0,2},{1,3},{2,0},{3,1},{4,6},{5,7},{6,4},{7,5},{8,10},{9,11},{10,... | collective-permute-start | bytes 344072 | tf_op jit(solution)/shard_map/ppermute | solution.py:36
  40.9 6.7 %collective-permute-start.21 = (bf16[8,7168]{1,0:T(8,128)(2,1)S(1)}, bf16[8,7168]{1,0:T(8,128)(2,1)S(1)}, u32[]{:S(2)}, u32[]{:S(2)}) collective-permute-start(bf16[8,7168]{1,0:T(8,128)(2,1)S(1)} %add_convert_fusion.6), channel_id=1, source_target_pairs={{0,2},{1,3},{2,0},{3,1},{4,6},{5,7},{6,4},{7,5},{8,10},{9,11},{10,... | collective-permute-start | bytes 344072 | tf_op jit(solution)/shard_map/ppermute | solution.py:36
  41.6 8.6 %collective-permute-start.25 = (bf16[8,7168]{1,0:T(8,128)(2,1)S(1)}, bf16[8,7168]{1,0:T(8,128)(2,1)S(1)}, u32[]{:S(2)}, u32[]{:S(2)}) collective-permute-start(bf16[8,7168]{1,0:T(8,128)(2,1)S(1)} %add_convert_fusion.3), channel_id=1, source_target_pairs={{0,2},{1,3},{2,0},{3,1},{4,6},{5,7},{6,4},{7,5},{8,10},{9,11},{10,... | collective-permute-start | bytes 344072 | tf_op jit(solution)/shard_map/ppermute | solution.py:36
  45.1 9.3 %collective-permute-start.27 = (bf16[8,7168]{1,0:T(8,128)(2,1)S(1)}, bf16[8,7168]{1,0:T(8,128)(2,1)S(1)}, u32[]{:S(2)}, u32[]{:S(2)}) collective-permute-start(bf16[8,7168]{1,0:T(8,128)(2,1)S(1)} %add_convert_fusion.1), channel_id=1, source_target_pairs={{0,4},{1,5},{2,6},{3,7},{4,8},{5,9},{6,10},{7,11},{8,12},{9,13},{1... | collective-permute-start | bytes 344072 | tf_op jit(solution)/shard_map/ppermute | solution.py:27
  45.2 7.9 %collective-permute-start.18 = (bf16[128,512]{1,0:T(8,128)(2,1)S(1)}, bf16[128,512]{1,0:T(8,128)(2,1)S(1)}, u32[]{:S(2)}, u32[]{:S(2)}) collective-permute-start(bf16[128,512]{1,0:T(8,128)(2,1)S(1)} %copy-done.7), channel_id=1, source_target_pairs={{0,1},{1,2},{2,3},{3,4},{4,5},{5,6},{6,7},{7,8},{8,9},{9,10},{10,1... | collective-permute-start | bytes 393224 | tf_op jit(solution)/shard_map/ppermute | solution.py:27
  47.6 6.9 %collective-permute-start.22 = (bf16[8,7168]{1,0:T(8,128)(2,1)S(1)}, bf16[8,7168]{1,0:T(8,128)(2,1)S(1)}, u32[]{:S(2)}, u32[]{:S(2)}) collective-permute-start(bf16[8,7168]{1,0:T(8,128)(2,1)S(1)} %add_convert_fusion.5), channel_id=1, source_target_pairs={{0,2},{1,3},{2,0},{3,1},{4,6},{5,7},{6,4},{7,5},{8,10},{9,11},{10,... | collective-permute-start | bytes 344072 | tf_op jit(solution)/shard_map/ppermute | solution.py:36
  49.4 8.7 %collective-permute-start.23 = (bf16[8,7168]{1,0:T(8,128)(2,1)S(1)}, bf16[8,7168]{1,0:T(8,128)(2,1)S(1)}, u32[]{:S(2)}, u32[]{:S(2)}) collective-permute-start(bf16[8,7168]{1,0:T(8,128)(2,1)S(1)} %add_convert_fusion.4), channel_id=1, source_target_pairs={{0,8},{1,9},{2,10},{3,11},{4,12},{5,13},{6,14},{7,15},{8,0},{9,1},... | collective-permute-start | bytes 344072 | tf_op jit(solution)/shard_map/ppermute | solution.py:27
  50.2 7.8 %collective-permute-start.26 = (bf16[8,7168]{1,0:T(8,128)(2,1)S(1)}, bf16[8,7168]{1,0:T(8,128)(2,1)S(1)}, u32[]{:S(2)}, u32[]{:S(2)}) collective-permute-start(bf16[8,7168]{1,0:T(8,128)(2,1)S(1)} %add_convert_fusion.2), channel_id=1, source_target_pairs={{0,12},{1,13},{2,14},{3,15},{4,0},{5,1},{6,2},{7,3},{8,4},{9,5},{1... | collective-permute-start | bytes 344072 | tf_op jit(solution)/shard_map/ppermute | solution.py:27
  (12 other events, 130.9 us)
